TPU v7x, 256 devices: a whole 4x4x8 slice. The times are simulated.
256 devices in a mesh: row: 8 (over x, y_lo), col: 16 (over z, core), slab: 2 (over y_hi).
Axes of the slice: x: 4, y: 4 (y_hi: 2, y_lo: 2; y = y_hi * 2 + y_lo), z: 8, core: 2. Of those that a mesh axis runs over, the one named last changes fastest.
Arguments:
- iterate: bfloat16 [4096, 9216], P(('row', 'col'), 'slab'), as said below
Outputs:
- update: bfloat16 [4096, 9216], P(('row', 'col'), 'slab')
Inputs may be any that keep to these rules, and one draw needn't show every extreme that they name: `iterate`: entries lie within plus or minus 3 / sqrt(9216).
All inputs are finite; a program needn't handle non-finite values.
Results may differ from a plain program's by a relative error of at most 0.0056.
Values may be sent and summed in bfloat16 or wider, within the bound.
No kernel may reach another device: no remote copies, remote signals or barrier semaphores. Data moves between devices by JAX's collectives and lax.ppermute only.
A program may use at most 64 MiB of HBM per device.

v0:
```python
import math

import jax
import jax.numpy as jnp
from jax import lax
from jax.sharding import PartitionSpec as P

coef_linear = 3.4445
coef_cubic = -4.775
coef_quintic = 2.0315
update_gain = 0.2 * math.sqrt(18432.0)


def sum_partner(poly_tile, operand):
    return lax.psum_scatter(
        jnp.dot(poly_tile, operand, preferred_element_type=jnp.float32),
        "col",
        scatter_dimension=0,
        tiled=True,
    )


def on_device(iterate):
    rows_dev = iterate.shape[0]
    row_count_axis = lax.axis_size("row")
    col_count_axis = lax.axis_size("col")
    own_rows = lax.all_gather(iterate, "col", axis=0, tiled=True)
    partner_rows = lax.all_gather(iterate, "row", axis=0, tiled=True)
    gram_part = lax.dot_general(
        own_rows, partner_rows, (((1,), (1,)), ((), ())), preferred_element_type=jnp.float32
    )
    gram_tile = lax.psum(gram_part, "slab").astype(jnp.bfloat16)
    tile_width = gram_tile.shape[1]
    column_block = lax.all_gather(gram_tile, "row", axis=0, tiled=True)
    grouped = column_block.reshape(row_count_axis, col_count_axis, rows_dev, tile_width)
    piece = lax.all_gather(gram_tile, "col", axis=1, tiled=True)
    count = piece.shape[1] // tile_width
    split = piece.reshape(piece.shape[0], count, row_count_axis, rows_dev)
    squared = jnp.einsum("iqab,aqbn->in", split, grouped, preferred_element_type=jnp.float32)
    poly_tile = (coef_cubic * gram_tile.astype(jnp.float32) + coef_quintic * squared).astype(
        jnp.bfloat16
    )
    applied = sum_partner(poly_tile, partner_rows)
    stepped = coef_linear * iterate.astype(jnp.float32) + applied
    return (update_gain * stepped).astype(jnp.bfloat16)


def solution(mesh):
    in_specs = (P(("row", "col"), "slab"),)
    out_specs = P(("row", "col"), "slab")
    return jax.shard_map(
        on_device, mesh=mesh, in_specs=in_specs, out_specs=out_specs, check_vma=False
    )
```

profile of v0, /device:TPU:1, one launch (start us, length us, event | category | flops | bytes accessed | tf_op | source)
XLA Modules:
  0.0 332.9 jit_solution(8615057409325133809)
XLA Ops:
  6.5 0.0 all-gather.7.cloned.1.call-start
  6.5 0.7 all-gather.7.cloned.1.call-update
  7.3 0.0 all-gather.5.cloned.1.call-start
  7.3 0.7 all-gather.5.cloned.1.call-update
  8.0 0.0 all-gather.9.cloned.1.call-start
  8.1 62.5 %all-gather.7.cloned.1.call-done = bf16[256,4608]{1,0:T(8,128)(2,1)} async-done(((bf16[32,4608]{1,0:T(8,128)(2,1)}), bf16[256,4608]{1,0:T(8,128)(2,1)}) %all-gather.7.cloned.1.call-update) | async-done | bytes 2359312 | tf_op jit(solution)/shard_map/all_gather | solution.py:28
  70.6 46.3 %all-gather.5.cloned.1.call-done = bf16[512,4608]{1,0:T(8,128)(2,1)} async-done(((bf16[32,4608]{1,0:T(8,128)(2,1)}), bf16[512,4608]{1,0:T(8,128)(2,1)}) %all-gather.5.cloned.1.call-update) | async-done | bytes 4718608 | tf_op jit(solution)/shard_map/all_gather | solution.py:27
  116.8 4.5 %fusion.23 = f32[512,256]{1,0:T(8,128)S(1)} fusion(bf16[512,4608]{1,0:T(8,128)(2,1)} %all-gather.5.cloned.1.call-done, bf16[256,4608]{1,0:T(8,128)(2,1)} %all-gather.7.cloned.1.call-done), kind=kOutput, calls=%fused_computation.14 | convolution fusion | flops 1207959552 | bytes 7602176 | tf_op jit(solution)/shard_map/dot_general | solution.py:29
  121.4 20.1 %all-reduce.1 = bf16[512,256]{1,0:T(8,128)(2,1)} all-reduce(f32[512,256]{1,0:T(8,128)S(1)} %fusion.23), channel_id=1, replica_groups=mesh['row'=8,'col'=16,'slab'=2] {'slab'}, use_global_device_ids=true, to_apply=%region_0.0 | all-reduce | flops 131072 | bytes 786432 | tf_op jit(solution)/shard_map/psum | solution.py:32
  141.5 0.0 all-gather.9.cloned.1.call-update
  141.5 0.0 all-gather.11.cloned.1.call-start
  141.6 0.5 all-gather.11.cloned.1.call-update
  142.1 0.0 copy-start.1
  142.1 0.0 copy-start.2
  142.1 0.0 reduce-scatter.2.cloned.1.call-start
  142.2 47.0 %all-gather.9.cloned.1.call-done = bf16[512,4096]{1,0:T(8,128)(2,1)} async-done(((bf16[512,256]{1,0:T(8,128)(2,1)}), bf16[512,4096]{1,0:T(8,128)(2,1)}) %all-gather.9.cloned.1.call-update) | async-done | bytes 4194320 | tf_op jit(solution)/shard_map/all_gather | solution.py:36
  189.2 6.6 %copy.2 = bf16[512,4096]{0,1:T(8,128)(2,1)} copy(bf16[512,4096]{1,0:T(8,128)(2,1)} %all-gather.9.cloned.1.call-done) | data formatting | bytes 8388608 | tf_op jit(solution)/shard_map/all_gather | solution.py:36
  195.8 46.1 %all-gather.11.cloned.1.call-done = bf16[4096,256]{1,0:T(8,128)(2,1)} async-done(((bf16[512,256]{1,0:T(8,128)(2,1)}), bf16[4096,256]{1,0:T(8,128)(2,1)}) %all-gather.11.cloned.1.call-update) | async-done | bytes 2097168 | tf_op jit(solution)/shard_map/all_gather | solution.py:34
  241.9 0.0 copy-done.1
  241.9 0.0 copy-done.2
  241.9 11.2 %fusion.15 = f32[512,4608]{1,0:T(8,128)} fusion(bf16[256,4608]{1,0:T(8,128)(2,1)S(1)} %copy-done.2, bf16[8,16,32,256]{3,2,1,0:T(8,128)(2,1)} %bitcast.19, bf16[512,16,8,32]{0,3,2,1:T(8,128)(2,1)} %bitcast.18, bf16[512,256]{1,0:T(8,128)(2,1)S(1)} %copy-done.1), kind=kOutput, calls=%fused_computation.6 | convolution fusion | flops 2282356736 | bytes 18350080 | tf_op jit(solution)/shard_map/dot_general | solution.py:16
  253.1 0.0 copy-start
  253.1 0.0 reduce-scatter.2.cloned.1.call-update
  253.1 71.4 %reduce-scatter.2.cloned.1.call-done = f32[32,4608]{1,0:T(8,128)} async-done(((f32[512,4608]{1,0:T(8,128)}), f32[32,4608]{1,0:T(8,128)}) %reduce-scatter.2.cloned.1.call-update) | async-done | bytes 589840 | tf_op jit(solution)/shard_map/reduce_scatter | solution.py:15
  324.5 0.0 copy-done
  324.5 1.9 multiply_convert_fusion
Async XLA Ops:
  6.5 64.1 %all-gather.7.cloned.1.call-start = ((), (), s32[]{:S(2)}) async-start(), calls=%async_computation.2 | async-start | bytes 2654208 | tf_op jit(solution)/shard_map/all_gather | solution.py:28
  7.3 109.6 %all-gather.5.cloned.1.call-start = ((), (), s32[]{:S(2)}) async-start(), calls=%async_computation.1 | async-start | bytes 5013504 | tf_op jit(solution)/shard_map/all_gather | solution.py:27
  8.0 181.2 %all-gather.9.cloned.1.call-start = ((), (), s32[]{:S(2)}) async-start(), calls=%async_computation.3 | async-start | bytes 4456448 | tf_op jit(solution)/shard_map/all_gather | solution.py:36
  141.5 100.4 %all-gather.11.cloned.1.call-start = ((), (), s32[]{:S(2)}) async-start(), calls=%async_computation.4 | async-start | bytes 2359296 | tf_op jit(solution)/shard_map/all_gather | solution.py:34
  142.1 99.8 %copy-start.1 = (bf16[512,256]{1,0:T(8,128)(2,1)S(1)}, bf16[512,256]{1,0:T(8,128)(2,1)}, u32[]{:S(2)}) copy-start(bf16[512,256]{1,0:T(8,128)(2,1)} %all-reduce.1) | copy-start | bytes 786436
  142.1 99.8 %copy-start.2 = (bf16[256,4608]{1,0:T(8,128)(2,1)S(1)}, bf16[256,4608]{1,0:T(8,128)(2,1)}, u32[]{:S(2)}) copy-start(bf16[256,4608]{1,0:T(8,128)(2,1)} %all-gather.7.cloned.1.call-done) | copy-start | bytes 7077892
  142.1 182.3 %reduce-scatter.2.cloned.1.call-start = ((), (), s32[]{:S(2)}) async-start(), calls=%async_computation.5 | async-start | bytes 10027008 | tf_op jit(solution)/shard_map/reduce_scatter | solution.py:15
  253.1 71.4 %copy-start = (bf16[32,4608]{1,0:T(8,128)(2,1)S(1)}, bf16[32,4608]{1,0:T(8,128)(2,1)}, u32[]{:S(2)}) copy-start(bf16[32,4608]{1,0:T(8,128)(2,1)} %param.1) | copy-start | bytes 884740
Sparse Core Ops, SparseCore 0:
  9.1 61.3 all-gather.6
  72.4 44.3 all-gather.4
  141.6 47.5 all-gather.8
  190.9 51.0 all-gather.10
  253.2 71.2 reduce-scatter.1
where the time goes:
time: 335 us; the launch traced here: 333 us
  waiting for transfers between devices  275 us (82%)
  blocking collectives  20.1 us (6%)
  matrix products  15.7 us (5%)
  between operations  13.2 us (4%)
  local copies, waits for them, and re-layouts  6.57 us (2%)
    reduce_scatter x1, waiting for transfers between devices, sum_partner(): lax.psum_scatter(jnp.dot(poly_tile, operand, preferred_element_type=jnp.f...  71.4 us
    all_gather x1, waiting for transfers between devices, on_device(): partner_rows = lax.all_gather(iterate, 'row', axis=0, tiled=True)  62.5 us
    all_gather x1, waiting for transfers between devices, on_device(): piece = lax.all_gather(gram_tile, 'col', axis=1, tiled=True)  47 us
    all_gather x1, waiting for transfers between devices, on_device(): own_rows = lax.all_gather(iterate, 'col', axis=0, tiled=True)  46.3 us
    all_gather x1, waiting for transfers between devices, on_device(): column_block = lax.all_gather(gram_tile, 'row', axis=0, tiled=True)  46.1 us
    psum x1, blocking collectives, on_device(): gram_tile = lax.psum(gram_part, 'slab').astype(jnp.bfloat16)  20.1 us
    dot_general x1, matrix products, sum_partner(): jnp.dot(poly_tile, operand, preferred_element_type=jnp.float32)  11.2 us
  transfers between devices with their start and end apart: 5, of which 5 were waited for; matrix products, arithmetic and copies ran while one was open for 2% of the time, Pallas kernels for 0%

commit v1 on v0

v1 whole, which is shorter than its diff:
```python
import math

import jax
import jax.numpy as jnp
from jax import lax
from jax.sharding import Mesh
from jax.sharding import PartitionSpec as P

coef_linear = 3.4445
coef_cubic = -4.775
coef_quintic = 2.0315
update_gain = 0.2 * math.sqrt(18432.0)

X, YL, Z, C, S = "x", "yl", "z", "c", "s"
NZ, NR = 8, 8
bf16, f32 = jnp.bfloat16, jnp.float32
COLS_Z = 768


def swap(a, axis):
    return lax.ppermute(a, axis, [(0, 1), (1, 0)])


def shift(a, axis, n, d):
    return lax.ppermute(a, axis, [((i + d) % n, i) for i in range(n)])


def ring_z(a):
    out = [None] * NZ
    out[0] = up = down = a
    for step in range(1, 4):
        up = shift(up, Z, NZ, 1)
        down = shift(down, Z, NZ, -1)
        out[step], out[NZ - step] = up, down
    half = a.shape[0] // 2
    out[4] = jnp.concatenate([shift(up[:half], Z, NZ, 1), shift(down[half:], Z, NZ, -1)])
    return out


def gather_r(a):
    copies = jnp.broadcast_to(a[None], (NR, *a.shape))
    return lax.all_to_all(copies, (X, YL), 0, 0, tiled=True)


def dot_t(a, b):
    return lax.dot_general(a, b, (((1,), (1,)), ((), ())), preferred_element_type=f32)


def on_device(iterate):
    core, z = lax.axis_index(C), lax.axis_index(Z)
    mine = lax.all_to_all(iterate, C, 1, 0, tiled=True)
    x_rows = lax.all_gather(mine, Z, axis=0, tiled=True)
    x_cols = gather_r(mine)
    halves = [x_cols[:, 32 * h : 32 * h + 32].reshape(256, -1) for h in (0, 1)]
    part = [dot_t(x_rows, h) for h in halves]

    first = core == 0
    own = jnp.where(first, part[0], part[1])
    other = jnp.where(first, part[1], part[0]).astype(bf16)
    own = own + swap(other, C).astype(f32)
    sent = own.astype(bf16)
    gram = (own + swap(sent, S).astype(f32)).astype(bf16)
    gram_o = swap(gram, C)
    g0 = jnp.where(first, gram, gram_o)
    g1 = jnp.where(first, gram_o, gram)
    tile = jnp.concatenate([g0, g1], axis=1)
    rows = lax.dynamic_index_in_dim(tile.reshape(NZ, 2, 32, 512), core, 1, keepdims=False)
    row_block = rows.reshape(256, 512)

    a_shards = ring_z(gram)
    b_all = gather_r(row_block).reshape(NR, NZ, 32, 512)
    squared = jnp.zeros((512, 512), f32)
    for d in range(NZ):
        b = lax.dynamic_index_in_dim(b_all, (z + d) % NZ, 1, keepdims=False).reshape(256, 512)
        squared = squared + jnp.dot(a_shards[d], b, preferred_element_type=f32)
    squared = squared + swap(squared.astype(bf16), C).astype(f32)
    poly = (coef_cubic * tile.astype(f32) + coef_quintic * squared).astype(bf16)

    x_ord = jnp.concatenate(halves, axis=0)
    part_z = jnp.dot(poly, x_ord[:, :COLS_Z], preferred_element_type=f32).astype(bf16)
    sum_z = lax.psum_scatter(part_z, Z, scatter_dimension=0, tiled=True).astype(f32)
    part_r = lax.dot_general(
        poly, x_rows[:, COLS_Z:], (((0,), (0,)), ((), ())), preferred_element_type=f32
    ).astype(bf16)
    part_r = part_r.reshape(2, NR, 32, -1).transpose(1, 0, 2, 3)
    sum_r = lax.all_to_all(part_r, (X, YL), 0, 0, tiled=True).astype(f32).sum(0).reshape(64, -1)
    applied = jnp.concatenate([sum_z, sum_r], axis=1)
    stepped = coef_linear * mine.astype(f32) + applied
    out = (update_gain * stepped).astype(bf16)
    return lax.all_to_all(out, C, 0, 1, tiled=True)


def solution(mesh):
    fine = Mesh(mesh.devices.reshape(4, 2, 8, 2, 2), (X, YL, Z, C, S))
    spec = P((X, YL, Z, C), S)
    return jax.shard_map(on_device, mesh=fine, in_specs=(spec,), out_specs=spec, check_vma=False)
```

time: 335 us -> 182 us (0.54)
  waiting for transfers between devices: 275 us -> 67.4 us
  starting transfers between devices: 0.16 us -> 29.6 us
  blocking collectives: 20.1 us -> 39.7 us
  local copies, waits for them, and re-layouts: 6.57 us -> 14 us
    all_gather x4 -> x1, waiting for transfers between devices: 202 us -> 0.01 us  [on_device(): x_rows = lax.all_gather(mine, Z, axis=0, tiled=True)]
    reduce_scatter x1, waiting for transfers between devices: 71.4 us -> 5.71 us  [on_device(): lax.psum_scatter(part_z, Z, scatter_dimension=0, tiled=True).astype(f32)]
    all_to_all x0 -> x3, blocking collectives: none -> 39.7 us  [the longest x1 23.9 us: on_device(): lax.all_to_all(part_r, (X, YL), 0, 0, tiled=True).astype(f32).sum(0)]
    all_to_all x0 -> x2, waiting for transfers between devices: none -> 34.6 us  [gather_r(): return lax.all_to_all(copies, (X, YL), 0, 0, tiled=True)]
    ppermute x0 -> x12, waiting for transfers between devices: none -> 27.1 us  [the longest x8 16.9 us: shift(): return lax.ppermute(a, axis, [((i + d) % n, i) for i in range(n)])]
    ppermute x0 -> x12, starting transfers between devices: none -> 21 us  [the longest x8 12.1 us: shift(): return lax.ppermute(a, axis, [((i + d) % n, i) for i in range(n)])]
    psum x1 -> x0, blocking collectives: 20.1 us -> none  [on_device(): gram_tile = lax.psum(gram_part, 'slab').astype(jnp.bfloat16)]
    all_to_all x0 -> x2, starting transfers between devices: none -> 8.49 us  [gather_r(): return lax.all_to_all(copies, (X, YL), 0, 0, tiled=True)]
  transfers between devices with their start and end apart: 5 -> 16, of which waited for: 5 -> 9; matrix products, arithmetic and copies ran while one was open for 2% -> 7% of each run, Pallas kernels for 0% -> 0%
where the time goes in v1:
time: 182 us; the launch traced here: 181 us
  waiting for transfers between devices  67.4 us (37%)
  blocking collectives  39.7 us (22%)
  starting transfers between devices  29.6 us (16%)
  matrix products  14.9 us (8%)
  local copies, waits for them, and re-layouts  14 us (8%)
  between operations  13.7 us (8%)
  other arithmetic  1.85 us (1%)
    all_to_all x2, waiting for transfers between devices, gather_r(): return lax.all_to_all(copies, (X, YL), 0, 0, tiled=True)  34.6 us
    all_to_all x1, blocking collectives, on_device(): lax.all_to_all(part_r, (X, YL), 0, 0, tiled=True).astype(f32).sum(0)  23.9 us
    ppermute x8, waiting for transfers between devices, shift(): return lax.ppermute(a, axis, [((i + d) % n, i) for i in range(n)])  16.9 us
    ppermute x8, starting transfers between devices, shift(): return lax.ppermute(a, axis, [((i + d) % n, i) for i in range(n)])  12.1 us
    ppermute x4, waiting for transfers between devices, swap(): return lax.ppermute(a, axis, [(0, 1), (1, 0)])  10.2 us
    ppermute x4, starting transfers between devices, swap(): return lax.ppermute(a, axis, [(0, 1), (1, 0)])  8.93 us
    all_to_all x2, starting transfers between devices, gather_r(): return lax.all_to_all(copies, (X, YL), 0, 0, tiled=True)  8.49 us
    all_to_all x1, blocking collectives, on_device(): return lax.all_to_all(out, C, 0, 1, tiled=True)  8.21 us
  transfers between devices with their start and end apart: 16, of which 9 were waited for; matrix products, arithmetic and copies ran while one was open for 7% of the time, Pallas kernels for 0%

profile of v1, /device:TPU:1, one launch (start us, length us, event | category | flops | bytes accessed | tf_op | source)
XLA Modules:
  0.0 181.1 jit_solution(17583313675064705943)
XLA Ops:
  7.5 7.6 %all_to_all.50 = bf16[32,2,2304]{2,0,1:T(8,128)(2,1)} all-to-all(bf16[32,2,2304]{2,0,1:T(8,128)(2,1)S(1)} %bitcast.62), channel_id=1, replica_groups=mesh['x'=4,'yl'=2,'z'=8,'c'=2,'s'=2] {'c'}, dimensions={1} | all-to-all | bytes 589824 | tf_op jit(solution)/shard_map/all_to_all | solution.py:51
  15.1 2.6 %broadcast_in_dim.6 = bf16[8,64,2304]{2,1,0:T(8,128)(2,1)} broadcast(bf16[64,2304]{1,0:T(8,128)(2,1)} %bitcast.58), dimensions={1,2} | broadcast | bytes 2654208 | tf_op jit(solution)/shard_map/broadcast_in_dim | solution.py:41
  17.7 3.6 %all-to-all-start.1 = ((bf16[8,64,2304]{2,1,0:T(8,128)(2,1)}), bf16[8,64,2304]{2,1,0:T(8,128)(2,1)S(1)}, u32[]{:S(2)}, u32[]{:S(2)}) async-start(bf16[8,64,2304]{2,1,0:T(8,128)(2,1)} %broadcast_in_dim.6), calls=%async_computation.1 | async-start | bytes 4718592 | tf_op jit(solution)/shard_map/all_to_all | solution.py:42
  21.3 34.6 %all-to-all-done.1 = bf16[8,64,2304]{2,1,0:T(8,128)(2,1)S(1)} async-done(((bf16[8,64,2304]{2,1,0:T(8,128)(2,1)}), bf16[8,64,2304]{2,1,0:T(8,128)(2,1)S(1)}, u32[]{:S(2)}, u32[]{:S(2)}) %all-to-all-start.1) | async-done | bytes 2359328 | tf_op jit(solution)/shard_map/all_to_all | solution.py:42
  57.1 2.9 %fusion.16 = f32[512,256]{0,1:T(8,128)S(1)} fusion(bf16[512,2304]{1,0:T(8,128)(2,1)} %all-gather.2.cloned.1.call-done, bf16[256,2304]{1,0:T(8,128)(2,1)} %bitcast.55), kind=kOutput, calls=%fused_computation.43 | convolution fusion | flops 603979776 | bytes 4063232 | tf_op jit(solution)/shard_map/dot_general | solution.py:46
  60.8 1.5 collective-permute-start
  63.6 2.8 %collective-permute-start.1 = (bf16[512,256]{0,1:T(8,128)(2,1)S(1)}, bf16[512,256]{0,1:T(8,128)(2,1)S(1)}, u32[]{:S(2)}, u32[]{:S(2)}) collective-permute-start(bf16[512,256]{0,1:T(8,128)(2,1)S(1)} %fusion.11), channel_id=1, source_target_pairs={{0,1},{1,0},{2,3},{3,2},{4,5},{5,4},{6,7},{7,6},{8,9},{9,8},{10,11... | collective-permute-start | bytes 786440 | tf_op jit(solution)/shard_map/ppermute | solution.py:21
  66.4 6.3 %collective-permute-done.1 = bf16[512,256]{0,1:T(8,128)(2,1)S(1)} collective-permute-done((bf16[512,256]{0,1:T(8,128)(2,1)S(1)}, bf16[512,256]{0,1:T(8,128)(2,1)S(1)}, u32[]{:S(2)}, u32[]{:S(2)}) %collective-permute-start.1) | collective-permute-done | bytes 262176 | tf_op jit(solution)/shard_map/ppermute | solution.py:21
  72.9 1.3 collective-permute-start.2
  76.4 1.5 broadcast_in_dim.15
  77.9 4.9 %all-to-all-start.2 = ((bf16[8,256,512]{2,1,0:T(8,128)(2,1)}), bf16[8,256,512]{2,1,0:T(8,128)(2,1)S(1)}, u32[]{:S(2)}, u32[]{:S(2)}) async-start(bf16[8,256,512]{2,1,0:T(8,128)(2,1)} %broadcast_in_dim.15), calls=%async_computation.2 | async-start | bytes 4194304 | tf_op jit(solution)/shard_map/all_to_all | solution.py:42
  83.7 3.1 %collective-permute-start.3 = (bf16[512,256]{0,1:T(8,128)(2,1)}, bf16[512,256]{0,1:T(8,128)(2,1)S(1)}, u32[]{:S(2)}, u32[]{:S(2)}) collective-permute-start(bf16[512,256]{0,1:T(8,128)(2,1)} %copy-done.6), channel_id=1, source_target_pairs={{4,0},{8,4},{12,8},{16,12},{20,16},{24,20},{28,24},{0,28},{5,1},{9... | collective-permute-start | bytes 786440 | tf_op jit(solution)/shard_map/ppermute | solution.py:25
  86.9 6.5 %collective-permute-done.7 = bf16[512,256]{0,1:T(8,128)(2,1)S(1)} collective-permute-done((bf16[512,256]{0,1:T(8,128)(2,1)}, bf16[512,256]{0,1:T(8,128)(2,1)S(1)}, u32[]{:S(2)}, u32[]{:S(2)}) %collective-permute-start.7) | collective-permute-done | bytes 262176 | tf_op jit(solution)/shard_map/ppermute | solution.py:25
  94.1 2.7 %collective-permute-start.4 = (bf16[512,256]{0,1:T(8,128)(2,1)S(1)}, bf16[512,256]{0,1:T(8,128)(2,1)}, u32[]{:S(2)}, u32[]{:S(2)}) collective-permute-start(bf16[512,256]{0,1:T(8,128)(2,1)S(1)} %collective-permute-done.3), channel_id=1, source_target_pairs={{4,0},{8,4},{12,8},{16,12},{20,16},{24,20},{28,24},{0,28},{5,1},{9... | collective-permute-start | bytes 786440 | tf_op jit(solution)/shard_map/ppermute | solution.py:25
  96.8 5.6 %collective-permute-done.8 = bf16[512,256]{0,1:T(8,128)(2,1)} collective-permute-done((bf16[512,256]{0,1:T(8,128)(2,1)S(1)}, bf16[512,256]{0,1:T(8,128)(2,1)}, u32[]{:S(2)}, u32[]{:S(2)}) %collective-permute-start.8) | collective-permute-done | bytes 262176 | tf_op jit(solution)/shard_map/ppermute | solution.py:25
  102.4 2.7 %collective-permute-start.5 = (bf16[512,256]{0,1:T(8,128)(2,1)}, bf16[512,256]{0,1:T(8,128)(2,1)}, u32[]{:S(2)}, u32[]{:S(2)}) collective-permute-start(bf16[512,256]{0,1:T(8,128)(2,1)} %collective-permute-done.4), channel_id=1, source_target_pairs={{4,0},{8,4},{12,8},{16,12},{20,16},{24,20},{28,24},{0,28},{5,1},{9... | collective-permute-start | bytes 786440 | tf_op jit(solution)/shard_map/ppermute | solution.py:25
  105.0 4.9 %collective-permute-done.9 = bf16[512,256]{0,1:T(8,128)(2,1)} collective-permute-done((bf16[512,256]{0,1:T(8,128)(2,1)}, bf16[512,256]{0,1:T(8,128)(2,1)}, u32[]{:S(2)}, u32[]{:S(2)}) %collective-permute-start.9) | collective-permute-done | bytes 262176 | tf_op jit(solution)/shard_map/ppermute | solution.py:25
  109.9 1.6 slice.27
  111.5 1.6 slice.26
  113.0 2.7 %collective-permute-start.6 = (bf16[256,256]{0,1:T(8,128)(2,1)}, bf16[256,256]{0,1:T(8,128)(2,1)}, u32[]{:S(2)}, u32[]{:S(2)}) collective-permute-start(bf16[256,256]{0,1:T(8,128)(2,1)} %slice.26), channel_id=1, source_target_pairs={{4,0},{8,4},{12,8},{16,12},{20,16},{24,20},{28,24},{0,28},{5,1},{9... | collective-permute-start | bytes 393224 | tf_op jit(solution)/shard_map/ppermute | solution.py:25
  117.4 1.3 fusion.18
  118.7 1.3 convolution_add_fusion.2
  120.4 1.3 fusion.7
  121.7 1.3 fusion.2
  123.0 1.4 fusion.15
  124.4 3.4 %collective-permute-start.11 = (bf16[512,512]{0,1:T(8,128)(2,1)S(1)}, bf16[512,512]{0,1:T(8,128)(2,1)S(1)}, u32[]{:S(2)}, u32[]{:S(2)}) collective-permute-start(bf16[512,512]{0,1:T(8,128)(2,1)S(1)} %get-tuple-element.19), channel_id=1, source_target_pairs={{0,2},{2,0},{1,3},{3,1},{4,6},{6,4},{5,7},{7,5},{8,10},{10,8},{9,1... | collective-permute-start | bytes 1572872 | tf_op jit(solution)/shard_map/ppermute | solution.py:21
  127.8 1.5 collective-permute-done.11
  130.4 1.5 convolution_convert_fusion.1
  132.3 2.0 %convolution_convert_fusion = bf16[512,1536]{1,0:T(8,128)(2,1)S(1)} fusion(bf16[512,512]{0,1:T(8,128)(2,1)} %copy-done.8, bf16[512,2304]{1,0:T(8,128)(2,1)S(1)} %copy-done.3), kind=kOutput, calls=%fused_computation.1 | convolution fusion | flops 806092800 | bytes 3670016 | tf_op jit(solution)/shard_map/dot_general | solution.py:82
  134.4 23.9 %all_to_all.51 = bf16[8,2,32,1536]{3,2,1,0:T(8,128)(2,1)S(1)} all-to-all(bf16[8,2,32,1536]{3,2,1,0:T(8,128)(2,1)S(1)} %bitcast.54), channel_id=1, replica_groups=mesh['x'=4,'yl'=2,'z'=8,'c'=2,'s'=2] {'x','yl'}, dimensions={0} | all-to-all | bytes 3145728 | tf_op jit(solution)/shard_map/all_to_all | solution.py:86
  158.5 5.7 %reduce-scatter.2.cloned.1.call-done = bf16[64,768]{1,0:T(8,128)(2,1)} async-done(((bf16[512,768]{1,0:T(8,128)(2,1)}), bf16[64,768]{1,0:T(8,128)(2,1)}) %reduce-scatter.2.cloned.1.call-update) | async-done | bytes 98320 | tf_op jit(solution)/shard_map/reduce_scatter | solution.py:81
  165.3 8.2 %all_to_all.52 = bf16[2,32,2304]{2,1,0:T(8,128)(2,1)S(1)} all-to-all(bf16[2,32,2304]{2,1,0:T(8,128)(2,1)S(1)} %fusion.6), channel_id=1, replica_groups=mesh['x'=4,'yl'=2,'z'=8,'c'=2,'s'=2] {'c'}, dimensions={0} | all-to-all | bytes 589824 | tf_op jit(solution)/shard_map/all_to_all | solution.py:90
  (62 shorter events, 13.8 us)
Async XLA Ops:
  6.5 50.5 %all-gather.2.cloned.1.call-start = ((), (), s32[]{:S(2)}) async-start(), calls=%async_computation.6 | async-start | bytes 2654208 | tf_op jit(solution)/shard_map/all_gather | solution.py:52
  17.7 38.2 %all-to-all-start.1 = ((bf16[8,64,2304]{2,1,0:T(8,128)(2,1)}), bf16[8,64,2304]{2,1,0:T(8,128)(2,1)S(1)}, u32[]{:S(2)}, u32[]{:S(2)}) async-start(bf16[8,64,2304]{2,1,0:T(8,128)(2,1)} %broadcast_in_dim.6), calls=%async_computation.1 | async-start | bytes 4718592 | tf_op jit(solution)/shard_map/all_to_all | solution.py:42
  57.1 2.9 %copy-start.2 = (bf16[512,2304]{1,0:T(8,128)(2,1)S(1)}, bf16[512,2304]{1,0:T(8,128)(2,1)}, u32[]{:S(2)}) copy-start(bf16[512,2304]{1,0:T(8,128)(2,1)} %all-gather.2.cloned.1.call-done) | copy-start | bytes 7077892
  60.8 2.6 %collective-permute-start = (bf16[512,256]{0,1:T(8,128)(2,1)S(1)}, bf16[512,256]{0,1:T(8,128)(2,1)S(1)}, u32[]{:S(2)}, u32[]{:S(2)}) collective-permute-start(bf16[512,256]{0,1:T(8,128)(2,1)S(1)} %get-tuple-element.17), channel_id=1, source_target_pairs={{0,2},{2,0},{1,3},{3,1},{4,6},{6,4},{5,7},{7,5},{8,10},{10,8},{9,1... | collective-permute-start | bytes 786440 | tf_op jit(solution)/shard_map/ppermute | solution.py:21
  63.6 9.1 %collective-permute-start.1 = (bf16[512,256]{0,1:T(8,128)(2,1)S(1)}, bf16[512,256]{0,1:T(8,128)(2,1)S(1)}, u32[]{:S(2)}, u32[]{:S(2)}) collective-permute-start(bf16[512,256]{0,1:T(8,128)(2,1)S(1)} %fusion.11), channel_id=1, source_target_pairs={{0,1},{1,0},{2,3},{3,2},{4,5},{5,4},{6,7},{7,6},{8,9},{9,8},{10,11... | collective-permute-start | bytes 786440 | tf_op jit(solution)/shard_map/ppermute | solution.py:21
  72.9 3.5 %copy-start.6 = (bf16[512,256]{0,1:T(8,128)(2,1)}, bf16[512,256]{0,1:T(8,128)(2,1)S(1)}, u32[]{:S(2)}) copy-start(bf16[512,256]{0,1:T(8,128)(2,1)S(1)} %add_convert_fusion.1) | copy-start | bytes 786436
  72.9 2.5 %collective-permute-start.2 = (bf16[512,256]{0,1:T(8,128)(2,1)S(1)}, bf16[512,256]{0,1:T(8,128)(2,1)S(1)}, u32[]{:S(2)}, u32[]{:S(2)}) collective-permute-start(bf16[512,256]{0,1:T(8,128)(2,1)S(1)} %add_convert_fusion.1), channel_id=1, source_target_pairs={{0,2},{2,0},{1,3},{3,1},{4,6},{6,4},{5,7},{7,5},{8,10},{10,8},{9,1... | collective-permute-start | bytes 786440 | tf_op jit(solution)/shard_map/ppermute | solution.py:21
  75.4 0.7 copy-start.4
  77.9 37.8 %all-to-all-start.2 = ((bf16[8,256,512]{2,1,0:T(8,128)(2,1)}), bf16[8,256,512]{2,1,0:T(8,128)(2,1)S(1)}, u32[]{:S(2)}, u32[]{:S(2)}) async-start(bf16[8,256,512]{2,1,0:T(8,128)(2,1)} %broadcast_in_dim.15), calls=%async_computation.2 | async-start | bytes 4194304 | tf_op jit(solution)/shard_map/all_to_all | solution.py:42
  82.8 81.5 %reduce-scatter.2.cloned.1.call-start = ((), (), s32[]{:S(2)}) async-start(), calls=%async_computation.7 | async-start | bytes 884736 | tf_op jit(solution)/shard_map/reduce_scatter | solution.py:81
  82.8 10.6 %collective-permute-start.7 = (bf16[512,256]{0,1:T(8,128)(2,1)}, bf16[512,256]{0,1:T(8,128)(2,1)S(1)}, u32[]{:S(2)}, u32[]{:S(2)}) collective-permute-start(bf16[512,256]{0,1:T(8,128)(2,1)} %copy-done.6), channel_id=1, source_target_pairs={{28,0},{0,4},{4,8},{8,12},{12,16},{16,20},{20,24},{24,28},{29,1},{... | collective-permute-start | bytes 786440 | tf_op jit(solution)/shard_map/ppermute | solution.py:25
  83.7 10.4 %collective-permute-start.3 = (bf16[512,256]{0,1:T(8,128)(2,1)}, bf16[512,256]{0,1:T(8,128)(2,1)S(1)}, u32[]{:S(2)}, u32[]{:S(2)}) collective-permute-start(bf16[512,256]{0,1:T(8,128)(2,1)} %copy-done.6), channel_id=1, source_target_pairs={{4,0},{8,4},{12,8},{16,12},{20,16},{24,20},{28,24},{0,28},{5,1},{9... | collective-permute-start | bytes 786440 | tf_op jit(solution)/shard_map/ppermute | solution.py:25
  93.4 0.7 copy-start.9
  94.1 8.3 %collective-permute-start.8 = (bf16[512,256]{0,1:T(8,128)(2,1)S(1)}, bf16[512,256]{0,1:T(8,128)(2,1)}, u32[]{:S(2)}, u32[]{:S(2)}) collective-permute-start(bf16[512,256]{0,1:T(8,128)(2,1)S(1)} %collective-permute-done.7), channel_id=1, source_target_pairs={{28,0},{0,4},{4,8},{8,12},{12,16},{16,20},{20,24},{24,28},{29,1},{... | collective-permute-start | bytes 786440 | tf_op jit(solution)/shard_map/ppermute | solution.py:25
  94.1 8.3 %copy-start.11 = (bf16[512,256]{0,1:T(8,128)(2,1)}, bf16[512,256]{0,1:T(8,128)(2,1)S(1)}, u32[]{:S(2)}) copy-start(bf16[512,256]{0,1:T(8,128)(2,1)S(1)} %collective-permute-done.3) | copy-start | bytes 786436
  94.1 8.3 %collective-permute-start.4 = (bf16[512,256]{0,1:T(8,128)(2,1)S(1)}, bf16[512,256]{0,1:T(8,128)(2,1)}, u32[]{:S(2)}, u32[]{:S(2)}) collective-permute-start(bf16[512,256]{0,1:T(8,128)(2,1)S(1)} %collective-permute-done.3), channel_id=1, source_target_pairs={{4,0},{8,4},{12,8},{16,12},{20,16},{24,20},{28,24},{0,28},{5,1},{9... | collective-permute-start | bytes 786440 | tf_op jit(solution)/shard_map/ppermute | solution.py:25
  102.3 7.5 %collective-permute-start.9 = (bf16[512,256]{0,1:T(8,128)(2,1)}, bf16[512,256]{0,1:T(8,128)(2,1)}, u32[]{:S(2)}, u32[]{:S(2)}) collective-permute-start(bf16[512,256]{0,1:T(8,128)(2,1)} %collective-permute-done.8), channel_id=1, source_target_pairs={{28,0},{0,4},{4,8},{8,12},{12,16},{16,20},{20,24},{24,28},{29,1},{... | collective-permute-start | bytes 786440 | tf_op jit(solution)/shard_map/ppermute | solution.py:25
  102.4 9.1 %collective-permute-start.5 = (bf16[512,256]{0,1:T(8,128)(2,1)}, bf16[512,256]{0,1:T(8,128)(2,1)}, u32[]{:S(2)}, u32[]{:S(2)}) collective-permute-start(bf16[512,256]{0,1:T(8,128)(2,1)} %collective-permute-done.4), channel_id=1, source_target_pairs={{4,0},{8,4},{12,8},{16,12},{20,16},{24,20},{28,24},{0,28},{5,1},{9... | collective-permute-start | bytes 786440 | tf_op jit(solution)/shard_map/ppermute | solution.py:25
  111.5 8.9 %collective-permute-start.10 = (bf16[256,256]{0,1:T(8,128)(2,1)}, bf16[256,256]{0,1:T(8,128)(2,1)}, u32[]{:S(2)}, u32[]{:S(2)}) collective-permute-start(bf16[256,256]{0,1:T(8,128)(2,1)} %slice.27), channel_id=1, source_target_pairs={{28,0},{0,4},{4,8},{8,12},{12,16},{16,20},{20,24},{24,28},{29,1},{... | collective-permute-start | bytes 393224 | tf_op jit(solution)/shard_map/ppermute | solution.py:25
  113.0 7.4 %collective-permute-start.6 = (bf16[256,256]{0,1:T(8,128)(2,1)}, bf16[256,256]{0,1:T(8,128)(2,1)}, u32[]{:S(2)}, u32[]{:S(2)}) collective-permute-start(bf16[256,256]{0,1:T(8,128)(2,1)} %slice.26), channel_id=1, source_target_pairs={{4,0},{8,4},{12,8},{16,12},{20,16},{24,20},{28,24},{0,28},{5,1},{9... | collective-permute-start | bytes 393224 | tf_op jit(solution)/shard_map/ppermute | solution.py:25
  115.7 1.0 copy-start.12
  115.9 1.2 copy-start.7
  118.7 1.4 copy-start.10
  123.0 6.3 %copy-start.5 = (bf16[512,256]{0,1:T(8,128)(2,1)S(1)}, bf16[512,256]{0,1:T(8,128)(2,1)}, u32[]{:S(2)}) copy-start(bf16[512,256]{0,1:T(8,128)(2,1)} %copy-done.4) | copy-start | bytes 786436
  124.4 6.0 %copy-start = (bf16[8,32,2304]{2,1,0:T(8,128)(2,1)S(1)}, bf16[8,32,2304]{2,1,0:T(8,128)(2,1)}, u32[]{:S(2)}) copy-start(bf16[8,32,2304]{2,1,0:T(8,128)(2,1)} %get-tuple-element.5) | copy-start | bytes 3538948
  124.4 4.9 %collective-permute-start.11 = (bf16[512,512]{0,1:T(8,128)(2,1)S(1)}, bf16[512,512]{0,1:T(8,128)(2,1)S(1)}, u32[]{:S(2)}, u32[]{:S(2)}) collective-permute-start(bf16[512,512]{0,1:T(8,128)(2,1)S(1)} %get-tuple-element.19), channel_id=1, source_target_pairs={{0,2},{2,0},{1,3},{3,1},{4,6},{6,4},{5,7},{7,5},{8,10},{10,8},{9,1... | collective-permute-start | bytes 1572872 | tf_op jit(solution)/shard_map/ppermute | solution.py:21
  129.6 0.8 copy-start.8
  130.4 1.9 %copy-start.3 = (bf16[512,2304]{1,0:T(8,128)(2,1)S(1)}, bf16[512,2304]{1,0:T(8,128)(2,1)}, u32[]{:S(2)}) copy-start(bf16[512,2304]{1,0:T(8,128)(2,1)} %all-gather.2.cloned.1.call-done) | copy-start | bytes 7077892
  158.3 6.8 %copy-start.1 = (bf16[32,2,2304]{2,0,1:T(8,128)(2,1)S(1)}, bf16[32,2,2304]{2,0,1:T(8,128)(2,1)}, u32[]{:S(2)}) copy-start(bf16[32,2,2304]{2,0,1:T(8,128)(2,1)} %all_to_all.50) | copy-start | bytes 884740
Sparse Core Ops, SparseCore 0:
  15.2 39.5 all-gather.1
  132.0 32.1 reduce-scatter.1

commit v2 on v1

v2 whole, which is shorter than its diff:
```python
import math

import jax
import jax.numpy as jnp
from jax import lax
from jax.sharding import Mesh
from jax.sharding import PartitionSpec as P

coef_linear = 3.4445
coef_cubic = -4.775
coef_quintic = 2.0315
update_gain = 0.2 * math.sqrt(18432.0)

X, YL, Z, C, S = "x", "yl", "z", "c", "s"
NZ, NR = 8, 8
bf16, f32 = jnp.bfloat16, jnp.float32
COLS_Z = 768


def swap(a):
    return lax.ppermute(a, C, [(0, 1), (1, 0)])


def swap_slab(a):
    return lax.ppermute(a, S, [(0, 1), (1, 0)])


def shift_z(a, d):
    return lax.ppermute(a, Z, [((i + d) % NZ, i) for i in range(NZ)])


def turn(a):
    pairs = []
    for i in range(NZ):
        pairs += [(2 * ((i + 1) % NZ), 2 * i), (2 * ((i - 1) % NZ) + 1, 2 * i + 1)]
    return lax.ppermute(a, (Z, C), pairs)


def ring_z(a, b):
    out = [a] + [None] * (NZ - 1)
    for step in range(1, 4):
        a = turn(a)
        b = turn(b)
        out[step], out[NZ - step] = a, swap(b)
    out[4] = turn(a)
    return out


def gather_r(a):
    copies = jnp.broadcast_to(a[None], (NR, *a.shape))
    return lax.all_to_all(copies, (X, YL), 0, 0, tiled=True)


def dot_t(a, b):
    return lax.dot_general(a, b, (((1,), (1,)), ((), ())), preferred_element_type=f32)


def on_device(iterate):
    core, z = lax.axis_index(C), lax.axis_index(Z)
    first = core == 0
    left, right = iterate[:, :2304], iterate[:, 2304:]
    got = swap(jnp.where(first, right, left))
    mine = jnp.concatenate([jnp.where(first, left, got), jnp.where(first, got, right)], axis=0)
    x_rows = lax.all_gather(mine, Z, axis=0, tiled=True)
    x_cols = gather_r(mine)
    halves = [x_cols[:, 32 * h : 32 * h + 32].reshape(256, -1) for h in (0, 1)]
    part = [dot_t(x_rows, h) for h in halves]

    own = jnp.where(first, part[0], part[1])
    other = jnp.where(first, part[1], part[0]).astype(bf16)
    own = own + swap(other).astype(f32)
    sent = own.astype(bf16)
    gram = (own + swap_slab(sent).astype(f32)).astype(bf16)
    gram_o = swap(gram)
    g0 = jnp.where(first, gram, gram_o)
    g1 = jnp.where(first, gram_o, gram)
    tile = jnp.concatenate([g0, g1], axis=1)
    rows = lax.dynamic_index_in_dim(tile.reshape(NZ, 2, 32, 512), core, 1, keepdims=False)
    row_block = rows.reshape(256, 512)

    a_shards = ring_z(gram, gram_o)
    b_all = gather_r(row_block).reshape(NR, NZ, 32, 512)
    up = 1 - 2 * core
    squared = jnp.zeros((512, 512), f32)
    for e in range(NZ):
        at = (z + up * e + NZ) % NZ
        b = lax.dynamic_index_in_dim(b_all, at, 1, keepdims=False).reshape(256, 512)
        squared = squared + jnp.dot(a_shards[e], b, preferred_element_type=f32)
    squared = squared + swap(squared.astype(bf16)).astype(f32)
    poly = (coef_cubic * tile.astype(f32) + coef_quintic * squared).astype(bf16)

    x_ord = jnp.concatenate(halves, axis=0)
    part_z = jnp.dot(poly, x_ord[:, :COLS_Z], preferred_element_type=f32).astype(bf16)
    part_z = part_z.reshape(NZ, 64, COLS_Z)
    take = lambda d: lax.dynamic_index_in_dim(part_z, (z - d + NZ) % NZ, 0, keepdims=False)
    got_z = [shift_z(take(d), d) for d in (4, 1, 7, 2, 6, 3, 5)]
    part_r = lax.dot_general(
        poly, x_rows[:, COLS_Z:], (((0,), (0,)), ((), ())), preferred_element_type=f32
    ).astype(bf16)
    part_r = part_r.reshape(2, NR, 32, -1).transpose(1, 0, 2, 3)
    got_r = lax.all_to_all(part_r, (X, YL), 0, 0, tiled=True)
    sum_z = sum([p.astype(f32) for p in got_z], take(0).astype(f32))
    sum_r = got_r.astype(f32).sum(0).reshape(64, -1)
    applied = jnp.concatenate([sum_z, sum_r], axis=1)
    stepped = coef_linear * mine.astype(f32) + applied
    out = (update_gain * stepped).astype(bf16)
    up_rows, low_rows = out[:32], out[32:]
    got = swap(jnp.where(first, low_rows, up_rows))
    own = jnp.where(first, up_rows, low_rows)
    return jnp.concatenate([jnp.where(first, own, got), jnp.where(first, got, own)], axis=1)


def solution(mesh):
    fine = Mesh(mesh.devices.reshape(4, 2, 8, 2, 2), (X, YL, Z, C, S))
    spec = P((X, YL, Z, C), S)
    return jax.shard_map(on_device, mesh=fine, in_specs=(spec,), out_specs=spec, check_vma=False)
```

time: 182 us -> 166 us (0.912)
  waiting for transfers between devices: 67.4 us -> 47.8 us
  starting transfers between devices: 29.6 us -> 46.7 us
  blocking collectives: 39.7 us -> 31.4 us
  local copies, waits for them, and re-layouts: 14 us -> 6.87 us
  other arithmetic: 1.85 us -> 4.6 us
    all_to_all x2 -> x1, waiting for transfers between devices: 34.6 us -> 3.79 us  [gather_r(): return lax.all_to_all(copies, (X, YL), 0, 0, tiled=True)]
    ppermute x12 -> x23, starting transfers between devices: 21 us -> 38.2 us  [the longest x8 19.7 us: swap(): return lax.ppermute(a, C, [(0, 1), (1, 0)])]
    all_to_all x3 -> x1, blocking collectives: 39.7 us -> 31.4 us  [gather_r(): return lax.all_to_all(copies, (X, YL), 0, 0, tiled=True)]
    ppermute x12 -> x23, waiting for transfers between devices: 27.1 us -> 35.2 us  [the longest x7 16.7 us: turn(): return lax.ppermute(a, (Z, C), pairs)]
    all_gather x1, waiting for transfers between devices: 0.01 us -> 7.01 us  [on_device(): x_rows = lax.all_gather(mine, Z, axis=0, tiled=True)]
    reduce_scatter x1 -> x0, waiting for transfers between devices: 5.71 us -> none  [on_device(): lax.psum_scatter(part_z, Z, scatter_dimension=0, tiled=True).astype(f32)]
    all_to_all x2 -> x1, starting transfers between devices: 8.49 us -> 4.88 us  [gather_r(): return lax.all_to_all(copies, (X, YL), 0, 0, tiled=True)]
    all_to_all x0 -> x1, starting transfers between devices: none -> 3.58 us  [on_device(): got_r = lax.all_to_all(part_r, (X, YL), 0, 0, tiled=True)]
  transfers between devices with their start and end apart: 16 -> 26, of which waited for: 9 -> 17; matrix products, arithmetic and copies ran while one was open for 7% -> 6% of each run, Pallas kernels for 0% -> 0%
where the time goes in v2:
time: 166 us
  waiting for transfers between devices  47.8 us (29%)
  starting transfers between devices  46.7 us (28%)
  blocking collectives  31.4 us (19%)
  matrix products  14.5 us (9%)
  between operations  13.9 us (8%)
  local copies, waits for them, and re-layouts  6.87 us (4%)
  other arithmetic  4.6 us (3%)
    all_to_all x1, blocking collectives, gather_r(): return lax.all_to_all(copies, (X, YL), 0, 0, tiled=True)  31.4 us
    ppermute x8, starting transfers between devices, swap(): return lax.ppermute(a, C, [(0, 1), (1, 0)])  19.7 us
    ppermute x7, waiting for transfers between devices, turn(): return lax.ppermute(a, (Z, C), pairs)  16.7 us
    ppermute x7, starting transfers between devices, shift_z(): return lax.ppermute(a, Z, [((i + d) % NZ, i) for i in range(NZ)])  13.8 us
    dot_general x8, matrix products, on_device(): squared = squared + jnp.dot(a_shards[e], b, preferred_element_type=f32)  8.51 us
    all_gather x1, waiting for transfers between devices, on_device(): x_rows = lax.all_gather(mine, Z, axis=0, tiled=True)  7.01 us
    ppermute x7, waiting for transfers between devices, shift_z(): return lax.ppermute(a, Z, [((i + d) % NZ, i) for i in range(NZ)])  6.33 us
    ppermute x1, waiting for transfers between devices, swap_slab(): return lax.ppermute(a, S, [(0, 1), (1, 0)])  6.29 us
  transfers between devices with their start and end apart: 26, of which 17 were waited for; matrix products, arithmetic and copies ran while one was open for 6% of the time, Pallas kernels for 0%

profile of v2, /device:TPU:1, one launch (start us, length us, event | category | flops | bytes accessed | tf_op | source)
XLA Modules:
  0.0 165.7 jit_solution(10105365300615061506)
XLA Ops:
  7.5 3.3 %collective-permute-start = (bf16[32,2304]{1,0:T(8,128)(2,1)S(1)}, bf16[32,2304]{1,0:T(8,128)(2,1)S(1)}, u32[]{:S(2)}, u32[]{:S(2)}) collective-permute-start(bf16[32,2304]{1,0:T(8,128)(2,1)S(1)} %broadcast_select_fusion.8), channel_id=1, source_target_pairs={{0,2},{2,0},{1,3},{3,1},{4,6},{6,4},{5,7},{7,5},{8,10},{10,8},{9,1... | collective-permute-start | bytes 442376 | tf_op jit(solution)/shard_map/ppermute | solution.py:21
  14.9 31.4 %all_to_all.15 = bf16[8,64,2304]{2,1,0:T(8,128)(2,1)S(1)} all-to-all(bf16[8,64,2304]{2,1,0:T(8,128)(2,1)S(1)} %broadcast_in_dim.6), channel_id=1, replica_groups=mesh['x'=4,'yl'=2,'z'=8,'c'=2,'s'=2] {'x','yl'}, dimensions={0} | all-to-all | bytes 4718592 | tf_op jit(solution)/shard_map/all_to_all | solution.py:51
  46.4 7.0 %all-gather.2.cloned.1.call-done = bf16[512,2304]{1,0:T(8,128)(2,1)} async-done(((bf16[64,2304]{1,0:T(8,128)(2,1)}), bf16[512,2304]{1,0:T(8,128)(2,1)}) %all-gather.2.cloned.1.call-update) | async-done | bytes 2359312 | tf_op jit(solution)/shard_map/all_gather | solution.py:64
  53.4 2.6 %fusion.16 = f32[512,256]{0,1:T(8,128)S(1)} fusion(bf16[512,2304]{1,0:T(8,128)(2,1)} %all-gather.2.cloned.1.call-done, bf16[256,2304]{1,0:T(8,128)(2,1)S(1)} %bitcast.61), kind=kOutput, calls=%fused_computation.60 | convolution fusion | flops 603979776 | bytes 4063232 | tf_op jit(solution)/shard_map/dot_general | solution.py:55
  56.9 3.7 %collective-permute-start.1 = (bf16[512,256]{0,1:T(8,128)(2,1)S(1)}, bf16[512,256]{0,1:T(8,128)(2,1)S(1)}, u32[]{:S(2)}, u32[]{:S(2)}) collective-permute-start(bf16[512,256]{0,1:T(8,128)(2,1)S(1)} %get-tuple-element.28), channel_id=1, source_target_pairs={{0,2},{2,0},{1,3},{3,1},{4,6},{6,4},{5,7},{7,5},{8,10},{10,8},{9,1... | collective-permute-start | bytes 786440 | tf_op jit(solution)/shard_map/ppermute | solution.py:21
  61.9 2.8 %collective-permute-start.2 = (bf16[512,256]{0,1:T(8,128)(2,1)S(1)}, bf16[512,256]{0,1:T(8,128)(2,1)S(1)}, u32[]{:S(2)}, u32[]{:S(2)}) collective-permute-start(bf16[512,256]{0,1:T(8,128)(2,1)S(1)} %fusion.12), channel_id=1, source_target_pairs={{0,1},{1,0},{2,3},{3,2},{4,5},{5,4},{6,7},{7,6},{8,9},{9,8},{10,11... | collective-permute-start | bytes 786440 | tf_op jit(solution)/shard_map/ppermute | solution.py:25
  64.7 6.3 %collective-permute-done.2 = bf16[512,256]{0,1:T(8,128)(2,1)S(1)} collective-permute-done((bf16[512,256]{0,1:T(8,128)(2,1)S(1)}, bf16[512,256]{0,1:T(8,128)(2,1)S(1)}, u32[]{:S(2)}, u32[]{:S(2)}) %collective-permute-start.2) | collective-permute-done | bytes 262176 | tf_op jit(solution)/shard_map/ppermute | solution.py:25
  74.7 1.5 broadcast_in_dim.15
  76.3 4.9 %all-to-all-start.1 = ((bf16[8,256,512]{2,1,0:T(8,128)(2,1)}), bf16[8,256,512]{2,1,0:T(8,128)(2,1)S(1)}, u32[]{:S(2)}, u32[]{:S(2)}) async-start(bf16[8,256,512]{2,1,0:T(8,128)(2,1)} %broadcast_in_dim.15), calls=%async_computation.1 | async-start | bytes 4194304 | tf_op jit(solution)/shard_map/all_to_all | solution.py:51
  83.0 5.1 %collective-permute-done.4 = bf16[512,256]{0,1:T(8,128)(2,1)S(1)} collective-permute-done((bf16[512,256]{0,1:T(8,128)(2,1)}, bf16[512,256]{0,1:T(8,128)(2,1)S(1)}, u32[]{:S(2)}, u32[]{:S(2)}) %collective-permute-start.4) | collective-permute-done | bytes 262176 | tf_op jit(solution)/shard_map/ppermute | solution.py:36
  88.8 2.1 %collective-permute-done.8 = bf16[512,256]{0,1:T(8,128)(2,1)S(1)} collective-permute-done((bf16[512,256]{0,1:T(8,128)(2,1)}, bf16[512,256]{0,1:T(8,128)(2,1)S(1)}, u32[]{:S(2)}, u32[]{:S(2)}) %collective-permute-start.8) | collective-permute-done | bytes 262176 | tf_op jit(solution)/shard_map/ppermute | solution.py:36
  90.9 4.7 %collective-permute-done.5 = bf16[512,256]{0,1:T(8,128)(2,1)} collective-permute-done((bf16[512,256]{0,1:T(8,128)(2,1)S(1)}, bf16[512,256]{0,1:T(8,128)(2,1)}, u32[]{:S(2)}, u32[]{:S(2)}) %collective-permute-start.5) | collective-permute-done | bytes 262176 | tf_op jit(solution)/shard_map/ppermute | solution.py:36
  95.6 2.8 %collective-permute-done.9 = bf16[512,256]{0,1:T(8,128)(2,1)} collective-permute-done((bf16[512,256]{0,1:T(8,128)(2,1)S(1)}, bf16[512,256]{0,1:T(8,128)(2,1)}, u32[]{:S(2)}, u32[]{:S(2)}) %collective-permute-start.9) | collective-permute-done | bytes 262176 | tf_op jit(solution)/shard_map/ppermute | solution.py:36
  98.4 4.8 %collective-permute-start.13 = (bf16[512,256]{0,1:T(8,128)(2,1)}, bf16[512,256]{0,1:T(8,128)(2,1)}, u32[]{:S(2)}, u32[]{:S(2)}) collective-permute-start(bf16[512,256]{0,1:T(8,128)(2,1)} %copy-done.14), channel_id=1, source_target_pairs={{0,2},{2,0},{1,3},{3,1},{4,6},{6,4},{5,7},{7,5},{8,10},{10,8},{9,1... | collective-permute-start | bytes 786440 | tf_op jit(solution)/shard_map/ppermute | solution.py:21
  103.2 2.1 %collective-permute-done.10 = bf16[512,256]{0,1:T(8,128)(2,1)} collective-permute-done((bf16[512,256]{0,1:T(8,128)(2,1)}, bf16[512,256]{0,1:T(8,128)(2,1)}, u32[]{:S(2)}, u32[]{:S(2)}) %collective-permute-start.10) | collective-permute-done | bytes 262176 | tf_op jit(solution)/shard_map/ppermute | solution.py:36
  105.3 3.0 %collective-permute-start.11 = (bf16[512,256]{0,1:T(8,128)(2,1)}, bf16[512,256]{0,1:T(8,128)(2,1)}, u32[]{:S(2)}, u32[]{:S(2)}) collective-permute-start(bf16[512,256]{0,1:T(8,128)(2,1)} %collective-permute-done.10), channel_id=1, source_target_pairs={{0,2},{2,0},{1,3},{3,1},{4,6},{6,4},{5,7},{7,5},{8,10},{10,8},{9,1... | collective-permute-start | bytes 786440 | tf_op jit(solution)/shard_map/ppermute | solution.py:21
  108.3 3.8 %all-to-all-done.1 = bf16[8,256,512]{2,1,0:T(8,128)(2,1)S(1)} async-done(((bf16[8,256,512]{2,1,0:T(8,128)(2,1)}), bf16[8,256,512]{2,1,0:T(8,128)(2,1)S(1)}, u32[]{:S(2)}, u32[]{:S(2)}) %all-to-all-start.1) | async-done | bytes 2097184 | tf_op jit(solution)/shard_map/all_to_all | solution.py:51
  113.7 1.3 convolution_add_fusion.3
  120.3 1.3 fusion.15
  121.7 1.5 collective-permute-start.14
  123.2 1.5 collective-permute-done.14
  127.3 3.6 %all-to-all-start.2 = ((bf16[8,2,32,1536]{3,2,1,0:T(8,128)(2,1)}), bf16[8,2,32,1536]{3,2,1,0:T(8,128)(2,1)S(1)}, u32[]{:S(2)}, u32[]{:S(2)}) async-start(bf16[8,2,32,1536]{3,2,1,0:T(8,128)(2,1)} %bitcast.57), calls=%async_computation.2 | async-start | bytes 3145728 | tf_op jit(solution)/shard_map/all_to_all | solution.py:101
  130.9 1.6 convolution_convert_fusion.1
  132.6 3.0 %collective-permute-start.15 = (bf16[64,768]{1,0:T(8,128)(2,1)S(1)}, bf16[64,768]{1,0:T(8,128)(2,1)S(1)}, u32[]{:S(2)}, u32[]{:S(2)}) collective-permute-start(bf16[64,768]{1,0:T(8,128)(2,1)S(1)} %get-tuple-element.15), channel_id=1, source_target_pairs={{16,0},{20,4},{24,8},{28,12},{0,16},{4,20},{8,24},{12,28},{17,1},{... | collective-permute-start | bytes 294920 | tf_op jit(solution)/shard_map/ppermute | solution.py:29
  135.6 1.8 %collective-permute-start.16 = (bf16[64,768]{1,0:T(8,128)(2,1)S(1)}, bf16[64,768]{1,0:T(8,128)(2,1)S(1)}, u32[]{:S(2)}, u32[]{:S(2)}) collective-permute-start(bf16[64,768]{1,0:T(8,128)(2,1)S(1)} %get-tuple-element.21), channel_id=1, source_target_pairs={{4,0},{8,4},{12,8},{16,12},{20,16},{24,20},{28,24},{0,28},{5,1},{9... | collective-permute-start | bytes 294920 | tf_op jit(solution)/shard_map/ppermute | solution.py:29
  137.5 1.6 collective-permute-start.18
  140.6 2.5 %collective-permute-start.20 = (bf16[64,768]{1,0:T(8,128)(2,1)S(1)}, bf16[64,768]{1,0:T(8,128)(2,1)S(1)}, u32[]{:S(2)}, u32[]{:S(2)}) collective-permute-start(bf16[64,768]{1,0:T(8,128)(2,1)S(1)} %get-tuple-element.17), channel_id=1, source_target_pairs={{12,0},{16,4},{20,8},{24,12},{28,16},{0,20},{4,24},{8,28},{13,1},{... | collective-permute-start | bytes 294920 | tf_op jit(solution)/shard_map/ppermute | solution.py:29
  143.1 4.2 %collective-permute-start.21 = (bf16[64,768]{1,0:T(8,128)(2,1)S(1)}, bf16[64,768]{1,0:T(8,128)(2,1)S(1)}, u32[]{:S(2)}, u32[]{:S(2)}) collective-permute-start(bf16[64,768]{1,0:T(8,128)(2,1)S(1)} %get-tuple-element.16), channel_id=1, source_target_pairs={{20,0},{24,4},{28,8},{0,12},{4,16},{8,20},{12,24},{16,28},{21,1},{... | collective-permute-start | bytes 294920 | tf_op jit(solution)/shard_map/ppermute | solution.py:29
  147.3 2.7 %collective-permute-done.18 = bf16[64,768]{1,0:T(8,128)(2,1)S(1)} collective-permute-done((bf16[64,768]{1,0:T(8,128)(2,1)S(1)}, bf16[64,768]{1,0:T(8,128)(2,1)S(1)}, u32[]{:S(2)}, u32[]{:S(2)}) %collective-permute-start.18) | collective-permute-done | bytes 98336 | tf_op jit(solution)/shard_map/ppermute | solution.py:29
  150.0 2.8 %collective-permute-done.20 = bf16[64,768]{1,0:T(8,128)(2,1)S(1)} collective-permute-done((bf16[64,768]{1,0:T(8,128)(2,1)S(1)}, bf16[64,768]{1,0:T(8,128)(2,1)S(1)}, u32[]{:S(2)}, u32[]{:S(2)}) %collective-permute-start.20) | collective-permute-done | bytes 98336 | tf_op jit(solution)/shard_map/ppermute | solution.py:29
  152.9 1.8 %all-to-all-done.2 = bf16[8,2,32,1536]{3,2,1,0:T(8,128)(2,1)S(1)} async-done(((bf16[8,2,32,1536]{3,2,1,0:T(8,128)(2,1)}), bf16[8,2,32,1536]{3,2,1,0:T(8,128)(2,1)S(1)}, u32[]{:S(2)}, u32[]{:S(2)}) %all-to-all-start.2) | async-done | bytes 1572896 | tf_op jit(solution)/shard_map/all_to_all | solution.py:101
  155.0 2.1 %collective-permute-start.22 = (bf16[32,2304]{1,0:T(8,128)(2,1)S(1)}, bf16[32,2304]{1,0:T(8,128)(2,1)S(1)}, u32[]{:S(2)}, u32[]{:S(2)}) collective-permute-start(bf16[32,2304]{1,0:T(8,128)(2,1)S(1)} %broadcast_select_fusion.4), channel_id=1, source_target_pairs={{0,2},{2,0},{1,3},{3,1},{4,6},{6,4},{5,7},{7,5},{8,10},{10,8},{9,1... | collective-permute-start | bytes 442376 | tf_op jit(solution)/shard_map/ppermute | solution.py:21
  (86 shorter events, 26.7 us)
Async XLA Ops:
  6.5 46.9 %all-gather.2.cloned.1.call-start = ((), (), s32[]{:S(2)}) async-start(), calls=%async_computation.3 | async-start | bytes 2654208 | tf_op jit(solution)/shard_map/all_gather | solution.py:64
  7.5 4.3 %collective-permute-start = (bf16[32,2304]{1,0:T(8,128)(2,1)S(1)}, bf16[32,2304]{1,0:T(8,128)(2,1)S(1)}, u32[]{:S(2)}, u32[]{:S(2)}) collective-permute-start(bf16[32,2304]{1,0:T(8,128)(2,1)S(1)} %broadcast_select_fusion.8), channel_id=1, source_target_pairs={{0,2},{2,0},{1,3},{3,1},{4,6},{6,4},{5,7},{7,5},{8,10},{10,8},{9,1... | collective-permute-start | bytes 442376 | tf_op jit(solution)/shard_map/ppermute | solution.py:21
  46.4 9.6 %copy-start = (bf16[8,32,2304]{2,1,0:T(8,128)(2,1)}, bf16[8,32,2304]{2,1,0:T(8,128)(2,1)S(1)}, u32[]{:S(2)}) copy-start(bf16[8,32,2304]{2,1,0:T(8,128)(2,1)S(1)} %get-tuple-element.5) | copy-start | bytes 3538948
  56.9 4.9 %collective-permute-start.1 = (bf16[512,256]{0,1:T(8,128)(2,1)S(1)}, bf16[512,256]{0,1:T(8,128)(2,1)S(1)}, u32[]{:S(2)}, u32[]{:S(2)}) collective-permute-start(bf16[512,256]{0,1:T(8,128)(2,1)S(1)} %get-tuple-element.28), channel_id=1, source_target_pairs={{0,2},{2,0},{1,3},{3,1},{4,6},{6,4},{5,7},{7,5},{8,10},{10,8},{9,1... | collective-permute-start | bytes 786440 | tf_op jit(solution)/shard_map/ppermute | solution.py:21
  61.9 9.1 %collective-permute-start.2 = (bf16[512,256]{0,1:T(8,128)(2,1)S(1)}, bf16[512,256]{0,1:T(8,128)(2,1)S(1)}, u32[]{:S(2)}, u32[]{:S(2)}) collective-permute-start(bf16[512,256]{0,1:T(8,128)(2,1)S(1)} %fusion.12), channel_id=1, source_target_pairs={{0,1},{1,0},{2,3},{3,2},{4,5},{5,4},{6,7},{7,6},{8,9},{9,8},{10,11... | collective-permute-start | bytes 786440 | tf_op jit(solution)/shard_map/ppermute | solution.py:25
  71.2 3.5 %copy-start.5 = (bf16[512,256]{0,1:T(8,128)(2,1)}, bf16[512,256]{0,1:T(8,128)(2,1)S(1)}, u32[]{:S(2)}) copy-start(bf16[512,256]{0,1:T(8,128)(2,1)S(1)} %add_convert_fusion.1) | copy-start | bytes 786436
  71.2 2.5 %collective-permute-start.3 = (bf16[512,256]{0,1:T(8,128)(2,1)S(1)}, bf16[512,256]{0,1:T(8,128)(2,1)S(1)}, u32[]{:S(2)}, u32[]{:S(2)}) collective-permute-start(bf16[512,256]{0,1:T(8,128)(2,1)S(1)} %add_convert_fusion.1), channel_id=1, source_target_pairs={{0,2},{2,0},{1,3},{3,1},{4,6},{6,4},{5,7},{7,5},{8,10},{10,8},{9,1... | collective-permute-start | bytes 786440 | tf_op jit(solution)/shard_map/ppermute | solution.py:21
  76.3 35.8 %all-to-all-start.1 = ((bf16[8,256,512]{2,1,0:T(8,128)(2,1)}), bf16[8,256,512]{2,1,0:T(8,128)(2,1)S(1)}, u32[]{:S(2)}, u32[]{:S(2)}) async-start(bf16[8,256,512]{2,1,0:T(8,128)(2,1)} %broadcast_in_dim.15), calls=%async_computation.1 | async-start | bytes 4194304 | tf_op jit(solution)/shard_map/all_to_all | solution.py:51
  81.1 6.9 %collective-permute-start.4 = (bf16[512,256]{0,1:T(8,128)(2,1)}, bf16[512,256]{0,1:T(8,128)(2,1)S(1)}, u32[]{:S(2)}, u32[]{:S(2)}) collective-permute-start(bf16[512,256]{0,1:T(8,128)(2,1)} %copy-done.5), channel_id=1, source_target_pairs={{4,0},{30,2},{8,4},{2,6},{12,8},{6,10},{16,12},{10,14},{20,16},{14... | collective-permute-start | bytes 786440 | tf_op jit(solution)/shard_map/ppermute | solution.py:36
  82.0 8.9 %collective-permute-start.8 = (bf16[512,256]{0,1:T(8,128)(2,1)}, bf16[512,256]{0,1:T(8,128)(2,1)S(1)}, u32[]{:S(2)}, u32[]{:S(2)}) collective-permute-start(bf16[512,256]{0,1:T(8,128)(2,1)} %copy-done.13), channel_id=1, source_target_pairs={{4,0},{30,2},{8,4},{2,6},{12,8},{6,10},{16,12},{10,14},{20,16},{14... | collective-permute-start | bytes 786440 | tf_op jit(solution)/shard_map/ppermute | solution.py:36
  88.8 6.7 %collective-permute-start.5 = (bf16[512,256]{0,1:T(8,128)(2,1)S(1)}, bf16[512,256]{0,1:T(8,128)(2,1)}, u32[]{:S(2)}, u32[]{:S(2)}) collective-permute-start(bf16[512,256]{0,1:T(8,128)(2,1)S(1)} %collective-permute-done.4), channel_id=1, source_target_pairs={{4,0},{30,2},{8,4},{2,6},{12,8},{6,10},{16,12},{10,14},{20,16},{14... | collective-permute-start | bytes 786440 | tf_op jit(solution)/shard_map/ppermute | solution.py:36
  90.9 4.7 %copy-start.14 = (bf16[512,256]{0,1:T(8,128)(2,1)}, bf16[512,256]{0,1:T(8,128)(2,1)S(1)}, u32[]{:S(2)}) copy-start(bf16[512,256]{0,1:T(8,128)(2,1)S(1)} %collective-permute-done.8) | copy-start | bytes 786436
  90.9 7.5 %collective-permute-start.9 = (bf16[512,256]{0,1:T(8,128)(2,1)S(1)}, bf16[512,256]{0,1:T(8,128)(2,1)}, u32[]{:S(2)}, u32[]{:S(2)}) collective-permute-start(bf16[512,256]{0,1:T(8,128)(2,1)S(1)} %collective-permute-done.8), channel_id=1, source_target_pairs={{4,0},{30,2},{8,4},{2,6},{12,8},{6,10},{16,12},{10,14},{20,16},{14... | collective-permute-start | bytes 786440 | tf_op jit(solution)/shard_map/ppermute | solution.py:36
  95.6 7.6 %collective-permute-start.6 = (bf16[512,256]{0,1:T(8,128)(2,1)}, bf16[512,256]{0,1:T(8,128)(2,1)}, u32[]{:S(2)}, u32[]{:S(2)}) collective-permute-start(bf16[512,256]{0,1:T(8,128)(2,1)} %collective-permute-done.5), channel_id=1, source_target_pairs={{4,0},{30,2},{8,4},{2,6},{12,8},{6,10},{16,12},{10,14},{20,16},{14... | collective-permute-start | bytes 786440 | tf_op jit(solution)/shard_map/ppermute | solution.py:36
  98.4 6.9 %collective-permute-start.10 = (bf16[512,256]{0,1:T(8,128)(2,1)}, bf16[512,256]{0,1:T(8,128)(2,1)}, u32[]{:S(2)}, u32[]{:S(2)}) collective-permute-start(bf16[512,256]{0,1:T(8,128)(2,1)} %collective-permute-done.9), channel_id=1, source_target_pairs={{4,0},{30,2},{8,4},{2,6},{12,8},{6,10},{16,12},{10,14},{20,16},{14... | collective-permute-start | bytes 786440 | tf_op jit(solution)/shard_map/ppermute | solution.py:36
  98.4 20.6 %collective-permute-start.13 = (bf16[512,256]{0,1:T(8,128)(2,1)}, bf16[512,256]{0,1:T(8,128)(2,1)}, u32[]{:S(2)}, u32[]{:S(2)}) collective-permute-start(bf16[512,256]{0,1:T(8,128)(2,1)} %copy-done.14), channel_id=1, source_target_pairs={{0,2},{2,0},{1,3},{3,1},{4,6},{6,4},{5,7},{7,5},{8,10},{10,8},{9,1... | collective-permute-start | bytes 786440 | tf_op jit(solution)/shard_map/ppermute | solution.py:21
  103.2 14.5 %collective-permute-start.12 = (bf16[512,256]{0,1:T(8,128)(2,1)}, bf16[512,256]{0,1:T(8,128)(2,1)}, u32[]{:S(2)}, u32[]{:S(2)}) collective-permute-start(bf16[512,256]{0,1:T(8,128)(2,1)} %collective-permute-done.9), channel_id=1, source_target_pairs={{0,2},{2,0},{1,3},{3,1},{4,6},{6,4},{5,7},{7,5},{8,10},{10,8},{9,1... | collective-permute-start | bytes 786440 | tf_op jit(solution)/shard_map/ppermute | solution.py:21
  103.2 13.2 %collective-permute-start.7 = (bf16[512,256]{0,1:T(8,128)(2,1)}, bf16[512,256]{0,1:T(8,128)(2,1)}, u32[]{:S(2)}, u32[]{:S(2)}) collective-permute-start(bf16[512,256]{0,1:T(8,128)(2,1)} %collective-permute-done.6), channel_id=1, source_target_pairs={{4,0},{30,2},{8,4},{2,6},{12,8},{6,10},{16,12},{10,14},{20,16},{14... | collective-permute-start | bytes 786440 | tf_op jit(solution)/shard_map/ppermute | solution.py:36
  105.3 15.0 %collective-permute-start.11 = (bf16[512,256]{0,1:T(8,128)(2,1)}, bf16[512,256]{0,1:T(8,128)(2,1)}, u32[]{:S(2)}, u32[]{:S(2)}) collective-permute-start(bf16[512,256]{0,1:T(8,128)(2,1)} %collective-permute-done.10), channel_id=1, source_target_pairs={{0,2},{2,0},{1,3},{3,1},{4,6},{6,4},{5,7},{7,5},{8,10},{10,8},{9,1... | collective-permute-start | bytes 786440 | tf_op jit(solution)/shard_map/ppermute | solution.py:21
  120.3 4.4 %copy-start.4 = (bf16[512,256]{0,1:T(8,128)(2,1)S(1)}, bf16[512,256]{0,1:T(8,128)(2,1)}, u32[]{:S(2)}) copy-start(bf16[512,256]{0,1:T(8,128)(2,1)} %copy-done.3) | copy-start | bytes 786436
  121.7 3.1 %collective-permute-start.14 = (bf16[512,512]{0,1:T(8,128)(2,1)S(1)}, bf16[512,512]{0,1:T(8,128)(2,1)S(1)}, u32[]{:S(2)}, u32[]{:S(2)}) collective-permute-start(bf16[512,512]{0,1:T(8,128)(2,1)S(1)} %get-tuple-element.30), channel_id=1, source_target_pairs={{0,2},{2,0},{1,3},{3,1},{4,6},{6,4},{5,7},{7,5},{8,10},{10,8},{9,1... | collective-permute-start | bytes 1572872 | tf_op jit(solution)/shard_map/ppermute | solution.py:21
  127.3 27.4 %all-to-all-start.2 = ((bf16[8,2,32,1536]{3,2,1,0:T(8,128)(2,1)}), bf16[8,2,32,1536]{3,2,1,0:T(8,128)(2,1)S(1)}, u32[]{:S(2)}, u32[]{:S(2)}) async-start(bf16[8,2,32,1536]{3,2,1,0:T(8,128)(2,1)} %bitcast.57), calls=%async_computation.2 | async-start | bytes 3145728 | tf_op jit(solution)/shard_map/all_to_all | solution.py:101
  132.6 22.3 %copy-start.8 = (bf16[32,2304]{1,0:T(8,128)(2,1)S(1)}, bf16[32,2304]{1,0:T(8,128)(2,1)}, u32[]{:S(2)}) copy-start(bf16[32,2304]{1,0:T(8,128)(2,1)} %copy-done.7) | copy-start | bytes 442372
  132.6 22.3 %copy-start.10 = (bf16[32,2304]{1,0:T(8,128)(2,1)S(1)}, bf16[32,2304]{1,0:T(8,128)(2,1)}, u32[]{:S(2)}) copy-start(bf16[32,2304]{1,0:T(8,128)(2,1)} %copy-done.9) | copy-start | bytes 442372
  132.6 8.0 %collective-permute-start.15 = (bf16[64,768]{1,0:T(8,128)(2,1)S(1)}, bf16[64,768]{1,0:T(8,128)(2,1)S(1)}, u32[]{:S(2)}, u32[]{:S(2)}) collective-permute-start(bf16[64,768]{1,0:T(8,128)(2,1)S(1)} %get-tuple-element.15), channel_id=1, source_target_pairs={{16,0},{20,4},{24,8},{28,12},{0,16},{4,20},{8,24},{12,28},{17,1},{... | collective-permute-start | bytes 294920 | tf_op jit(solution)/shard_map/ppermute | solution.py:29
  135.6 7.5 %collective-permute-start.16 = (bf16[64,768]{1,0:T(8,128)(2,1)S(1)}, bf16[64,768]{1,0:T(8,128)(2,1)S(1)}, u32[]{:S(2)}, u32[]{:S(2)}) collective-permute-start(bf16[64,768]{1,0:T(8,128)(2,1)S(1)} %get-tuple-element.21), channel_id=1, source_target_pairs={{4,0},{8,4},{12,8},{16,12},{20,16},{24,20},{28,24},{0,28},{5,1},{9... | collective-permute-start | bytes 294920 | tf_op jit(solution)/shard_map/ppermute | solution.py:29
  137.5 9.8 %collective-permute-start.17 = (bf16[64,768]{1,0:T(8,128)(2,1)S(1)}, bf16[64,768]{1,0:T(8,128)(2,1)S(1)}, u32[]{:S(2)}, u32[]{:S(2)}) collective-permute-start(bf16[64,768]{1,0:T(8,128)(2,1)S(1)} %get-tuple-element.20), channel_id=1, source_target_pairs={{28,0},{0,4},{4,8},{8,12},{12,16},{16,20},{20,24},{24,28},{29,1},{... | collective-permute-start | bytes 294920 | tf_op jit(solution)/shard_map/ppermute | solution.py:29
  137.5 12.5 %collective-permute-start.18 = (bf16[64,768]{1,0:T(8,128)(2,1)S(1)}, bf16[64,768]{1,0:T(8,128)(2,1)S(1)}, u32[]{:S(2)}, u32[]{:S(2)}) collective-permute-start(bf16[64,768]{1,0:T(8,128)(2,1)S(1)} %get-tuple-element.19), channel_id=1, source_target_pairs={{8,0},{12,4},{16,8},{20,12},{24,16},{28,20},{0,24},{4,28},{9,1},{1... | collective-permute-start | bytes 294920 | tf_op jit(solution)/shard_map/ppermute | solution.py:29
  139.1 10.9 %collective-permute-start.19 = (bf16[64,768]{1,0:T(8,128)(2,1)S(1)}, bf16[64,768]{1,0:T(8,128)(2,1)S(1)}, u32[]{:S(2)}, u32[]{:S(2)}) collective-permute-start(bf16[64,768]{1,0:T(8,128)(2,1)S(1)} %get-tuple-element.18), channel_id=1, source_target_pairs={{24,0},{28,4},{0,8},{4,12},{8,16},{12,20},{16,24},{20,28},{25,1},{... | collective-permute-start | bytes 294920 | tf_op jit(solution)/shard_map/ppermute | solution.py:29
  140.6 12.2 %collective-permute-start.20 = (bf16[64,768]{1,0:T(8,128)(2,1)S(1)}, bf16[64,768]{1,0:T(8,128)(2,1)S(1)}, u32[]{:S(2)}, u32[]{:S(2)}) collective-permute-start(bf16[64,768]{1,0:T(8,128)(2,1)S(1)} %get-tuple-element.17), channel_id=1, source_target_pairs={{12,0},{16,4},{20,8},{24,12},{28,16},{0,20},{4,24},{8,28},{13,1},{... | collective-permute-start | bytes 294920 | tf_op jit(solution)/shard_map/ppermute | solution.py:29
  143.1 9.7 %collective-permute-start.21 = (bf16[64,768]{1,0:T(8,128)(2,1)S(1)}, bf16[64,768]{1,0:T(8,128)(2,1)S(1)}, u32[]{:S(2)}, u32[]{:S(2)}) collective-permute-start(bf16[64,768]{1,0:T(8,128)(2,1)S(1)} %get-tuple-element.16), channel_id=1, source_target_pairs={{20,0},{24,4},{28,8},{0,12},{4,16},{8,20},{12,24},{16,28},{21,1},{... | collective-permute-start | bytes 294920 | tf_op jit(solution)/shard_map/ppermute | solution.py:29
  155.0 3.1 %collective-permute-start.22 = (bf16[32,2304]{1,0:T(8,128)(2,1)S(1)}, bf16[32,2304]{1,0:T(8,128)(2,1)S(1)}, u32[]{:S(2)}, u32[]{:S(2)}) collective-permute-start(bf16[32,2304]{1,0:T(8,128)(2,1)S(1)} %broadcast_select_fusion.4), channel_id=1, source_target_pairs={{0,2},{2,0},{1,3},{3,1},{4,6},{6,4},{5,7},{7,5},{8,10},{10,8},{9,1... | collective-permute-start | bytes 442376 | tf_op jit(solution)/shard_map/ppermute | solution.py:21
  (9 other events, 14.1 us)
Sparse Core Ops, SparseCore 0:
  13.8 39.5 all-gather.1

commit v3 on v2

v3 whole, which is shorter than its diff:
```python
import math

import jax
import jax.numpy as jnp
from jax import lax
from jax.sharding import Mesh
from jax.sharding import PartitionSpec as P

coef_linear = 3.4445
coef_cubic = -4.775
coef_quintic = 2.0315
update_gain = 0.2 * math.sqrt(18432.0)

X, YL, Z, C, S = "x", "yl", "z", "c", "s"
NZ, NR = 8, 8
bf16, f32 = jnp.bfloat16, jnp.float32
COLS_Z = 768


def swap(a):
    return lax.ppermute(a, C, [(0, 1), (1, 0)])


def swap_slab(a):
    return lax.ppermute(a, S, [(0, 1), (1, 0)])


def shift_z(a, d):
    return lax.ppermute(a, Z, [((i + d) % NZ, i) for i in range(NZ)])


def turn(a):
    pairs = []
    for i in range(NZ):
        pairs += [(2 * ((i + 1) % NZ), 2 * i), (2 * ((i - 1) % NZ) + 1, 2 * i + 1)]
    return lax.ppermute(a, (Z, C), pairs)


def ring_z(a, b):
    mine, others = [a] + [None] * (NZ - 1), [b] + [None] * (NZ - 1)
    for step in range(1, 4):
        a = turn(a)
        b = turn(b)
        mine[step], others[step] = a, b
        mine[NZ - step], others[NZ - step] = swap(b), swap(a)
    mine[4] = turn(a)
    others[4] = swap(mine[4])
    return mine, others


def gather_r(a):
    copies = jnp.broadcast_to(a[None], (NR, *a.shape))
    return lax.all_to_all(copies, (X, YL), 0, 0, tiled=True)


def pick(a, index, axis):
    return lax.dynamic_index_in_dim(a, index, axis, keepdims=False)


def dot(a, b):
    return jnp.dot(a, b, preferred_element_type=f32)


def dot_t(a, b):
    return lax.dot_general(a, b, (((1,), (1,)), ((), ())), preferred_element_type=f32)


def t_dot(a, b):
    return lax.dot_general(a, b, (((0,), (0,)), ((), ())), preferred_element_type=f32)


ORDER = (0, 1, 7, 2, 6, 3, 5, 4)


def on_device(iterate):
    core, z = lax.axis_index(C), lax.axis_index(Z)
    first = core == 0
    up = 1 - 2 * core
    place = [(z + up * e + NZ) % NZ for e in range(NZ)]
    got = swap(iterate)
    top, low = jnp.where(first, iterate, got), jnp.where(first, got, iterate)
    chip = jnp.concatenate([top, low], axis=0).reshape(64, 2, 2304)
    mine, others = pick(chip, core, 1), pick(chip, 1 - core, 1)
    x_cols = gather_r(mine).reshape(NR, 2, 32, 2304)
    pieces = ring_z(mine, others)[0]
    x_rows = jnp.zeros((NZ, 64, 2304), bf16)
    for e in ORDER:
        x_rows = lax.dynamic_update_index_in_dim(x_rows, pieces[e], place[e], 0)
    x_rows = x_rows.reshape(512, 2304)
    cols_m = pick(x_cols, core, 1).reshape(256, 2304)
    cols_o = pick(x_cols, 1 - core, 1).reshape(256, 2304)

    other = dot_t(x_rows, cols_o).astype(bf16)
    own = dot_t(x_rows, cols_m) + swap(other).astype(f32)
    gram = (own + swap_slab(own.astype(bf16)).astype(f32)).astype(bf16)

    b_all = gather_r(gram).reshape(NR, NZ, 2, 32, 256)
    a_mine, a_others = ring_z(gram, swap(gram))
    squared = jnp.zeros((512, 256), f32)
    for e in ORDER:
        b = pick(b_all, place[e], 1)
        squared = squared + dot(a_mine[e], pick(b, core, 1).reshape(256, 256))
        squared = squared + dot(a_others[e], pick(b, 1 - core, 1).reshape(256, 256))
    poly_m = (coef_cubic * gram.astype(f32) + coef_quintic * squared).astype(bf16)
    poly_o = swap(poly_m)

    rest = x_rows[:, COLS_Z:]
    part_r = jnp.stack([t_dot(p, rest).astype(bf16).reshape(NR, 32, -1) for p in (poly_m, poly_o)], 1)
    got_r = lax.all_to_all(part_r, (X, YL), 0, 0, tiled=True)
    part_z = dot(poly_m, cols_m[:, :COLS_Z]) + dot(poly_o, cols_o[:, :COLS_Z])
    part_z = part_z.astype(bf16).reshape(NZ, 64, COLS_Z)
    take = lambda d: pick(part_z, (z - d + NZ) % NZ, 0)
    got_z = [shift_z(take(d), d) for d in (4, 1, 7, 2, 6, 3, 5)]
    sum_z = sum([p.astype(f32) for p in got_z], take(0).astype(f32)).reshape(2, 32, COLS_Z)
    sum_r = got_r.astype(f32).sum(0)

    def finish(half, k):
        applied = jnp.concatenate([pick(sum_z, half, 0), sum_r[k]], axis=1)
        stepped = coef_linear * pick(mine.reshape(2, 32, 2304), half, 0).astype(f32) + applied
        return (update_gain * stepped).astype(bf16)

    got = swap(finish(1 - core, 1))
    own = finish(core, 0)
    return jnp.concatenate([jnp.where(first, own, got), jnp.where(first, got, own)], axis=1)


def solution(mesh):
    fine = Mesh(mesh.devices.reshape(4, 2, 8, 2, 2), (X, YL, Z, C, S))
    spec = P((X, YL, Z, C), S)
    return jax.shard_map(on_device, mesh=fine, in_specs=(spec,), out_specs=spec, check_vma=False)
```

time: 166 us -> 162 us (0.976)
  blocking collectives: 31.4 us -> 0 us
  starting transfers between devices: 46.7 us -> 70.3 us
  between operations: 13.9 us -> 0.54 us
  local copies, waits for them, and re-layouts: 6.87 us -> 15.5 us
  waiting for transfers between devices: 47.8 us -> 55.5 us
    all_to_all x1 -> x0, blocking collectives: 31.4 us -> none  [gather_r(): return lax.all_to_all(copies, (X, YL), 0, 0, tiled=True)]
    ppermute x8 -> x15, starting transfers between devices: 19.7 us -> 30.8 us  [swap(): return lax.ppermute(a, C, [(0, 1), (1, 0)])]
    ppermute x7 -> x14, waiting for transfers between devices: 16.7 us -> 25.5 us  [turn(): return lax.ppermute(a, (Z, C), pairs)]
    ppermute x7 -> x14, starting transfers between devices: 1.89 us -> 10 us  [turn(): return lax.ppermute(a, (Z, C), pairs)]
    all_to_all x1 -> x2, waiting for transfers between devices: 3.79 us -> 11.4 us  [gather_r(): return lax.all_to_all(copies, (X, YL), 0, 0, tiled=True)]
    all_gather x1 -> x0, waiting for transfers between devices: 7.01 us -> none  [on_device(): x_rows = lax.all_gather(mine, Z, axis=0, tiled=True)]
    dynamic_update_slice x0 -> x8, local copies, waits for them, and re-layouts: none -> 5.25 us  [on_device(): x_rows = lax.dynamic_update_index_in_dim(x_rows, pieces[e], place[e], 0)]
    all_to_all x1 -> x2, starting transfers between devices: 4.88 us -> 8.63 us  [gather_r(): return lax.all_to_all(copies, (X, YL), 0, 0, tiled=True)]
  transfers between devices with their start and end apart: 26 -> 40, of which waited for: 17 -> 18; matrix products, arithmetic and copies ran while one was open for 6% -> 13% of each run, Pallas kernels for 0% -> 0%
where the time goes in v3:
time: 162 us; the launch traced here: 161 us
  starting transfers between devices  70.3 us (43%)
  waiting for transfers between devices  55.5 us (34%)
  matrix products  15.8 us (10%)
  local copies, waits for them, and re-layouts  15.5 us (10%)
  other arithmetic  3.64 us (2%)
    ppermute x15, starting transfers between devices, swap(): return lax.ppermute(a, C, [(0, 1), (1, 0)])  30.8 us
    ppermute x14, waiting for transfers between devices, turn(): return lax.ppermute(a, (Z, C), pairs)  25.5 us
    ppermute x7, starting transfers between devices, shift_z(): return lax.ppermute(a, Z, [((i + d) % NZ, i) for i in range(NZ)])  14.4 us
    dot_general x18, matrix products, dot(): return jnp.dot(a, b, preferred_element_type=f32)  13 us
    all_to_all x2, waiting for transfers between devices, gather_r(): return lax.all_to_all(copies, (X, YL), 0, 0, tiled=True)  11.4 us
    ppermute x14, starting transfers between devices, turn(): return lax.ppermute(a, (Z, C), pairs)  10 us
    all_to_all x2, starting transfers between devices, gather_r(): return lax.all_to_all(copies, (X, YL), 0, 0, tiled=True)  8.63 us
    ppermute x7, waiting for transfers between devices, shift_z(): return lax.ppermute(a, Z, [((i + d) % NZ, i) for i in range(NZ)])  8.16 us
  transfers between devices with their start and end apart: 40, of which 18 were waited for; matrix products, arithmetic and copies ran while one was open for 13% of the time, Pallas kernels for 0%

profile of v3, /device:TPU:1, one launch (start us, length us, event | category | flops | bytes accessed | tf_op | source)
XLA Modules:
  0.0 161.2 jit_solution(265383279482145347)
XLA Ops:
  0.0 3.2 %collective-permute-start = (bf16[32,4608]{1,0:T(8,128)(2,1)}, bf16[32,4608]{1,0:T(8,128)(2,1)S(1)}, u32[]{:S(2)}, u32[]{:S(2)}) collective-permute-start(bf16[32,4608]{1,0:T(8,128)(2,1)} %param.1), channel_id=1, source_target_pairs={{0,2},{2,0},{1,3},{3,1},{4,6},{6,4},{5,7},{7,5},{8,10},{10,8},{9,1... | collective-permute-start | bytes 884744 | tf_op jit(solution)/shard_map/ppermute | solution.py:21
  10.5 1.6 broadcast_in_dim.49
  12.0 5.0 %all-to-all-start = ((bf16[8,64,2304]{2,1,0:T(8,128)(2,1)}), bf16[8,64,2304]{2,1,0:T(8,128)(2,1)S(1)}, u32[]{:S(2)}, u32[]{:S(2)}) async-start(bf16[8,64,2304]{2,1,0:T(8,128)(2,1)} %broadcast_in_dim.49), calls=%async_computation | async-start | bytes 4718592 | tf_op jit(solution)/shard_map/all_to_all | solution.py:53
  17.1 4.3 %collective-permute-start.3 = (bf16[64,2304]{1,0:T(8,128)(2,1)S(1)}, bf16[64,2304]{1,0:T(8,128)(2,1)S(1)}, u32[]{:S(2)}, u32[]{:S(2)}) collective-permute-start(bf16[64,2304]{1,0:T(8,128)(2,1)S(1)} %collective-permute-done.2), channel_id=1, source_target_pairs={{0,2},{2,0},{1,3},{3,1},{4,6},{6,4},{5,7},{7,5},{8,10},{10,8},{9,1... | collective-permute-start | bytes 884744 | tf_op jit(solution)/shard_map/ppermute | solution.py:21
  22.9 5.6 %collective-permute-done.5 = bf16[64,2304]{1,0:T(8,128)(2,1)S(1)} collective-permute-done((bf16[64,2304]{1,0:T(8,128)(2,1)S(1)}, bf16[64,2304]{1,0:T(8,128)(2,1)S(1)}, u32[]{:S(2)}, u32[]{:S(2)}) %collective-permute-start.5) | collective-permute-done | bytes 294944 | tf_op jit(solution)/shard_map/ppermute | solution.py:36
  28.9 2.7 %collective-permute-done.4 = bf16[64,2304]{1,0:T(8,128)(2,1)S(1)} collective-permute-done((bf16[64,2304]{1,0:T(8,128)(2,1)S(1)}, bf16[64,2304]{1,0:T(8,128)(2,1)S(1)}, u32[]{:S(2)}, u32[]{:S(2)}) %collective-permute-start.4) | collective-permute-done | bytes 294944 | tf_op jit(solution)/shard_map/ppermute | solution.py:36
  33.1 2.1 %collective-permute-done.8 = bf16[64,2304]{1,0:T(8,128)(2,1)S(1)} collective-permute-done((bf16[64,2304]{1,0:T(8,128)(2,1)S(1)}, bf16[64,2304]{1,0:T(8,128)(2,1)S(1)}, u32[]{:S(2)}, u32[]{:S(2)}) %collective-permute-start.8) | collective-permute-done | bytes 294944 | tf_op jit(solution)/shard_map/ppermute | solution.py:36
  35.7 3.0 %collective-permute-done.7 = bf16[64,2304]{1,0:T(8,128)(2,1)S(1)} collective-permute-done((bf16[64,2304]{1,0:T(8,128)(2,1)S(1)}, bf16[64,2304]{1,0:T(8,128)(2,1)S(1)}, u32[]{:S(2)}, u32[]{:S(2)}) %collective-permute-start.7) | collective-permute-done | bytes 294944 | tf_op jit(solution)/shard_map/ppermute | solution.py:36
  40.9 4.5 %collective-permute-done.10 = bf16[64,2304]{1,0:T(8,128)(2,1)S(1)} collective-permute-done((bf16[64,2304]{1,0:T(8,128)(2,1)S(1)}, bf16[64,2304]{1,0:T(8,128)(2,1)S(1)}, u32[]{:S(2)}, u32[]{:S(2)}) %collective-permute-start.10) | collective-permute-done | bytes 294944 | tf_op jit(solution)/shard_map/ppermute | solution.py:36
  46.2 1.6 %all-to-all-done = bf16[8,64,2304]{2,1,0:T(8,128)(2,1)S(1)} async-done(((bf16[8,64,2304]{2,1,0:T(8,128)(2,1)}), bf16[8,64,2304]{2,1,0:T(8,128)(2,1)S(1)}, u32[]{:S(2)}, u32[]{:S(2)}) %all-to-all-start) | async-done | bytes 2359328 | tf_op jit(solution)/shard_map/all_to_all | solution.py:53
  48.1 2.3 %copy-done.1 = bf16[8,64,2304]{2,1,0:T(8,128)(2,1)S(1)} copy-done((bf16[8,64,2304]{2,1,0:T(8,128)(2,1)S(1)}, bf16[8,64,2304]{2,1,0:T(8,128)(2,1)}, u32[]{:S(2)}) %copy-start.1) | copy-done | bytes 2359320
  51.2 3.0 %collective-permute-start.11 = (bf16[512,256]{1,0:T(8,128)(2,1)S(1)}, bf16[512,256]{1,0:T(8,128)(2,1)S(1)}, u32[]{:S(2)}, u32[]{:S(2)}) collective-permute-start(bf16[512,256]{1,0:T(8,128)(2,1)S(1)} %convolution_convert_fusion.2), channel_id=1, source_target_pairs={{0,2},{2,0},{1,3},{3,1},{4,6},{6,4},{5,7},{7,5},{8,10},{10,8},{9,1... | collective-permute-start | bytes 786440 | tf_op jit(solution)/shard_map/ppermute | solution.py:21
  56.2 2.9 %collective-permute-start.12 = (bf16[512,256]{1,0:T(8,128)(2,1)S(1)}, bf16[512,256]{1,0:T(8,128)(2,1)S(1)}, u32[]{:S(2)}, u32[]{:S(2)}) collective-permute-start(bf16[512,256]{1,0:T(8,128)(2,1)S(1)} %get-tuple-element.42), channel_id=1, source_target_pairs={{0,1},{1,0},{2,3},{3,2},{4,5},{5,4},{6,7},{7,6},{8,9},{9,8},{10,11... | collective-permute-start | bytes 786440 | tf_op jit(solution)/shard_map/ppermute | solution.py:25
  59.1 6.4 %collective-permute-done.12 = bf16[512,256]{1,0:T(8,128)(2,1)S(1)} collective-permute-done((bf16[512,256]{1,0:T(8,128)(2,1)S(1)}, bf16[512,256]{1,0:T(8,128)(2,1)S(1)}, u32[]{:S(2)}, u32[]{:S(2)}) %collective-permute-start.12) | collective-permute-done | bytes 262176 | tf_op jit(solution)/shard_map/ppermute | solution.py:25
  67.1 3.6 %all-to-all-start.1 = ((bf16[8,512,256]{2,1,0:T(8,128)(2,1)}), bf16[8,512,256]{2,1,0:T(8,128)(2,1)S(1)}, u32[]{:S(2)}, u32[]{:S(2)}) async-start(bf16[8,512,256]{2,1,0:T(8,128)(2,1)} %broadcast_in_dim.50), calls=%async_computation.1 | async-start | bytes 4194304 | tf_op jit(solution)/shard_map/all_to_all | solution.py:53
  72.0 2.2 %collective-permute-start.14 = (bf16[512,256]{1,0:T(8,128)(2,1)S(1)}, bf16[512,256]{1,0:T(8,128)(2,1)}, u32[]{:S(2)}, u32[]{:S(2)}) collective-permute-start(bf16[512,256]{1,0:T(8,128)(2,1)S(1)} %add_convert_fusion.1), channel_id=1, source_target_pairs={{4,0},{30,2},{8,4},{2,6},{12,8},{6,10},{16,12},{10,14},{20,16},{14... | collective-permute-start | bytes 786440 | tf_op jit(solution)/shard_map/ppermute | solution.py:36
  75.4 3.8 %collective-permute-done.14 = bf16[512,256]{1,0:T(8,128)(2,1)} collective-permute-done((bf16[512,256]{1,0:T(8,128)(2,1)S(1)}, bf16[512,256]{1,0:T(8,128)(2,1)}, u32[]{:S(2)}, u32[]{:S(2)}) %collective-permute-start.14) | collective-permute-done | bytes 262176 | tf_op jit(solution)/shard_map/ppermute | solution.py:36
  79.8 2.1 %collective-permute-done.15 = bf16[512,256]{1,0:T(8,128)(2,1)} collective-permute-done((bf16[512,256]{1,0:T(8,128)(2,1)S(1)}, bf16[512,256]{1,0:T(8,128)(2,1)}, u32[]{:S(2)}, u32[]{:S(2)}) %collective-permute-start.15) | collective-permute-done | bytes 262176 | tf_op jit(solution)/shard_map/ppermute | solution.py:36
  82.6 3.3 %collective-permute-start.17 = (bf16[512,256]{1,0:T(8,128)(2,1)}, bf16[512,256]{1,0:T(8,128)(2,1)}, u32[]{:S(2)}, u32[]{:S(2)}) collective-permute-start(bf16[512,256]{1,0:T(8,128)(2,1)} %collective-permute-done.14), channel_id=1, source_target_pairs={{0,2},{2,0},{1,3},{3,1},{4,6},{6,4},{5,7},{7,5},{8,10},{10,8},{9,1... | collective-permute-start | bytes 786440 | tf_op jit(solution)/shard_map/ppermute | solution.py:21
  87.4 1.5 collective-permute-done.19
  88.9 2.1 %collective-permute-start.20 = (bf16[512,256]{1,0:T(8,128)(2,1)}, bf16[512,256]{1,0:T(8,128)(2,1)}, u32[]{:S(2)}, u32[]{:S(2)}) collective-permute-start(bf16[512,256]{1,0:T(8,128)(2,1)} %collective-permute-done.19), channel_id=1, source_target_pairs={{0,2},{2,0},{1,3},{3,1},{4,6},{6,4},{5,7},{7,5},{8,10},{10,8},{9,1... | collective-permute-start | bytes 786440 | tf_op jit(solution)/shard_map/ppermute | solution.py:21
  91.0 9.8 %all-to-all-done.1 = bf16[8,512,256]{2,1,0:T(8,128)(2,1)S(1)} async-done(((bf16[8,512,256]{2,1,0:T(8,128)(2,1)}), bf16[8,512,256]{2,1,0:T(8,128)(2,1)S(1)}, u32[]{:S(2)}, u32[]{:S(2)}) %all-to-all-start.1) | async-done | bytes 2097184 | tf_op jit(solution)/shard_map/all_to_all | solution.py:53
  103.6 2.3 %collective-permute-start.23 = (bf16[512,256]{1,0:T(8,128)(2,1)}, bf16[512,256]{1,0:T(8,128)(2,1)S(1)}, u32[]{:S(2)}, u32[]{:S(2)}) collective-permute-start(bf16[512,256]{1,0:T(8,128)(2,1)} %collective-permute-done.19), channel_id=1, source_target_pairs={{4,0},{30,2},{8,4},{2,6},{12,8},{6,10},{16,12},{10,14},{20,16},{14... | collective-permute-start | bytes 786440 | tf_op jit(solution)/shard_map/ppermute | solution.py:36
  108.4 5.2 %collective-permute-start.25 = (bf16[512,256]{1,0:T(8,128)(2,1)S(1)}, bf16[512,256]{1,0:T(8,128)(2,1)S(1)}, u32[]{:S(2)}, u32[]{:S(2)}) collective-permute-start(bf16[512,256]{1,0:T(8,128)(2,1)S(1)} %collective-permute-done.22), channel_id=1, source_target_pairs={{0,2},{2,0},{1,3},{3,1},{4,6},{6,4},{5,7},{7,5},{8,10},{10,8},{9,1... | collective-permute-start | bytes 786440 | tf_op jit(solution)/shard_map/ppermute | solution.py:21
  113.7 2.1 %collective-permute-start.27 = (bf16[512,256]{1,0:T(8,128)(2,1)S(1)}, bf16[512,256]{1,0:T(8,128)(2,1)S(1)}, u32[]{:S(2)}, u32[]{:S(2)}) collective-permute-start(bf16[512,256]{1,0:T(8,128)(2,1)S(1)} %collective-permute-done.26), channel_id=1, source_target_pairs={{0,2},{2,0},{1,3},{3,1},{4,6},{6,4},{5,7},{7,5},{8,10},{10,8},{9,1... | collective-permute-start | bytes 786440 | tf_op jit(solution)/shard_map/ppermute | solution.py:21
  125.7 3.6 %all-to-all-start.2 = ((bf16[8,2,32,1536]{3,2,1,0:T(8,128)(2,1)}), bf16[8,2,32,1536]{3,2,1,0:T(8,128)(2,1)S(1)}, u32[]{:S(2)}, u32[]{:S(2)}) async-start(bf16[8,2,32,1536]{3,2,1,0:T(8,128)(2,1)} %pad_maximum_fusion), calls=%async_computation.2 | async-start | bytes 3145728 | tf_op jit(solution)/shard_map/all_to_all | solution.py:109
  132.2 5.7 %collective-permute-start.29 = (bf16[64,768]{1,0:T(8,128)(2,1)S(1)}, bf16[64,768]{1,0:T(8,128)(2,1)S(1)}, u32[]{:S(2)}, u32[]{:S(2)}) collective-permute-start(bf16[64,768]{1,0:T(8,128)(2,1)S(1)} %get-tuple-element.27), channel_id=1, source_target_pairs={{16,0},{20,4},{24,8},{28,12},{0,16},{4,20},{8,24},{12,28},{17,1},{... | collective-permute-start | bytes 294920 | tf_op jit(solution)/shard_map/ppermute | solution.py:29
  140.0 1.7 %collective-permute-start.33 = (bf16[64,768]{1,0:T(8,128)(2,1)S(1)}, bf16[64,768]{1,0:T(8,128)(2,1)S(1)}, u32[]{:S(2)}, u32[]{:S(2)}) collective-permute-start(bf16[64,768]{1,0:T(8,128)(2,1)S(1)} %get-tuple-element.30), channel_id=1, source_target_pairs={{24,0},{28,4},{0,8},{4,12},{8,16},{12,20},{16,24},{20,28},{25,1},{... | collective-permute-start | bytes 294920 | tf_op jit(solution)/shard_map/ppermute | solution.py:29
  141.7 4.6 %collective-permute-start.34 = (bf16[64,768]{1,0:T(8,128)(2,1)S(1)}, bf16[64,768]{1,0:T(8,128)(2,1)S(1)}, u32[]{:S(2)}, u32[]{:S(2)}) collective-permute-start(bf16[64,768]{1,0:T(8,128)(2,1)S(1)} %get-tuple-element.29), channel_id=1, source_target_pairs={{12,0},{16,4},{20,8},{24,12},{28,16},{0,20},{4,24},{8,28},{13,1},{... | collective-permute-start | bytes 294920 | tf_op jit(solution)/shard_map/ppermute | solution.py:29
  146.6 4.2 %collective-permute-done.32 = bf16[64,768]{1,0:T(8,128)(2,1)S(1)} collective-permute-done((bf16[64,768]{1,0:T(8,128)(2,1)S(1)}, bf16[64,768]{1,0:T(8,128)(2,1)S(1)}, u32[]{:S(2)}, u32[]{:S(2)}) %collective-permute-start.32) | collective-permute-done | bytes 98336 | tf_op jit(solution)/shard_map/ppermute | solution.py:29
  150.8 3.9 %collective-permute-done.34 = bf16[64,768]{1,0:T(8,128)(2,1)S(1)} collective-permute-done((bf16[64,768]{1,0:T(8,128)(2,1)S(1)}, bf16[64,768]{1,0:T(8,128)(2,1)S(1)}, u32[]{:S(2)}, u32[]{:S(2)}) %collective-permute-start.34) | collective-permute-done | bytes 98336 | tf_op jit(solution)/shard_map/ppermute | solution.py:29
  155.2 4.2 %collective-permute-start.36 = (bf16[32,2304]{1,0:T(8,128)(2,1)S(1)}, bf16[32,2304]{1,0:T(8,128)(2,1)S(1)}, u32[]{:S(2)}, u32[]{:S(2)}) collective-permute-start(bf16[32,2304]{1,0:T(8,128)(2,1)S(1)} %fusion.18), channel_id=1, source_target_pairs={{0,2},{2,0},{1,3},{3,1},{4,6},{6,4},{5,7},{7,5},{8,10},{10,8},{9,1... | collective-permute-start | bytes 442376 | tf_op jit(solution)/shard_map/ppermute | solution.py:21
  (113 shorter events, 46.4 us)
Async XLA Ops:
  7.1 9.9 %collective-permute-start.2 = (bf16[64,2304]{1,0:T(8,128)(2,1)S(1)}, bf16[64,2304]{1,0:T(8,128)(2,1)S(1)}, u32[]{:S(2)}, u32[]{:S(2)}) collective-permute-start(bf16[64,2304]{1,0:T(8,128)(2,1)S(1)} %bitcast.155), channel_id=1, source_target_pairs={{4,0},{30,2},{8,4},{2,6},{12,8},{6,10},{16,12},{10,14},{20,16},{14... | collective-permute-start | bytes 884744 | tf_op jit(solution)/shard_map/ppermute | solution.py:36
  8.9 13.2 %collective-permute-start.1 = (bf16[64,2304]{1,0:T(8,128)(2,1)S(1)}, bf16[64,2304]{1,0:T(8,128)(2,1)S(1)}, u32[]{:S(2)}, u32[]{:S(2)}) collective-permute-start(bf16[64,2304]{1,0:T(8,128)(2,1)S(1)} %bitcast.124), channel_id=1, source_target_pairs={{4,0},{30,2},{8,4},{2,6},{12,8},{6,10},{16,12},{10,14},{20,16},{14... | collective-permute-start | bytes 884744 | tf_op jit(solution)/shard_map/ppermute | solution.py:36
  12.0 35.9 %all-to-all-start = ((bf16[8,64,2304]{2,1,0:T(8,128)(2,1)}), bf16[8,64,2304]{2,1,0:T(8,128)(2,1)S(1)}, u32[]{:S(2)}, u32[]{:S(2)}) async-start(bf16[8,64,2304]{2,1,0:T(8,128)(2,1)} %broadcast_in_dim.49), calls=%async_computation | async-start | bytes 4718592 | tf_op jit(solution)/shard_map/all_to_all | solution.py:53
  17.1 14.6 %collective-permute-start.3 = (bf16[64,2304]{1,0:T(8,128)(2,1)S(1)}, bf16[64,2304]{1,0:T(8,128)(2,1)S(1)}, u32[]{:S(2)}, u32[]{:S(2)}) collective-permute-start(bf16[64,2304]{1,0:T(8,128)(2,1)S(1)} %collective-permute-done.2), channel_id=1, source_target_pairs={{0,2},{2,0},{1,3},{3,1},{4,6},{6,4},{5,7},{7,5},{8,10},{10,8},{9,1... | collective-permute-start | bytes 884744 | tf_op jit(solution)/shard_map/ppermute | solution.py:21
  21.4 7.1 %collective-permute-start.5 = (bf16[64,2304]{1,0:T(8,128)(2,1)S(1)}, bf16[64,2304]{1,0:T(8,128)(2,1)S(1)}, u32[]{:S(2)}, u32[]{:S(2)}) collective-permute-start(bf16[64,2304]{1,0:T(8,128)(2,1)S(1)} %collective-permute-done.2), channel_id=1, source_target_pairs={{4,0},{30,2},{8,4},{2,6},{12,8},{6,10},{16,12},{10,14},{20,16},{14... | collective-permute-start | bytes 884744 | tf_op jit(solution)/shard_map/ppermute | solution.py:36
  22.1 9.5 %collective-permute-start.4 = (bf16[64,2304]{1,0:T(8,128)(2,1)S(1)}, bf16[64,2304]{1,0:T(8,128)(2,1)S(1)}, u32[]{:S(2)}, u32[]{:S(2)}) collective-permute-start(bf16[64,2304]{1,0:T(8,128)(2,1)S(1)} %collective-permute-done.1), channel_id=1, source_target_pairs={{4,0},{30,2},{8,4},{2,6},{12,8},{6,10},{16,12},{10,14},{20,16},{14... | collective-permute-start | bytes 884744 | tf_op jit(solution)/shard_map/ppermute | solution.py:36
  28.5 10.2 %collective-permute-start.6 = (bf16[64,2304]{1,0:T(8,128)(2,1)S(1)}, bf16[64,2304]{1,0:T(8,128)(2,1)S(1)}, u32[]{:S(2)}, u32[]{:S(2)}) collective-permute-start(bf16[64,2304]{1,0:T(8,128)(2,1)S(1)} %collective-permute-done.5), channel_id=1, source_target_pairs={{0,2},{2,0},{1,3},{3,1},{4,6},{6,4},{5,7},{7,5},{8,10},{10,8},{9,1... | collective-permute-start | bytes 884744 | tf_op jit(solution)/shard_map/ppermute | solution.py:21
  31.6 7.1 %collective-permute-start.7 = (bf16[64,2304]{1,0:T(8,128)(2,1)S(1)}, bf16[64,2304]{1,0:T(8,128)(2,1)S(1)}, u32[]{:S(2)}, u32[]{:S(2)}) collective-permute-start(bf16[64,2304]{1,0:T(8,128)(2,1)S(1)} %collective-permute-done.4), channel_id=1, source_target_pairs={{4,0},{30,2},{8,4},{2,6},{12,8},{6,10},{16,12},{10,14},{20,16},{14... | collective-permute-start | bytes 884744 | tf_op jit(solution)/shard_map/ppermute | solution.py:36
  56.2 9.3 %collective-permute-start.12 = (bf16[512,256]{1,0:T(8,128)(2,1)S(1)}, bf16[512,256]{1,0:T(8,128)(2,1)S(1)}, u32[]{:S(2)}, u32[]{:S(2)}) collective-permute-start(bf16[512,256]{1,0:T(8,128)(2,1)S(1)} %get-tuple-element.42), channel_id=1, source_target_pairs={{0,1},{1,0},{2,3},{3,2},{4,5},{5,4},{6,7},{7,6},{8,9},{9,8},{10,11... | collective-permute-start | bytes 786440 | tf_op jit(solution)/shard_map/ppermute | solution.py:25
  67.1 33.7 %all-to-all-start.1 = ((bf16[8,512,256]{2,1,0:T(8,128)(2,1)}), bf16[8,512,256]{2,1,0:T(8,128)(2,1)S(1)}, u32[]{:S(2)}, u32[]{:S(2)}) async-start(bf16[8,512,256]{2,1,0:T(8,128)(2,1)} %broadcast_in_dim.50), calls=%async_computation.1 | async-start | bytes 4194304 | tf_op jit(solution)/shard_map/all_to_all | solution.py:53
  72.0 7.2 %collective-permute-start.14 = (bf16[512,256]{1,0:T(8,128)(2,1)S(1)}, bf16[512,256]{1,0:T(8,128)(2,1)}, u32[]{:S(2)}, u32[]{:S(2)}) collective-permute-start(bf16[512,256]{1,0:T(8,128)(2,1)S(1)} %add_convert_fusion.1), channel_id=1, source_target_pairs={{4,0},{30,2},{8,4},{2,6},{12,8},{6,10},{16,12},{10,14},{20,16},{14... | collective-permute-start | bytes 786440 | tf_op jit(solution)/shard_map/ppermute | solution.py:36
  74.2 7.8 %collective-permute-start.15 = (bf16[512,256]{1,0:T(8,128)(2,1)S(1)}, bf16[512,256]{1,0:T(8,128)(2,1)}, u32[]{:S(2)}, u32[]{:S(2)}) collective-permute-start(bf16[512,256]{1,0:T(8,128)(2,1)S(1)} %collective-permute-done.13), channel_id=1, source_target_pairs={{4,0},{30,2},{8,4},{2,6},{12,8},{6,10},{16,12},{10,14},{20,16},{14... | collective-permute-start | bytes 786440 | tf_op jit(solution)/shard_map/ppermute | solution.py:36
  79.2 6.9 %collective-permute-start.18 = (bf16[512,256]{1,0:T(8,128)(2,1)}, bf16[512,256]{1,0:T(8,128)(2,1)S(1)}, u32[]{:S(2)}, u32[]{:S(2)}) collective-permute-start(bf16[512,256]{1,0:T(8,128)(2,1)} %collective-permute-done.14), channel_id=1, source_target_pairs={{4,0},{30,2},{8,4},{2,6},{12,8},{6,10},{16,12},{10,14},{20,16},{14... | collective-permute-start | bytes 786440 | tf_op jit(solution)/shard_map/ppermute | solution.py:36
  82.0 6.9 %collective-permute-start.19 = (bf16[512,256]{1,0:T(8,128)(2,1)}, bf16[512,256]{1,0:T(8,128)(2,1)}, u32[]{:S(2)}, u32[]{:S(2)}) collective-permute-start(bf16[512,256]{1,0:T(8,128)(2,1)} %collective-permute-done.15), channel_id=1, source_target_pairs={{4,0},{30,2},{8,4},{2,6},{12,8},{6,10},{16,12},{10,14},{20,16},{14... | collective-permute-start | bytes 786440 | tf_op jit(solution)/shard_map/ppermute | solution.py:36
  82.6 21.0 %collective-permute-start.17 = (bf16[512,256]{1,0:T(8,128)(2,1)}, bf16[512,256]{1,0:T(8,128)(2,1)}, u32[]{:S(2)}, u32[]{:S(2)}) collective-permute-start(bf16[512,256]{1,0:T(8,128)(2,1)} %collective-permute-done.14), channel_id=1, source_target_pairs={{0,2},{2,0},{1,3},{3,1},{4,6},{6,4},{5,7},{7,5},{8,10},{10,8},{9,1... | collective-permute-start | bytes 786440 | tf_op jit(solution)/shard_map/ppermute | solution.py:21
  86.0 22.4 %collective-permute-start.16 = (bf16[512,256]{1,0:T(8,128)(2,1)}, bf16[512,256]{1,0:T(8,128)(2,1)}, u32[]{:S(2)}, u32[]{:S(2)}) collective-permute-start(bf16[512,256]{1,0:T(8,128)(2,1)} %collective-permute-done.15), channel_id=1, source_target_pairs={{0,2},{2,0},{1,3},{3,1},{4,6},{6,4},{5,7},{7,5},{8,10},{10,8},{9,1... | collective-permute-start | bytes 786440 | tf_op jit(solution)/shard_map/ppermute | solution.py:21
  86.1 31.1 %collective-permute-start.21 = (bf16[512,256]{1,0:T(8,128)(2,1)S(1)}, bf16[512,256]{1,0:T(8,128)(2,1)}, u32[]{:S(2)}, u32[]{:S(2)}) collective-permute-start(bf16[512,256]{1,0:T(8,128)(2,1)S(1)} %collective-permute-done.18), channel_id=1, source_target_pairs={{0,2},{2,0},{1,3},{3,1},{4,6},{6,4},{5,7},{7,5},{8,10},{10,8},{9,1... | collective-permute-start | bytes 786440 | tf_op jit(solution)/shard_map/ppermute | solution.py:21
  87.4 18.5 %collective-permute-start.22 = (bf16[512,256]{1,0:T(8,128)(2,1)S(1)}, bf16[512,256]{1,0:T(8,128)(2,1)S(1)}, u32[]{:S(2)}, u32[]{:S(2)}) collective-permute-start(bf16[512,256]{1,0:T(8,128)(2,1)S(1)} %collective-permute-done.18), channel_id=1, source_target_pairs={{4,0},{30,2},{8,4},{2,6},{12,8},{6,10},{16,12},{10,14},{20,16},{14... | collective-permute-start | bytes 786440 | tf_op jit(solution)/shard_map/ppermute | solution.py:36
  88.9 30.6 %collective-permute-start.20 = (bf16[512,256]{1,0:T(8,128)(2,1)}, bf16[512,256]{1,0:T(8,128)(2,1)}, u32[]{:S(2)}, u32[]{:S(2)}) collective-permute-start(bf16[512,256]{1,0:T(8,128)(2,1)} %collective-permute-done.19), channel_id=1, source_target_pairs={{0,2},{2,0},{1,3},{3,1},{4,6},{6,4},{5,7},{7,5},{8,10},{10,8},{9,1... | collective-permute-start | bytes 786440 | tf_op jit(solution)/shard_map/ppermute | solution.py:21
  103.6 10.0 %collective-permute-start.23 = (bf16[512,256]{1,0:T(8,128)(2,1)}, bf16[512,256]{1,0:T(8,128)(2,1)S(1)}, u32[]{:S(2)}, u32[]{:S(2)}) collective-permute-start(bf16[512,256]{1,0:T(8,128)(2,1)} %collective-permute-done.19), channel_id=1, source_target_pairs={{4,0},{30,2},{8,4},{2,6},{12,8},{6,10},{16,12},{10,14},{20,16},{14... | collective-permute-start | bytes 786440 | tf_op jit(solution)/shard_map/ppermute | solution.py:36
  105.9 7.8 %collective-permute-start.26 = (bf16[512,256]{1,0:T(8,128)(2,1)S(1)}, bf16[512,256]{1,0:T(8,128)(2,1)S(1)}, u32[]{:S(2)}, u32[]{:S(2)}) collective-permute-start(bf16[512,256]{1,0:T(8,128)(2,1)S(1)} %collective-permute-done.22), channel_id=1, source_target_pairs={{4,0},{30,2},{8,4},{2,6},{12,8},{6,10},{16,12},{10,14},{20,16},{14... | collective-permute-start | bytes 786440 | tf_op jit(solution)/shard_map/ppermute | solution.py:36
  108.4 12.5 %collective-permute-start.25 = (bf16[512,256]{1,0:T(8,128)(2,1)S(1)}, bf16[512,256]{1,0:T(8,128)(2,1)S(1)}, u32[]{:S(2)}, u32[]{:S(2)}) collective-permute-start(bf16[512,256]{1,0:T(8,128)(2,1)S(1)} %collective-permute-done.22), channel_id=1, source_target_pairs={{0,2},{2,0},{1,3},{3,1},{4,6},{6,4},{5,7},{7,5},{8,10},{10,8},{9,1... | collective-permute-start | bytes 786440 | tf_op jit(solution)/shard_map/ppermute | solution.py:21
  113.6 7.9 %collective-permute-start.24 = (bf16[512,256]{1,0:T(8,128)(2,1)S(1)}, bf16[512,256]{1,0:T(8,128)(2,1)S(1)}, u32[]{:S(2)}, u32[]{:S(2)}) collective-permute-start(bf16[512,256]{1,0:T(8,128)(2,1)S(1)} %collective-permute-done.23), channel_id=1, source_target_pairs={{0,2},{2,0},{1,3},{3,1},{4,6},{6,4},{5,7},{7,5},{8,10},{10,8},{9,1... | collective-permute-start | bytes 786440 | tf_op jit(solution)/shard_map/ppermute | solution.py:21
  113.7 8.0 %collective-permute-start.27 = (bf16[512,256]{1,0:T(8,128)(2,1)S(1)}, bf16[512,256]{1,0:T(8,128)(2,1)S(1)}, u32[]{:S(2)}, u32[]{:S(2)}) collective-permute-start(bf16[512,256]{1,0:T(8,128)(2,1)S(1)} %collective-permute-done.26), channel_id=1, source_target_pairs={{0,2},{2,0},{1,3},{3,1},{4,6},{6,4},{5,7},{7,5},{8,10},{10,8},{9,1... | collective-permute-start | bytes 786440 | tf_op jit(solution)/shard_map/ppermute | solution.py:21
  125.7 29.2 %all-to-all-start.2 = ((bf16[8,2,32,1536]{3,2,1,0:T(8,128)(2,1)}), bf16[8,2,32,1536]{3,2,1,0:T(8,128)(2,1)S(1)}, u32[]{:S(2)}, u32[]{:S(2)}) async-start(bf16[8,2,32,1536]{3,2,1,0:T(8,128)(2,1)} %pad_maximum_fusion), calls=%async_computation.2 | async-start | bytes 3145728 | tf_op jit(solution)/shard_map/all_to_all | solution.py:109
  132.2 9.5 %collective-permute-start.29 = (bf16[64,768]{1,0:T(8,128)(2,1)S(1)}, bf16[64,768]{1,0:T(8,128)(2,1)S(1)}, u32[]{:S(2)}, u32[]{:S(2)}) collective-permute-start(bf16[64,768]{1,0:T(8,128)(2,1)S(1)} %get-tuple-element.27), channel_id=1, source_target_pairs={{16,0},{20,4},{24,8},{28,12},{0,16},{4,20},{8,24},{12,28},{17,1},{... | collective-permute-start | bytes 294920 | tf_op jit(solution)/shard_map/ppermute | solution.py:29
  137.9 8.4 %collective-permute-start.30 = (bf16[64,768]{1,0:T(8,128)(2,1)S(1)}, bf16[64,768]{1,0:T(8,128)(2,1)S(1)}, u32[]{:S(2)}, u32[]{:S(2)}) collective-permute-start(bf16[64,768]{1,0:T(8,128)(2,1)S(1)} %get-tuple-element.33), channel_id=1, source_target_pairs={{4,0},{8,4},{12,8},{16,12},{20,16},{24,20},{28,24},{0,28},{5,1},{9... | collective-permute-start | bytes 294920 | tf_op jit(solution)/shard_map/ppermute | solution.py:29
  138.8 7.8 %collective-permute-start.31 = (bf16[64,768]{1,0:T(8,128)(2,1)S(1)}, bf16[64,768]{1,0:T(8,128)(2,1)S(1)}, u32[]{:S(2)}, u32[]{:S(2)}) collective-permute-start(bf16[64,768]{1,0:T(8,128)(2,1)S(1)} %get-tuple-element.32), channel_id=1, source_target_pairs={{28,0},{0,4},{4,8},{8,12},{12,16},{16,20},{20,24},{24,28},{29,1},{... | collective-permute-start | bytes 294920 | tf_op jit(solution)/shard_map/ppermute | solution.py:29
  139.4 11.4 %collective-permute-start.32 = (bf16[64,768]{1,0:T(8,128)(2,1)S(1)}, bf16[64,768]{1,0:T(8,128)(2,1)S(1)}, u32[]{:S(2)}, u32[]{:S(2)}) collective-permute-start(bf16[64,768]{1,0:T(8,128)(2,1)S(1)} %get-tuple-element.31), channel_id=1, source_target_pairs={{8,0},{12,4},{16,8},{20,12},{24,16},{28,20},{0,24},{4,28},{9,1},{1... | collective-permute-start | bytes 294920 | tf_op jit(solution)/shard_map/ppermute | solution.py:29
  140.0 10.8 %collective-permute-start.33 = (bf16[64,768]{1,0:T(8,128)(2,1)S(1)}, bf16[64,768]{1,0:T(8,128)(2,1)S(1)}, u32[]{:S(2)}, u32[]{:S(2)}) collective-permute-start(bf16[64,768]{1,0:T(8,128)(2,1)S(1)} %get-tuple-element.30), channel_id=1, source_target_pairs={{24,0},{28,4},{0,8},{4,12},{8,16},{12,20},{16,24},{20,28},{25,1},{... | collective-permute-start | bytes 294920 | tf_op jit(solution)/shard_map/ppermute | solution.py:29
  141.7 13.0 %collective-permute-start.34 = (bf16[64,768]{1,0:T(8,128)(2,1)S(1)}, bf16[64,768]{1,0:T(8,128)(2,1)S(1)}, u32[]{:S(2)}, u32[]{:S(2)}) collective-permute-start(bf16[64,768]{1,0:T(8,128)(2,1)S(1)} %get-tuple-element.29), channel_id=1, source_target_pairs={{12,0},{16,4},{20,8},{24,12},{28,16},{0,20},{4,24},{8,28},{13,1},{... | collective-permute-start | bytes 294920 | tf_op jit(solution)/shard_map/ppermute | solution.py:29
  146.3 8.5 %collective-permute-start.35 = (bf16[64,768]{1,0:T(8,128)(2,1)S(1)}, bf16[64,768]{1,0:T(8,128)(2,1)S(1)}, u32[]{:S(2)}, u32[]{:S(2)}) collective-permute-start(bf16[64,768]{1,0:T(8,128)(2,1)S(1)} %get-tuple-element.28), channel_id=1, source_target_pairs={{20,0},{24,4},{28,8},{0,12},{4,16},{8,20},{12,24},{16,28},{21,1},{... | collective-permute-start | bytes 294920 | tf_op jit(solution)/shard_map/ppermute | solution.py:29
  (15 other events, 60.0 us)

commit v4 on v3

v4 whole, which is shorter than its diff:
```python
import math

import jax
import jax.numpy as jnp
from jax import lax
from jax.experimental import pallas as pl
from jax.experimental.pallas import tpu as pltpu
from jax.sharding import Mesh
from jax.sharding import PartitionSpec as P

coef_linear = 3.4445
coef_cubic = -4.775
coef_quintic = 2.0315
update_gain = 0.2 * math.sqrt(18432.0)

X, YL, Z, C, S = "x", "yl", "z", "c", "s"
NZ, NR = 8, 8
ROWS, COLS = 32, 4608
TILE = 256
bf16, f32 = jnp.bfloat16, jnp.float32
ORDER = (0, 1, 7, 2, 6, 3, 5, 4)
PARTS = 16
K_PARTS = 2
OUT_PARTS = 9


def swap(a):
    return lax.ppermute(a, C, [(0, 1), (1, 0)])


def swap_slab(a):
    return lax.ppermute(a, S, [(0, 1), (1, 0)])


def turn(a):
    pairs = []
    for i in range(NZ):
        pairs += [(2 * ((i + 1) % NZ), 2 * i), (2 * ((i - 1) % NZ) + 1, 2 * i + 1)]
    return lax.ppermute(a, (Z, C), pairs)


def ring_z(a):
    b = swap(a)
    mine, others = [a] + [None] * (NZ - 1), [b] + [None] * (NZ - 1)
    for step in range(1, 4):
        a = turn(a)
        b = turn(b)
        mine[step], others[step] = a, b
        mine[NZ - step], others[NZ - step] = swap(b), swap(a)
    mine[4] = turn(a)
    others[4] = swap(mine[4])
    return [part[e] for e in ORDER for part in (mine, others)]


def where_from(i):
    core, z = lax.axis_index(C), lax.axis_index(Z)
    e = ORDER[i // 2]
    return (z + e + core * (NZ - 2 * e) + NZ) % NZ, core if i % 2 == 0 else 1 - core


def gather_r(a):
    copies = jnp.broadcast_to(a[None], (NR, *a.shape))
    return lax.all_to_all(copies, (X, YL), 0, 0, tiled=True)


def gram_kernel(*refs):
    pieces, (cols_ref, rows_ref, own_ref, sent_ref), (x, y, sem, sem_out) = refs[:PARTS], refs[PARTS:-4], refs[-4:]
    width = COLS // K_PARTS
    copies = []
    for k in range(K_PARTS):
        cut = pl.ds(k * width, width)
        group = [pltpu.make_async_copy(cols_ref.at[:, cut], y.at[:, cut], sem.at[k, PARTS])]
        for i, piece in enumerate(pieces):
            z, h = where_from(i)
            at = pl.ds(pl.multiple_of((2 * z + h) * ROWS, ROWS), ROWS)
            group.append(pltpu.make_async_copy(piece.at[:, cut], x.at[at, cut], sem.at[k, i]))
        for copy in group:
            copy.start()
        copies.append(group)
    total = None
    outs = []
    for k in range(K_PARTS):
        cut = pl.ds(k * width, width)
        for copy in copies[k]:
            copy.wait()
        out = pltpu.make_async_copy(x.at[:, cut], rows_ref.at[:, cut], sem_out.at[k])
        out.start()
        outs.append(out)
        term = lax.dot_general(x[:, cut], y[:, cut], (((1,), (1,)), ((), ())), preferred_element_type=f32)
        total = term if total is None else total + term
    own_ref[...] = total
    sent_ref[...] = total.astype(bf16)
    for out in outs:
        out.wait()


def gram_part(pieces, cols):
    n = 2 * NZ * ROWS
    return pl.pallas_call(
        gram_kernel,
        out_shape=(
            jax.ShapeDtypeStruct((n, COLS), bf16),
            jax.ShapeDtypeStruct((n, TILE), f32),
            jax.ShapeDtypeStruct((n, TILE), bf16),
        ),
        in_specs=[pl.BlockSpec(memory_space=pl.ANY)] * (PARTS + 1),
        out_specs=(
            pl.BlockSpec(memory_space=pl.ANY),
            pl.BlockSpec(memory_space=pltpu.VMEM),
            pl.BlockSpec(memory_space=pltpu.VMEM),
        ),
        scratch_shapes=[
            pltpu.VMEM((n, COLS), bf16),
            pltpu.VMEM((TILE, COLS), bf16),
            pltpu.SemaphoreType.DMA((K_PARTS, PARTS + 1)),
            pltpu.SemaphoreType.DMA((K_PARTS,)),
        ],
        compiler_params=pltpu.CompilerParams(vmem_limit_bytes=32 << 20),
        cost_estimate=pl.CostEstimate(flops=2 * n * TILE * COLS, bytes_accessed=12 << 20, transcendentals=0),
        name="gram_part",
    )(*pieces, cols)


def product_kernel(*refs):
    a_refs, (b_ref, rows_ref, out_ref), (a, b, x, out, sem_a, sem_b, sem_x, sem_out) = (
        refs[:PARTS],
        refs[PARTS:-8],
        refs[-8:],
    )
    copies = []
    for i, ref in enumerate(a_refs):
        z, h = where_from(i)
        copies.append(pltpu.make_async_copy(ref, a.at[:, pl.ds(i * TILE, TILE)], sem_a.at[i]))
        copies.append(pltpu.make_async_copy(b_ref.at[:, z, h], b.at[i], sem_b.at[i]))
    for copy in copies:
        copy.start()
    load = pltpu.make_async_copy(rows_ref, x, sem_x)
    load.start()
    for copy in copies:
        copy.wait()
    squared = jnp.dot(a[...], b[...].reshape(PARTS * TILE, TILE), preferred_element_type=f32)
    gram = a[:, pl.ds(0, TILE)].astype(f32)
    poly = (coef_cubic * gram + coef_quintic * squared).astype(bf16)
    load.wait()
    width = COLS // OUT_PARTS
    outs = []
    for k in range(OUT_PARTS):
        cut = pl.ds(k * width, width)
        term = lax.dot_general(poly, x[:, cut], (((0,), (0,)), ((), ())), preferred_element_type=f32)
        out[:, cut] = term.astype(bf16)
        copy = pltpu.make_async_copy(out.at[:, cut], out_ref.at[:, cut], sem_out.at[k])
        copy.start()
        outs.append(copy)
    for copy in outs:
        copy.wait()


def product_part(a_parts, b, rows):
    n = 2 * NZ * ROWS
    return pl.pallas_call(
        product_kernel,
        out_shape=jax.ShapeDtypeStruct((TILE, COLS), bf16),
        in_specs=[pl.BlockSpec(memory_space=pl.ANY)] * (PARTS + 2),
        out_specs=pl.BlockSpec(memory_space=pl.ANY),
        scratch_shapes=[
            pltpu.VMEM((n, PARTS * TILE), bf16),
            pltpu.VMEM((PARTS, NR, ROWS, TILE), bf16),
            pltpu.VMEM((n, COLS), bf16),
            pltpu.VMEM((TILE, COLS), bf16),
            pltpu.SemaphoreType.DMA((PARTS,)),
            pltpu.SemaphoreType.DMA((PARTS,)),
            pltpu.SemaphoreType.DMA,
            pltpu.SemaphoreType.DMA((OUT_PARTS,)),
        ],
        compiler_params=pltpu.CompilerParams(vmem_limit_bytes=32 << 20),
        cost_estimate=pl.CostEstimate(
            flops=2 * n * TILE * (COLS + PARTS * TILE), bytes_accessed=14 << 20, transcendentals=0
        ),
        name="product_part",
    )(*a_parts, b, rows)


def on_device(iterate):
    cols = gather_r(iterate).reshape(TILE, COLS)
    rows, own, sent = gram_part(ring_z(iterate), cols)
    gram = (own + swap_slab(sent).astype(f32)).astype(bf16)
    every = gather_r(gram).reshape(NR, NZ, 2, ROWS, TILE)
    part = product_part(ring_z(gram), every, rows)
    got = lax.all_to_all(part.reshape(NR, ROWS, COLS), (X, YL), 0, 0, tiled=True)
    stepped = coef_linear * iterate.astype(f32) + got.astype(f32).sum(0)
    return (update_gain * stepped).astype(bf16)


def solution(mesh):
    fine = Mesh(mesh.devices.reshape(4, 2, 8, 2, 2), (X, YL, Z, C, S))
    spec = P((X, YL, Z, C), S)
    return jax.shard_map(on_device, mesh=fine, in_specs=(spec,), out_specs=spec, check_vma=False)
```

time: 162 us -> 183 us (1.13)
  blocking collectives: 0 us -> 34.4 us
  local copies, waits for them, and re-layouts: 15.5 us -> 48.6 us
  waiting for transfers between devices: 55.5 us -> 34.8 us
  starting transfers between devices: 70.3 us -> 51.1 us
  matrix products: 15.8 us -> 0 us
  Pallas kernels: 0 us -> 12.1 us
  other arithmetic: 3.64 us -> 1.19 us
    unnamed x15 -> x102, local copies, waits for them, and re-layouts: 5.09 us -> 44.6 us
    all_to_all x0 -> x1, blocking collectives: none -> 34.4 us  [on_device(): lax.all_to_all(part.reshape(NR, ROWS, COLS), (X, YL), 0, 0, tiled=True)]
    dot_general x22 -> x0, matrix products: 15.8 us -> none  [the longest x18 13 us: dot(): return jnp.dot(a, b, preferred_element_type=f32)]
    ppermute x7 -> x0, starting transfers between devices: 14.4 us -> none  [shift_z(): return lax.ppermute(a, Z, [((i + d) % NZ, i) for i in range(NZ)])]
    pallas_call x0 -> x2, Pallas kernels: none -> 12.1 us  [the longest x1 7.8 us: product_part(): pl.pallas_call(product_kernel, out_shape=jax.ShapeDtypeStruct((TILE, COLS...]
    all_to_all x2, waiting for transfers between devices: 11.4 us -> 0.01 us  [gather_r(): return lax.all_to_all(copies, (X, YL), 0, 0, tiled=True)]
    ppermute x14, starting transfers between devices: 10 us -> 1.75 us  [turn(): return lax.ppermute(a, (Z, C), pairs)]
    ppermute x7 -> x0, waiting for transfers between devices: 8.16 us -> none  [shift_z(): return lax.ppermute(a, Z, [((i + d) % NZ, i) for i in range(NZ)])]
  transfers between devices with their start and end apart: 40 -> 33, of which waited for: 18 -> 9; matrix products, arithmetic and copies ran while one was open for 13% -> 0% of each run, Pallas kernels for 0% -> 0%
where the time goes in v4:
time: 183 us; the launch traced here: 182 us
  starting transfers between devices  51.1 us (28%)
  local copies, waits for them, and re-layouts  48.6 us (27%)
  waiting for transfers between devices  34.8 us (19%)
  blocking collectives  34.4 us (19%)
  Pallas kernels  12.1 us (7%)
    unnamed x102, local copies, waits for them, and re-layouts  44.6 us
    ppermute x16, starting transfers between devices, swap(): return lax.ppermute(a, C, [(0, 1), (1, 0)])  35.4 us
    all_to_all x1, blocking collectives, on_device(): lax.all_to_all(part.reshape(NR, ROWS, COLS), (X, YL), 0, 0, tiled=True)  34.4 us
    ppermute x14, waiting for transfers between devices, turn(): return lax.ppermute(a, (Z, C), pairs)  28 us
    all_to_all x2, starting transfers between devices, gather_r(): return lax.all_to_all(copies, (X, YL), 0, 0, tiled=True)  11.4 us
    pallas_call x1, Pallas kernels, product_part(): pl.pallas_call(product_kernel, out_shape=jax.ShapeDtypeStruct((TILE, COLS...  7.8 us
    ppermute x1, waiting for transfers between devices, swap_slab(): return lax.ppermute(a, S, [(0, 1), (1, 0)])  6.79 us
    pallas_call x1, Pallas kernels, gram_part(): pl.pallas_call(gram_kernel, out_shape=(jax.ShapeDtypeStruct((n, COLS), bf...  4.3 us
  transfers between devices with their start and end apart: 33, of which 9 were waited for; matrix products, arithmetic and copies ran while one was open for 0% of the time, Pallas kernels for 0%

profile of v4, /device:TPU:1, one launch (start us, length us, event | category | flops | bytes accessed | tf_op | source)
XLA Modules:
  0.0 182.3 jit_solution(4803376786422889283)
XLA Ops:
  0.0 2.5 %broadcast_in_dim.4 = bf16[8,32,4608]{2,1,0:T(8,128)(2,1)} broadcast(bf16[32,4608]{1,0:T(8,128)(2,1)} %refs_0_.1), dimensions={1,2} | broadcast | bytes 2654208 | tf_op jit(solution)/shard_map/broadcast_in_dim | solution.py:62
  2.5 6.0 %all-to-all-start = ((bf16[8,32,4608]{2,1,0:T(8,128)(2,1)}), bf16[8,32,4608]{2,1,0:T(8,128)(2,1)S(1)}, u32[]{:S(2)}, u32[]{:S(2)}) async-start(bf16[8,32,4608]{2,1,0:T(8,128)(2,1)} %broadcast_in_dim.4), calls=%async_computation | async-start | bytes 4718592 | tf_op jit(solution)/shard_map/all_to_all | solution.py:63
  8.5 1.7 collective-permute-start.1
  10.2 5.2 %collective-permute-start = (bf16[32,4608]{1,0:T(8,128)(2,1)S(1)}, bf16[32,4608]{1,0:T(8,128)(2,1)S(1)}, u32[]{:S(2)}, u32[]{:S(2)}) collective-permute-start(bf16[32,4608]{1,0:T(8,128)(2,1)S(1)} %copy-done.2), channel_id=1, source_target_pairs={{0,2},{2,0},{1,3},{3,1},{4,6},{6,4},{5,7},{7,5},{8,10},{10,8},{9,1... | collective-permute-start | bytes 884744 | tf_op jit(solution)/shard_map/ppermute | solution.py:28
  15.4 3.2 %collective-permute-done.1.refs_2_ = bf16[32,4608]{1,0:T(8,128)(2,1)S(1)} collective-permute-done((bf16[32,4608]{1,0:T(8,128)(2,1)S(1)}, bf16[32,4608]{1,0:T(8,128)(2,1)S(1)}, u32[]{:S(2)}, u32[]{:S(2)}) %collective-permute-start.1) | collective-permute-done | bytes 294944 | tf_op jit(solution)/shard_map/ppermute | solution.py:39
  18.6 7.1 %collective-permute-done.5.refs_6_ = bf16[32,4608]{1,0:T(8,128)(2,1)S(1)} collective-permute-done((bf16[32,4608]{1,0:T(8,128)(2,1)S(1)}, bf16[32,4608]{1,0:T(8,128)(2,1)S(1)}, u32[]{:S(2)}, u32[]{:S(2)}) %collective-permute-start.5) | collective-permute-done | bytes 294944 | tf_op jit(solution)/shard_map/ppermute | solution.py:39
  25.7 3.2 %collective-permute-done.2.refs_3_ = bf16[32,4608]{1,0:T(8,128)(2,1)S(1)} collective-permute-done((bf16[32,4608]{1,0:T(8,128)(2,1)S(1)}, bf16[32,4608]{1,0:T(8,128)(2,1)S(1)}, u32[]{:S(2)}, u32[]{:S(2)}) %collective-permute-start.2) | collective-permute-done | bytes 294944 | tf_op jit(solution)/shard_map/ppermute | solution.py:39
  28.8 5.6 %collective-permute-start.4 = (bf16[32,4608]{1,0:T(8,128)(2,1)S(1)}, bf16[32,4608]{1,0:T(8,128)(2,1)S(1)}, u32[]{:S(2)}, u32[]{:S(2)}) collective-permute-start(bf16[32,4608]{1,0:T(8,128)(2,1)S(1)} %collective-permute-done.1.refs_2_), channel_id=1, source_target_pairs={{0,2},{2,0},{1,3},{3,1},{4,6},{6,4},{5,7},{7,5},{8,10},{10,8},{9,1... | collective-permute-start | bytes 884744 | tf_op jit(solution)/shard_map/ppermute | solution.py:28
  34.5 1.3 collective-permute-done.6.refs_7_
  35.8 6.6 %collective-permute-start.3 = (bf16[32,4608]{1,0:T(8,128)(2,1)S(1)}, bf16[32,4608]{1,0:T(8,128)(2,1)S(1)}, u32[]{:S(2)}, u32[]{:S(2)}) collective-permute-start(bf16[32,4608]{1,0:T(8,128)(2,1)S(1)} %collective-permute-done.2.refs_3_), channel_id=1, source_target_pairs={{0,2},{2,0},{1,3},{3,1},{4,6},{6,4},{5,7},{7,5},{8,10},{10,8},{9,1... | collective-permute-start | bytes 884744 | tf_op jit(solution)/shard_map/ppermute | solution.py:28
  52.1 1.0 copy-done.4
  54.0 1.0 copy-done.8
  55.0 1.0 copy-done.10
  55.9 1.0 copy-done.12
  57.8 1.0 copy-done.16
  58.8 1.0 copy-done.18
  63.6 4.3 %gram_part.1 = (bf16[512,4608]{1,0:T(8,128)(2,1)S(1)}, f32[512,256]{1,0:T(8,128)S(1)}, bf16[512,256]{1,0:T(8,128)(2,1)S(1)}) custom-call(bf16[32,4608]{1,0:T(8,128)(2,1)S(1)} %copy-done.2, bf16[32,4608]{1,0:T(8,128)(2,1)S(1)} %collective-permute-done.refs_1_, bf16[32,4608]{1,0:T(8,128)(2,1)S(1)} %collective-permute-done.1.refs_2_, ...), custom_call_target="tpu_custom_call" | custom-call | flops 1207959552 | bytes 12582912 | tf_op jit(solution)/shard_map/gram_part/pallas_call | solution.py:99
  67.9 2.2 %copy-done = bf16[512,4608]{1,0:T(8,128)(2,1)} copy-done((bf16[512,4608]{1,0:T(8,128)(2,1)}, bf16[512,4608]{1,0:T(8,128)(2,1)S(1)}, u32[]{:S(2)}) %copy-start) | copy-done | bytes 4718616
  70.1 2.6 %collective-permute-start.15 = (bf16[512,256]{1,0:T(8,128)(2,1)S(1)}, bf16[512,256]{1,0:T(8,128)(2,1)S(1)}, u32[]{:S(2)}, u32[]{:S(2)}) collective-permute-start(bf16[512,256]{1,0:T(8,128)(2,1)S(1)} %get-tuple-element.9), channel_id=1, source_target_pairs={{0,1},{1,0},{2,3},{3,2},{4,5},{5,4},{6,7},{7,6},{8,9},{9,8},{10,11... | collective-permute-start | bytes 786440 | tf_op jit(solution)/shard_map/ppermute | solution.py:32
  72.8 6.8 %collective-permute-done.15 = bf16[512,256]{1,0:T(8,128)(2,1)S(1)} collective-permute-done((bf16[512,256]{1,0:T(8,128)(2,1)S(1)}, bf16[512,256]{1,0:T(8,128)(2,1)S(1)}, u32[]{:S(2)}, u32[]{:S(2)}) %collective-permute-start.15) | collective-permute-done | bytes 262176 | tf_op jit(solution)/shard_map/ppermute | solution.py:32
  79.6 1.4 broadcast_in_dim.5
  81.1 5.4 %all-to-all-start.1 = ((bf16[8,512,256]{2,1,0:T(8,128)(2,1)}), bf16[8,512,256]{2,1,0:T(8,128)(2,1)S(1)}, u32[]{:S(2)}, u32[]{:S(2)}) async-start(bf16[8,512,256]{2,1,0:T(8,128)(2,1)} %broadcast_in_dim.5), calls=%async_computation.1 | async-start | bytes 4194304 | tf_op jit(solution)/shard_map/all_to_all | solution.py:63
  86.4 3.7 %collective-permute-start.16 = (bf16[512,256]{1,0:T(8,128)(2,1)S(1)}, bf16[512,256]{1,0:T(8,128)(2,1)S(1)}, u32[]{:S(2)}, u32[]{:S(2)}) collective-permute-start(bf16[512,256]{1,0:T(8,128)(2,1)S(1)} %add_convert_fusion.refs_0_), channel_id=1, source_target_pairs={{0,2},{2,0},{1,3},{3,1},{4,6},{6,4},{5,7},{7,5},{8,10},{10,8},{9,1... | collective-permute-start | bytes 786440 | tf_op jit(solution)/shard_map/ppermute | solution.py:28
  90.1 2.7 %collective-permute-done.17.refs_2_ = bf16[512,256]{1,0:T(8,128)(2,1)S(1)} collective-permute-done((bf16[512,256]{1,0:T(8,128)(2,1)S(1)}, bf16[512,256]{1,0:T(8,128)(2,1)S(1)}, u32[]{:S(2)}, u32[]{:S(2)}) %collective-permute-start.17) | collective-permute-done | bytes 262176 | tf_op jit(solution)/shard_map/ppermute | solution.py:39
  92.9 6.7 %collective-permute-done.21.refs_6_ = bf16[512,256]{1,0:T(8,128)(2,1)S(1)} collective-permute-done((bf16[512,256]{1,0:T(8,128)(2,1)S(1)}, bf16[512,256]{1,0:T(8,128)(2,1)S(1)}, u32[]{:S(2)}, u32[]{:S(2)}) %collective-permute-start.21) | collective-permute-done | bytes 262176 | tf_op jit(solution)/shard_map/ppermute | solution.py:39
  99.6 2.8 %collective-permute-done.18.refs_3_ = bf16[512,256]{1,0:T(8,128)(2,1)S(1)} collective-permute-done((bf16[512,256]{1,0:T(8,128)(2,1)S(1)}, bf16[512,256]{1,0:T(8,128)(2,1)S(1)}, u32[]{:S(2)}, u32[]{:S(2)}) %collective-permute-start.18) | collective-permute-done | bytes 262176 | tf_op jit(solution)/shard_map/ppermute | solution.py:39
  102.4 5.7 %collective-permute-start.20 = (bf16[512,256]{1,0:T(8,128)(2,1)S(1)}, bf16[512,256]{1,0:T(8,128)(2,1)S(1)}, u32[]{:S(2)}, u32[]{:S(2)}) collective-permute-start(bf16[512,256]{1,0:T(8,128)(2,1)S(1)} %collective-permute-done.17.refs_2_), channel_id=1, source_target_pairs={{0,2},{2,0},{1,3},{3,1},{4,6},{6,4},{5,7},{7,5},{8,10},{10,8},{9,1... | collective-permute-start | bytes 786440 | tf_op jit(solution)/shard_map/ppermute | solution.py:28
  108.1 1.0 collective-permute-done.22.refs_7_
  109.1 6.5 %collective-permute-start.19 = (bf16[512,256]{1,0:T(8,128)(2,1)S(1)}, bf16[512,256]{1,0:T(8,128)(2,1)S(1)}, u32[]{:S(2)}, u32[]{:S(2)}) collective-permute-start(bf16[512,256]{1,0:T(8,128)(2,1)S(1)} %collective-permute-done.18.refs_3_), channel_id=1, source_target_pairs={{0,2},{2,0},{1,3},{3,1},{4,6},{6,4},{5,7},{7,5},{8,10},{10,8},{9,1... | collective-permute-start | bytes 786440 | tf_op jit(solution)/shard_map/ppermute | solution.py:28
  125.2 2.3 %copy-done.1 = bf16[512,4608]{1,0:T(8,128)(2,1)S(1)} copy-done((bf16[512,4608]{1,0:T(8,128)(2,1)S(1)}, bf16[512,4608]{1,0:T(8,128)(2,1)}, u32[]{:S(2)}) %copy-start.1) | copy-done | bytes 4718616
  139.0 7.8 %product_part.1 = bf16[256,4608]{1,0:T(8,128)(2,1)S(1)} custom-call(bf16[512,256]{1,0:T(8,128)(2,1)S(1)} %add_convert_fusion.refs_0_, bf16[512,256]{1,0:T(8,128)(2,1)S(1)} %collective-permute-done.16.refs_1_, bf16[512,256]{1,0:T(8,128)(2,1)S(1)} %collective-permute-done.17.refs_2_, bf16[512,256]{1,0:T(8,128)(2,1)S(1)} %copy-done.28, ...), custom_call_target="tpu_custom_call" | custom-call | flops 2281701376 | bytes 14680064 | tf_op jit(solution)/shard_map/product_part/pallas_call | solution.py:160
  146.8 34.4 %all_to_all.15 = bf16[8,32,4608]{2,1,0:T(8,128)(2,1)S(1)} all-to-all(bf16[8,32,4608]{2,1,0:T(8,128)(2,1)S(1)} %bitcast.4), channel_id=1, replica_groups=mesh['x'=4,'yl'=2,'z'=8,'c'=2,'s'=2] {'x','yl'}, dimensions={0} | all-to-all | bytes 4718592 | tf_op jit(solution)/shard_map/all_to_all | solution.py:189
  (144 shorter events, 37.6 us)
Async XLA Ops:
  2.5 49.5 %all-to-all-start = ((bf16[8,32,4608]{2,1,0:T(8,128)(2,1)}), bf16[8,32,4608]{2,1,0:T(8,128)(2,1)S(1)}, u32[]{:S(2)}, u32[]{:S(2)}) async-start(bf16[8,32,4608]{2,1,0:T(8,128)(2,1)} %broadcast_in_dim.4), calls=%async_computation | async-start | bytes 4718592 | tf_op jit(solution)/shard_map/all_to_all | solution.py:63
  8.5 10.1 %collective-permute-start.1 = (bf16[32,4608]{1,0:T(8,128)(2,1)S(1)}, bf16[32,4608]{1,0:T(8,128)(2,1)S(1)}, u32[]{:S(2)}, u32[]{:S(2)}) collective-permute-start(bf16[32,4608]{1,0:T(8,128)(2,1)S(1)} %copy-done.2), channel_id=1, source_target_pairs={{4,0},{30,2},{8,4},{2,6},{12,8},{6,10},{16,12},{10,14},{20,16},{14... | collective-permute-start | bytes 884744 | tf_op jit(solution)/shard_map/ppermute | solution.py:39
  10.2 8.4 %collective-permute-start = (bf16[32,4608]{1,0:T(8,128)(2,1)S(1)}, bf16[32,4608]{1,0:T(8,128)(2,1)S(1)}, u32[]{:S(2)}, u32[]{:S(2)}) collective-permute-start(bf16[32,4608]{1,0:T(8,128)(2,1)S(1)} %copy-done.2), channel_id=1, source_target_pairs={{0,2},{2,0},{1,3},{3,1},{4,6},{6,4},{5,7},{7,5},{8,10},{10,8},{9,1... | collective-permute-start | bytes 884744 | tf_op jit(solution)/shard_map/ppermute | solution.py:28
  18.6 7.1 %collective-permute-start.5 = (bf16[32,4608]{1,0:T(8,128)(2,1)S(1)}, bf16[32,4608]{1,0:T(8,128)(2,1)S(1)}, u32[]{:S(2)}, u32[]{:S(2)}) collective-permute-start(bf16[32,4608]{1,0:T(8,128)(2,1)S(1)} %collective-permute-done.1.refs_2_), channel_id=1, source_target_pairs={{4,0},{30,2},{8,4},{2,6},{12,8},{6,10},{16,12},{10,14},{20,16},{14... | collective-permute-start | bytes 884744 | tf_op jit(solution)/shard_map/ppermute | solution.py:39
  18.6 10.2 %collective-permute-start.2 = (bf16[32,4608]{1,0:T(8,128)(2,1)S(1)}, bf16[32,4608]{1,0:T(8,128)(2,1)S(1)}, u32[]{:S(2)}, u32[]{:S(2)}) collective-permute-start(bf16[32,4608]{1,0:T(8,128)(2,1)S(1)} %collective-permute-done.refs_1_), channel_id=1, source_target_pairs={{4,0},{30,2},{8,4},{2,6},{12,8},{6,10},{16,12},{10,14},{20,16},{14... | collective-permute-start | bytes 884744 | tf_op jit(solution)/shard_map/ppermute | solution.py:39
  25.7 8.8 %collective-permute-start.9 = (bf16[32,4608]{1,0:T(8,128)(2,1)S(1)}, bf16[32,4608]{1,0:T(8,128)(2,1)S(1)}, u32[]{:S(2)}, u32[]{:S(2)}) collective-permute-start(bf16[32,4608]{1,0:T(8,128)(2,1)S(1)} %collective-permute-done.5.refs_6_), channel_id=1, source_target_pairs={{4,0},{30,2},{8,4},{2,6},{12,8},{6,10},{16,12},{10,14},{20,16},{14... | collective-permute-start | bytes 884744 | tf_op jit(solution)/shard_map/ppermute | solution.py:39
  28.8 6.9 %collective-permute-start.6 = (bf16[32,4608]{1,0:T(8,128)(2,1)S(1)}, bf16[32,4608]{1,0:T(8,128)(2,1)S(1)}, u32[]{:S(2)}, u32[]{:S(2)}) collective-permute-start(bf16[32,4608]{1,0:T(8,128)(2,1)S(1)} %collective-permute-done.2.refs_3_), channel_id=1, source_target_pairs={{4,0},{30,2},{8,4},{2,6},{12,8},{6,10},{16,12},{10,14},{20,16},{14... | collective-permute-start | bytes 884744 | tf_op jit(solution)/shard_map/ppermute | solution.py:39
  28.8 14.3 %collective-permute-start.4 = (bf16[32,4608]{1,0:T(8,128)(2,1)S(1)}, bf16[32,4608]{1,0:T(8,128)(2,1)S(1)}, u32[]{:S(2)}, u32[]{:S(2)}) collective-permute-start(bf16[32,4608]{1,0:T(8,128)(2,1)S(1)} %collective-permute-done.1.refs_2_), channel_id=1, source_target_pairs={{0,2},{2,0},{1,3},{3,1},{4,6},{6,4},{5,7},{7,5},{8,10},{10,8},{9,1... | collective-permute-start | bytes 884744 | tf_op jit(solution)/shard_map/ppermute | solution.py:28
  34.5 10.1 %collective-permute-start.8 = (bf16[32,4608]{1,0:T(8,128)(2,1)S(1)}, bf16[32,4608]{1,0:T(8,128)(2,1)S(1)}, u32[]{:S(2)}, u32[]{:S(2)}) collective-permute-start(bf16[32,4608]{1,0:T(8,128)(2,1)S(1)} %collective-permute-done.5.refs_6_), channel_id=1, source_target_pairs={{0,2},{2,0},{1,3},{3,1},{4,6},{6,4},{5,7},{7,5},{8,10},{10,8},{9,1... | collective-permute-start | bytes 884744 | tf_op jit(solution)/shard_map/ppermute | solution.py:28
  34.5 12.0 %collective-permute-start.13 = (bf16[32,4608]{1,0:T(8,128)(2,1)S(1)}, bf16[32,4608]{1,0:T(8,128)(2,1)S(1)}, u32[]{:S(2)}, u32[]{:S(2)}) collective-permute-start(bf16[32,4608]{1,0:T(8,128)(2,1)S(1)} %collective-permute-done.9.refs_10_), channel_id=1, source_target_pairs={{4,0},{30,2},{8,4},{2,6},{12,8},{6,10},{16,12},{10,14},{20,16},{14... | collective-permute-start | bytes 884744 | tf_op jit(solution)/shard_map/ppermute | solution.py:39
  35.8 11.4 %collective-permute-start.10 = (bf16[32,4608]{1,0:T(8,128)(2,1)S(1)}, bf16[32,4608]{1,0:T(8,128)(2,1)S(1)}, u32[]{:S(2)}, u32[]{:S(2)}) collective-permute-start(bf16[32,4608]{1,0:T(8,128)(2,1)S(1)} %collective-permute-done.6.refs_7_), channel_id=1, source_target_pairs={{4,0},{30,2},{8,4},{2,6},{12,8},{6,10},{16,12},{10,14},{20,16},{14... | collective-permute-start | bytes 884744 | tf_op jit(solution)/shard_map/ppermute | solution.py:39
  35.8 12.7 %collective-permute-start.3 = (bf16[32,4608]{1,0:T(8,128)(2,1)S(1)}, bf16[32,4608]{1,0:T(8,128)(2,1)S(1)}, u32[]{:S(2)}, u32[]{:S(2)}) collective-permute-start(bf16[32,4608]{1,0:T(8,128)(2,1)S(1)} %collective-permute-done.2.refs_3_), channel_id=1, source_target_pairs={{0,2},{2,0},{1,3},{3,1},{4,6},{6,4},{5,7},{7,5},{8,10},{10,8},{9,1... | collective-permute-start | bytes 884744 | tf_op jit(solution)/shard_map/ppermute | solution.py:28
  43.8 5.3 %collective-permute-start.12 = (bf16[32,4608]{1,0:T(8,128)(2,1)S(1)}, bf16[32,4608]{1,0:T(8,128)(2,1)S(1)}, u32[]{:S(2)}, u32[]{:S(2)}) collective-permute-start(bf16[32,4608]{1,0:T(8,128)(2,1)S(1)} %collective-permute-done.9.refs_10_), channel_id=1, source_target_pairs={{0,2},{2,0},{1,3},{3,1},{4,6},{6,4},{5,7},{7,5},{8,10},{10,8},{9,1... | collective-permute-start | bytes 884744 | tf_op jit(solution)/shard_map/ppermute | solution.py:28
  45.2 4.7 %collective-permute-start.7 = (bf16[32,4608]{1,0:T(8,128)(2,1)S(1)}, bf16[32,4608]{1,0:T(8,128)(2,1)S(1)}, u32[]{:S(2)}, u32[]{:S(2)}) collective-permute-start(bf16[32,4608]{1,0:T(8,128)(2,1)S(1)} %collective-permute-done.6.refs_7_), channel_id=1, source_target_pairs={{0,2},{2,0},{1,3},{3,1},{4,6},{6,4},{5,7},{7,5},{8,10},{10,8},{9,1... | collective-permute-start | bytes 884744 | tf_op jit(solution)/shard_map/ppermute | solution.py:28
  46.5 4.2 %collective-permute-start.14 = (bf16[32,4608]{1,0:T(8,128)(2,1)S(1)}, bf16[32,4608]{1,0:T(8,128)(2,1)S(1)}, u32[]{:S(2)}, u32[]{:S(2)}) collective-permute-start(bf16[32,4608]{1,0:T(8,128)(2,1)S(1)} %collective-permute-done.13.refs_14_), channel_id=1, source_target_pairs={{0,2},{2,0},{1,3},{3,1},{4,6},{6,4},{5,7},{7,5},{8,10},{10,8},{9,1... | collective-permute-start | bytes 884744 | tf_op jit(solution)/shard_map/ppermute | solution.py:28
  47.2 4.1 %collective-permute-start.11 = (bf16[32,4608]{1,0:T(8,128)(2,1)S(1)}, bf16[32,4608]{1,0:T(8,128)(2,1)S(1)}, u32[]{:S(2)}, u32[]{:S(2)}) collective-permute-start(bf16[32,4608]{1,0:T(8,128)(2,1)S(1)} %collective-permute-done.10.refs_11_), channel_id=1, source_target_pairs={{0,2},{2,0},{1,3},{3,1},{4,6},{6,4},{5,7},{7,5},{8,10},{10,8},{9,1... | collective-permute-start | bytes 884744 | tf_op jit(solution)/shard_map/ppermute | solution.py:28
  70.1 9.4 %collective-permute-start.15 = (bf16[512,256]{1,0:T(8,128)(2,1)S(1)}, bf16[512,256]{1,0:T(8,128)(2,1)S(1)}, u32[]{:S(2)}, u32[]{:S(2)}) collective-permute-start(bf16[512,256]{1,0:T(8,128)(2,1)S(1)} %get-tuple-element.9), channel_id=1, source_target_pairs={{0,1},{1,0},{2,3},{3,2},{4,5},{5,4},{6,7},{7,6},{8,9},{9,8},{10,11... | collective-permute-start | bytes 786440 | tf_op jit(solution)/shard_map/ppermute | solution.py:32
  81.1 44.2 %all-to-all-start.1 = ((bf16[8,512,256]{2,1,0:T(8,128)(2,1)}), bf16[8,512,256]{2,1,0:T(8,128)(2,1)S(1)}, u32[]{:S(2)}, u32[]{:S(2)}) async-start(bf16[8,512,256]{2,1,0:T(8,128)(2,1)} %broadcast_in_dim.5), calls=%async_computation.1 | async-start | bytes 4194304 | tf_op jit(solution)/shard_map/all_to_all | solution.py:63
  86.4 6.4 %collective-permute-start.17 = (bf16[512,256]{1,0:T(8,128)(2,1)S(1)}, bf16[512,256]{1,0:T(8,128)(2,1)S(1)}, u32[]{:S(2)}, u32[]{:S(2)}) collective-permute-start(bf16[512,256]{1,0:T(8,128)(2,1)S(1)} %add_convert_fusion.refs_0_), channel_id=1, source_target_pairs={{4,0},{30,2},{8,4},{2,6},{12,8},{6,10},{16,12},{10,14},{20,16},{14... | collective-permute-start | bytes 786440 | tf_op jit(solution)/shard_map/ppermute | solution.py:39
  86.4 6.4 %collective-permute-start.16 = (bf16[512,256]{1,0:T(8,128)(2,1)S(1)}, bf16[512,256]{1,0:T(8,128)(2,1)S(1)}, u32[]{:S(2)}, u32[]{:S(2)}) collective-permute-start(bf16[512,256]{1,0:T(8,128)(2,1)S(1)} %add_convert_fusion.refs_0_), channel_id=1, source_target_pairs={{0,2},{2,0},{1,3},{3,1},{4,6},{6,4},{5,7},{7,5},{8,10},{10,8},{9,1... | collective-permute-start | bytes 786440 | tf_op jit(solution)/shard_map/ppermute | solution.py:28
  92.8 6.7 %collective-permute-start.21 = (bf16[512,256]{1,0:T(8,128)(2,1)S(1)}, bf16[512,256]{1,0:T(8,128)(2,1)S(1)}, u32[]{:S(2)}, u32[]{:S(2)}) collective-permute-start(bf16[512,256]{1,0:T(8,128)(2,1)S(1)} %collective-permute-done.17.refs_2_), channel_id=1, source_target_pairs={{4,0},{30,2},{8,4},{2,6},{12,8},{6,10},{16,12},{10,14},{20,16},{14... | collective-permute-start | bytes 786440 | tf_op jit(solution)/shard_map/ppermute | solution.py:39
  92.8 9.5 %collective-permute-start.18 = (bf16[512,256]{1,0:T(8,128)(2,1)S(1)}, bf16[512,256]{1,0:T(8,128)(2,1)S(1)}, u32[]{:S(2)}, u32[]{:S(2)}) collective-permute-start(bf16[512,256]{1,0:T(8,128)(2,1)S(1)} %collective-permute-done.16.refs_1_), channel_id=1, source_target_pairs={{4,0},{30,2},{8,4},{2,6},{12,8},{6,10},{16,12},{10,14},{20,16},{14... | collective-permute-start | bytes 786440 | tf_op jit(solution)/shard_map/ppermute | solution.py:39
  99.6 8.5 %collective-permute-start.25 = (bf16[512,256]{1,0:T(8,128)(2,1)S(1)}, bf16[512,256]{1,0:T(8,128)(2,1)S(1)}, u32[]{:S(2)}, u32[]{:S(2)}) collective-permute-start(bf16[512,256]{1,0:T(8,128)(2,1)S(1)} %collective-permute-done.21.refs_6_), channel_id=1, source_target_pairs={{4,0},{30,2},{8,4},{2,6},{12,8},{6,10},{16,12},{10,14},{20,16},{14... | collective-permute-start | bytes 786440 | tf_op jit(solution)/shard_map/ppermute | solution.py:39
  102.4 6.7 %collective-permute-start.22 = (bf16[512,256]{1,0:T(8,128)(2,1)S(1)}, bf16[512,256]{1,0:T(8,128)(2,1)S(1)}, u32[]{:S(2)}, u32[]{:S(2)}) collective-permute-start(bf16[512,256]{1,0:T(8,128)(2,1)S(1)} %collective-permute-done.18.refs_3_), channel_id=1, source_target_pairs={{4,0},{30,2},{8,4},{2,6},{12,8},{6,10},{16,12},{10,14},{20,16},{14... | collective-permute-start | bytes 786440 | tf_op jit(solution)/shard_map/ppermute | solution.py:39
  102.4 14.0 %collective-permute-start.20 = (bf16[512,256]{1,0:T(8,128)(2,1)S(1)}, bf16[512,256]{1,0:T(8,128)(2,1)S(1)}, u32[]{:S(2)}, u32[]{:S(2)}) collective-permute-start(bf16[512,256]{1,0:T(8,128)(2,1)S(1)} %collective-permute-done.17.refs_2_), channel_id=1, source_target_pairs={{0,2},{2,0},{1,3},{3,1},{4,6},{6,4},{5,7},{7,5},{8,10},{10,8},{9,1... | collective-permute-start | bytes 786440 | tf_op jit(solution)/shard_map/ppermute | solution.py:28
  108.1 9.7 %collective-permute-start.24 = (bf16[512,256]{1,0:T(8,128)(2,1)S(1)}, bf16[512,256]{1,0:T(8,128)(2,1)S(1)}, u32[]{:S(2)}, u32[]{:S(2)}) collective-permute-start(bf16[512,256]{1,0:T(8,128)(2,1)S(1)} %collective-permute-done.21.refs_6_), channel_id=1, source_target_pairs={{0,2},{2,0},{1,3},{3,1},{4,6},{6,4},{5,7},{7,5},{8,10},{10,8},{9,1... | collective-permute-start | bytes 786440 | tf_op jit(solution)/shard_map/ppermute | solution.py:28
  108.1 11.7 %collective-permute-start.29 = (bf16[512,256]{1,0:T(8,128)(2,1)S(1)}, bf16[512,256]{1,0:T(8,128)(2,1)S(1)}, u32[]{:S(2)}, u32[]{:S(2)}) collective-permute-start(bf16[512,256]{1,0:T(8,128)(2,1)S(1)} %collective-permute-done.25.refs_10_), channel_id=1, source_target_pairs={{4,0},{30,2},{8,4},{2,6},{12,8},{6,10},{16,12},{10,14},{20,16},{14... | collective-permute-start | bytes 786440 | tf_op jit(solution)/shard_map/ppermute | solution.py:39
  109.1 11.4 %collective-permute-start.26 = (bf16[512,256]{1,0:T(8,128)(2,1)S(1)}, bf16[512,256]{1,0:T(8,128)(2,1)S(1)}, u32[]{:S(2)}, u32[]{:S(2)}) collective-permute-start(bf16[512,256]{1,0:T(8,128)(2,1)S(1)} %collective-permute-done.22.refs_7_), channel_id=1, source_target_pairs={{4,0},{30,2},{8,4},{2,6},{12,8},{6,10},{16,12},{10,14},{20,16},{14... | collective-permute-start | bytes 786440 | tf_op jit(solution)/shard_map/ppermute | solution.py:39
  109.1 12.6 %collective-permute-start.19 = (bf16[512,256]{1,0:T(8,128)(2,1)S(1)}, bf16[512,256]{1,0:T(8,128)(2,1)S(1)}, u32[]{:S(2)}, u32[]{:S(2)}) collective-permute-start(bf16[512,256]{1,0:T(8,128)(2,1)S(1)} %collective-permute-done.18.refs_3_), channel_id=1, source_target_pairs={{0,2},{2,0},{1,3},{3,1},{4,6},{6,4},{5,7},{7,5},{8,10},{10,8},{9,1... | collective-permute-start | bytes 786440 | tf_op jit(solution)/shard_map/ppermute | solution.py:28
  117.1 5.3 %collective-permute-start.28 = (bf16[512,256]{1,0:T(8,128)(2,1)S(1)}, bf16[512,256]{1,0:T(8,128)(2,1)S(1)}, u32[]{:S(2)}, u32[]{:S(2)}) collective-permute-start(bf16[512,256]{1,0:T(8,128)(2,1)S(1)} %collective-permute-done.25.refs_10_), channel_id=1, source_target_pairs={{0,2},{2,0},{1,3},{3,1},{4,6},{6,4},{5,7},{7,5},{8,10},{10,8},{9,1... | collective-permute-start | bytes 786440 | tf_op jit(solution)/shard_map/ppermute | solution.py:28
  118.5 4.6 %collective-permute-start.23 = (bf16[512,256]{1,0:T(8,128)(2,1)S(1)}, bf16[512,256]{1,0:T(8,128)(2,1)S(1)}, u32[]{:S(2)}, u32[]{:S(2)}) collective-permute-start(bf16[512,256]{1,0:T(8,128)(2,1)S(1)} %collective-permute-done.22.refs_7_), channel_id=1, source_target_pairs={{0,2},{2,0},{1,3},{3,1},{4,6},{6,4},{5,7},{7,5},{8,10},{10,8},{9,1... | collective-permute-start | bytes 786440 | tf_op jit(solution)/shard_map/ppermute | solution.py:28
  119.7 4.1 %collective-permute-start.30 = (bf16[512,256]{1,0:T(8,128)(2,1)S(1)}, bf16[512,256]{1,0:T(8,128)(2,1)S(1)}, u32[]{:S(2)}, u32[]{:S(2)}) collective-permute-start(bf16[512,256]{1,0:T(8,128)(2,1)S(1)} %collective-permute-done.29.refs_14_), channel_id=1, source_target_pairs={{0,2},{2,0},{1,3},{3,1},{4,6},{6,4},{5,7},{7,5},{8,10},{10,8},{9,1... | collective-permute-start | bytes 786440 | tf_op jit(solution)/shard_map/ppermute | solution.py:28
  (52 other events, 54.7 us)

commit v5 on v4

v5 whole, which is shorter than its diff:
```python
import math

import jax
import jax.numpy as jnp
from jax import lax
from jax.experimental import pallas as pl
from jax.experimental.pallas import tpu as pltpu
from jax.sharding import Mesh
from jax.sharding import PartitionSpec as P

coef_linear = 3.4445
coef_cubic = -4.775
coef_quintic = 2.0315
update_gain = 0.2 * math.sqrt(18432.0)

X, YL, Z, C, S = "x", "yl", "z", "c", "s"
NZ, NR = 8, 8
ROWS, COLS = 32, 4608
TILE = 256
bf16, f32 = jnp.bfloat16, jnp.float32
ORDER = (0, 1, 7, 2, 6, 3, 5, 4)
PARTS = 16
COLS_Z = 1536
LATE = 11
WIDTH = 512
GROUPS = 4
K_PARTS = 3
VMEM = pl.BlockSpec(memory_space=pltpu.VMEM)
HBM = pl.BlockSpec(memory_space=pltpu.HBM)


def swap(a):
    return lax.ppermute(a, C, [(0, 1), (1, 0)])


def swap_slab(a):
    return lax.ppermute(a, S, [(0, 1), (1, 0)])


def turn(a):
    pairs = []
    for i in range(NZ):
        pairs += [(2 * ((i + 1) % NZ), 2 * i), (2 * ((i - 1) % NZ) + 1, 2 * i + 1)]
    return lax.ppermute(a, (Z, C), pairs)


def far(a):
    return pltpu.with_memory_space_constraint(a, pltpu.HBM)


def ring_z(a, b=None):
    b = swap(a) if b is None else b
    mine, others = [a] + [None] * (NZ - 1), [b] + [None] * (NZ - 1)
    for step in range(1, 4):
        a = turn(a)
        b = turn(b)
        mine[step], others[step] = a, b
        mine[NZ - step], others[NZ - step] = swap(b), swap(a)
    mine[4] = turn(a)
    others[4] = swap(mine[4])
    return [part[e] for e in ORDER for part in (mine, others)]


def where_from(i):
    core, z = lax.axis_index(C), lax.axis_index(Z)
    e = ORDER[i // 2]
    return (z + e + core * (NZ - 2 * e) + NZ) % NZ, core if i % 2 == 0 else 1 - core


def near(a):
    return pltpu.with_memory_space_constraint(a, pltpu.VMEM)


def copies_kernel(a_ref, out_ref, sem):
    copies = [pltpu.make_async_copy(a_ref, out_ref.at[i], sem.at[i]) for i in range(NR)]
    for copy in copies:
        copy.start()
    for copy in copies:
        copy.wait()


def gather_r(a):
    copies = pl.pallas_call(
        copies_kernel,
        out_shape=pltpu.HBM((NR, *a.shape), a.dtype),
        in_specs=[VMEM],
        out_specs=HBM,
        scratch_shapes=[pltpu.SemaphoreType.DMA((NR,))],
        compiler_params=pltpu.CompilerParams(vmem_limit_bytes=1 << 20),
        name="copies",
    )(near(a))
    return lax.all_to_all(copies, (X, YL), 0, 0, tiled=True)


def gram_kernel(*refs):
    pieces, (cols_ref, rows_ref, cut_ref, own_ref, sent_ref, x, sem, sem_out) = refs[:PARTS], refs[PARTS:]
    width = COLS // K_PARTS
    cuts = [pl.ds(k * width, width) for k in range(K_PARTS)]
    copies = []
    for k, cut in enumerate(cuts):
        for i, piece in enumerate(pieces):
            z, h = where_from(i)
            copies.append(pltpu.make_async_copy(piece.at[:, cut], x.at[2 * z + h, :, cut], sem.at[k, i]))
            copies[-1].start()
    outs = [pltpu.make_async_copy(cols_ref.at[:, :, pl.ds(0, COLS_Z)], cut_ref, sem_out.at[K_PARTS])]
    outs[0].start()
    total = None
    for k, cut in enumerate(cuts):
        for copy in copies[k * PARTS : (k + 1) * PARTS]:
            copy.wait()
        outs.append(pltpu.make_async_copy(x.at[:, :, cut], rows_ref.at[:, :, cut], sem_out.at[k]))
        outs[-1].start()
        left = x[:, :, cut].reshape(PARTS * ROWS, width)
        right = cols_ref[:, :, cut].reshape(TILE, width)
        term = lax.dot_general(left, right, (((1,), (1,)), ((), ())), preferred_element_type=f32)
        total = term if total is None else total + term
    own_ref[...] = total
    sent_ref[...] = total.astype(bf16)
    for out in outs:
        out.wait()


def gram_part(pieces, cols):
    n = PARTS * ROWS
    return pl.pallas_call(
        gram_kernel,
        out_shape=(
            pltpu.HBM((PARTS, ROWS, COLS), bf16),
            pltpu.HBM((NR, ROWS, COLS_Z), bf16),
            pltpu.VMEM((n, TILE), f32),
            pltpu.VMEM((n, TILE), bf16),
        ),
        in_specs=[HBM] * LATE + [VMEM] * (PARTS - LATE) + [VMEM],
        out_specs=(HBM, HBM, VMEM, VMEM),
        scratch_shapes=[
            pltpu.VMEM((PARTS, ROWS, COLS), bf16),
            pltpu.SemaphoreType.DMA((K_PARTS, PARTS)),
            pltpu.SemaphoreType.DMA((K_PARTS + 1,)),
        ],
        compiler_params=pltpu.CompilerParams(vmem_limit_bytes=12 << 20),
        cost_estimate=pl.CostEstimate(flops=2 * n * TILE * COLS, bytes_accessed=12 << 20, transcendentals=0),
        name="gram_part",
    )(*[far(p) for p in pieces[:LATE]], *[near(p) for p in pieces[LATE:]], near(cols))


def product_kernel(*refs):
    a_refs, refs = refs[:PARTS], refs[PARTS:]
    b_ref, rows_ref, cut_ref, out_ref, own_ref, other_ref, a, b, x, y, part, out, sem_a, sem_b, sem_x, sem_out = refs
    copies = []
    for i, ref in enumerate(a_refs):
        z, h = where_from(i)
        copies.append(pltpu.make_async_copy(ref, a.at[:, pl.ds(i * TILE, TILE)], sem_a.at[i]))
        copies.append(pltpu.make_async_copy(b_ref.at[:, 2 * z + h], b.at[i], sem_b.at[i]))
    loads = [pltpu.make_async_copy(cut_ref, y, sem_x.at[0]), pltpu.make_async_copy(rows_ref, x, sem_x.at[1])]
    for copy in copies + loads:
        copy.start()
    squared = None
    size = PARTS // GROUPS
    for g in range(GROUPS):
        for copy in copies[2 * g * size : 2 * (g + 1) * size]:
            copy.wait()
        left = a[:, pl.ds(g * size * TILE, size * TILE)]
        right = b[pl.ds(g * size, size)].reshape(size * TILE, TILE)
        term = jnp.dot(left, right, preferred_element_type=f32)
        squared = term if squared is None else squared + term
    gram = a[:, pl.ds(0, TILE)].astype(f32)
    poly = (coef_cubic * gram + coef_quintic * squared).astype(bf16)
    loads[0].wait()
    for k in range(COLS_Z // WIDTH):
        cut = pl.ds(k * WIDTH, WIDTH)
        term = jnp.dot(poly, y[:, :, cut].reshape(TILE, WIDTH), preferred_element_type=f32)
        part[:, :, :, cut] = term.astype(bf16).reshape(NZ, 2, ROWS, WIDTH)
    core = lax.axis_index(C)
    outs = [
        pltpu.make_async_copy(part.at[:, 1 - core], other_ref, sem_x.at[0]),
        pltpu.make_async_copy(part.at[:, core], own_ref, sem_x.at[2]),
    ]
    for copy in outs:
        copy.start()
    loads[1].wait()
    for k in range((COLS - COLS_Z) // WIDTH):
        cut = pl.ds(k * WIDTH, WIDTH)
        right = x[:, :, pl.ds(COLS_Z + k * WIDTH, WIDTH)].reshape(PARTS * ROWS, WIDTH)
        term = lax.dot_general(poly, right, (((0,), (0,)), ((), ())), preferred_element_type=f32)
        out[:, :, cut] = term.astype(bf16).reshape(NR, ROWS, WIDTH)
        outs.append(pltpu.make_async_copy(out.at[:, :, cut], out_ref.at[:, :, cut], sem_out.at[k]))
        outs[-1].start()
    for copy in outs:
        copy.wait()


def product_part(a_parts, b, rows, cut):
    n = PARTS * ROWS
    return pl.pallas_call(
        product_kernel,
        out_shape=(
            pltpu.HBM((NR, ROWS, COLS - COLS_Z), bf16),
            pltpu.HBM((NZ, ROWS, COLS_Z), bf16),
            pltpu.HBM((NZ, ROWS, COLS_Z), bf16),
        ),
        in_specs=[HBM] * LATE + [VMEM] * (PARTS - LATE) + [VMEM, HBM, HBM],
        out_specs=(HBM, HBM, HBM),
        scratch_shapes=[
            pltpu.VMEM((n, PARTS * TILE), bf16),
            pltpu.VMEM((PARTS, NR, ROWS, TILE), bf16),
            pltpu.VMEM((PARTS, ROWS, COLS), bf16),
            pltpu.VMEM((NR, ROWS, COLS_Z), bf16),
            pltpu.VMEM((NZ, 2, ROWS, COLS_Z), bf16),
            pltpu.VMEM((NR, ROWS, COLS - COLS_Z), bf16),
            pltpu.SemaphoreType.DMA((PARTS,)),
            pltpu.SemaphoreType.DMA((PARTS,)),
            pltpu.SemaphoreType.DMA((3,)),
            pltpu.SemaphoreType.DMA(((COLS - COLS_Z) // WIDTH,)),
        ],
        compiler_params=pltpu.CompilerParams(vmem_limit_bytes=28 << 20),
        cost_estimate=pl.CostEstimate(
            flops=2 * n * TILE * (COLS + PARTS * TILE), bytes_accessed=14 << 20, transcendentals=0
        ),
        name="product_part",
    )(*[far(p) for p in a_parts[:LATE]], *[near(p) for p in a_parts[LATE:]], near(b), far(rows), far(cut))


def shift_z(a, d):
    return lax.ppermute(a, Z, [((i + d) % NZ, i) for i in range(NZ)])


def on_device(iterate):
    z = lax.axis_index(Z)
    cols = gather_r(iterate)
    rows, cut, own, sent = gram_part(ring_z(iterate), cols)
    gram = (own + swap_slab(sent).astype(f32)).astype(bf16)
    mine, twin = lax.optimization_barrier((gram, swap(gram)))
    a_parts = ring_z(gram, twin)
    every = gather_r(mine).reshape(NR, PARTS, ROWS, TILE)
    parts, own, other = product_part(a_parts, every, rows, cut)
    got = lax.all_to_all(parts, (X, YL), 0, 0, tiled=True)
    own = (own.astype(f32) + swap(other).astype(f32)).astype(bf16)
    take = lambda d: lax.dynamic_index_in_dim(own, (z - d + NZ) % NZ, 0, keepdims=False)
    got_z = [take(0)] + [shift_z(take(d), d) for d in (4, 1, 7, 2, 6, 3, 5)]
    sums = [sum(p.astype(f32) for p in got_z), got.astype(f32).sum(0)]
    total = coef_linear * iterate.astype(f32) + jnp.concatenate(sums, axis=1)
    return (update_gain * total).astype(bf16)


def solution(mesh):
    fine = Mesh(mesh.devices.reshape(4, 2, 8, 2, 2), (X, YL, Z, C, S))
    spec = P((X, YL, Z, C), S)
    return jax.shard_map(on_device, mesh=fine, in_specs=(spec,), out_specs=spec, check_vma=False)
```

time: 183 us -> 146 us (0.80); the launches traced: 182 us -> 143 us
  local copies, waits for them, and re-layouts: 48.6 us -> 5.06 us
  blocking collectives: 34.4 us -> 0 us
  starting transfers between devices: 51.1 us -> 71.2 us
  waiting for transfers between devices: 34.8 us -> 47.6 us
  Pallas kernels: 12.1 us -> 15.7 us
  other arithmetic: 1.19 us -> 3.49 us
    unnamed x102 -> x56, local copies, waits for them, and re-layouts: 44.6 us -> 5 us
    all_to_all x1 -> x0, blocking collectives: 34.4 us -> none  [on_device(): lax.all_to_all(part.reshape(NR, ROWS, COLS), (X, YL), 0, 0, tiled=True)]
    ppermute x0 -> x7, starting transfers between devices: none -> 13.1 us  [shift_z(): return lax.ppermute(a, Z, [((i + d) % NZ, i) for i in range(NZ)])]
    ppermute x0 -> x7, waiting for transfers between devices: none -> 6.13 us  [shift_z(): return lax.ppermute(a, Z, [((i + d) % NZ, i) for i in range(NZ)])]
    all_to_all x0 -> x1, starting transfers between devices: none -> 5.34 us  [on_device(): got = lax.all_to_all(parts, (X, YL), 0, 0, tiled=True)]
    ppermute x14, waiting for transfers between devices: 28 us -> 32.3 us  [turn(): return lax.ppermute(a, (Z, C), pairs)]
    broadcast_in_dim x2 -> x0, local copies, waits for them, and re-layouts: 3.97 us -> none  [gather_r(): copies = jnp.broadcast_to(a[None], (NR, *a.shape))]
    pallas_call x2 -> x4, Pallas kernels: 12.1 us -> 15.7 us  [the longest x1 7.71 us: product_part(): pl.pallas_call(product_kernel, out_shape=(pltpu.HBM((NR, ROWS, COLS - COL...]
  transfers between devices with their start and end apart: 33 -> 42, of which waited for: 9 -> 19; matrix products, arithmetic and copies ran while one was open for 0% -> 2% of each run, Pallas kernels for 0% -> 0%
where the time goes in v5:
time: 146 us; the launch traced here: 143 us
  starting transfers between devices  71.2 us (49%)
  waiting for transfers between devices  47.6 us (33%)
  Pallas kernels  15.7 us (11%)
  local copies, waits for them, and re-layouts  5.06 us (3%)
  other arithmetic  3.49 us (2%)
    ppermute x17, starting transfers between devices, swap(): return lax.ppermute(a, C, [(0, 1), (1, 0)])  36.3 us
    ppermute x14, waiting for transfers between devices, turn(): return lax.ppermute(a, (Z, C), pairs)  32.3 us
    ppermute x7, starting transfers between devices, shift_z(): return lax.ppermute(a, Z, [((i + d) % NZ, i) for i in range(NZ)])  13.1 us
    all_to_all x2, starting transfers between devices, gather_r(): return lax.all_to_all(copies, (X, YL), 0, 0, tiled=True)  11.4 us
    pallas_call x1, Pallas kernels, product_part(): pl.pallas_call(product_kernel, out_shape=(pltpu.HBM((NR, ROWS, COLS - COL...  7.71 us
    ppermute x1, waiting for transfers between devices, swap_slab(): return lax.ppermute(a, S, [(0, 1), (1, 0)])  6.4 us
    ppermute x7, waiting for transfers between devices, shift_z(): return lax.ppermute(a, Z, [((i + d) % NZ, i) for i in range(NZ)])  6.13 us
    all_to_all x1, starting transfers between devices, on_device(): got = lax.all_to_all(parts, (X, YL), 0, 0, tiled=True)  5.34 us
  transfers between devices with their start and end apart: 42, of which 19 were waited for; matrix products, arithmetic and copies ran while one was open for 2% of the time, Pallas kernels for 0%

profile of v5, /device:TPU:1, one launch (start us, length us, event | category | flops | bytes accessed | tf_op | source)
XLA Modules:
  0.0 143.4 jit_solution(12549095887160568533)
XLA Ops:
  1.0 1.5 %copies.2 = bf16[8,32,4608]{2,1,0:T(8,128)(2,1)} custom-call(bf16[32,4608]{1,0:T(8,128)(2,1)S(1)} %copy-done), custom_call_target="tpu_custom_call" | custom-call | tf_op jit(solution)/shard_map/copies/pallas_call | solution.py:83
  2.4 6.0 %all-to-all-start = ((bf16[8,32,4608]{2,1,0:T(8,128)(2,1)}), bf16[8,32,4608]{2,1,0:T(8,128)(2,1)S(1)}, u32[]{:S(2)}, u32[]{:S(2)}) async-start(bf16[8,32,4608]{2,1,0:T(8,128)(2,1)} %copies.2), calls=%async_computation | async-start | bytes 4718592 | tf_op jit(solution)/shard_map/all_to_all | solution.py:92
  8.5 1.7 %collective-permute-start.1 = (bf16[32,4608]{1,0:T(8,128)(2,1)S(1)}, bf16[32,4608]{1,0:T(8,128)(2,1)S(1)}, u32[]{:S(2)}, u32[]{:S(2)}) collective-permute-start(bf16[32,4608]{1,0:T(8,128)(2,1)S(1)} %copy-done.1), channel_id=1, source_target_pairs={{4,0},{30,2},{8,4},{2,6},{12,8},{6,10},{16,12},{10,14},{20,16},{14... | collective-permute-start | bytes 884744 | tf_op jit(solution)/shard_map/ppermute | solution.py:44
  10.2 5.2 %collective-permute-start = (bf16[32,4608]{1,0:T(8,128)(2,1)S(1)}, bf16[32,4608]{1,0:T(8,128)(2,1)S(1)}, u32[]{:S(2)}, u32[]{:S(2)}) collective-permute-start(bf16[32,4608]{1,0:T(8,128)(2,1)S(1)} %copy-done.1), channel_id=1, source_target_pairs={{0,2},{2,0},{1,3},{3,1},{4,6},{6,4},{5,7},{7,5},{8,10},{10,8},{9,1... | collective-permute-start | bytes 884744 | tf_op jit(solution)/shard_map/ppermute | solution.py:33
  15.3 3.2 %collective-permute-done.1.refs_2_ = bf16[32,4608]{1,0:T(8,128)(2,1)S(1)} collective-permute-done((bf16[32,4608]{1,0:T(8,128)(2,1)S(1)}, bf16[32,4608]{1,0:T(8,128)(2,1)S(1)}, u32[]{:S(2)}, u32[]{:S(2)}) %collective-permute-start.1) | collective-permute-done | bytes 294944 | tf_op jit(solution)/shard_map/ppermute | solution.py:44
  18.6 7.0 %collective-permute-done.5.refs_6_ = bf16[32,4608]{1,0:T(8,128)(2,1)S(1)} collective-permute-done((bf16[32,4608]{1,0:T(8,128)(2,1)S(1)}, bf16[32,4608]{1,0:T(8,128)(2,1)S(1)}, u32[]{:S(2)}, u32[]{:S(2)}) %collective-permute-start.5) | collective-permute-done | bytes 294944 | tf_op jit(solution)/shard_map/ppermute | solution.py:44
  25.6 3.2 %collective-permute-done.2.refs_3_ = bf16[32,4608]{1,0:T(8,128)(2,1)S(1)} collective-permute-done((bf16[32,4608]{1,0:T(8,128)(2,1)S(1)}, bf16[32,4608]{1,0:T(8,128)(2,1)S(1)}, u32[]{:S(2)}, u32[]{:S(2)}) %collective-permute-start.2) | collective-permute-done | bytes 294944 | tf_op jit(solution)/shard_map/ppermute | solution.py:44
  28.8 5.6 %collective-permute-start.4 = (bf16[32,4608]{1,0:T(8,128)(2,1)S(1)}, bf16[32,4608]{1,0:T(8,128)(2,1)S(1)}, u32[]{:S(2)}, u32[]{:S(2)}) collective-permute-start(bf16[32,4608]{1,0:T(8,128)(2,1)S(1)} %collective-permute-done.1.refs_2_), channel_id=1, source_target_pairs={{0,2},{2,0},{1,3},{3,1},{4,6},{6,4},{5,7},{7,5},{8,10},{10,8},{9,1... | collective-permute-start | bytes 884744 | tf_op jit(solution)/shard_map/ppermute | solution.py:33
  35.7 6.6 %collective-permute-start.3 = (bf16[32,4608]{1,0:T(8,128)(2,1)S(1)}, bf16[32,4608]{1,0:T(8,128)(2,1)S(1)}, u32[]{:S(2)}, u32[]{:S(2)}) collective-permute-start(bf16[32,4608]{1,0:T(8,128)(2,1)S(1)} %collective-permute-done.2.refs_3_), channel_id=1, source_target_pairs={{0,2},{2,0},{1,3},{3,1},{4,6},{6,4},{5,7},{7,5},{8,10},{10,8},{9,1... | collective-permute-start | bytes 884744 | tf_op jit(solution)/shard_map/ppermute | solution.py:33
  44.4 2.1 %collective-permute-start.11 = (bf16[32,4608]{1,0:T(8,128)(2,1)S(1)}, bf16[32,4608]{1,0:T(8,128)(2,1)S(1)}, u32[]{:S(2)}, u32[]{:S(2)}) collective-permute-start(bf16[32,4608]{1,0:T(8,128)(2,1)S(1)} %collective-permute-done.10.refs_11_), channel_id=1, source_target_pairs={{0,2},{2,0},{1,3},{3,1},{4,6},{6,4},{5,7},{7,5},{8,10},{10,8},{9,1... | collective-permute-start | bytes 884744 | tf_op jit(solution)/shard_map/ppermute | solution.py:33
  49.4 5.1 %gram_part.1 = (bf16[16,32,4608]{2,1,0:T(8,128)(2,1)}, bf16[8,32,1536]{2,1,0:T(8,128)(2,1)}, f32[512,256]{1,0:T(8,128)S(1)}, bf16[512,256]{1,0:T(8,128)(2,1)S(1)}) custom-call(bf16[32,4608]{1,0:T(8,128)(2,1)} %refs_0_.1, bf16[32,4608]{1,0:T(8,128)(2,1)} %copy-done.9, bf16[32,4608]{1,0:T(8,128)(2,1)} %copy-done.8, bf16[32,4608]{1,0:T(8,128)(2,1)} %copy-done.11, ...), custom_call_target="tpu_custom_call" | custom-call | flops 1207959552 | bytes 12582912 | tf_op jit(solution)/shard_map/gram_part/pallas_call | solution.py:125
  54.5 2.9 %collective-permute-start.15 = (bf16[512,256]{1,0:T(8,128)(2,1)S(1)}, bf16[512,256]{1,0:T(8,128)(2,1)S(1)}, u32[]{:S(2)}, u32[]{:S(2)}) collective-permute-start(bf16[512,256]{1,0:T(8,128)(2,1)S(1)} %get-tuple-element.15), channel_id=1, source_target_pairs={{0,1},{1,0},{2,3},{3,2},{4,5},{5,4},{6,7},{7,6},{8,9},{9,8},{10,11... | collective-permute-start | bytes 786440 | tf_op jit(solution)/shard_map/ppermute | solution.py:37
  57.4 6.4 %collective-permute-done.15 = bf16[512,256]{1,0:T(8,128)(2,1)S(1)} collective-permute-done((bf16[512,256]{1,0:T(8,128)(2,1)S(1)}, bf16[512,256]{1,0:T(8,128)(2,1)S(1)}, u32[]{:S(2)}, u32[]{:S(2)}) %collective-permute-start.15) | collective-permute-done | bytes 262176 | tf_op jit(solution)/shard_map/ppermute | solution.py:37
  63.9 1.3 collective-permute-start.16
  66.4 1.4 copies.3
  67.8 5.4 %all-to-all-start.1 = ((bf16[8,512,256]{2,1,0:T(8,128)(2,1)}), bf16[8,512,256]{2,1,0:T(8,128)(2,1)S(1)}, u32[]{:S(2)}, u32[]{:S(2)}) async-start(bf16[8,512,256]{2,1,0:T(8,128)(2,1)} %copies.3), calls=%async_computation.1 | async-start | bytes 4194304 | tf_op jit(solution)/shard_map/all_to_all | solution.py:92
  73.3 7.3 %collective-permute-done.17.refs_2_ = bf16[512,256]{1,0:T(8,128)(2,1)S(1)} collective-permute-done((bf16[512,256]{1,0:T(8,128)(2,1)S(1)}, bf16[512,256]{1,0:T(8,128)(2,1)S(1)}, u32[]{:S(2)}, u32[]{:S(2)}) %collective-permute-start.17) | collective-permute-done | bytes 262176 | tf_op jit(solution)/shard_map/ppermute | solution.py:44
  80.7 2.8 %collective-permute-done.18.refs_3_ = bf16[512,256]{1,0:T(8,128)(2,1)S(1)} collective-permute-done((bf16[512,256]{1,0:T(8,128)(2,1)S(1)}, bf16[512,256]{1,0:T(8,128)(2,1)S(1)}, u32[]{:S(2)}, u32[]{:S(2)}) %collective-permute-start.18) | collective-permute-done | bytes 262176 | tf_op jit(solution)/shard_map/ppermute | solution.py:44
  83.5 3.9 %collective-permute-done.21.refs_6_ = bf16[512,256]{1,0:T(8,128)(2,1)S(1)} collective-permute-done((bf16[512,256]{1,0:T(8,128)(2,1)S(1)}, bf16[512,256]{1,0:T(8,128)(2,1)S(1)}, u32[]{:S(2)}, u32[]{:S(2)}) %collective-permute-start.21) | collective-permute-done | bytes 262176 | tf_op jit(solution)/shard_map/ppermute | solution.py:44
  87.4 5.3 %collective-permute-start.20 = (bf16[512,256]{1,0:T(8,128)(2,1)S(1)}, bf16[512,256]{1,0:T(8,128)(2,1)S(1)}, u32[]{:S(2)}, u32[]{:S(2)}) collective-permute-start(bf16[512,256]{1,0:T(8,128)(2,1)S(1)} %collective-permute-done.17.refs_2_), channel_id=1, source_target_pairs={{0,2},{2,0},{1,3},{3,1},{4,6},{6,4},{5,7},{7,5},{8,10},{10,8},{9,1... | collective-permute-start | bytes 786440 | tf_op jit(solution)/shard_map/ppermute | solution.py:33
  92.8 1.3 collective-permute-done.25.refs_10_
  94.1 6.2 %collective-permute-start.24 = (bf16[512,256]{1,0:T(8,128)(2,1)S(1)}, bf16[512,256]{1,0:T(8,128)(2,1)S(1)}, u32[]{:S(2)}, u32[]{:S(2)}) collective-permute-start(bf16[512,256]{1,0:T(8,128)(2,1)S(1)} %collective-permute-done.21.refs_6_), channel_id=1, source_target_pairs={{0,2},{2,0},{1,3},{3,1},{4,6},{6,4},{5,7},{7,5},{8,10},{10,8},{9,1... | collective-permute-start | bytes 786440 | tf_op jit(solution)/shard_map/ppermute | solution.py:33
  100.9 1.4 collective-permute-done.29.refs_14_
  102.3 1.9 %collective-permute-start.30 = (bf16[512,256]{1,0:T(8,128)(2,1)S(1)}, bf16[512,256]{1,0:T(8,128)(2,1)S(1)}, u32[]{:S(2)}, u32[]{:S(2)}) collective-permute-start(bf16[512,256]{1,0:T(8,128)(2,1)S(1)} %collective-permute-done.29.refs_14_), channel_id=1, source_target_pairs={{0,2},{2,0},{1,3},{3,1},{4,6},{6,4},{5,7},{7,5},{8,10},{10,8},{9,1... | collective-permute-start | bytes 786440 | tf_op jit(solution)/shard_map/ppermute | solution.py:33
  105.4 7.7 %product_part.1 = (bf16[8,32,3072]{2,1,0:T(8,128)(2,1)}, bf16[8,32,1536]{2,1,0:T(8,128)(2,1)}, bf16[8,32,1536]{2,1,0:T(8,128)(2,1)}) custom-call(bf16[512,256]{1,0:T(8,128)(2,1)} %copy-done.3, bf16[512,256]{1,0:T(8,128)(2,1)} %copy-done.18, bf16[512,256]{1,0:T(8,128)(2,1)} %copy-done.19, bf16[512,256]{1,0:T(8,128)(2,1)} %copy-done.20, ...), custom_call_target="tpu_custom_call" | custom-call | flops 2281701376 | bytes 14680064 | tf_op jit(solution)/shard_map/product_part/pallas_call | solution.py:194
  113.5 5.3 %all-to-all-start.2 = ((bf16[8,32,3072]{2,1,0:T(8,128)(2,1)}), bf16[8,32,3072]{2,1,0:T(8,128)(2,1)S(1)}, u32[]{:S(2)}, u32[]{:S(2)}) async-start(bf16[8,32,3072]{2,1,0:T(8,128)(2,1)} %get-tuple-element.22), calls=%async_computation.2 | async-start | bytes 3145728 | tf_op jit(solution)/shard_map/all_to_all | solution.py:236
  119.8 1.3 add_convert_fusion
  122.4 3.4 %collective-permute-start.33 = (bf16[32,1536]{1,0:T(8,128)(2,1)S(1)}, bf16[32,1536]{1,0:T(8,128)(2,1)S(1)}, u32[]{:S(2)}, u32[]{:S(2)}) collective-permute-start(bf16[32,1536]{1,0:T(8,128)(2,1)S(1)} %get-tuple-element.29), channel_id=1, source_target_pairs={{4,0},{8,4},{12,8},{16,12},{20,16},{24,20},{28,24},{0,28},{5,1},{9... | collective-permute-start | bytes 294920 | tf_op jit(solution)/shard_map/ppermute | solution.py:224
  129.0 3.8 %collective-permute-start.37 = (bf16[32,1536]{1,0:T(8,128)(2,1)S(1)}, bf16[32,1536]{1,0:T(8,128)(2,1)}, u32[]{:S(2)}, u32[]{:S(2)}) collective-permute-start(bf16[32,1536]{1,0:T(8,128)(2,1)S(1)} %get-tuple-element.25), channel_id=1, source_target_pairs={{12,0},{16,4},{20,8},{24,12},{28,16},{0,20},{4,24},{8,28},{13,1},{... | collective-permute-start | bytes 294920 | tf_op jit(solution)/shard_map/ppermute | solution.py:224
  132.7 2.3 %collective-permute-start.38 = (bf16[32,1536]{1,0:T(8,128)(2,1)S(1)}, bf16[32,1536]{1,0:T(8,128)(2,1)}, u32[]{:S(2)}, u32[]{:S(2)}) collective-permute-start(bf16[32,1536]{1,0:T(8,128)(2,1)S(1)} %get-tuple-element.24), channel_id=1, source_target_pairs={{20,0},{24,4},{28,8},{0,12},{4,16},{8,20},{12,24},{16,28},{21,1},{... | collective-permute-start | bytes 294920 | tf_op jit(solution)/shard_map/ppermute | solution.py:224
  135.1 1.9 %collective-permute-done.35 = bf16[32,1536]{1,0:T(8,128)(2,1)S(1)} collective-permute-done((bf16[32,1536]{1,0:T(8,128)(2,1)S(1)}, bf16[32,1536]{1,0:T(8,128)(2,1)S(1)}, u32[]{:S(2)}, u32[]{:S(2)}) %collective-permute-start.35) | collective-permute-done | bytes 98336 | tf_op jit(solution)/shard_map/ppermute | solution.py:224
  138.1 2.3 %collective-permute-done.38 = bf16[32,1536]{1,0:T(8,128)(2,1)} collective-permute-done((bf16[32,1536]{1,0:T(8,128)(2,1)S(1)}, bf16[32,1536]{1,0:T(8,128)(2,1)}, u32[]{:S(2)}, u32[]{:S(2)}) %collective-permute-start.38) | collective-permute-done | bytes 98336 | tf_op jit(solution)/shard_map/ppermute | solution.py:224
  (118 shorter events, 20.4 us)
Async XLA Ops:
  2.4 46.0 %all-to-all-start = ((bf16[8,32,4608]{2,1,0:T(8,128)(2,1)}), bf16[8,32,4608]{2,1,0:T(8,128)(2,1)S(1)}, u32[]{:S(2)}, u32[]{:S(2)}) async-start(bf16[8,32,4608]{2,1,0:T(8,128)(2,1)} %copies.2), calls=%async_computation | async-start | bytes 4718592 | tf_op jit(solution)/shard_map/all_to_all | solution.py:92
  8.5 10.1 %collective-permute-start.1 = (bf16[32,4608]{1,0:T(8,128)(2,1)S(1)}, bf16[32,4608]{1,0:T(8,128)(2,1)S(1)}, u32[]{:S(2)}, u32[]{:S(2)}) collective-permute-start(bf16[32,4608]{1,0:T(8,128)(2,1)S(1)} %copy-done.1), channel_id=1, source_target_pairs={{4,0},{30,2},{8,4},{2,6},{12,8},{6,10},{16,12},{10,14},{20,16},{14... | collective-permute-start | bytes 884744 | tf_op jit(solution)/shard_map/ppermute | solution.py:44
  10.2 8.4 %collective-permute-start = (bf16[32,4608]{1,0:T(8,128)(2,1)S(1)}, bf16[32,4608]{1,0:T(8,128)(2,1)S(1)}, u32[]{:S(2)}, u32[]{:S(2)}) collective-permute-start(bf16[32,4608]{1,0:T(8,128)(2,1)S(1)} %copy-done.1), channel_id=1, source_target_pairs={{0,2},{2,0},{1,3},{3,1},{4,6},{6,4},{5,7},{7,5},{8,10},{10,8},{9,1... | collective-permute-start | bytes 884744 | tf_op jit(solution)/shard_map/ppermute | solution.py:33
  18.5 7.1 %collective-permute-start.5 = (bf16[32,4608]{1,0:T(8,128)(2,1)S(1)}, bf16[32,4608]{1,0:T(8,128)(2,1)S(1)}, u32[]{:S(2)}, u32[]{:S(2)}) collective-permute-start(bf16[32,4608]{1,0:T(8,128)(2,1)S(1)} %collective-permute-done.1.refs_2_), channel_id=1, source_target_pairs={{4,0},{30,2},{8,4},{2,6},{12,8},{6,10},{16,12},{10,14},{20,16},{14... | collective-permute-start | bytes 884744 | tf_op jit(solution)/shard_map/ppermute | solution.py:44
  18.5 10.2 %collective-permute-start.2 = (bf16[32,4608]{1,0:T(8,128)(2,1)S(1)}, bf16[32,4608]{1,0:T(8,128)(2,1)S(1)}, u32[]{:S(2)}, u32[]{:S(2)}) collective-permute-start(bf16[32,4608]{1,0:T(8,128)(2,1)S(1)} %collective-permute-done.refs_1_), channel_id=1, source_target_pairs={{4,0},{30,2},{8,4},{2,6},{12,8},{6,10},{16,12},{10,14},{20,16},{14... | collective-permute-start | bytes 884744 | tf_op jit(solution)/shard_map/ppermute | solution.py:44
  25.6 8.8 %collective-permute-start.9 = (bf16[32,4608]{1,0:T(8,128)(2,1)S(1)}, bf16[32,4608]{1,0:T(8,128)(2,1)S(1)}, u32[]{:S(2)}, u32[]{:S(2)}) collective-permute-start(bf16[32,4608]{1,0:T(8,128)(2,1)S(1)} %collective-permute-done.5.refs_6_), channel_id=1, source_target_pairs={{4,0},{30,2},{8,4},{2,6},{12,8},{6,10},{16,12},{10,14},{20,16},{14... | collective-permute-start | bytes 884744 | tf_op jit(solution)/shard_map/ppermute | solution.py:44
  28.8 6.9 %collective-permute-start.6 = (bf16[32,4608]{1,0:T(8,128)(2,1)S(1)}, bf16[32,4608]{1,0:T(8,128)(2,1)S(1)}, u32[]{:S(2)}, u32[]{:S(2)}) collective-permute-start(bf16[32,4608]{1,0:T(8,128)(2,1)S(1)} %collective-permute-done.2.refs_3_), channel_id=1, source_target_pairs={{4,0},{30,2},{8,4},{2,6},{12,8},{6,10},{16,12},{10,14},{20,16},{14... | collective-permute-start | bytes 884744 | tf_op jit(solution)/shard_map/ppermute | solution.py:44
  28.8 13.6 %collective-permute-start.4 = (bf16[32,4608]{1,0:T(8,128)(2,1)S(1)}, bf16[32,4608]{1,0:T(8,128)(2,1)S(1)}, u32[]{:S(2)}, u32[]{:S(2)}) collective-permute-start(bf16[32,4608]{1,0:T(8,128)(2,1)S(1)} %collective-permute-done.1.refs_2_), channel_id=1, source_target_pairs={{0,2},{2,0},{1,3},{3,1},{4,6},{6,4},{5,7},{7,5},{8,10},{10,8},{9,1... | collective-permute-start | bytes 884744 | tf_op jit(solution)/shard_map/ppermute | solution.py:33
  34.4 8.0 %collective-permute-start.8 = (bf16[32,4608]{1,0:T(8,128)(2,1)S(1)}, bf16[32,4608]{1,0:T(8,128)(2,1)S(1)}, u32[]{:S(2)}, u32[]{:S(2)}) collective-permute-start(bf16[32,4608]{1,0:T(8,128)(2,1)S(1)} %collective-permute-done.5.refs_6_), channel_id=1, source_target_pairs={{0,2},{2,0},{1,3},{3,1},{4,6},{6,4},{5,7},{7,5},{8,10},{10,8},{9,1... | collective-permute-start | bytes 884744 | tf_op jit(solution)/shard_map/ppermute | solution.py:33
  34.4 8.5 %collective-permute-start.13 = (bf16[32,4608]{1,0:T(8,128)(2,1)S(1)}, bf16[32,4608]{1,0:T(8,128)(2,1)S(1)}, u32[]{:S(2)}, u32[]{:S(2)}) collective-permute-start(bf16[32,4608]{1,0:T(8,128)(2,1)S(1)} %collective-permute-done.9.refs_10_), channel_id=1, source_target_pairs={{4,0},{30,2},{8,4},{2,6},{12,8},{6,10},{16,12},{10,14},{20,16},{14... | collective-permute-start | bytes 884744 | tf_op jit(solution)/shard_map/ppermute | solution.py:44
  35.7 8.7 %collective-permute-start.10 = (bf16[32,4608]{1,0:T(8,128)(2,1)S(1)}, bf16[32,4608]{1,0:T(8,128)(2,1)S(1)}, u32[]{:S(2)}, u32[]{:S(2)}) collective-permute-start(bf16[32,4608]{1,0:T(8,128)(2,1)S(1)} %collective-permute-done.6.refs_7_), channel_id=1, source_target_pairs={{4,0},{30,2},{8,4},{2,6},{12,8},{6,10},{16,12},{10,14},{20,16},{14... | collective-permute-start | bytes 884744 | tf_op jit(solution)/shard_map/ppermute | solution.py:44
  35.7 10.9 %collective-permute-start.3 = (bf16[32,4608]{1,0:T(8,128)(2,1)S(1)}, bf16[32,4608]{1,0:T(8,128)(2,1)S(1)}, u32[]{:S(2)}, u32[]{:S(2)}) collective-permute-start(bf16[32,4608]{1,0:T(8,128)(2,1)S(1)} %collective-permute-done.2.refs_3_), channel_id=1, source_target_pairs={{0,2},{2,0},{1,3},{3,1},{4,6},{6,4},{5,7},{7,5},{8,10},{10,8},{9,1... | collective-permute-start | bytes 884744 | tf_op jit(solution)/shard_map/ppermute | solution.py:33
  54.5 9.3 %collective-permute-start.15 = (bf16[512,256]{1,0:T(8,128)(2,1)S(1)}, bf16[512,256]{1,0:T(8,128)(2,1)S(1)}, u32[]{:S(2)}, u32[]{:S(2)}) collective-permute-start(bf16[512,256]{1,0:T(8,128)(2,1)S(1)} %get-tuple-element.15), channel_id=1, source_target_pairs={{0,1},{1,0},{2,3},{3,2},{4,5},{5,4},{6,7},{7,6},{8,9},{9,8},{10,11... | collective-permute-start | bytes 786440 | tf_op jit(solution)/shard_map/ppermute | solution.py:37
  67.8 37.6 %all-to-all-start.1 = ((bf16[8,512,256]{2,1,0:T(8,128)(2,1)}), bf16[8,512,256]{2,1,0:T(8,128)(2,1)S(1)}, u32[]{:S(2)}, u32[]{:S(2)}) async-start(bf16[8,512,256]{2,1,0:T(8,128)(2,1)} %copies.3), calls=%async_computation.1 | async-start | bytes 4194304 | tf_op jit(solution)/shard_map/all_to_all | solution.py:92
  73.1 7.5 %collective-permute-start.17 = (bf16[512,256]{1,0:T(8,128)(2,1)S(1)}, bf16[512,256]{1,0:T(8,128)(2,1)S(1)}, u32[]{:S(2)}, u32[]{:S(2)}) collective-permute-start(bf16[512,256]{1,0:T(8,128)(2,1)S(1)} %add_convert_fusion.1.a_ref.refs_0_), channel_id=1, source_target_pairs={{4,0},{30,2},{8,4},{2,6},{12,8},{6,10},{16,12},{10,14},{20,16},{14... | collective-permute-start | bytes 786440 | tf_op jit(solution)/shard_map/ppermute | solution.py:44
  73.2 10.2 %collective-permute-start.18 = (bf16[512,256]{1,0:T(8,128)(2,1)S(1)}, bf16[512,256]{1,0:T(8,128)(2,1)S(1)}, u32[]{:S(2)}, u32[]{:S(2)}) collective-permute-start(bf16[512,256]{1,0:T(8,128)(2,1)S(1)} %collective-permute-done.16.refs_1_), channel_id=1, source_target_pairs={{4,0},{30,2},{8,4},{2,6},{12,8},{6,10},{16,12},{10,14},{20,16},{14... | collective-permute-start | bytes 786440 | tf_op jit(solution)/shard_map/ppermute | solution.py:44
  80.7 6.7 %collective-permute-start.21 = (bf16[512,256]{1,0:T(8,128)(2,1)S(1)}, bf16[512,256]{1,0:T(8,128)(2,1)S(1)}, u32[]{:S(2)}, u32[]{:S(2)}) collective-permute-start(bf16[512,256]{1,0:T(8,128)(2,1)S(1)} %collective-permute-done.17.refs_2_), channel_id=1, source_target_pairs={{4,0},{30,2},{8,4},{2,6},{12,8},{6,10},{16,12},{10,14},{20,16},{14... | collective-permute-start | bytes 786440 | tf_op jit(solution)/shard_map/ppermute | solution.py:44
  83.5 9.2 %collective-permute-start.22 = (bf16[512,256]{1,0:T(8,128)(2,1)S(1)}, bf16[512,256]{1,0:T(8,128)(2,1)S(1)}, u32[]{:S(2)}, u32[]{:S(2)}) collective-permute-start(bf16[512,256]{1,0:T(8,128)(2,1)S(1)} %collective-permute-done.18.refs_3_), channel_id=1, source_target_pairs={{4,0},{30,2},{8,4},{2,6},{12,8},{6,10},{16,12},{10,14},{20,16},{14... | collective-permute-start | bytes 786440 | tf_op jit(solution)/shard_map/ppermute | solution.py:44
  87.4 6.7 %collective-permute-start.25 = (bf16[512,256]{1,0:T(8,128)(2,1)S(1)}, bf16[512,256]{1,0:T(8,128)(2,1)S(1)}, u32[]{:S(2)}, u32[]{:S(2)}) collective-permute-start(bf16[512,256]{1,0:T(8,128)(2,1)S(1)} %collective-permute-done.21.refs_6_), channel_id=1, source_target_pairs={{4,0},{30,2},{8,4},{2,6},{12,8},{6,10},{16,12},{10,14},{20,16},{14... | collective-permute-start | bytes 786440 | tf_op jit(solution)/shard_map/ppermute | solution.py:44
  87.4 12.9 %collective-permute-start.20 = (bf16[512,256]{1,0:T(8,128)(2,1)S(1)}, bf16[512,256]{1,0:T(8,128)(2,1)S(1)}, u32[]{:S(2)}, u32[]{:S(2)}) collective-permute-start(bf16[512,256]{1,0:T(8,128)(2,1)S(1)} %collective-permute-done.17.refs_2_), channel_id=1, source_target_pairs={{0,2},{2,0},{1,3},{3,1},{4,6},{6,4},{5,7},{7,5},{8,10},{10,8},{9,1... | collective-permute-start | bytes 786440 | tf_op jit(solution)/shard_map/ppermute | solution.py:33
  92.7 7.7 %collective-permute-start.19 = (bf16[512,256]{1,0:T(8,128)(2,1)S(1)}, bf16[512,256]{1,0:T(8,128)(2,1)S(1)}, u32[]{:S(2)}, u32[]{:S(2)}) collective-permute-start(bf16[512,256]{1,0:T(8,128)(2,1)S(1)} %collective-permute-done.18.refs_3_), channel_id=1, source_target_pairs={{0,2},{2,0},{1,3},{3,1},{4,6},{6,4},{5,7},{7,5},{8,10},{10,8},{9,1... | collective-permute-start | bytes 786440 | tf_op jit(solution)/shard_map/ppermute | solution.py:33
  92.7 8.1 %collective-permute-start.26 = (bf16[512,256]{1,0:T(8,128)(2,1)S(1)}, bf16[512,256]{1,0:T(8,128)(2,1)S(1)}, u32[]{:S(2)}, u32[]{:S(2)}) collective-permute-start(bf16[512,256]{1,0:T(8,128)(2,1)S(1)} %collective-permute-done.22.refs_7_), channel_id=1, source_target_pairs={{4,0},{30,2},{8,4},{2,6},{12,8},{6,10},{16,12},{10,14},{20,16},{14... | collective-permute-start | bytes 786440 | tf_op jit(solution)/shard_map/ppermute | solution.py:44
  94.1 8.2 %collective-permute-start.29 = (bf16[512,256]{1,0:T(8,128)(2,1)S(1)}, bf16[512,256]{1,0:T(8,128)(2,1)S(1)}, u32[]{:S(2)}, u32[]{:S(2)}) collective-permute-start(bf16[512,256]{1,0:T(8,128)(2,1)S(1)} %collective-permute-done.25.refs_10_), channel_id=1, source_target_pairs={{4,0},{30,2},{8,4},{2,6},{12,8},{6,10},{16,12},{10,14},{20,16},{14... | collective-permute-start | bytes 786440 | tf_op jit(solution)/shard_map/ppermute | solution.py:44
  94.1 10.1 %collective-permute-start.24 = (bf16[512,256]{1,0:T(8,128)(2,1)S(1)}, bf16[512,256]{1,0:T(8,128)(2,1)S(1)}, u32[]{:S(2)}, u32[]{:S(2)}) collective-permute-start(bf16[512,256]{1,0:T(8,128)(2,1)S(1)} %collective-permute-done.21.refs_6_), channel_id=1, source_target_pairs={{0,2},{2,0},{1,3},{3,1},{4,6},{6,4},{5,7},{7,5},{8,10},{10,8},{9,1... | collective-permute-start | bytes 786440 | tf_op jit(solution)/shard_map/ppermute | solution.py:33
  113.5 28.9 %all-to-all-start.2 = ((bf16[8,32,3072]{2,1,0:T(8,128)(2,1)}), bf16[8,32,3072]{2,1,0:T(8,128)(2,1)S(1)}, u32[]{:S(2)}, u32[]{:S(2)}) async-start(bf16[8,32,3072]{2,1,0:T(8,128)(2,1)} %get-tuple-element.22), calls=%async_computation.2 | async-start | bytes 3145728 | tf_op jit(solution)/shard_map/all_to_all | solution.py:236
  121.2 7.8 %collective-permute-start.32 = (bf16[32,1536]{1,0:T(8,128)(2,1)S(1)}, bf16[32,1536]{1,0:T(8,128)(2,1)S(1)}, u32[]{:S(2)}, u32[]{:S(2)}) collective-permute-start(bf16[32,1536]{1,0:T(8,128)(2,1)S(1)} %get-tuple-element.23), channel_id=1, source_target_pairs={{16,0},{20,4},{24,8},{28,12},{0,16},{4,20},{8,24},{12,28},{17,1},{... | collective-permute-start | bytes 294920 | tf_op jit(solution)/shard_map/ppermute | solution.py:224
  122.4 10.3 %collective-permute-start.33 = (bf16[32,1536]{1,0:T(8,128)(2,1)S(1)}, bf16[32,1536]{1,0:T(8,128)(2,1)S(1)}, u32[]{:S(2)}, u32[]{:S(2)}) collective-permute-start(bf16[32,1536]{1,0:T(8,128)(2,1)S(1)} %get-tuple-element.29), channel_id=1, source_target_pairs={{4,0},{8,4},{12,8},{16,12},{20,16},{24,20},{28,24},{0,28},{5,1},{9... | collective-permute-start | bytes 294920 | tf_op jit(solution)/shard_map/ppermute | solution.py:224
  125.8 9.2 %collective-permute-start.34 = (bf16[32,1536]{1,0:T(8,128)(2,1)S(1)}, bf16[32,1536]{1,0:T(8,128)(2,1)S(1)}, u32[]{:S(2)}, u32[]{:S(2)}) collective-permute-start(bf16[32,1536]{1,0:T(8,128)(2,1)S(1)} %get-tuple-element.28), channel_id=1, source_target_pairs={{28,0},{0,4},{4,8},{8,12},{12,16},{16,20},{20,24},{24,28},{29,1},{... | collective-permute-start | bytes 294920 | tf_op jit(solution)/shard_map/ppermute | solution.py:224
  125.9 11.1 %collective-permute-start.35 = (bf16[32,1536]{1,0:T(8,128)(2,1)S(1)}, bf16[32,1536]{1,0:T(8,128)(2,1)S(1)}, u32[]{:S(2)}, u32[]{:S(2)}) collective-permute-start(bf16[32,1536]{1,0:T(8,128)(2,1)S(1)} %get-tuple-element.27), channel_id=1, source_target_pairs={{8,0},{12,4},{16,8},{20,12},{24,16},{28,20},{0,24},{4,28},{9,1},{1... | collective-permute-start | bytes 294920 | tf_op jit(solution)/shard_map/ppermute | solution.py:224
  127.0 10.0 %collective-permute-start.36 = (bf16[32,1536]{1,0:T(8,128)(2,1)S(1)}, bf16[32,1536]{1,0:T(8,128)(2,1)}, u32[]{:S(2)}, u32[]{:S(2)}) collective-permute-start(bf16[32,1536]{1,0:T(8,128)(2,1)S(1)} %get-tuple-element.26), channel_id=1, source_target_pairs={{24,0},{28,4},{0,8},{4,12},{8,16},{12,20},{16,24},{20,28},{25,1},{... | collective-permute-start | bytes 294920 | tf_op jit(solution)/shard_map/ppermute | solution.py:224
  129.0 9.2 %collective-permute-start.37 = (bf16[32,1536]{1,0:T(8,128)(2,1)S(1)}, bf16[32,1536]{1,0:T(8,128)(2,1)}, u32[]{:S(2)}, u32[]{:S(2)}) collective-permute-start(bf16[32,1536]{1,0:T(8,128)(2,1)S(1)} %get-tuple-element.25), channel_id=1, source_target_pairs={{12,0},{16,4},{20,8},{24,12},{28,16},{0,20},{4,24},{8,28},{13,1},{... | collective-permute-start | bytes 294920 | tf_op jit(solution)/shard_map/ppermute | solution.py:224
  132.7 7.7 %collective-permute-start.38 = (bf16[32,1536]{1,0:T(8,128)(2,1)S(1)}, bf16[32,1536]{1,0:T(8,128)(2,1)}, u32[]{:S(2)}, u32[]{:S(2)}) collective-permute-start(bf16[32,1536]{1,0:T(8,128)(2,1)S(1)} %get-tuple-element.24), channel_id=1, source_target_pairs={{20,0},{24,4},{28,8},{0,12},{4,16},{8,20},{12,24},{16,28},{21,1},{... | collective-permute-start | bytes 294920 | tf_op jit(solution)/shard_map/ppermute | solution.py:224
  (38 other events, 309.1 us)

commit v6 on v5

v6 whole, which is shorter than its diff:
```python
import functools
import math

import jax
import jax.numpy as jnp
from jax import lax
from jax.experimental import pallas as pl
from jax.experimental.pallas import tpu as pltpu
from jax.sharding import Mesh
from jax.sharding import PartitionSpec as P

coef_linear = 3.4445
coef_cubic = -4.775
coef_quintic = 2.0315
update_gain = 0.2 * math.sqrt(18432.0)

X, YL, Z, C, S = "x", "yl", "z", "c", "s"
NZ, NR = 8, 8
ROWS, COLS = 32, 4608
TILE = 256
bf16, f32 = jnp.bfloat16, jnp.float32
ORDER = (0, 1, 7, 2, 6, 3, 5, 4)
PARTS = 16
COLS_Z = 1280
LATE = 11
EARLY = 12
NEAR = 0
WIDTH_Z, WIDTH = 640, 256
VMEM = pl.BlockSpec(memory_space=pltpu.VMEM)
HBM = pl.BlockSpec(memory_space=pltpu.HBM)


def swap(a):
    return lax.ppermute(a, C, [(0, 1), (1, 0)])


def swap_slab(a):
    return lax.ppermute(a, S, [(0, 1), (1, 0)])


def turn(a):
    pairs = []
    for i in range(NZ):
        pairs += [(2 * ((i + 1) % NZ), 2 * i), (2 * ((i - 1) % NZ) + 1, 2 * i + 1)]
    return lax.ppermute(a, (Z, C), pairs)


def far(a):
    return pltpu.with_memory_space_constraint(a, pltpu.HBM)


def ring_z(a, b):
    mine, others = [a] + [None] * (NZ - 1), [b] + [None] * (NZ - 1)
    for step in range(1, 4):
        a = turn(a)
        b = turn(b)
        mine[step], others[step] = a, b
        mine[NZ - step], others[NZ - step] = swap(b), swap(a)
    mine[4] = turn(a)
    others[4] = swap(mine[4])
    return [part[e] for e in ORDER for part in (mine, others)]


def where_from(i):
    core, z = lax.axis_index(C), lax.axis_index(Z)
    e = ORDER[i // 2]
    return (z + e + core * (NZ - 2 * e) + NZ) % NZ, core if i % 2 == 0 else 1 - core


def near(a):
    return pltpu.with_memory_space_constraint(a, pltpu.VMEM)


def spread(a_ref, out_ref, sem):
    copies = [pltpu.make_async_copy(a_ref, out_ref.at[i], sem.at[i]) for i in range(NR)]
    for copy in copies:
        copy.start()
    for copy in copies:
        copy.wait()


def copies_of(a):
    return pl.pallas_call(
        spread,
        out_shape=pltpu.HBM((NR, *a.shape), a.dtype),
        in_specs=[VMEM],
        out_specs=HBM,
        scratch_shapes=[pltpu.SemaphoreType.DMA((NR,))],
        compiler_params=pltpu.CompilerParams(vmem_limit_bytes=1 << 20),
        cost_estimate=pl.CostEstimate(flops=0, bytes_accessed=5 << 20, transcendentals=0),
        name="copies",
    )(near(a))


def gather_r(copies):
    return lax.all_to_all(copies, (X, YL), 0, 0, tiled=True)


def join_kernel(own_a, got_a, own_b, got_b, gram_ref):
    for i in range(PARTS):
        z, h = where_from(i)
        if i < EARLY:
            rows = pl.ds(i * ROWS, ROWS)
            value = own_a[rows, :] + got_a[rows, :].astype(f32)
        else:
            rows = pl.ds((i - EARLY) * ROWS, ROWS)
            value = own_b[rows, :] + got_b[rows, :].astype(f32)
        gram_ref[2 * z + h] = value.astype(bf16)


def join(*parts):
    return pl.pallas_call(
        join_kernel,
        out_shape=pltpu.VMEM((PARTS, ROWS, TILE), bf16),
        in_specs=[VMEM] * 4,
        out_specs=VMEM,
        compiler_params=pltpu.CompilerParams(vmem_limit_bytes=4 << 20),
        name="join",
    )(*[near(p) for p in parts])


def gram_kernel(count, cut, *refs):
    pieces, cols_ref, own_ref, sent_ref = refs[:count], refs[count], refs[count + 1], refs[count + 2]
    x, sem = refs[-2:]
    copies = [pltpu.make_async_copy(piece, x.at[i], sem.at[i]) for i, piece in enumerate(pieces)]
    if cut:
        copies.append(pltpu.make_async_copy(cols_ref.at[:, :, pl.ds(0, COLS_Z)], refs[count + 3], sem.at[count]))
    for copy in copies:
        copy.start()
    for copy in copies[:count]:
        copy.wait()
    left = x[...].reshape(count * ROWS, COLS)
    right = cols_ref[...].reshape(TILE, COLS)
    total = lax.dot_general(left, right, (((1,), (1,)), ((), ())), preferred_element_type=f32)
    own_ref[...] = total
    sent_ref[...] = total.astype(bf16)
    for copy in copies[count:]:
        copy.wait()


def gram_part(pieces, near_from, cols, cut):
    count = len(pieces)
    n = count * ROWS
    outs = [pltpu.VMEM((n, TILE), f32), pltpu.VMEM((n, TILE), bf16)]
    if cut:
        outs.append(pltpu.HBM((NR, ROWS, COLS_Z), bf16))
    return pl.pallas_call(
        functools.partial(gram_kernel, count, cut),
        out_shape=tuple(outs),
        in_specs=[HBM] * near_from + [VMEM] * (count - near_from) + [VMEM],
        out_specs=(VMEM, VMEM, HBM)[: len(outs)],
        scratch_shapes=[
            pltpu.VMEM((count, ROWS, COLS), bf16),
            pltpu.SemaphoreType.DMA((count + 1,)),
        ],
        compiler_params=pltpu.CompilerParams(vmem_limit_bytes=10 << 20),
        cost_estimate=pl.CostEstimate(flops=2 * n * TILE * COLS, bytes_accessed=6 << 20, transcendentals=0),
        name="gram_part",
    )(*[far(p) for p in pieces[:near_from]], *[near(p) for p in pieces[near_from:]], near(cols))


def product_kernel(*refs):
    a_refs, refs = refs[:PARTS], refs[PARTS:]
    x_refs, refs = refs[:PARTS], refs[PARTS:]
    b_ref, cut_ref, out_ref, own_ref, other_ref, a, x, y, part, out, sem_a, sem_x, sem_out = refs
    copies = []
    for i, ref in enumerate(a_refs):
        z, h = where_from(i)
        copies.append(pltpu.make_async_copy(ref, a.at[i], sem_a.at[i]))
    loads = [pltpu.make_async_copy(cut_ref, y, sem_x.at[PARTS])]
    for i, ref in enumerate(x_refs):
        z, h = where_from(i)
        loads.append(pltpu.make_async_copy(ref.at[:, pl.ds(COLS_Z, COLS - COLS_Z)], x.at[2 * z + h], sem_x.at[i]))
    for copy in copies + loads:
        copy.start()
    squared = None
    for i in range(PARTS):
        z, h = where_from(i)
        copies[i].wait()
        term = jnp.dot(a[i], b_ref[:, 2 * z + h].reshape(TILE, TILE), preferred_element_type=f32)
        squared = term if squared is None else squared + term
    gram = a[0].astype(f32)
    poly = coef_cubic * gram + coef_quintic * squared
    poly_t = poly.T.astype(bf16)
    poly = poly.astype(bf16)
    loads[0].wait()
    for k in range(COLS_Z // WIDTH_Z):
        cut = pl.ds(k * WIDTH_Z, WIDTH_Z)
        term = jnp.dot(poly, y[:, :, cut].reshape(TILE, WIDTH_Z), preferred_element_type=f32)
        part[:, :, :, cut] = term.astype(bf16).reshape(NZ, 2, ROWS, WIDTH_Z)
    core = lax.axis_index(C)
    outs = [
        pltpu.make_async_copy(part.at[:, 1 - core], other_ref, sem_x.at[PARTS + 1]),
        pltpu.make_async_copy(part.at[:, core], own_ref, sem_x.at[PARTS + 2]),
    ]
    for copy in outs:
        copy.start()
    for load in loads[1:]:
        load.wait()
    for k in range((COLS - COLS_Z) // WIDTH):
        cut = pl.ds(k * WIDTH, WIDTH)
        right = x[:, :, cut].reshape(PARTS * ROWS, WIDTH)
        term = jnp.dot(poly_t, right, preferred_element_type=f32)
        out[:, :, cut] = term.astype(bf16).reshape(NR, ROWS, WIDTH)
        outs.append(pltpu.make_async_copy(out.at[:, :, cut], out_ref.at[:, :, cut], sem_out.at[k]))
        outs[-1].start()
    for copy in outs:
        copy.wait()


def product_part(a_parts, x_parts, b, cut):
    n = PARTS * ROWS
    return pl.pallas_call(
        product_kernel,
        out_shape=(
            pltpu.HBM((NR, ROWS, COLS - COLS_Z), bf16),
            pltpu.HBM((NZ, ROWS, COLS_Z), bf16),
            pltpu.HBM((NZ, ROWS, COLS_Z), bf16),
        ),
        in_specs=[HBM] * LATE + [VMEM] * (PARTS - LATE) + [HBM] * PARTS + [VMEM, HBM],
        out_specs=(HBM, HBM, HBM),
        scratch_shapes=[
            pltpu.VMEM((PARTS, n, TILE), bf16),
            pltpu.VMEM((PARTS, ROWS, COLS - COLS_Z), bf16),
            pltpu.VMEM((NR, ROWS, COLS_Z), bf16),
            pltpu.VMEM((NZ, 2, ROWS, COLS_Z), bf16),
            pltpu.VMEM((NR, ROWS, COLS - COLS_Z), bf16),
            pltpu.SemaphoreType.DMA((PARTS,)),
            pltpu.SemaphoreType.DMA((PARTS + 3,)),
            pltpu.SemaphoreType.DMA(((COLS - COLS_Z) // WIDTH,)),
        ],
        compiler_params=pltpu.CompilerParams(vmem_limit_bytes=28 << 20),
        cost_estimate=pl.CostEstimate(
            flops=2 * n * TILE * (COLS + PARTS * TILE), bytes_accessed=14 << 20, transcendentals=0
        ),
        name="product_part",
    )(*[far(p) for p in a_parts[:LATE]], *[near(p) for p in a_parts[LATE:]], *[far(p) for p in x_parts], near(b), far(cut))


def shift_z(a, d):
    return lax.ppermute(a, Z, [((i + d) % NZ, i) for i in range(NZ)])


def on_device(iterate):
    z = lax.axis_index(Z)
    copies, twin = lax.optimization_barrier((copies_of(iterate), swap(iterate)))
    cols = gather_r(copies)
    pieces = ring_z(iterate, twin)
    own_a, sent_a, cut = gram_part(pieces[:EARLY], EARLY, cols, True)
    got_a = swap_slab(sent_a)
    own_b, sent_b = gram_part(pieces[EARLY:], NEAR, cols, False)
    gram = join(own_a, got_a, own_b, swap_slab(sent_b))
    gram = gram.reshape(PARTS * ROWS, TILE)
    copies, twin = lax.optimization_barrier((copies_of(gram), swap(gram)))
    every = gather_r(copies).reshape(NR, PARTS, ROWS, TILE)
    parts, own, other = product_part(ring_z(gram, twin), pieces, every, cut)
    got = lax.all_to_all(parts, (X, YL), 0, 0, tiled=True)
    own = (own.astype(f32) + swap(other).astype(f32)).astype(bf16)
    take = lambda d: lax.dynamic_index_in_dim(own, (z - d + NZ) % NZ, 0, keepdims=False)
    got_z = [take(0)] + [shift_z(take(d), d) for d in (4, 1, 7, 2, 6, 3, 5)]
    sums = [sum(p.astype(f32) for p in got_z), got.astype(f32).sum(0)]
    total = coef_linear * iterate.astype(f32) + jnp.concatenate(sums, axis=1)
    return (update_gain * total).astype(bf16)


def solution(mesh):
    fine = Mesh(mesh.devices.reshape(4, 2, 8, 2, 2), (X, YL, Z, C, S))
    spec = P((X, YL, Z, C), S)
    return jax.shard_map(on_device, mesh=fine, in_specs=(spec,), out_specs=spec, check_vma=False)
```

time: 146 us -> 138 us (0.945); the launches traced: 143 us -> 138 us
  starting transfers between devices: 71.2 us -> 67.6 us
  local copies, waits for them, and re-layouts: 5.06 us -> 3.32 us
    ppermute x17, starting transfers between devices: 36.3 us -> 32.2 us  [swap(): return lax.ppermute(a, C, [(0, 1), (1, 0)])]
    ppermute x14, starting transfers between devices: 2.15 us -> 5.21 us  [turn(): return lax.ppermute(a, (Z, C), pairs)]
    all_to_all x1, waiting for transfers between devices: 0.87 us -> 3.62 us  [on_device(): got = lax.all_to_all(parts, (X, YL), 0, 0, tiled=True)]
    all_to_all x2, starting transfers between devices: 11.4 us -> 8.75 us  [gather_r(): return lax.all_to_all(copies, (X, YL), 0, 0, tiled=True)]
    ppermute x1 -> x2, waiting for transfers between devices: 6.4 us -> 4.34 us  [swap_slab(): return lax.ppermute(a, S, [(0, 1), (1, 0)])]
    unnamed x56, local copies, waits for them, and re-layouts: 5 us -> 3.27 us
    ppermute x17, waiting for transfers between devices: 1.94 us -> 0.41 us  [swap(): return lax.ppermute(a, C, [(0, 1), (1, 0)])]
    ppermute x14, waiting for transfers between devices: 32.3 us -> 33.8 us  [turn(): return lax.ppermute(a, (Z, C), pairs)]
  transfers between devices with their start and end apart: 42 -> 43, of which waited for: 19 -> 16; matrix products, arithmetic and copies ran while one was open for 2% -> 2% of each run, Pallas kernels for 0% -> 5%
where the time goes in v6:
time: 138 us
  starting transfers between devices  67.6 us (49%)
  waiting for transfers between devices  48.2 us (35%)
  Pallas kernels  15.1 us (11%)
  local copies, waits for them, and re-layouts  3.32 us (2%)
  other arithmetic  3.25 us (2%)
    ppermute x14, waiting for transfers between devices, turn(): return lax.ppermute(a, (Z, C), pairs)  33.8 us
    ppermute x17, starting transfers between devices, swap(): return lax.ppermute(a, C, [(0, 1), (1, 0)])  32.2 us
    ppermute x7, starting transfers between devices, shift_z(): return lax.ppermute(a, Z, [((i + d) % NZ, i) for i in range(NZ)])  12.7 us
    all_to_all x2, starting transfers between devices, gather_r(): return lax.all_to_all(copies, (X, YL), 0, 0, tiled=True)  8.75 us
    pallas_call x1, Pallas kernels, product_part(): pl.pallas_call(product_kernel, out_shape=(pltpu.HBM((NR, ROWS, COLS - COL...  7.63 us
    ppermute x7, waiting for transfers between devices, shift_z(): return lax.ppermute(a, Z, [((i + d) % NZ, i) for i in range(NZ)])  6.08 us
    all_to_all x1, starting transfers between devices, on_device(): got = lax.all_to_all(parts, (X, YL), 0, 0, tiled=True)  5.42 us
    ppermute x14, starting transfers between devices, turn(): return lax.ppermute(a, (Z, C), pairs)  5.21 us
  transfers between devices with their start and end apart: 43, of which 16 were waited for; matrix products, arithmetic and copies ran while one was open for 2% of the time, Pallas kernels for 5%

profile of v6, /device:TPU:1, one launch (start us, length us, event | category | flops | bytes accessed | tf_op | source)
XLA Modules:
  0.0 137.9 jit_solution(1452438494977787206)
XLA Ops:
  0.0 3.2 %collective-permute-start = (bf16[32,4608]{1,0:T(8,128)(2,1)}, bf16[32,4608]{1,0:T(8,128)(2,1)S(1)}, u32[]{:S(2)}, u32[]{:S(2)}) collective-permute-start(bf16[32,4608]{1,0:T(8,128)(2,1)} %refs_16_.1), channel_id=1, source_target_pairs={{0,2},{2,0},{1,3},{3,1},{4,6},{6,4},{5,7},{7,5},{8,10},{10,8},{9,1... | collective-permute-start | bytes 884744 | tf_op jit(solution)/shard_map/ppermute | solution.py:34
  5.7 3.8 %all-to-all-start = ((bf16[8,32,4608]{2,1,0:T(8,128)(2,1)}), bf16[8,32,4608]{2,1,0:T(8,128)(2,1)S(1)}, u32[]{:S(2)}, u32[]{:S(2)}) async-start(bf16[8,32,4608]{2,1,0:T(8,128)(2,1)} %copies.2), calls=%async_computation | async-start | bytes 4718592 | tf_op jit(solution)/shard_map/all_to_all | solution.py:96
  10.9 1.6 %collective-permute-start.2 = (bf16[32,4608]{1,0:T(8,128)(2,1)S(1)}, bf16[32,4608]{1,0:T(8,128)(2,1)S(1)}, u32[]{:S(2)}, u32[]{:S(2)}) collective-permute-start(bf16[32,4608]{1,0:T(8,128)(2,1)S(1)} %collective-permute-done.refs_1_.refs_17_), channel_id=1, source_target_pairs={{4,0},{30,2},{8,4},{2,6},{12,8},{6,10},{16,12},{10,14},{20,16},{14... | collective-permute-start | bytes 884744 | tf_op jit(solution)/shard_map/ppermute | solution.py:45
  12.5 6.7 %collective-permute-done.1.refs_2_.refs_18_ = bf16[32,4608]{1,0:T(8,128)(2,1)S(1)} collective-permute-done((bf16[32,4608]{1,0:T(8,128)(2,1)S(1)}, bf16[32,4608]{1,0:T(8,128)(2,1)S(1)}, u32[]{:S(2)}, u32[]{:S(2)}) %collective-permute-start.1) | collective-permute-done | bytes 294944 | tf_op jit(solution)/shard_map/ppermute | solution.py:45
  19.2 2.9 %collective-permute-done.2.refs_3_.refs_19_ = bf16[32,4608]{1,0:T(8,128)(2,1)S(1)} collective-permute-done((bf16[32,4608]{1,0:T(8,128)(2,1)S(1)}, bf16[32,4608]{1,0:T(8,128)(2,1)S(1)}, u32[]{:S(2)}, u32[]{:S(2)}) %collective-permute-start.2) | collective-permute-done | bytes 294944 | tf_op jit(solution)/shard_map/ppermute | solution.py:45
  22.1 4.2 %collective-permute-done.5.refs_6_.refs_22_ = bf16[32,4608]{1,0:T(8,128)(2,1)S(1)} collective-permute-done((bf16[32,4608]{1,0:T(8,128)(2,1)S(1)}, bf16[32,4608]{1,0:T(8,128)(2,1)S(1)}, u32[]{:S(2)}, u32[]{:S(2)}) %collective-permute-start.5) | collective-permute-done | bytes 294944 | tf_op jit(solution)/shard_map/ppermute | solution.py:45
  26.3 4.9 %collective-permute-start.4 = (bf16[32,4608]{1,0:T(8,128)(2,1)S(1)}, bf16[32,4608]{1,0:T(8,128)(2,1)S(1)}, u32[]{:S(2)}, u32[]{:S(2)}) collective-permute-start(bf16[32,4608]{1,0:T(8,128)(2,1)S(1)} %collective-permute-done.1.refs_2_.refs_18_), channel_id=1, source_target_pairs={{0,2},{2,0},{1,3},{3,1},{4,6},{6,4},{5,7},{7,5},{8,10},{10,8},{9,1... | collective-permute-start | bytes 884744 | tf_op jit(solution)/shard_map/ppermute | solution.py:34
  31.3 2.0 %collective-permute-done.9.refs_10_.refs_26_ = bf16[32,4608]{1,0:T(8,128)(2,1)} collective-permute-done((bf16[32,4608]{1,0:T(8,128)(2,1)S(1)}, bf16[32,4608]{1,0:T(8,128)(2,1)}, u32[]{:S(2)}, u32[]{:S(2)}) %collective-permute-start.9) | collective-permute-done | bytes 294944 | tf_op jit(solution)/shard_map/ppermute | solution.py:45
  33.4 5.9 %collective-permute-start.8 = (bf16[32,4608]{1,0:T(8,128)(2,1)S(1)}, bf16[32,4608]{1,0:T(8,128)(2,1)S(1)}, u32[]{:S(2)}, u32[]{:S(2)}) collective-permute-start(bf16[32,4608]{1,0:T(8,128)(2,1)S(1)} %collective-permute-done.5.refs_6_.refs_22_), channel_id=1, source_target_pairs={{0,2},{2,0},{1,3},{3,1},{4,6},{6,4},{5,7},{7,5},{8,10},{10,8},{9,1... | collective-permute-start | bytes 884744 | tf_op jit(solution)/shard_map/ppermute | solution.py:34
  39.9 1.7 %collective-permute-done.14.refs_2_.refs_30_ = bf16[32,4608]{1,0:T(8,128)(2,1)S(1)} collective-permute-done((bf16[32,4608]{1,0:T(8,128)(2,1)}, bf16[32,4608]{1,0:T(8,128)(2,1)S(1)}, u32[]{:S(2)}, u32[]{:S(2)}) %collective-permute-start.14) | collective-permute-done | bytes 294944 | tf_op jit(solution)/shard_map/ppermute | solution.py:45
  41.6 2.3 %collective-permute-start.15 = (bf16[32,4608]{1,0:T(8,128)(2,1)S(1)}, bf16[32,4608]{1,0:T(8,128)(2,1)S(1)}, u32[]{:S(2)}, u32[]{:S(2)}) collective-permute-start(bf16[32,4608]{1,0:T(8,128)(2,1)S(1)} %collective-permute-done.14.refs_2_.refs_30_), channel_id=1, source_target_pairs={{0,2},{2,0},{1,3},{3,1},{4,6},{6,4},{5,7},{7,5},{8,10},{10,8},{9,1... | collective-permute-start | bytes 884744 | tf_op jit(solution)/shard_map/ppermute | solution.py:34
  44.6 3.4 %gram_part.2 = (f32[384,256]{1,0:T(8,128)S(1)}, bf16[384,256]{1,0:T(8,128)(2,1)S(1)}, bf16[8,32,1280]{2,1,0:T(8,128)(2,1)}) custom-call(bf16[32,4608]{1,0:T(8,128)(2,1)} %refs_16_.1, bf16[32,4608]{1,0:T(8,128)(2,1)} %copy-done.8, bf16[32,4608]{1,0:T(8,128)(2,1)} %copy-done.9, bf16[32,4608]{1,0:T(8,128)(2,1)} %copy-done.10, bf16[32,4608]{1,0:T(8,128)(2,1)} %copy-done.14, ...), custom_call_target="tpu_custom_call" | custom-call | flops 905969664 | bytes 6291456 | tf_op jit(solution)/shard_map/gram_part/pallas_call | solution.py:147
  48.0 2.7 %collective-permute-start.11 = (bf16[384,256]{1,0:T(8,128)(2,1)S(1)}, bf16[384,256]{1,0:T(8,128)(2,1)S(1)}, u32[]{:S(2)}, u32[]{:S(2)}) collective-permute-start(bf16[384,256]{1,0:T(8,128)(2,1)S(1)} %get-tuple-element.20), channel_id=1, source_target_pairs={{0,1},{1,0},{2,3},{3,2},{4,5},{5,4},{6,7},{7,6},{8,9},{9,8},{10,11... | collective-permute-start | bytes 589832 | tf_op jit(solution)/shard_map/ppermute | solution.py:38
  52.6 4.3 %collective-permute-done.16.got_b = bf16[128,256]{1,0:T(8,128)(2,1)S(1)} collective-permute-done((bf16[128,256]{1,0:T(8,128)(2,1)S(1)}, bf16[128,256]{1,0:T(8,128)(2,1)S(1)}, u32[]{:S(2)}, u32[]{:S(2)}) %collective-permute-start.16) | collective-permute-done | bytes 65568 | tf_op jit(solution)/shard_map/ppermute | solution.py:38
  57.0 1.9 %collective-permute-start.17 = (bf16[512,256]{1,0:T(8,128)(2,1)S(1)}, bf16[512,256]{1,0:T(8,128)(2,1)S(1)}, u32[]{:S(2)}, u32[]{:S(2)}) collective-permute-start(bf16[512,256]{1,0:T(8,128)(2,1)S(1)} %bitcast.20), channel_id=1, source_target_pairs={{0,2},{2,0},{1,3},{3,1},{4,6},{6,4},{5,7},{7,5},{8,10},{10,8},{9,1... | collective-permute-start | bytes 786440 | tf_op jit(solution)/shard_map/ppermute | solution.py:34
  60.3 5.0 %all-to-all-start.1 = ((bf16[8,512,256]{2,1,0:T(8,128)(2,1)}), bf16[8,512,256]{2,1,0:T(8,128)(2,1)S(1)}, u32[]{:S(2)}, u32[]{:S(2)}) async-start(bf16[8,512,256]{2,1,0:T(8,128)(2,1)} %copies.3), calls=%async_computation.1 | async-start | bytes 4194304 | tf_op jit(solution)/shard_map/all_to_all | solution.py:96
  65.6 1.6 %collective-permute-start.19 = (bf16[512,256]{1,0:T(8,128)(2,1)S(1)}, bf16[512,256]{1,0:T(8,128)(2,1)S(1)}, u32[]{:S(2)}, u32[]{:S(2)}) collective-permute-start(bf16[512,256]{1,0:T(8,128)(2,1)S(1)} %collective-permute-done.17.refs_1_), channel_id=1, source_target_pairs={{4,0},{30,2},{8,4},{2,6},{12,8},{6,10},{16,12},{10,14},{20,16},{14... | collective-permute-start | bytes 786440 | tf_op jit(solution)/shard_map/ppermute | solution.py:45
  67.3 6.3 %collective-permute-done.18.refs_2_ = bf16[512,256]{1,0:T(8,128)(2,1)S(1)} collective-permute-done((bf16[512,256]{1,0:T(8,128)(2,1)S(1)}, bf16[512,256]{1,0:T(8,128)(2,1)S(1)}, u32[]{:S(2)}, u32[]{:S(2)}) %collective-permute-start.18) | collective-permute-done | bytes 262176 | tf_op jit(solution)/shard_map/ppermute | solution.py:45
  73.6 2.8 %collective-permute-done.19.refs_3_ = bf16[512,256]{1,0:T(8,128)(2,1)S(1)} collective-permute-done((bf16[512,256]{1,0:T(8,128)(2,1)S(1)}, bf16[512,256]{1,0:T(8,128)(2,1)S(1)}, u32[]{:S(2)}, u32[]{:S(2)}) %collective-permute-start.19) | collective-permute-done | bytes 262176 | tf_op jit(solution)/shard_map/ppermute | solution.py:45
  76.4 3.9 %collective-permute-done.22.refs_6_ = bf16[512,256]{1,0:T(8,128)(2,1)S(1)} collective-permute-done((bf16[512,256]{1,0:T(8,128)(2,1)S(1)}, bf16[512,256]{1,0:T(8,128)(2,1)S(1)}, u32[]{:S(2)}, u32[]{:S(2)}) %collective-permute-start.22) | collective-permute-done | bytes 262176 | tf_op jit(solution)/shard_map/ppermute | solution.py:45
  80.4 4.8 %collective-permute-start.21 = (bf16[512,256]{1,0:T(8,128)(2,1)S(1)}, bf16[512,256]{1,0:T(8,128)(2,1)S(1)}, u32[]{:S(2)}, u32[]{:S(2)}) collective-permute-start(bf16[512,256]{1,0:T(8,128)(2,1)S(1)} %collective-permute-done.18.refs_2_), channel_id=1, source_target_pairs={{0,2},{2,0},{1,3},{3,1},{4,6},{6,4},{5,7},{7,5},{8,10},{10,8},{9,1... | collective-permute-start | bytes 786440 | tf_op jit(solution)/shard_map/ppermute | solution.py:34
  85.2 1.8 %collective-permute-done.26.refs_10_ = bf16[512,256]{1,0:T(8,128)(2,1)S(1)} collective-permute-done((bf16[512,256]{1,0:T(8,128)(2,1)S(1)}, bf16[512,256]{1,0:T(8,128)(2,1)S(1)}, u32[]{:S(2)}, u32[]{:S(2)}) %collective-permute-start.26) | collective-permute-done | bytes 262176 | tf_op jit(solution)/shard_map/ppermute | solution.py:45
  87.1 5.6 %collective-permute-start.25 = (bf16[512,256]{1,0:T(8,128)(2,1)S(1)}, bf16[512,256]{1,0:T(8,128)(2,1)S(1)}, u32[]{:S(2)}, u32[]{:S(2)}) collective-permute-start(bf16[512,256]{1,0:T(8,128)(2,1)S(1)} %collective-permute-done.22.refs_6_), channel_id=1, source_target_pairs={{0,2},{2,0},{1,3},{3,1},{4,6},{6,4},{5,7},{7,5},{8,10},{10,8},{9,1... | collective-permute-start | bytes 786440 | tf_op jit(solution)/shard_map/ppermute | solution.py:34
  94.8 1.9 %collective-permute-start.31 = (bf16[512,256]{1,0:T(8,128)(2,1)S(1)}, bf16[512,256]{1,0:T(8,128)(2,1)S(1)}, u32[]{:S(2)}, u32[]{:S(2)}) collective-permute-start(bf16[512,256]{1,0:T(8,128)(2,1)S(1)} %collective-permute-done.30.refs_14_), channel_id=1, source_target_pairs={{0,2},{2,0},{1,3},{3,1},{4,6},{6,4},{5,7},{7,5},{8,10},{10,8},{9,1... | collective-permute-start | bytes 786440 | tf_op jit(solution)/shard_map/ppermute | solution.py:34
  97.8 7.6 %product_part.1 = (bf16[8,32,3328]{2,1,0:T(8,128)(2,1)}, bf16[8,32,1280]{2,1,0:T(8,128)(2,1)}, bf16[8,32,1280]{2,1,0:T(8,128)(2,1)}) custom-call(bf16[512,256]{1,0:T(8,128)(2,1)} %bitcast.23, bf16[512,256]{1,0:T(8,128)(2,1)} %copy-done.18, bf16[512,256]{1,0:T(8,128)(2,1)} %copy-done.19, bf16[512,256]{1,0:T(8,128)(2,1)} %copy-done.20, ...), custom_call_target="tpu_custom_call" | custom-call | flops 2281701376 | bytes 14680064 | tf_op jit(solution)/shard_map/product_part/pallas_call | solution.py:213
  105.9 5.4 %all-to-all-start.2 = ((bf16[8,32,3328]{2,1,0:T(8,128)(2,1)}), bf16[8,32,3328]{2,1,0:T(8,128)(2,1)S(1)}, u32[]{:S(2)}, u32[]{:S(2)}) async-start(bf16[8,32,3328]{2,1,0:T(8,128)(2,1)} %get-tuple-element.28), calls=%async_computation.2 | async-start | bytes 3407872 | tf_op jit(solution)/shard_map/all_to_all | solution.py:257
  113.5 3.5 %collective-permute-start.33 = (bf16[32,1280]{1,0:T(8,128)(2,1)S(1)}, bf16[32,1280]{1,0:T(8,128)(2,1)S(1)}, u32[]{:S(2)}, u32[]{:S(2)}) collective-permute-start(bf16[32,1280]{1,0:T(8,128)(2,1)S(1)} %get-tuple-element.29), channel_id=1, source_target_pairs={{16,0},{20,4},{24,8},{28,12},{0,16},{4,20},{8,24},{12,28},{17,1},{... | collective-permute-start | bytes 245768 | tf_op jit(solution)/shard_map/ppermute | solution.py:241
  119.3 1.5 %collective-permute-start.37 = (bf16[32,1280]{1,0:T(8,128)(2,1)S(1)}, bf16[32,1280]{1,0:T(8,128)(2,1)S(1)}, u32[]{:S(2)}, u32[]{:S(2)}) collective-permute-start(bf16[32,1280]{1,0:T(8,128)(2,1)S(1)} %get-tuple-element.32), channel_id=1, source_target_pairs={{24,0},{28,4},{0,8},{4,12},{8,16},{12,20},{16,24},{20,28},{25,1},{... | collective-permute-start | bytes 245768 | tf_op jit(solution)/shard_map/ppermute | solution.py:241
  120.9 4.2 %collective-permute-start.38 = (bf16[32,1280]{1,0:T(8,128)(2,1)S(1)}, bf16[32,1280]{1,0:T(8,128)(2,1)S(1)}, u32[]{:S(2)}, u32[]{:S(2)}) collective-permute-start(bf16[32,1280]{1,0:T(8,128)(2,1)S(1)} %get-tuple-element.31), channel_id=1, source_target_pairs={{12,0},{16,4},{20,8},{24,12},{28,16},{0,20},{4,24},{8,28},{13,1},{... | collective-permute-start | bytes 245768 | tf_op jit(solution)/shard_map/ppermute | solution.py:241
  126.3 3.6 %collective-permute-done.38 = bf16[32,1280]{1,0:T(8,128)(2,1)S(1)} collective-permute-done((bf16[32,1280]{1,0:T(8,128)(2,1)S(1)}, bf16[32,1280]{1,0:T(8,128)(2,1)S(1)}, u32[]{:S(2)}, u32[]{:S(2)}) %collective-permute-start.38) | collective-permute-done | bytes 81952 | tf_op jit(solution)/shard_map/ppermute | solution.py:241
  129.9 2.4 %collective-permute-done.39 = bf16[32,1280]{1,0:T(8,128)(2,1)} collective-permute-done((bf16[32,1280]{1,0:T(8,128)(2,1)S(1)}, bf16[32,1280]{1,0:T(8,128)(2,1)}, u32[]{:S(2)}, u32[]{:S(2)}) %collective-permute-start.39) | collective-permute-done | bytes 81952 | tf_op jit(solution)/shard_map/ppermute | solution.py:241
  133.3 3.6 %all-to-all-done.2 = bf16[8,32,3328]{2,1,0:T(8,128)(2,1)S(1)} async-done(((bf16[8,32,3328]{2,1,0:T(8,128)(2,1)}), bf16[8,32,3328]{2,1,0:T(8,128)(2,1)S(1)}, u32[]{:S(2)}, u32[]{:S(2)}) %all-to-all-start.2) | async-done | bytes 1703968 | tf_op jit(solution)/shard_map/all_to_all | solution.py:257
  (121 shorter events, 20.5 us)
Async XLA Ops:
  5.7 38.9 %all-to-all-start = ((bf16[8,32,4608]{2,1,0:T(8,128)(2,1)}), bf16[8,32,4608]{2,1,0:T(8,128)(2,1)S(1)}, u32[]{:S(2)}, u32[]{:S(2)}) async-start(bf16[8,32,4608]{2,1,0:T(8,128)(2,1)} %copies.2), calls=%async_computation | async-start | bytes 4718592 | tf_op jit(solution)/shard_map/all_to_all | solution.py:96
  9.5 9.7 %collective-permute-start.1 = (bf16[32,4608]{1,0:T(8,128)(2,1)S(1)}, bf16[32,4608]{1,0:T(8,128)(2,1)S(1)}, u32[]{:S(2)}, u32[]{:S(2)}) collective-permute-start(bf16[32,4608]{1,0:T(8,128)(2,1)S(1)} %copy-done.1), channel_id=1, source_target_pairs={{4,0},{30,2},{8,4},{2,6},{12,8},{6,10},{16,12},{10,14},{20,16},{14... | collective-permute-start | bytes 884744 | tf_op jit(solution)/shard_map/ppermute | solution.py:45
  10.9 11.2 %collective-permute-start.2 = (bf16[32,4608]{1,0:T(8,128)(2,1)S(1)}, bf16[32,4608]{1,0:T(8,128)(2,1)S(1)}, u32[]{:S(2)}, u32[]{:S(2)}) collective-permute-start(bf16[32,4608]{1,0:T(8,128)(2,1)S(1)} %collective-permute-done.refs_1_.refs_17_), channel_id=1, source_target_pairs={{4,0},{30,2},{8,4},{2,6},{12,8},{6,10},{16,12},{10,14},{20,16},{14... | collective-permute-start | bytes 884744 | tf_op jit(solution)/shard_map/ppermute | solution.py:45
  19.2 7.1 %collective-permute-start.5 = (bf16[32,4608]{1,0:T(8,128)(2,1)S(1)}, bf16[32,4608]{1,0:T(8,128)(2,1)S(1)}, u32[]{:S(2)}, u32[]{:S(2)}) collective-permute-start(bf16[32,4608]{1,0:T(8,128)(2,1)S(1)} %collective-permute-done.1.refs_2_.refs_18_), channel_id=1, source_target_pairs={{4,0},{30,2},{8,4},{2,6},{12,8},{6,10},{16,12},{10,14},{20,16},{14... | collective-permute-start | bytes 884744 | tf_op jit(solution)/shard_map/ppermute | solution.py:45
  22.1 9.2 %collective-permute-start.6 = (bf16[32,4608]{1,0:T(8,128)(2,1)S(1)}, bf16[32,4608]{1,0:T(8,128)(2,1)S(1)}, u32[]{:S(2)}, u32[]{:S(2)}) collective-permute-start(bf16[32,4608]{1,0:T(8,128)(2,1)S(1)} %collective-permute-done.2.refs_3_.refs_19_), channel_id=1, source_target_pairs={{4,0},{30,2},{8,4},{2,6},{12,8},{6,10},{16,12},{10,14},{20,16},{14... | collective-permute-start | bytes 884744 | tf_op jit(solution)/shard_map/ppermute | solution.py:45
  26.3 7.1 %collective-permute-start.9 = (bf16[32,4608]{1,0:T(8,128)(2,1)S(1)}, bf16[32,4608]{1,0:T(8,128)(2,1)}, u32[]{:S(2)}, u32[]{:S(2)}) collective-permute-start(bf16[32,4608]{1,0:T(8,128)(2,1)S(1)} %collective-permute-done.5.refs_6_.refs_22_), channel_id=1, source_target_pairs={{4,0},{30,2},{8,4},{2,6},{12,8},{6,10},{16,12},{10,14},{20,16},{14... | collective-permute-start | bytes 884744 | tf_op jit(solution)/shard_map/ppermute | solution.py:45
  26.3 13.0 %collective-permute-start.4 = (bf16[32,4608]{1,0:T(8,128)(2,1)S(1)}, bf16[32,4608]{1,0:T(8,128)(2,1)S(1)}, u32[]{:S(2)}, u32[]{:S(2)}) collective-permute-start(bf16[32,4608]{1,0:T(8,128)(2,1)S(1)} %collective-permute-done.1.refs_2_.refs_18_), channel_id=1, source_target_pairs={{0,2},{2,0},{1,3},{3,1},{4,6},{6,4},{5,7},{7,5},{8,10},{10,8},{9,1... | collective-permute-start | bytes 884744 | tf_op jit(solution)/shard_map/ppermute | solution.py:34
  31.2 8.1 %collective-permute-start.3 = (bf16[32,4608]{1,0:T(8,128)(2,1)S(1)}, bf16[32,4608]{1,0:T(8,128)(2,1)S(1)}, u32[]{:S(2)}, u32[]{:S(2)}) collective-permute-start(bf16[32,4608]{1,0:T(8,128)(2,1)S(1)} %collective-permute-done.2.refs_3_.refs_19_), channel_id=1, source_target_pairs={{0,2},{2,0},{1,3},{3,1},{4,6},{6,4},{5,7},{7,5},{8,10},{10,8},{9,1... | collective-permute-start | bytes 884744 | tf_op jit(solution)/shard_map/ppermute | solution.py:34
  31.2 8.6 %collective-permute-start.10 = (bf16[32,4608]{1,0:T(8,128)(2,1)S(1)}, bf16[32,4608]{1,0:T(8,128)(2,1)}, u32[]{:S(2)}, u32[]{:S(2)}) collective-permute-start(bf16[32,4608]{1,0:T(8,128)(2,1)S(1)} %collective-permute-done.6.refs_7_.refs_23_), channel_id=1, source_target_pairs={{4,0},{30,2},{8,4},{2,6},{12,8},{6,10},{16,12},{10,14},{20,16},{14... | collective-permute-start | bytes 884744 | tf_op jit(solution)/shard_map/ppermute | solution.py:45
  33.4 8.2 %collective-permute-start.14 = (bf16[32,4608]{1,0:T(8,128)(2,1)}, bf16[32,4608]{1,0:T(8,128)(2,1)S(1)}, u32[]{:S(2)}, u32[]{:S(2)}) collective-permute-start(bf16[32,4608]{1,0:T(8,128)(2,1)} %collective-permute-done.9.refs_10_.refs_26_), channel_id=1, source_target_pairs={{4,0},{30,2},{8,4},{2,6},{12,8},{6,10},{16,12},{10,14},{20,16},{14... | collective-permute-start | bytes 884744 | tf_op jit(solution)/shard_map/ppermute | solution.py:45
  33.4 10.5 %collective-permute-start.8 = (bf16[32,4608]{1,0:T(8,128)(2,1)S(1)}, bf16[32,4608]{1,0:T(8,128)(2,1)S(1)}, u32[]{:S(2)}, u32[]{:S(2)}) collective-permute-start(bf16[32,4608]{1,0:T(8,128)(2,1)S(1)} %collective-permute-done.5.refs_6_.refs_22_), channel_id=1, source_target_pairs={{0,2},{2,0},{1,3},{3,1},{4,6},{6,4},{5,7},{7,5},{8,10},{10,8},{9,1... | collective-permute-start | bytes 884744 | tf_op jit(solution)/shard_map/ppermute | solution.py:34
  39.4 11.3 %collective-permute-start.13 = (bf16[32,4608]{1,0:T(8,128)(2,1)}, bf16[32,4608]{1,0:T(8,128)(2,1)S(1)}, u32[]{:S(2)}, u32[]{:S(2)}) collective-permute-start(bf16[32,4608]{1,0:T(8,128)(2,1)} %collective-permute-done.9.refs_10_.refs_26_), channel_id=1, source_target_pairs={{0,2},{2,0},{1,3},{3,1},{4,6},{6,4},{5,7},{7,5},{8,10},{10,8},{9,1... | collective-permute-start | bytes 884744 | tf_op jit(solution)/shard_map/ppermute | solution.py:34
  39.8 10.9 %collective-permute-start.12 = (bf16[32,4608]{1,0:T(8,128)(2,1)}, bf16[32,4608]{1,0:T(8,128)(2,1)S(1)}, u32[]{:S(2)}, u32[]{:S(2)}) collective-permute-start(bf16[32,4608]{1,0:T(8,128)(2,1)} %collective-permute-done.10.refs_11_.refs_27_), channel_id=1, source_target_pairs={{0,2},{2,0},{1,3},{3,1},{4,6},{6,4},{5,7},{7,5},{8,10},{10,8},{9,1... | collective-permute-start | bytes 884744 | tf_op jit(solution)/shard_map/ppermute | solution.py:34
  41.6 9.2 %collective-permute-start.15 = (bf16[32,4608]{1,0:T(8,128)(2,1)S(1)}, bf16[32,4608]{1,0:T(8,128)(2,1)S(1)}, u32[]{:S(2)}, u32[]{:S(2)}) collective-permute-start(bf16[32,4608]{1,0:T(8,128)(2,1)S(1)} %collective-permute-done.14.refs_2_.refs_30_), channel_id=1, source_target_pairs={{0,2},{2,0},{1,3},{3,1},{4,6},{6,4},{5,7},{7,5},{8,10},{10,8},{9,1... | collective-permute-start | bytes 884744 | tf_op jit(solution)/shard_map/ppermute | solution.py:34
  48.0 8.9 %collective-permute-start.11 = (bf16[384,256]{1,0:T(8,128)(2,1)S(1)}, bf16[384,256]{1,0:T(8,128)(2,1)S(1)}, u32[]{:S(2)}, u32[]{:S(2)}) collective-permute-start(bf16[384,256]{1,0:T(8,128)(2,1)S(1)} %get-tuple-element.20), channel_id=1, source_target_pairs={{0,1},{1,0},{2,3},{3,2},{4,5},{5,4},{6,7},{7,6},{8,9},{9,8},{10,11... | collective-permute-start | bytes 589832 | tf_op jit(solution)/shard_map/ppermute | solution.py:38
  60.3 37.5 %all-to-all-start.1 = ((bf16[8,512,256]{2,1,0:T(8,128)(2,1)}), bf16[8,512,256]{2,1,0:T(8,128)(2,1)S(1)}, u32[]{:S(2)}, u32[]{:S(2)}) async-start(bf16[8,512,256]{2,1,0:T(8,128)(2,1)} %copies.3), calls=%async_computation.1 | async-start | bytes 4194304 | tf_op jit(solution)/shard_map/all_to_all | solution.py:96
  65.3 8.3 %collective-permute-start.18 = (bf16[512,256]{1,0:T(8,128)(2,1)S(1)}, bf16[512,256]{1,0:T(8,128)(2,1)S(1)}, u32[]{:S(2)}, u32[]{:S(2)}) collective-permute-start(bf16[512,256]{1,0:T(8,128)(2,1)S(1)} %bitcast.22), channel_id=1, source_target_pairs={{4,0},{30,2},{8,4},{2,6},{12,8},{6,10},{16,12},{10,14},{20,16},{14... | collective-permute-start | bytes 786440 | tf_op jit(solution)/shard_map/ppermute | solution.py:45
  65.6 10.8 %collective-permute-start.19 = (bf16[512,256]{1,0:T(8,128)(2,1)S(1)}, bf16[512,256]{1,0:T(8,128)(2,1)S(1)}, u32[]{:S(2)}, u32[]{:S(2)}) collective-permute-start(bf16[512,256]{1,0:T(8,128)(2,1)S(1)} %collective-permute-done.17.refs_1_), channel_id=1, source_target_pairs={{4,0},{30,2},{8,4},{2,6},{12,8},{6,10},{16,12},{10,14},{20,16},{14... | collective-permute-start | bytes 786440 | tf_op jit(solution)/shard_map/ppermute | solution.py:45
  76.4 8.7 %collective-permute-start.23 = (bf16[512,256]{1,0:T(8,128)(2,1)S(1)}, bf16[512,256]{1,0:T(8,128)(2,1)S(1)}, u32[]{:S(2)}, u32[]{:S(2)}) collective-permute-start(bf16[512,256]{1,0:T(8,128)(2,1)S(1)} %collective-permute-done.19.refs_3_), channel_id=1, source_target_pairs={{4,0},{30,2},{8,4},{2,6},{12,8},{6,10},{16,12},{10,14},{20,16},{14... | collective-permute-start | bytes 786440 | tf_op jit(solution)/shard_map/ppermute | solution.py:45
  80.4 12.4 %collective-permute-start.21 = (bf16[512,256]{1,0:T(8,128)(2,1)S(1)}, bf16[512,256]{1,0:T(8,128)(2,1)S(1)}, u32[]{:S(2)}, u32[]{:S(2)}) collective-permute-start(bf16[512,256]{1,0:T(8,128)(2,1)S(1)} %collective-permute-done.18.refs_2_), channel_id=1, source_target_pairs={{0,2},{2,0},{1,3},{3,1},{4,6},{6,4},{5,7},{7,5},{8,10},{10,8},{9,1... | collective-permute-start | bytes 786440 | tf_op jit(solution)/shard_map/ppermute | solution.py:34
  85.1 7.7 %collective-permute-start.20 = (bf16[512,256]{1,0:T(8,128)(2,1)S(1)}, bf16[512,256]{1,0:T(8,128)(2,1)S(1)}, u32[]{:S(2)}, u32[]{:S(2)}) collective-permute-start(bf16[512,256]{1,0:T(8,128)(2,1)S(1)} %collective-permute-done.19.refs_3_), channel_id=1, source_target_pairs={{0,2},{2,0},{1,3},{3,1},{4,6},{6,4},{5,7},{7,5},{8,10},{10,8},{9,1... | collective-permute-start | bytes 786440 | tf_op jit(solution)/shard_map/ppermute | solution.py:34
  85.1 8.1 %collective-permute-start.27 = (bf16[512,256]{1,0:T(8,128)(2,1)S(1)}, bf16[512,256]{1,0:T(8,128)(2,1)S(1)}, u32[]{:S(2)}, u32[]{:S(2)}) collective-permute-start(bf16[512,256]{1,0:T(8,128)(2,1)S(1)} %collective-permute-done.23.refs_7_), channel_id=1, source_target_pairs={{4,0},{30,2},{8,4},{2,6},{12,8},{6,10},{16,12},{10,14},{20,16},{14... | collective-permute-start | bytes 786440 | tf_op jit(solution)/shard_map/ppermute | solution.py:45
  87.1 7.7 %collective-permute-start.30 = (bf16[512,256]{1,0:T(8,128)(2,1)S(1)}, bf16[512,256]{1,0:T(8,128)(2,1)S(1)}, u32[]{:S(2)}, u32[]{:S(2)}) collective-permute-start(bf16[512,256]{1,0:T(8,128)(2,1)S(1)} %collective-permute-done.26.refs_10_), channel_id=1, source_target_pairs={{4,0},{30,2},{8,4},{2,6},{12,8},{6,10},{16,12},{10,14},{20,16},{14... | collective-permute-start | bytes 786440 | tf_op jit(solution)/shard_map/ppermute | solution.py:45
  87.1 9.5 %collective-permute-start.25 = (bf16[512,256]{1,0:T(8,128)(2,1)S(1)}, bf16[512,256]{1,0:T(8,128)(2,1)S(1)}, u32[]{:S(2)}, u32[]{:S(2)}) collective-permute-start(bf16[512,256]{1,0:T(8,128)(2,1)S(1)} %collective-permute-done.22.refs_6_), channel_id=1, source_target_pairs={{0,2},{2,0},{1,3},{3,1},{4,6},{6,4},{5,7},{7,5},{8,10},{10,8},{9,1... | collective-permute-start | bytes 786440 | tf_op jit(solution)/shard_map/ppermute | solution.py:34
  105.9 31.0 %all-to-all-start.2 = ((bf16[8,32,3328]{2,1,0:T(8,128)(2,1)}), bf16[8,32,3328]{2,1,0:T(8,128)(2,1)S(1)}, u32[]{:S(2)}, u32[]{:S(2)}) async-start(bf16[8,32,3328]{2,1,0:T(8,128)(2,1)} %get-tuple-element.28), calls=%async_computation.2 | async-start | bytes 3407872 | tf_op jit(solution)/shard_map/all_to_all | solution.py:257
  113.5 7.4 %collective-permute-start.33 = (bf16[32,1280]{1,0:T(8,128)(2,1)S(1)}, bf16[32,1280]{1,0:T(8,128)(2,1)S(1)}, u32[]{:S(2)}, u32[]{:S(2)}) collective-permute-start(bf16[32,1280]{1,0:T(8,128)(2,1)S(1)} %get-tuple-element.29), channel_id=1, source_target_pairs={{16,0},{20,4},{24,8},{28,12},{0,16},{4,20},{8,24},{12,28},{17,1},{... | collective-permute-start | bytes 245768 | tf_op jit(solution)/shard_map/ppermute | solution.py:241
  116.9 8.1 %collective-permute-start.34 = (bf16[32,1280]{1,0:T(8,128)(2,1)S(1)}, bf16[32,1280]{1,0:T(8,128)(2,1)S(1)}, u32[]{:S(2)}, u32[]{:S(2)}) collective-permute-start(bf16[32,1280]{1,0:T(8,128)(2,1)S(1)} %get-tuple-element.35), channel_id=1, source_target_pairs={{4,0},{8,4},{12,8},{16,12},{20,16},{24,20},{28,24},{0,28},{5,1},{9... | collective-permute-start | bytes 245768 | tf_op jit(solution)/shard_map/ppermute | solution.py:241
  118.1 8.2 %collective-permute-start.35 = (bf16[32,1280]{1,0:T(8,128)(2,1)S(1)}, bf16[32,1280]{1,0:T(8,128)(2,1)S(1)}, u32[]{:S(2)}, u32[]{:S(2)}) collective-permute-start(bf16[32,1280]{1,0:T(8,128)(2,1)S(1)} %get-tuple-element.34), channel_id=1, source_target_pairs={{28,0},{0,4},{4,8},{8,12},{12,16},{16,20},{20,24},{24,28},{29,1},{... | collective-permute-start | bytes 245768 | tf_op jit(solution)/shard_map/ppermute | solution.py:241
  118.4 7.9 %collective-permute-start.36 = (bf16[32,1280]{1,0:T(8,128)(2,1)S(1)}, bf16[32,1280]{1,0:T(8,128)(2,1)S(1)}, u32[]{:S(2)}, u32[]{:S(2)}) collective-permute-start(bf16[32,1280]{1,0:T(8,128)(2,1)S(1)} %get-tuple-element.33), channel_id=1, source_target_pairs={{8,0},{12,4},{16,8},{20,12},{24,16},{28,20},{0,24},{4,28},{9,1},{1... | collective-permute-start | bytes 245768 | tf_op jit(solution)/shard_map/ppermute | solution.py:241
  119.3 7.0 %collective-permute-start.37 = (bf16[32,1280]{1,0:T(8,128)(2,1)S(1)}, bf16[32,1280]{1,0:T(8,128)(2,1)S(1)}, u32[]{:S(2)}, u32[]{:S(2)}) collective-permute-start(bf16[32,1280]{1,0:T(8,128)(2,1)S(1)} %get-tuple-element.32), channel_id=1, source_target_pairs={{24,0},{28,4},{0,8},{4,12},{8,16},{12,20},{16,24},{20,28},{25,1},{... | collective-permute-start | bytes 245768 | tf_op jit(solution)/shard_map/ppermute | solution.py:241
  120.9 9.0 %collective-permute-start.38 = (bf16[32,1280]{1,0:T(8,128)(2,1)S(1)}, bf16[32,1280]{1,0:T(8,128)(2,1)S(1)}, u32[]{:S(2)}, u32[]{:S(2)}) collective-permute-start(bf16[32,1280]{1,0:T(8,128)(2,1)S(1)} %get-tuple-element.31), channel_id=1, source_target_pairs={{12,0},{16,4},{20,8},{24,12},{28,16},{0,20},{4,24},{8,28},{13,1},{... | collective-permute-start | bytes 245768 | tf_op jit(solution)/shard_map/ppermute | solution.py:241
  125.0 7.3 %collective-permute-start.39 = (bf16[32,1280]{1,0:T(8,128)(2,1)S(1)}, bf16[32,1280]{1,0:T(8,128)(2,1)}, u32[]{:S(2)}, u32[]{:S(2)}) collective-permute-start(bf16[32,1280]{1,0:T(8,128)(2,1)S(1)} %get-tuple-element.30), channel_id=1, source_target_pairs={{20,0},{24,4},{28,8},{0,12},{4,16},{8,20},{12,24},{16,28},{21,1},{... | collective-permute-start | bytes 245768 | tf_op jit(solution)/shard_map/ppermute | solution.py:241
  (39 other events, 296.3 us)

commit v7 on v6

--- a/solution.py
+++ b/solution.py
@@ -21,11 +21,12 @@
 bf16, f32 = jnp.bfloat16, jnp.float32
 ORDER = (0, 1, 7, 2, 6, 3, 5, 4)
 PARTS = 16
-COLS_Z = 1280
+COLS_Z = 1536
 LATE = 11
 EARLY = 12
 NEAR = 0
-WIDTH_Z, WIDTH = 640, 256
+WIDTH_Z, WIDTH = 512, 256
+SINGLE = {4: 6, 0: 7}
 VMEM = pl.BlockSpec(memory_space=pltpu.VMEM)
 HBM = pl.BlockSpec(memory_space=pltpu.HBM)
 
@@ -188,11 +189,16 @@
         cut = pl.ds(k * WIDTH_Z, WIDTH_Z)
         term = jnp.dot(poly, y[:, :, cut].reshape(TILE, WIDTH_Z), preferred_element_type=f32)
         part[:, :, :, cut] = term.astype(bf16).reshape(NZ, 2, ROWS, WIDTH_Z)
-    core = lax.axis_index(C)
-    outs = [
-        pltpu.make_async_copy(part.at[:, 1 - core], other_ref, sem_x.at[PARTS + 1]),
-        pltpu.make_async_copy(part.at[:, core], own_ref, sem_x.at[PARTS + 2]),
-    ]
+    core, z = lax.axis_index(C), lax.axis_index(Z)
+    outs = []
+    for e in range(5):
+        for ref, c in ((other_ref, 1 - core), (own_ref, core)):
+            at = (z + e + c * (NZ - 2 * e)) % NZ
+            if e in (0, 4):
+                block = (part.at[at, c], ref.at[SINGLE[e]])
+            else:
+                block = (part.at[at], ref.at[pl.ds(2 * e - 2, 2)])
+            outs.append(pltpu.make_async_copy(*block, sem_x.at[PARTS + 1 + len(outs)]))
     for copy in outs:
         copy.start()
     for load in loads[1:]:
@@ -226,7 +232,7 @@
             pltpu.VMEM((NZ, 2, ROWS, COLS_Z), bf16),
             pltpu.VMEM((NR, ROWS, COLS - COLS_Z), bf16),
             pltpu.SemaphoreType.DMA((PARTS,)),
-            pltpu.SemaphoreType.DMA((PARTS + 3,)),
+            pltpu.SemaphoreType.DMA((PARTS + 11,)),
             pltpu.SemaphoreType.DMA(((COLS - COLS_Z) // WIDTH,)),
         ],
         compiler_params=pltpu.CompilerParams(vmem_limit_bytes=28 << 20),
@@ -237,12 +243,15 @@
     )(*[far(p) for p in a_parts[:LATE]], *[near(p) for p in a_parts[LATE:]], *[far(p) for p in x_parts], near(b), far(cut))
 
 
-def shift_z(a, d):
-    return lax.ppermute(a, Z, [((i + d) % NZ, i) for i in range(NZ)])
+def cast(a, e):
+    pairs = []
+    for i in range(NZ):
+        pairs += [(2 * ((i - e) % NZ), 2 * i), (2 * ((i + e) % NZ) + 1, 2 * i + 1)]
+    return lax.ppermute(a, (Z, C), pairs)
 
 
 def on_device(iterate):
-    z = lax.axis_index(Z)
+    core = lax.axis_index(C)
     copies, twin = lax.optimization_barrier((copies_of(iterate), swap(iterate)))
     cols = gather_r(copies)
     pieces = ring_z(iterate, twin)
@@ -256,10 +265,14 @@
     parts, own, other = product_part(ring_z(gram, twin), pieces, every, cut)
     got = lax.all_to_all(parts, (X, YL), 0, 0, tiled=True)
     own = (own.astype(f32) + swap(other).astype(f32)).astype(bf16)
-    take = lambda d: lax.dynamic_index_in_dim(own, (z - d + NZ) % NZ, 0, keepdims=False)
-    got_z = [take(0)] + [shift_z(take(d), d) for d in (4, 1, 7, 2, 6, 3, 5)]
-    sums = [sum(p.astype(f32) for p in got_z), got.astype(f32).sum(0)]
-    total = coef_linear * iterate.astype(f32) + jnp.concatenate(sums, axis=1)
+    last = cast(own[6], 4)
+    pairs = [cast(own[2 * e - 2 : 2 * e], e) for e in (3, 2, 1)]
+    both = sum(p.astype(f32) for p in pairs)
+    here = jnp.where(core == 0, both[0], both[1])
+    there = jnp.where(core == 0, both[1], both[0]).astype(bf16)
+    sum_z = here + last.astype(f32) + own[7].astype(f32) + swap(there).astype(f32)
+    sum_r = got.astype(f32).sum(0)
+    total = coef_linear * iterate.astype(f32) + jnp.concatenate([sum_z, sum_r], axis=1)
     return (update_gain * total).astype(bf16)
 
 

time: 138 us -> 137 us (level)
  waiting for transfers between devices: 48.2 us -> 52.8 us
  starting transfers between devices: 67.6 us -> 63.7 us
  other arithmetic: 3.25 us -> 1.36 us
    ppermute x7 -> x4, waiting for transfers between devices: 6.08 us -> 11.4 us  [cast(): return lax.ppermute(a, (Z, C), pairs)]
    ppermute x7 -> x4, starting transfers between devices: 12.7 us -> 8.95 us  [cast(): return lax.ppermute(a, (Z, C), pairs)]
    all_to_all x1, waiting for transfers between devices: 3.62 us -> 1.52 us  [on_device(): got = lax.all_to_all(parts, (X, YL), 0, 0, tiled=True)]
    unnamed x56 -> x54, local copies, waits for them, and re-layouts: 3.27 us -> 2.49 us
    ppermute x17 -> x18, starting transfers between devices: 32.2 us -> 32.1 us  [swap(): return lax.ppermute(a, C, [(0, 1), (1, 0)])]
  transfers between devices with their start and end apart: 43 -> 41, of which waited for: 16 -> 17; matrix products, arithmetic and copies ran while one was open for 2% -> 0% of each run, Pallas kernels for 5% -> 6%
where the time goes in v7:
time: 137 us; the launch traced here: 136 us
  starting transfers between devices  63.7 us (46%)
  waiting for transfers between devices  52.8 us (39%)
  Pallas kernels  15.4 us (11%)
  local copies, waits for them, and re-layouts  2.53 us (2%)
    ppermute x14, waiting for transfers between devices, turn(): return lax.ppermute(a, (Z, C), pairs)  33.9 us
    ppermute x18, starting transfers between devices, swap(): return lax.ppermute(a, C, [(0, 1), (1, 0)])  32.1 us
    ppermute x4, waiting for transfers between devices, cast(): return lax.ppermute(a, (Z, C), pairs)  11.4 us
    ppermute x4, starting transfers between devices, cast(): return lax.ppermute(a, (Z, C), pairs)  8.95 us
    all_to_all x2, starting transfers between devices, gather_r(): return lax.all_to_all(copies, (X, YL), 0, 0, tiled=True)  8.74 us
    pallas_call x1, Pallas kernels, product_part(): pl.pallas_call(product_kernel, out_shape=(pltpu.HBM((NR, ROWS, COLS - COL...  7.72 us
    all_to_all x1, starting transfers between devices, on_device(): got = lax.all_to_all(parts, (X, YL), 0, 0, tiled=True)  5.4 us
    ppermute x14, starting transfers between devices, turn(): return lax.ppermute(a, (Z, C), pairs)  5.21 us
  transfers between devices with their start and end apart: 41, of which 17 were waited for; matrix products, arithmetic and copies ran while one was open for 0% of the time, Pallas kernels for 6%

profile of v7, /device:TPU:1, one launch (start us, length us, event | category | flops | bytes accessed | tf_op | source)
XLA Modules:
  0.0 136.2 jit_solution(17893481184648742467)
XLA Ops:
  0.0 3.2 %collective-permute-start = (bf16[32,4608]{1,0:T(8,128)(2,1)}, bf16[32,4608]{1,0:T(8,128)(2,1)S(1)}, u32[]{:S(2)}, u32[]{:S(2)}) collective-permute-start(bf16[32,4608]{1,0:T(8,128)(2,1)} %refs_16_.1), channel_id=1, source_target_pairs={{0,2},{2,0},{1,3},{3,1},{4,6},{6,4},{5,7},{7,5},{8,10},{10,8},{9,1... | collective-permute-start | bytes 884744 | tf_op jit(solution)/shard_map/ppermute | solution.py:35
  5.8 3.8 %all-to-all-start = ((bf16[8,32,4608]{2,1,0:T(8,128)(2,1)}), bf16[8,32,4608]{2,1,0:T(8,128)(2,1)S(1)}, u32[]{:S(2)}, u32[]{:S(2)}) async-start(bf16[8,32,4608]{2,1,0:T(8,128)(2,1)} %copies.2), calls=%async_computation | async-start | bytes 4718592 | tf_op jit(solution)/shard_map/all_to_all | solution.py:97
  10.9 1.6 %collective-permute-start.2 = (bf16[32,4608]{1,0:T(8,128)(2,1)S(1)}, bf16[32,4608]{1,0:T(8,128)(2,1)S(1)}, u32[]{:S(2)}, u32[]{:S(2)}) collective-permute-start(bf16[32,4608]{1,0:T(8,128)(2,1)S(1)} %collective-permute-done.refs_1_.refs_17_), channel_id=1, source_target_pairs={{4,0},{30,2},{8,4},{2,6},{12,8},{6,10},{16,12},{10,14},{20,16},{14... | collective-permute-start | bytes 884744 | tf_op jit(solution)/shard_map/ppermute | solution.py:46
  12.6 6.7 %collective-permute-done.1.refs_2_.refs_18_ = bf16[32,4608]{1,0:T(8,128)(2,1)S(1)} collective-permute-done((bf16[32,4608]{1,0:T(8,128)(2,1)S(1)}, bf16[32,4608]{1,0:T(8,128)(2,1)S(1)}, u32[]{:S(2)}, u32[]{:S(2)}) %collective-permute-start.1) | collective-permute-done | bytes 294944 | tf_op jit(solution)/shard_map/ppermute | solution.py:46
  19.3 2.9 %collective-permute-done.2.refs_3_.refs_19_ = bf16[32,4608]{1,0:T(8,128)(2,1)S(1)} collective-permute-done((bf16[32,4608]{1,0:T(8,128)(2,1)S(1)}, bf16[32,4608]{1,0:T(8,128)(2,1)S(1)}, u32[]{:S(2)}, u32[]{:S(2)}) %collective-permute-start.2) | collective-permute-done | bytes 294944 | tf_op jit(solution)/shard_map/ppermute | solution.py:46
  22.1 4.2 %collective-permute-done.5.refs_6_.refs_22_ = bf16[32,4608]{1,0:T(8,128)(2,1)S(1)} collective-permute-done((bf16[32,4608]{1,0:T(8,128)(2,1)S(1)}, bf16[32,4608]{1,0:T(8,128)(2,1)S(1)}, u32[]{:S(2)}, u32[]{:S(2)}) %collective-permute-start.5) | collective-permute-done | bytes 294944 | tf_op jit(solution)/shard_map/ppermute | solution.py:46
  26.3 4.9 %collective-permute-start.4 = (bf16[32,4608]{1,0:T(8,128)(2,1)S(1)}, bf16[32,4608]{1,0:T(8,128)(2,1)S(1)}, u32[]{:S(2)}, u32[]{:S(2)}) collective-permute-start(bf16[32,4608]{1,0:T(8,128)(2,1)S(1)} %collective-permute-done.1.refs_2_.refs_18_), channel_id=1, source_target_pairs={{0,2},{2,0},{1,3},{3,1},{4,6},{6,4},{5,7},{7,5},{8,10},{10,8},{9,1... | collective-permute-start | bytes 884744 | tf_op jit(solution)/shard_map/ppermute | solution.py:35
  31.4 2.0 %collective-permute-done.9.refs_10_.refs_26_ = bf16[32,4608]{1,0:T(8,128)(2,1)} collective-permute-done((bf16[32,4608]{1,0:T(8,128)(2,1)S(1)}, bf16[32,4608]{1,0:T(8,128)(2,1)}, u32[]{:S(2)}, u32[]{:S(2)}) %collective-permute-start.9) | collective-permute-done | bytes 294944 | tf_op jit(solution)/shard_map/ppermute | solution.py:46
  33.4 5.9 %collective-permute-start.8 = (bf16[32,4608]{1,0:T(8,128)(2,1)S(1)}, bf16[32,4608]{1,0:T(8,128)(2,1)S(1)}, u32[]{:S(2)}, u32[]{:S(2)}) collective-permute-start(bf16[32,4608]{1,0:T(8,128)(2,1)S(1)} %collective-permute-done.5.refs_6_.refs_22_), channel_id=1, source_target_pairs={{0,2},{2,0},{1,3},{3,1},{4,6},{6,4},{5,7},{7,5},{8,10},{10,8},{9,1... | collective-permute-start | bytes 884744 | tf_op jit(solution)/shard_map/ppermute | solution.py:35
  40.0 1.7 %collective-permute-done.14.refs_2_.refs_30_ = bf16[32,4608]{1,0:T(8,128)(2,1)S(1)} collective-permute-done((bf16[32,4608]{1,0:T(8,128)(2,1)}, bf16[32,4608]{1,0:T(8,128)(2,1)S(1)}, u32[]{:S(2)}, u32[]{:S(2)}) %collective-permute-start.14) | collective-permute-done | bytes 294944 | tf_op jit(solution)/shard_map/ppermute | solution.py:46
  41.6 2.3 %collective-permute-start.15 = (bf16[32,4608]{1,0:T(8,128)(2,1)S(1)}, bf16[32,4608]{1,0:T(8,128)(2,1)S(1)}, u32[]{:S(2)}, u32[]{:S(2)}) collective-permute-start(bf16[32,4608]{1,0:T(8,128)(2,1)S(1)} %collective-permute-done.14.refs_2_.refs_30_), channel_id=1, source_target_pairs={{0,2},{2,0},{1,3},{3,1},{4,6},{6,4},{5,7},{7,5},{8,10},{10,8},{9,1... | collective-permute-start | bytes 884744 | tf_op jit(solution)/shard_map/ppermute | solution.py:35
  44.7 3.5 %gram_part.2 = (f32[384,256]{1,0:T(8,128)S(1)}, bf16[384,256]{1,0:T(8,128)(2,1)S(1)}, bf16[8,32,1536]{2,1,0:T(8,128)(2,1)}) custom-call(bf16[32,4608]{1,0:T(8,128)(2,1)} %refs_16_.1, bf16[32,4608]{1,0:T(8,128)(2,1)} %copy-done.8, bf16[32,4608]{1,0:T(8,128)(2,1)} %copy-done.9, bf16[32,4608]{1,0:T(8,128)(2,1)} %copy-done.10, bf16[32,4608]{1,0:T(8,128)(2,1)} %copy-done.14, ...), custom_call_target="tpu_custom_call" | custom-call | flops 905969664 | bytes 6291456 | tf_op jit(solution)/shard_map/gram_part/pallas_call | solution.py:148
  48.1 2.7 %collective-permute-start.11 = (bf16[384,256]{1,0:T(8,128)(2,1)S(1)}, bf16[384,256]{1,0:T(8,128)(2,1)S(1)}, u32[]{:S(2)}, u32[]{:S(2)}) collective-permute-start(bf16[384,256]{1,0:T(8,128)(2,1)S(1)} %get-tuple-element.20), channel_id=1, source_target_pairs={{0,1},{1,0},{2,3},{3,2},{4,5},{5,4},{6,7},{7,6},{8,9},{9,8},{10,11... | collective-permute-start | bytes 589832 | tf_op jit(solution)/shard_map/ppermute | solution.py:39
  52.7 4.3 %collective-permute-done.16.got_b = bf16[128,256]{1,0:T(8,128)(2,1)S(1)} collective-permute-done((bf16[128,256]{1,0:T(8,128)(2,1)S(1)}, bf16[128,256]{1,0:T(8,128)(2,1)S(1)}, u32[]{:S(2)}, u32[]{:S(2)}) %collective-permute-start.16) | collective-permute-done | bytes 65568 | tf_op jit(solution)/shard_map/ppermute | solution.py:39
  57.1 1.9 %collective-permute-start.17 = (bf16[512,256]{1,0:T(8,128)(2,1)S(1)}, bf16[512,256]{1,0:T(8,128)(2,1)S(1)}, u32[]{:S(2)}, u32[]{:S(2)}) collective-permute-start(bf16[512,256]{1,0:T(8,128)(2,1)S(1)} %bitcast.16), channel_id=1, source_target_pairs={{0,2},{2,0},{1,3},{3,1},{4,6},{6,4},{5,7},{7,5},{8,10},{10,8},{9,1... | collective-permute-start | bytes 786440 | tf_op jit(solution)/shard_map/ppermute | solution.py:35
  60.5 5.0 %all-to-all-start.1 = ((bf16[8,512,256]{2,1,0:T(8,128)(2,1)}), bf16[8,512,256]{2,1,0:T(8,128)(2,1)S(1)}, u32[]{:S(2)}, u32[]{:S(2)}) async-start(bf16[8,512,256]{2,1,0:T(8,128)(2,1)} %copies.3), calls=%async_computation.1 | async-start | bytes 4194304 | tf_op jit(solution)/shard_map/all_to_all | solution.py:97
  65.8 1.6 %collective-permute-start.19 = (bf16[512,256]{1,0:T(8,128)(2,1)S(1)}, bf16[512,256]{1,0:T(8,128)(2,1)S(1)}, u32[]{:S(2)}, u32[]{:S(2)}) collective-permute-start(bf16[512,256]{1,0:T(8,128)(2,1)S(1)} %collective-permute-done.17.refs_1_), channel_id=1, source_target_pairs={{4,0},{30,2},{8,4},{2,6},{12,8},{6,10},{16,12},{10,14},{20,16},{14... | collective-permute-start | bytes 786440 | tf_op jit(solution)/shard_map/ppermute | solution.py:46
  67.4 6.3 %collective-permute-done.18.refs_2_ = bf16[512,256]{1,0:T(8,128)(2,1)S(1)} collective-permute-done((bf16[512,256]{1,0:T(8,128)(2,1)S(1)}, bf16[512,256]{1,0:T(8,128)(2,1)S(1)}, u32[]{:S(2)}, u32[]{:S(2)}) %collective-permute-start.18) | collective-permute-done | bytes 262176 | tf_op jit(solution)/shard_map/ppermute | solution.py:46
  73.8 2.8 %collective-permute-done.19.refs_3_ = bf16[512,256]{1,0:T(8,128)(2,1)S(1)} collective-permute-done((bf16[512,256]{1,0:T(8,128)(2,1)S(1)}, bf16[512,256]{1,0:T(8,128)(2,1)S(1)}, u32[]{:S(2)}, u32[]{:S(2)}) %collective-permute-start.19) | collective-permute-done | bytes 262176 | tf_op jit(solution)/shard_map/ppermute | solution.py:46
  76.6 3.9 %collective-permute-done.22.refs_6_ = bf16[512,256]{1,0:T(8,128)(2,1)S(1)} collective-permute-done((bf16[512,256]{1,0:T(8,128)(2,1)S(1)}, bf16[512,256]{1,0:T(8,128)(2,1)S(1)}, u32[]{:S(2)}, u32[]{:S(2)}) %collective-permute-start.22) | collective-permute-done | bytes 262176 | tf_op jit(solution)/shard_map/ppermute | solution.py:46
  80.5 4.7 %collective-permute-start.21 = (bf16[512,256]{1,0:T(8,128)(2,1)S(1)}, bf16[512,256]{1,0:T(8,128)(2,1)S(1)}, u32[]{:S(2)}, u32[]{:S(2)}) collective-permute-start(bf16[512,256]{1,0:T(8,128)(2,1)S(1)} %collective-permute-done.18.refs_2_), channel_id=1, source_target_pairs={{0,2},{2,0},{1,3},{3,1},{4,6},{6,4},{5,7},{7,5},{8,10},{10,8},{9,1... | collective-permute-start | bytes 786440 | tf_op jit(solution)/shard_map/ppermute | solution.py:35
  85.3 1.9 %collective-permute-done.26.refs_10_ = bf16[512,256]{1,0:T(8,128)(2,1)S(1)} collective-permute-done((bf16[512,256]{1,0:T(8,128)(2,1)S(1)}, bf16[512,256]{1,0:T(8,128)(2,1)S(1)}, u32[]{:S(2)}, u32[]{:S(2)}) %collective-permute-start.26) | collective-permute-done | bytes 262176 | tf_op jit(solution)/shard_map/ppermute | solution.py:46
  87.3 5.6 %collective-permute-start.25 = (bf16[512,256]{1,0:T(8,128)(2,1)S(1)}, bf16[512,256]{1,0:T(8,128)(2,1)S(1)}, u32[]{:S(2)}, u32[]{:S(2)}) collective-permute-start(bf16[512,256]{1,0:T(8,128)(2,1)S(1)} %collective-permute-done.22.refs_6_), channel_id=1, source_target_pairs={{0,2},{2,0},{1,3},{3,1},{4,6},{6,4},{5,7},{7,5},{8,10},{10,8},{9,1... | collective-permute-start | bytes 786440 | tf_op jit(solution)/shard_map/ppermute | solution.py:35
  94.9 1.9 %collective-permute-start.31 = (bf16[512,256]{1,0:T(8,128)(2,1)S(1)}, bf16[512,256]{1,0:T(8,128)(2,1)S(1)}, u32[]{:S(2)}, u32[]{:S(2)}) collective-permute-start(bf16[512,256]{1,0:T(8,128)(2,1)S(1)} %collective-permute-done.30.refs_14_), channel_id=1, source_target_pairs={{0,2},{2,0},{1,3},{3,1},{4,6},{6,4},{5,7},{7,5},{8,10},{10,8},{9,1... | collective-permute-start | bytes 786440 | tf_op jit(solution)/shard_map/ppermute | solution.py:35
  97.9 7.7 %product_part.1 = (bf16[8,32,3072]{2,1,0:T(8,128)(2,1)}, bf16[8,32,1536]{2,1,0:T(8,128)(2,1)}, bf16[8,32,1536]{2,1,0:T(8,128)(2,1)}) custom-call(bf16[512,256]{1,0:T(8,128)(2,1)} %bitcast.19, bf16[512,256]{1,0:T(8,128)(2,1)} %copy-done.17, bf16[512,256]{1,0:T(8,128)(2,1)} %copy-done.18, bf16[512,256]{1,0:T(8,128)(2,1)} %copy-done.19, ...), custom_call_target="tpu_custom_call" | custom-call | flops 2281701376 | bytes 14680064 | tf_op jit(solution)/shard_map/product_part/pallas_call | solution.py:219
  106.1 5.4 %all-to-all-start.2 = ((bf16[8,32,3072]{2,1,0:T(8,128)(2,1)}), bf16[8,32,3072]{2,1,0:T(8,128)(2,1)S(1)}, u32[]{:S(2)}, u32[]{:S(2)}) async-start(bf16[8,32,3072]{2,1,0:T(8,128)(2,1)} %get-tuple-element.28), calls=%async_computation.2 | async-start | bytes 3145728 | tf_op jit(solution)/shard_map/all_to_all | solution.py:266
  111.7 3.0 %collective-permute-start.33 = (bf16[2,32,1536]{2,1,0:T(8,128)(2,1)S(1)}, bf16[2,32,1536]{2,1,0:T(8,128)(2,1)S(1)}, u32[]{:S(2)}, u32[]{:S(2)}) collective-permute-start(bf16[2,32,1536]{2,1,0:T(8,128)(2,1)S(1)} %get-tuple-element.29), channel_id=1, source_target_pairs={{20,0},{14,2},{24,4},{18,6},{28,8},{22,10},{0,12},{26,14},{4,16},{... | collective-permute-start | bytes 589832 | tf_op jit(solution)/shard_map/ppermute | solution.py:250
  114.7 1.6 %collective-permute-start.34 = (bf16[2,32,1536]{2,1,0:T(8,128)(2,1)S(1)}, bf16[2,32,1536]{2,1,0:T(8,128)(2,1)S(1)}, u32[]{:S(2)}, u32[]{:S(2)}) collective-permute-start(bf16[2,32,1536]{2,1,0:T(8,128)(2,1)S(1)} %get-tuple-element.31), channel_id=1, source_target_pairs={{24,0},{10,2},{28,4},{14,6},{0,8},{18,10},{4,12},{22,14},{8,16},{2... | collective-permute-start | bytes 589832 | tf_op jit(solution)/shard_map/ppermute | solution.py:250
  116.4 4.3 %collective-permute-start.36 = (bf16[32,1536]{1,0:T(8,128)(2,1)S(1)}, bf16[32,1536]{1,0:T(8,128)(2,1)S(1)}, u32[]{:S(2)}, u32[]{:S(2)}) collective-permute-start(bf16[32,1536]{1,0:T(8,128)(2,1)S(1)} %slice_bitcast_fusion.1), channel_id=1, source_target_pairs={{16,0},{18,2},{20,4},{22,6},{24,8},{26,10},{28,12},{30,14},{0,16},... | collective-permute-start | bytes 294920 | tf_op jit(solution)/shard_map/ppermute | solution.py:250
  120.7 2.0 %collective-permute-done.33 = bf16[2,32,1536]{2,1,0:T(8,128)(2,1)S(1)} collective-permute-done((bf16[2,32,1536]{2,1,0:T(8,128)(2,1)S(1)}, bf16[2,32,1536]{2,1,0:T(8,128)(2,1)S(1)}, u32[]{:S(2)}, u32[]{:S(2)}) %collective-permute-start.33) | collective-permute-done | bytes 196640 | tf_op jit(solution)/shard_map/ppermute | solution.py:250
  122.7 7.5 %collective-permute-done.34 = bf16[2,32,1536]{2,1,0:T(8,128)(2,1)S(1)} collective-permute-done((bf16[2,32,1536]{2,1,0:T(8,128)(2,1)S(1)}, bf16[2,32,1536]{2,1,0:T(8,128)(2,1)S(1)}, u32[]{:S(2)}, u32[]{:S(2)}) %collective-permute-start.34) | collective-permute-done | bytes 196640 | tf_op jit(solution)/shard_map/ppermute | solution.py:250
  130.2 1.9 %collective-permute-done.35 = bf16[2,32,1536]{2,1,0:T(8,128)(2,1)S(1)} collective-permute-done((bf16[2,32,1536]{2,1,0:T(8,128)(2,1)S(1)}, bf16[2,32,1536]{2,1,0:T(8,128)(2,1)S(1)}, u32[]{:S(2)}, u32[]{:S(2)}) %collective-permute-start.35) | collective-permute-done | bytes 196640 | tf_op jit(solution)/shard_map/ppermute | solution.py:250
  (118 shorter events, 17.0 us)
Async XLA Ops:
  5.8 38.9 %all-to-all-start = ((bf16[8,32,4608]{2,1,0:T(8,128)(2,1)}), bf16[8,32,4608]{2,1,0:T(8,128)(2,1)S(1)}, u32[]{:S(2)}, u32[]{:S(2)}) async-start(bf16[8,32,4608]{2,1,0:T(8,128)(2,1)} %copies.2), calls=%async_computation | async-start | bytes 4718592 | tf_op jit(solution)/shard_map/all_to_all | solution.py:97
  9.5 9.7 %collective-permute-start.1 = (bf16[32,4608]{1,0:T(8,128)(2,1)S(1)}, bf16[32,4608]{1,0:T(8,128)(2,1)S(1)}, u32[]{:S(2)}, u32[]{:S(2)}) collective-permute-start(bf16[32,4608]{1,0:T(8,128)(2,1)S(1)} %copy-done.1), channel_id=1, source_target_pairs={{4,0},{30,2},{8,4},{2,6},{12,8},{6,10},{16,12},{10,14},{20,16},{14... | collective-permute-start | bytes 884744 | tf_op jit(solution)/shard_map/ppermute | solution.py:46
  10.9 11.2 %collective-permute-start.2 = (bf16[32,4608]{1,0:T(8,128)(2,1)S(1)}, bf16[32,4608]{1,0:T(8,128)(2,1)S(1)}, u32[]{:S(2)}, u32[]{:S(2)}) collective-permute-start(bf16[32,4608]{1,0:T(8,128)(2,1)S(1)} %collective-permute-done.refs_1_.refs_17_), channel_id=1, source_target_pairs={{4,0},{30,2},{8,4},{2,6},{12,8},{6,10},{16,12},{10,14},{20,16},{14... | collective-permute-start | bytes 884744 | tf_op jit(solution)/shard_map/ppermute | solution.py:46
  19.3 7.1 %collective-permute-start.5 = (bf16[32,4608]{1,0:T(8,128)(2,1)S(1)}, bf16[32,4608]{1,0:T(8,128)(2,1)S(1)}, u32[]{:S(2)}, u32[]{:S(2)}) collective-permute-start(bf16[32,4608]{1,0:T(8,128)(2,1)S(1)} %collective-permute-done.1.refs_2_.refs_18_), channel_id=1, source_target_pairs={{4,0},{30,2},{8,4},{2,6},{12,8},{6,10},{16,12},{10,14},{20,16},{14... | collective-permute-start | bytes 884744 | tf_op jit(solution)/shard_map/ppermute | solution.py:46
  22.1 9.2 %collective-permute-start.6 = (bf16[32,4608]{1,0:T(8,128)(2,1)S(1)}, bf16[32,4608]{1,0:T(8,128)(2,1)S(1)}, u32[]{:S(2)}, u32[]{:S(2)}) collective-permute-start(bf16[32,4608]{1,0:T(8,128)(2,1)S(1)} %collective-permute-done.2.refs_3_.refs_19_), channel_id=1, source_target_pairs={{4,0},{30,2},{8,4},{2,6},{12,8},{6,10},{16,12},{10,14},{20,16},{14... | collective-permute-start | bytes 884744 | tf_op jit(solution)/shard_map/ppermute | solution.py:46
  26.3 7.1 %collective-permute-start.9 = (bf16[32,4608]{1,0:T(8,128)(2,1)S(1)}, bf16[32,4608]{1,0:T(8,128)(2,1)}, u32[]{:S(2)}, u32[]{:S(2)}) collective-permute-start(bf16[32,4608]{1,0:T(8,128)(2,1)S(1)} %collective-permute-done.5.refs_6_.refs_22_), channel_id=1, source_target_pairs={{4,0},{30,2},{8,4},{2,6},{12,8},{6,10},{16,12},{10,14},{20,16},{14... | collective-permute-start | bytes 884744 | tf_op jit(solution)/shard_map/ppermute | solution.py:46
  26.3 13.0 %collective-permute-start.4 = (bf16[32,4608]{1,0:T(8,128)(2,1)S(1)}, bf16[32,4608]{1,0:T(8,128)(2,1)S(1)}, u32[]{:S(2)}, u32[]{:S(2)}) collective-permute-start(bf16[32,4608]{1,0:T(8,128)(2,1)S(1)} %collective-permute-done.1.refs_2_.refs_18_), channel_id=1, source_target_pairs={{0,2},{2,0},{1,3},{3,1},{4,6},{6,4},{5,7},{7,5},{8,10},{10,8},{9,1... | collective-permute-start | bytes 884744 | tf_op jit(solution)/shard_map/ppermute | solution.py:35
  31.3 8.1 %collective-permute-start.3 = (bf16[32,4608]{1,0:T(8,128)(2,1)S(1)}, bf16[32,4608]{1,0:T(8,128)(2,1)S(1)}, u32[]{:S(2)}, u32[]{:S(2)}) collective-permute-start(bf16[32,4608]{1,0:T(8,128)(2,1)S(1)} %collective-permute-done.2.refs_3_.refs_19_), channel_id=1, source_target_pairs={{0,2},{2,0},{1,3},{3,1},{4,6},{6,4},{5,7},{7,5},{8,10},{10,8},{9,1... | collective-permute-start | bytes 884744 | tf_op jit(solution)/shard_map/ppermute | solution.py:35
  31.3 8.6 %collective-permute-start.10 = (bf16[32,4608]{1,0:T(8,128)(2,1)S(1)}, bf16[32,4608]{1,0:T(8,128)(2,1)}, u32[]{:S(2)}, u32[]{:S(2)}) collective-permute-start(bf16[32,4608]{1,0:T(8,128)(2,1)S(1)} %collective-permute-done.6.refs_7_.refs_23_), channel_id=1, source_target_pairs={{4,0},{30,2},{8,4},{2,6},{12,8},{6,10},{16,12},{10,14},{20,16},{14... | collective-permute-start | bytes 884744 | tf_op jit(solution)/shard_map/ppermute | solution.py:46
  33.4 8.2 %collective-permute-start.14 = (bf16[32,4608]{1,0:T(8,128)(2,1)}, bf16[32,4608]{1,0:T(8,128)(2,1)S(1)}, u32[]{:S(2)}, u32[]{:S(2)}) collective-permute-start(bf16[32,4608]{1,0:T(8,128)(2,1)} %collective-permute-done.9.refs_10_.refs_26_), channel_id=1, source_target_pairs={{4,0},{30,2},{8,4},{2,6},{12,8},{6,10},{16,12},{10,14},{20,16},{14... | collective-permute-start | bytes 884744 | tf_op jit(solution)/shard_map/ppermute | solution.py:46
  33.4 10.5 %collective-permute-start.8 = (bf16[32,4608]{1,0:T(8,128)(2,1)S(1)}, bf16[32,4608]{1,0:T(8,128)(2,1)S(1)}, u32[]{:S(2)}, u32[]{:S(2)}) collective-permute-start(bf16[32,4608]{1,0:T(8,128)(2,1)S(1)} %collective-permute-done.5.refs_6_.refs_22_), channel_id=1, source_target_pairs={{0,2},{2,0},{1,3},{3,1},{4,6},{6,4},{5,7},{7,5},{8,10},{10,8},{9,1... | collective-permute-start | bytes 884744 | tf_op jit(solution)/shard_map/ppermute | solution.py:35
  39.4 11.4 %collective-permute-start.13 = (bf16[32,4608]{1,0:T(8,128)(2,1)}, bf16[32,4608]{1,0:T(8,128)(2,1)S(1)}, u32[]{:S(2)}, u32[]{:S(2)}) collective-permute-start(bf16[32,4608]{1,0:T(8,128)(2,1)} %collective-permute-done.9.refs_10_.refs_26_), channel_id=1, source_target_pairs={{0,2},{2,0},{1,3},{3,1},{4,6},{6,4},{5,7},{7,5},{8,10},{10,8},{9,1... | collective-permute-start | bytes 884744 | tf_op jit(solution)/shard_map/ppermute | solution.py:35
  39.9 11.0 %collective-permute-start.12 = (bf16[32,4608]{1,0:T(8,128)(2,1)}, bf16[32,4608]{1,0:T(8,128)(2,1)S(1)}, u32[]{:S(2)}, u32[]{:S(2)}) collective-permute-start(bf16[32,4608]{1,0:T(8,128)(2,1)} %collective-permute-done.10.refs_11_.refs_27_), channel_id=1, source_target_pairs={{0,2},{2,0},{1,3},{3,1},{4,6},{6,4},{5,7},{7,5},{8,10},{10,8},{9,1... | collective-permute-start | bytes 884744 | tf_op jit(solution)/shard_map/ppermute | solution.py:35
  41.6 9.2 %collective-permute-start.15 = (bf16[32,4608]{1,0:T(8,128)(2,1)S(1)}, bf16[32,4608]{1,0:T(8,128)(2,1)S(1)}, u32[]{:S(2)}, u32[]{:S(2)}) collective-permute-start(bf16[32,4608]{1,0:T(8,128)(2,1)S(1)} %collective-permute-done.14.refs_2_.refs_30_), channel_id=1, source_target_pairs={{0,2},{2,0},{1,3},{3,1},{4,6},{6,4},{5,7},{7,5},{8,10},{10,8},{9,1... | collective-permute-start | bytes 884744 | tf_op jit(solution)/shard_map/ppermute | solution.py:35
  48.1 8.9 %collective-permute-start.11 = (bf16[384,256]{1,0:T(8,128)(2,1)S(1)}, bf16[384,256]{1,0:T(8,128)(2,1)S(1)}, u32[]{:S(2)}, u32[]{:S(2)}) collective-permute-start(bf16[384,256]{1,0:T(8,128)(2,1)S(1)} %get-tuple-element.20), channel_id=1, source_target_pairs={{0,1},{1,0},{2,3},{3,2},{4,5},{5,4},{6,7},{7,6},{8,9},{9,8},{10,11... | collective-permute-start | bytes 589832 | tf_op jit(solution)/shard_map/ppermute | solution.py:39
  60.5 37.4 %all-to-all-start.1 = ((bf16[8,512,256]{2,1,0:T(8,128)(2,1)}), bf16[8,512,256]{2,1,0:T(8,128)(2,1)S(1)}, u32[]{:S(2)}, u32[]{:S(2)}) async-start(bf16[8,512,256]{2,1,0:T(8,128)(2,1)} %copies.3), calls=%async_computation.1 | async-start | bytes 4194304 | tf_op jit(solution)/shard_map/all_to_all | solution.py:97
  65.4 8.3 %collective-permute-start.18 = (bf16[512,256]{1,0:T(8,128)(2,1)S(1)}, bf16[512,256]{1,0:T(8,128)(2,1)S(1)}, u32[]{:S(2)}, u32[]{:S(2)}) collective-permute-start(bf16[512,256]{1,0:T(8,128)(2,1)S(1)} %bitcast.18), channel_id=1, source_target_pairs={{4,0},{30,2},{8,4},{2,6},{12,8},{6,10},{16,12},{10,14},{20,16},{14... | collective-permute-start | bytes 786440 | tf_op jit(solution)/shard_map/ppermute | solution.py:46
  65.8 10.8 %collective-permute-start.19 = (bf16[512,256]{1,0:T(8,128)(2,1)S(1)}, bf16[512,256]{1,0:T(8,128)(2,1)S(1)}, u32[]{:S(2)}, u32[]{:S(2)}) collective-permute-start(bf16[512,256]{1,0:T(8,128)(2,1)S(1)} %collective-permute-done.17.refs_1_), channel_id=1, source_target_pairs={{4,0},{30,2},{8,4},{2,6},{12,8},{6,10},{16,12},{10,14},{20,16},{14... | collective-permute-start | bytes 786440 | tf_op jit(solution)/shard_map/ppermute | solution.py:46
  73.8 6.7 %collective-permute-start.22 = (bf16[512,256]{1,0:T(8,128)(2,1)S(1)}, bf16[512,256]{1,0:T(8,128)(2,1)S(1)}, u32[]{:S(2)}, u32[]{:S(2)}) collective-permute-start(bf16[512,256]{1,0:T(8,128)(2,1)S(1)} %collective-permute-done.18.refs_2_), channel_id=1, source_target_pairs={{4,0},{30,2},{8,4},{2,6},{12,8},{6,10},{16,12},{10,14},{20,16},{14... | collective-permute-start | bytes 786440 | tf_op jit(solution)/shard_map/ppermute | solution.py:46
  76.6 8.6 %collective-permute-start.23 = (bf16[512,256]{1,0:T(8,128)(2,1)S(1)}, bf16[512,256]{1,0:T(8,128)(2,1)S(1)}, u32[]{:S(2)}, u32[]{:S(2)}) collective-permute-start(bf16[512,256]{1,0:T(8,128)(2,1)S(1)} %collective-permute-done.19.refs_3_), channel_id=1, source_target_pairs={{4,0},{30,2},{8,4},{2,6},{12,8},{6,10},{16,12},{10,14},{20,16},{14... | collective-permute-start | bytes 786440 | tf_op jit(solution)/shard_map/ppermute | solution.py:46
  80.5 6.7 %collective-permute-start.26 = (bf16[512,256]{1,0:T(8,128)(2,1)S(1)}, bf16[512,256]{1,0:T(8,128)(2,1)S(1)}, u32[]{:S(2)}, u32[]{:S(2)}) collective-permute-start(bf16[512,256]{1,0:T(8,128)(2,1)S(1)} %collective-permute-done.22.refs_6_), channel_id=1, source_target_pairs={{4,0},{30,2},{8,4},{2,6},{12,8},{6,10},{16,12},{10,14},{20,16},{14... | collective-permute-start | bytes 786440 | tf_op jit(solution)/shard_map/ppermute | solution.py:46
  80.5 12.3 %collective-permute-start.21 = (bf16[512,256]{1,0:T(8,128)(2,1)S(1)}, bf16[512,256]{1,0:T(8,128)(2,1)S(1)}, u32[]{:S(2)}, u32[]{:S(2)}) collective-permute-start(bf16[512,256]{1,0:T(8,128)(2,1)S(1)} %collective-permute-done.18.refs_2_), channel_id=1, source_target_pairs={{0,2},{2,0},{1,3},{3,1},{4,6},{6,4},{5,7},{7,5},{8,10},{10,8},{9,1... | collective-permute-start | bytes 786440 | tf_op jit(solution)/shard_map/ppermute | solution.py:35
  85.2 7.7 %collective-permute-start.20 = (bf16[512,256]{1,0:T(8,128)(2,1)S(1)}, bf16[512,256]{1,0:T(8,128)(2,1)S(1)}, u32[]{:S(2)}, u32[]{:S(2)}) collective-permute-start(bf16[512,256]{1,0:T(8,128)(2,1)S(1)} %collective-permute-done.19.refs_3_), channel_id=1, source_target_pairs={{0,2},{2,0},{1,3},{3,1},{4,6},{6,4},{5,7},{7,5},{8,10},{10,8},{9,1... | collective-permute-start | bytes 786440 | tf_op jit(solution)/shard_map/ppermute | solution.py:35
  85.2 8.1 %collective-permute-start.27 = (bf16[512,256]{1,0:T(8,128)(2,1)S(1)}, bf16[512,256]{1,0:T(8,128)(2,1)S(1)}, u32[]{:S(2)}, u32[]{:S(2)}) collective-permute-start(bf16[512,256]{1,0:T(8,128)(2,1)S(1)} %collective-permute-done.23.refs_7_), channel_id=1, source_target_pairs={{4,0},{30,2},{8,4},{2,6},{12,8},{6,10},{16,12},{10,14},{20,16},{14... | collective-permute-start | bytes 786440 | tf_op jit(solution)/shard_map/ppermute | solution.py:46
  87.3 7.6 %collective-permute-start.30 = (bf16[512,256]{1,0:T(8,128)(2,1)S(1)}, bf16[512,256]{1,0:T(8,128)(2,1)S(1)}, u32[]{:S(2)}, u32[]{:S(2)}) collective-permute-start(bf16[512,256]{1,0:T(8,128)(2,1)S(1)} %collective-permute-done.26.refs_10_), channel_id=1, source_target_pairs={{4,0},{30,2},{8,4},{2,6},{12,8},{6,10},{16,12},{10,14},{20,16},{14... | collective-permute-start | bytes 786440 | tf_op jit(solution)/shard_map/ppermute | solution.py:46
  87.3 9.5 %collective-permute-start.25 = (bf16[512,256]{1,0:T(8,128)(2,1)S(1)}, bf16[512,256]{1,0:T(8,128)(2,1)S(1)}, u32[]{:S(2)}, u32[]{:S(2)}) collective-permute-start(bf16[512,256]{1,0:T(8,128)(2,1)S(1)} %collective-permute-done.22.refs_6_), channel_id=1, source_target_pairs={{0,2},{2,0},{1,3},{3,1},{4,6},{6,4},{5,7},{7,5},{8,10},{10,8},{9,1... | collective-permute-start | bytes 786440 | tf_op jit(solution)/shard_map/ppermute | solution.py:35
  105.6 5.9 %collective-permute-start.32 = (bf16[8,32,1536]{2,1,0:T(8,128)(2,1)}, bf16[8,32,1536]{2,1,0:T(8,128)(2,1)S(1)}, u32[]{:S(2)}, u32[]{:S(2)}) collective-permute-start(bf16[8,32,1536]{2,1,0:T(8,128)(2,1)} %get-tuple-element.27), channel_id=1, source_target_pairs={{0,2},{2,0},{1,3},{3,1},{4,6},{6,4},{5,7},{7,5},{8,10},{10,8},{9,1... | collective-permute-start | bytes 2359304 | tf_op jit(solution)/shard_map/ppermute | solution.py:35
  106.1 29.1 %all-to-all-start.2 = ((bf16[8,32,3072]{2,1,0:T(8,128)(2,1)}), bf16[8,32,3072]{2,1,0:T(8,128)(2,1)S(1)}, u32[]{:S(2)}, u32[]{:S(2)}) async-start(bf16[8,32,3072]{2,1,0:T(8,128)(2,1)} %get-tuple-element.28), calls=%async_computation.2 | async-start | bytes 3145728 | tf_op jit(solution)/shard_map/all_to_all | solution.py:266
  111.7 11.0 %collective-permute-start.33 = (bf16[2,32,1536]{2,1,0:T(8,128)(2,1)S(1)}, bf16[2,32,1536]{2,1,0:T(8,128)(2,1)S(1)}, u32[]{:S(2)}, u32[]{:S(2)}) collective-permute-start(bf16[2,32,1536]{2,1,0:T(8,128)(2,1)S(1)} %get-tuple-element.29), channel_id=1, source_target_pairs={{20,0},{14,2},{24,4},{18,6},{28,8},{22,10},{0,12},{26,14},{4,16},{... | collective-permute-start | bytes 589832 | tf_op jit(solution)/shard_map/ppermute | solution.py:250
  114.7 15.4 %collective-permute-start.34 = (bf16[2,32,1536]{2,1,0:T(8,128)(2,1)S(1)}, bf16[2,32,1536]{2,1,0:T(8,128)(2,1)S(1)}, u32[]{:S(2)}, u32[]{:S(2)}) collective-permute-start(bf16[2,32,1536]{2,1,0:T(8,128)(2,1)S(1)} %get-tuple-element.31), channel_id=1, source_target_pairs={{24,0},{10,2},{28,4},{14,6},{0,8},{18,10},{4,12},{22,14},{8,16},{2... | collective-permute-start | bytes 589832 | tf_op jit(solution)/shard_map/ppermute | solution.py:250
  116.4 15.7 %collective-permute-start.35 = (bf16[2,32,1536]{2,1,0:T(8,128)(2,1)S(1)}, bf16[2,32,1536]{2,1,0:T(8,128)(2,1)S(1)}, u32[]{:S(2)}, u32[]{:S(2)}) collective-permute-start(bf16[2,32,1536]{2,1,0:T(8,128)(2,1)S(1)} %get-tuple-element.30), channel_id=1, source_target_pairs={{28,0},{6,2},{0,4},{10,6},{4,8},{14,10},{8,12},{18,14},{12,16},{22... | collective-permute-start | bytes 589832 | tf_op jit(solution)/shard_map/ppermute | solution.py:250
  116.4 15.9 %collective-permute-start.36 = (bf16[32,1536]{1,0:T(8,128)(2,1)S(1)}, bf16[32,1536]{1,0:T(8,128)(2,1)S(1)}, u32[]{:S(2)}, u32[]{:S(2)}) collective-permute-start(bf16[32,1536]{1,0:T(8,128)(2,1)S(1)} %slice_bitcast_fusion.1), channel_id=1, source_target_pairs={{16,0},{18,2},{20,4},{22,6},{24,8},{26,10},{28,12},{30,14},{0,16},... | collective-permute-start | bytes 294920 | tf_op jit(solution)/shard_map/ppermute | solution.py:250
  (36 other events, 256.3 us)

commit v8 on v7

--- a/solution.py
+++ b/solution.py
@@ -25,8 +25,9 @@
 LATE = 11
 EARLY = 12
 NEAR = 0
-WIDTH_Z, WIDTH = 512, 256
+WIDTH_Z, WIDTH = 768, 768
 SINGLE = {4: 6, 0: 7}
+TOGETHER = 2
 VMEM = pl.BlockSpec(memory_space=pltpu.VMEM)
 HBM = pl.BlockSpec(memory_space=pltpu.HBM)
 
@@ -167,7 +168,8 @@
     copies = []
     for i, ref in enumerate(a_refs):
         z, h = where_from(i)
-        copies.append(pltpu.make_async_copy(ref, a.at[i], sem_a.at[i]))
+        at = pl.ds(i % TOGETHER * TILE, TILE)
+        copies.append(pltpu.make_async_copy(ref, a.at[i // TOGETHER, :, at], sem_a.at[i]))
     loads = [pltpu.make_async_copy(cut_ref, y, sem_x.at[PARTS])]
     for i, ref in enumerate(x_refs):
         z, h = where_from(i)
@@ -175,12 +177,15 @@
     for copy in copies + loads:
         copy.start()
     squared = None
-    for i in range(PARTS):
-        z, h = where_from(i)
-        copies[i].wait()
-        term = jnp.dot(a[i], b_ref[:, 2 * z + h].reshape(TILE, TILE), preferred_element_type=f32)
+    for g in range(PARTS // TOGETHER):
+        right = []
+        for i in range(g * TOGETHER, (g + 1) * TOGETHER):
+            z, h = where_from(i)
+            copies[i].wait()
+            right.append(b_ref[:, 2 * z + h].reshape(TILE, TILE))
+        term = jnp.dot(a[g], jnp.concatenate(right), preferred_element_type=f32)
         squared = term if squared is None else squared + term
-    gram = a[0].astype(f32)
+    gram = a[0, :, pl.ds(0, TILE)].astype(f32)
     poly = coef_cubic * gram + coef_quintic * squared
     poly_t = poly.T.astype(bf16)
     poly = poly.astype(bf16)
@@ -226,7 +231,7 @@
         in_specs=[HBM] * LATE + [VMEM] * (PARTS - LATE) + [HBM] * PARTS + [VMEM, HBM],
         out_specs=(HBM, HBM, HBM),
         scratch_shapes=[
-            pltpu.VMEM((PARTS, n, TILE), bf16),
+            pltpu.VMEM((PARTS // TOGETHER, n, TOGETHER * TILE), bf16),
             pltpu.VMEM((PARTS, ROWS, COLS - COLS_Z), bf16),
             pltpu.VMEM((NR, ROWS, COLS_Z), bf16),
             pltpu.VMEM((NZ, 2, ROWS, COLS_Z), bf16),

time: 137 us -> 137 us (level)
  no operation moved by 1% of the time
where the time goes in v8:
time: 137 us; the launch traced here: 136 us
  starting transfers between devices  63.7 us (46%)
  waiting for transfers between devices  52.8 us (39%)
  Pallas kernels  15.3 us (11%)
  local copies, waits for them, and re-layouts  2.53 us (2%)
    ppermute x14, waiting for transfers between devices, turn(): return lax.ppermute(a, (Z, C), pairs)  33.9 us
    ppermute x18, starting transfers between devices, swap(): return lax.ppermute(a, C, [(0, 1), (1, 0)])  32.1 us
    ppermute x4, waiting for transfers between devices, cast(): return lax.ppermute(a, (Z, C), pairs)  11.4 us
    ppermute x4, starting transfers between devices, cast(): return lax.ppermute(a, (Z, C), pairs)  8.95 us
    all_to_all x2, starting transfers between devices, gather_r(): return lax.all_to_all(copies, (X, YL), 0, 0, tiled=True)  8.74 us
    pallas_call x1, Pallas kernels, product_part(): pl.pallas_call(product_kernel, out_shape=(pltpu.HBM((NR, ROWS, COLS - COL...  7.69 us
    all_to_all x1, starting transfers between devices, on_device(): got = lax.all_to_all(parts, (X, YL), 0, 0, tiled=True)  5.39 us
    ppermute x14, starting transfers between devices, turn(): return lax.ppermute(a, (Z, C), pairs)  5.21 us
  transfers between devices with their start and end apart: 41, of which 17 were waited for; matrix products, arithmetic and copies ran while one was open for 0% of the time, Pallas kernels for 6%

profile of v8, /device:TPU:1, one launch (start us, length us, event | category | flops | bytes accessed | tf_op | source)
XLA Modules:
  0.0 136.2 jit_solution(14265962523655050293)
XLA Ops:
  0.0 3.2 %collective-permute-start = (bf16[32,4608]{1,0:T(8,128)(2,1)}, bf16[32,4608]{1,0:T(8,128)(2,1)S(1)}, u32[]{:S(2)}, u32[]{:S(2)}) collective-permute-start(bf16[32,4608]{1,0:T(8,128)(2,1)} %refs_16_.1), channel_id=1, source_target_pairs={{0,2},{2,0},{1,3},{3,1},{4,6},{6,4},{5,7},{7,5},{8,10},{10,8},{9,1... | collective-permute-start | bytes 884744 | tf_op jit(solution)/shard_map/ppermute | solution.py:36
  5.8 3.8 %all-to-all-start = ((bf16[8,32,4608]{2,1,0:T(8,128)(2,1)}), bf16[8,32,4608]{2,1,0:T(8,128)(2,1)S(1)}, u32[]{:S(2)}, u32[]{:S(2)}) async-start(bf16[8,32,4608]{2,1,0:T(8,128)(2,1)} %copies.2), calls=%async_computation | async-start | bytes 4718592 | tf_op jit(solution)/shard_map/all_to_all | solution.py:98
  10.9 1.6 %collective-permute-start.2 = (bf16[32,4608]{1,0:T(8,128)(2,1)S(1)}, bf16[32,4608]{1,0:T(8,128)(2,1)S(1)}, u32[]{:S(2)}, u32[]{:S(2)}) collective-permute-start(bf16[32,4608]{1,0:T(8,128)(2,1)S(1)} %collective-permute-done.refs_1_.refs_17_), channel_id=1, source_target_pairs={{4,0},{30,2},{8,4},{2,6},{12,8},{6,10},{16,12},{10,14},{20,16},{14... | collective-permute-start | bytes 884744 | tf_op jit(solution)/shard_map/ppermute | solution.py:47
  12.6 6.7 %collective-permute-done.1.refs_2_.refs_18_ = bf16[32,4608]{1,0:T(8,128)(2,1)S(1)} collective-permute-done((bf16[32,4608]{1,0:T(8,128)(2,1)S(1)}, bf16[32,4608]{1,0:T(8,128)(2,1)S(1)}, u32[]{:S(2)}, u32[]{:S(2)}) %collective-permute-start.1) | collective-permute-done | bytes 294944 | tf_op jit(solution)/shard_map/ppermute | solution.py:47
  19.3 2.9 %collective-permute-done.2.refs_3_.refs_19_ = bf16[32,4608]{1,0:T(8,128)(2,1)S(1)} collective-permute-done((bf16[32,4608]{1,0:T(8,128)(2,1)S(1)}, bf16[32,4608]{1,0:T(8,128)(2,1)S(1)}, u32[]{:S(2)}, u32[]{:S(2)}) %collective-permute-start.2) | collective-permute-done | bytes 294944 | tf_op jit(solution)/shard_map/ppermute | solution.py:47
  22.1 4.2 %collective-permute-done.5.refs_6_.refs_22_ = bf16[32,4608]{1,0:T(8,128)(2,1)S(1)} collective-permute-done((bf16[32,4608]{1,0:T(8,128)(2,1)S(1)}, bf16[32,4608]{1,0:T(8,128)(2,1)S(1)}, u32[]{:S(2)}, u32[]{:S(2)}) %collective-permute-start.5) | collective-permute-done | bytes 294944 | tf_op jit(solution)/shard_map/ppermute | solution.py:47
  26.3 4.9 %collective-permute-start.4 = (bf16[32,4608]{1,0:T(8,128)(2,1)S(1)}, bf16[32,4608]{1,0:T(8,128)(2,1)S(1)}, u32[]{:S(2)}, u32[]{:S(2)}) collective-permute-start(bf16[32,4608]{1,0:T(8,128)(2,1)S(1)} %collective-permute-done.1.refs_2_.refs_18_), channel_id=1, source_target_pairs={{0,2},{2,0},{1,3},{3,1},{4,6},{6,4},{5,7},{7,5},{8,10},{10,8},{9,1... | collective-permute-start | bytes 884744 | tf_op jit(solution)/shard_map/ppermute | solution.py:36
  31.4 2.0 %collective-permute-done.9.refs_10_.refs_26_ = bf16[32,4608]{1,0:T(8,128)(2,1)} collective-permute-done((bf16[32,4608]{1,0:T(8,128)(2,1)S(1)}, bf16[32,4608]{1,0:T(8,128)(2,1)}, u32[]{:S(2)}, u32[]{:S(2)}) %collective-permute-start.9) | collective-permute-done | bytes 294944 | tf_op jit(solution)/shard_map/ppermute | solution.py:47
  33.4 5.9 %collective-permute-start.8 = (bf16[32,4608]{1,0:T(8,128)(2,1)S(1)}, bf16[32,4608]{1,0:T(8,128)(2,1)S(1)}, u32[]{:S(2)}, u32[]{:S(2)}) collective-permute-start(bf16[32,4608]{1,0:T(8,128)(2,1)S(1)} %collective-permute-done.5.refs_6_.refs_22_), channel_id=1, source_target_pairs={{0,2},{2,0},{1,3},{3,1},{4,6},{6,4},{5,7},{7,5},{8,10},{10,8},{9,1... | collective-permute-start | bytes 884744 | tf_op jit(solution)/shard_map/ppermute | solution.py:36
  40.0 1.7 %collective-permute-done.14.refs_2_.refs_30_ = bf16[32,4608]{1,0:T(8,128)(2,1)S(1)} collective-permute-done((bf16[32,4608]{1,0:T(8,128)(2,1)}, bf16[32,4608]{1,0:T(8,128)(2,1)S(1)}, u32[]{:S(2)}, u32[]{:S(2)}) %collective-permute-start.14) | collective-permute-done | bytes 294944 | tf_op jit(solution)/shard_map/ppermute | solution.py:47
  41.6 2.3 %collective-permute-start.15 = (bf16[32,4608]{1,0:T(8,128)(2,1)S(1)}, bf16[32,4608]{1,0:T(8,128)(2,1)S(1)}, u32[]{:S(2)}, u32[]{:S(2)}) collective-permute-start(bf16[32,4608]{1,0:T(8,128)(2,1)S(1)} %collective-permute-done.14.refs_2_.refs_30_), channel_id=1, source_target_pairs={{0,2},{2,0},{1,3},{3,1},{4,6},{6,4},{5,7},{7,5},{8,10},{10,8},{9,1... | collective-permute-start | bytes 884744 | tf_op jit(solution)/shard_map/ppermute | solution.py:36
  44.7 3.5 %gram_part.2 = (f32[384,256]{1,0:T(8,128)S(1)}, bf16[384,256]{1,0:T(8,128)(2,1)S(1)}, bf16[8,32,1536]{2,1,0:T(8,128)(2,1)}) custom-call(bf16[32,4608]{1,0:T(8,128)(2,1)} %refs_16_.1, bf16[32,4608]{1,0:T(8,128)(2,1)} %copy-done.8, bf16[32,4608]{1,0:T(8,128)(2,1)} %copy-done.9, bf16[32,4608]{1,0:T(8,128)(2,1)} %copy-done.10, bf16[32,4608]{1,0:T(8,128)(2,1)} %copy-done.14, ...), custom_call_target="tpu_custom_call" | custom-call | flops 905969664 | bytes 6291456 | tf_op jit(solution)/shard_map/gram_part/pallas_call | solution.py:149
  48.1 2.7 %collective-permute-start.11 = (bf16[384,256]{1,0:T(8,128)(2,1)S(1)}, bf16[384,256]{1,0:T(8,128)(2,1)S(1)}, u32[]{:S(2)}, u32[]{:S(2)}) collective-permute-start(bf16[384,256]{1,0:T(8,128)(2,1)S(1)} %get-tuple-element.20), channel_id=1, source_target_pairs={{0,1},{1,0},{2,3},{3,2},{4,5},{5,4},{6,7},{7,6},{8,9},{9,8},{10,11... | collective-permute-start | bytes 589832 | tf_op jit(solution)/shard_map/ppermute | solution.py:40
  52.7 4.3 %collective-permute-done.16.got_b = bf16[128,256]{1,0:T(8,128)(2,1)S(1)} collective-permute-done((bf16[128,256]{1,0:T(8,128)(2,1)S(1)}, bf16[128,256]{1,0:T(8,128)(2,1)S(1)}, u32[]{:S(2)}, u32[]{:S(2)}) %collective-permute-start.16) | collective-permute-done | bytes 65568 | tf_op jit(solution)/shard_map/ppermute | solution.py:40
  57.1 1.9 %collective-permute-start.17 = (bf16[512,256]{1,0:T(8,128)(2,1)S(1)}, bf16[512,256]{1,0:T(8,128)(2,1)S(1)}, u32[]{:S(2)}, u32[]{:S(2)}) collective-permute-start(bf16[512,256]{1,0:T(8,128)(2,1)S(1)} %bitcast.16), channel_id=1, source_target_pairs={{0,2},{2,0},{1,3},{3,1},{4,6},{6,4},{5,7},{7,5},{8,10},{10,8},{9,1... | collective-permute-start | bytes 786440 | tf_op jit(solution)/shard_map/ppermute | solution.py:36
  60.5 5.0 %all-to-all-start.1 = ((bf16[8,512,256]{2,1,0:T(8,128)(2,1)}), bf16[8,512,256]{2,1,0:T(8,128)(2,1)S(1)}, u32[]{:S(2)}, u32[]{:S(2)}) async-start(bf16[8,512,256]{2,1,0:T(8,128)(2,1)} %copies.3), calls=%async_computation.1 | async-start | bytes 4194304 | tf_op jit(solution)/shard_map/all_to_all | solution.py:98
  65.8 1.6 %collective-permute-start.19 = (bf16[512,256]{1,0:T(8,128)(2,1)S(1)}, bf16[512,256]{1,0:T(8,128)(2,1)S(1)}, u32[]{:S(2)}, u32[]{:S(2)}) collective-permute-start(bf16[512,256]{1,0:T(8,128)(2,1)S(1)} %collective-permute-done.17.refs_1_), channel_id=1, source_target_pairs={{4,0},{30,2},{8,4},{2,6},{12,8},{6,10},{16,12},{10,14},{20,16},{14... | collective-permute-start | bytes 786440 | tf_op jit(solution)/shard_map/ppermute | solution.py:47
  67.4 6.3 %collective-permute-done.18.refs_2_ = bf16[512,256]{1,0:T(8,128)(2,1)S(1)} collective-permute-done((bf16[512,256]{1,0:T(8,128)(2,1)S(1)}, bf16[512,256]{1,0:T(8,128)(2,1)S(1)}, u32[]{:S(2)}, u32[]{:S(2)}) %collective-permute-start.18) | collective-permute-done | bytes 262176 | tf_op jit(solution)/shard_map/ppermute | solution.py:47
  73.8 2.8 %collective-permute-done.19.refs_3_ = bf16[512,256]{1,0:T(8,128)(2,1)S(1)} collective-permute-done((bf16[512,256]{1,0:T(8,128)(2,1)S(1)}, bf16[512,256]{1,0:T(8,128)(2,1)S(1)}, u32[]{:S(2)}, u32[]{:S(2)}) %collective-permute-start.19) | collective-permute-done | bytes 262176 | tf_op jit(solution)/shard_map/ppermute | solution.py:47
  76.6 3.9 %collective-permute-done.22.refs_6_ = bf16[512,256]{1,0:T(8,128)(2,1)S(1)} collective-permute-done((bf16[512,256]{1,0:T(8,128)(2,1)S(1)}, bf16[512,256]{1,0:T(8,128)(2,1)S(1)}, u32[]{:S(2)}, u32[]{:S(2)}) %collective-permute-start.22) | collective-permute-done | bytes 262176 | tf_op jit(solution)/shard_map/ppermute | solution.py:47
  80.5 4.7 %collective-permute-start.21 = (bf16[512,256]{1,0:T(8,128)(2,1)S(1)}, bf16[512,256]{1,0:T(8,128)(2,1)S(1)}, u32[]{:S(2)}, u32[]{:S(2)}) collective-permute-start(bf16[512,256]{1,0:T(8,128)(2,1)S(1)} %collective-permute-done.18.refs_2_), channel_id=1, source_target_pairs={{0,2},{2,0},{1,3},{3,1},{4,6},{6,4},{5,7},{7,5},{8,10},{10,8},{9,1... | collective-permute-start | bytes 786440 | tf_op jit(solution)/shard_map/ppermute | solution.py:36
  85.3 1.9 %collective-permute-done.26.refs_10_ = bf16[512,256]{1,0:T(8,128)(2,1)S(1)} collective-permute-done((bf16[512,256]{1,0:T(8,128)(2,1)S(1)}, bf16[512,256]{1,0:T(8,128)(2,1)S(1)}, u32[]{:S(2)}, u32[]{:S(2)}) %collective-permute-start.26) | collective-permute-done | bytes 262176 | tf_op jit(solution)/shard_map/ppermute | solution.py:47
  87.3 5.6 %collective-permute-start.25 = (bf16[512,256]{1,0:T(8,128)(2,1)S(1)}, bf16[512,256]{1,0:T(8,128)(2,1)S(1)}, u32[]{:S(2)}, u32[]{:S(2)}) collective-permute-start(bf16[512,256]{1,0:T(8,128)(2,1)S(1)} %collective-permute-done.22.refs_6_), channel_id=1, source_target_pairs={{0,2},{2,0},{1,3},{3,1},{4,6},{6,4},{5,7},{7,5},{8,10},{10,8},{9,1... | collective-permute-start | bytes 786440 | tf_op jit(solution)/shard_map/ppermute | solution.py:36
  94.9 1.9 %collective-permute-start.31 = (bf16[512,256]{1,0:T(8,128)(2,1)S(1)}, bf16[512,256]{1,0:T(8,128)(2,1)S(1)}, u32[]{:S(2)}, u32[]{:S(2)}) collective-permute-start(bf16[512,256]{1,0:T(8,128)(2,1)S(1)} %collective-permute-done.30.refs_14_), channel_id=1, source_target_pairs={{0,2},{2,0},{1,3},{3,1},{4,6},{6,4},{5,7},{7,5},{8,10},{10,8},{9,1... | collective-permute-start | bytes 786440 | tf_op jit(solution)/shard_map/ppermute | solution.py:36
  97.9 7.7 %product_part.1 = (bf16[8,32,3072]{2,1,0:T(8,128)(2,1)}, bf16[8,32,1536]{2,1,0:T(8,128)(2,1)}, bf16[8,32,1536]{2,1,0:T(8,128)(2,1)}) custom-call(bf16[512,256]{1,0:T(8,128)(2,1)} %bitcast.19, bf16[512,256]{1,0:T(8,128)(2,1)} %copy-done.17, bf16[512,256]{1,0:T(8,128)(2,1)} %copy-done.18, bf16[512,256]{1,0:T(8,128)(2,1)} %copy-done.19, ...), custom_call_target="tpu_custom_call" | custom-call | flops 2281701376 | bytes 14680064 | tf_op jit(solution)/shard_map/product_part/pallas_call | solution.py:224
  106.0 5.4 %all-to-all-start.2 = ((bf16[8,32,3072]{2,1,0:T(8,128)(2,1)}), bf16[8,32,3072]{2,1,0:T(8,128)(2,1)S(1)}, u32[]{:S(2)}, u32[]{:S(2)}) async-start(bf16[8,32,3072]{2,1,0:T(8,128)(2,1)} %get-tuple-element.28), calls=%async_computation.2 | async-start | bytes 3145728 | tf_op jit(solution)/shard_map/all_to_all | solution.py:271
  111.7 3.0 %collective-permute-start.33 = (bf16[2,32,1536]{2,1,0:T(8,128)(2,1)S(1)}, bf16[2,32,1536]{2,1,0:T(8,128)(2,1)S(1)}, u32[]{:S(2)}, u32[]{:S(2)}) collective-permute-start(bf16[2,32,1536]{2,1,0:T(8,128)(2,1)S(1)} %get-tuple-element.29), channel_id=1, source_target_pairs={{20,0},{14,2},{24,4},{18,6},{28,8},{22,10},{0,12},{26,14},{4,16},{... | collective-permute-start | bytes 589832 | tf_op jit(solution)/shard_map/ppermute | solution.py:255
  114.7 1.6 %collective-permute-start.34 = (bf16[2,32,1536]{2,1,0:T(8,128)(2,1)S(1)}, bf16[2,32,1536]{2,1,0:T(8,128)(2,1)S(1)}, u32[]{:S(2)}, u32[]{:S(2)}) collective-permute-start(bf16[2,32,1536]{2,1,0:T(8,128)(2,1)S(1)} %get-tuple-element.31), channel_id=1, source_target_pairs={{24,0},{10,2},{28,4},{14,6},{0,8},{18,10},{4,12},{22,14},{8,16},{2... | collective-permute-start | bytes 589832 | tf_op jit(solution)/shard_map/ppermute | solution.py:255
  116.4 4.3 %collective-permute-start.36 = (bf16[32,1536]{1,0:T(8,128)(2,1)S(1)}, bf16[32,1536]{1,0:T(8,128)(2,1)S(1)}, u32[]{:S(2)}, u32[]{:S(2)}) collective-permute-start(bf16[32,1536]{1,0:T(8,128)(2,1)S(1)} %slice_bitcast_fusion.1), channel_id=1, source_target_pairs={{16,0},{18,2},{20,4},{22,6},{24,8},{26,10},{28,12},{30,14},{0,16},... | collective-permute-start | bytes 294920 | tf_op jit(solution)/shard_map/ppermute | solution.py:255
  120.7 2.0 %collective-permute-done.33 = bf16[2,32,1536]{2,1,0:T(8,128)(2,1)S(1)} collective-permute-done((bf16[2,32,1536]{2,1,0:T(8,128)(2,1)S(1)}, bf16[2,32,1536]{2,1,0:T(8,128)(2,1)S(1)}, u32[]{:S(2)}, u32[]{:S(2)}) %collective-permute-start.33) | collective-permute-done | bytes 196640 | tf_op jit(solution)/shard_map/ppermute | solution.py:255
  122.6 7.5 %collective-permute-done.34 = bf16[2,32,1536]{2,1,0:T(8,128)(2,1)S(1)} collective-permute-done((bf16[2,32,1536]{2,1,0:T(8,128)(2,1)S(1)}, bf16[2,32,1536]{2,1,0:T(8,128)(2,1)S(1)}, u32[]{:S(2)}, u32[]{:S(2)}) %collective-permute-start.34) | collective-permute-done | bytes 196640 | tf_op jit(solution)/shard_map/ppermute | solution.py:255
  130.2 1.9 %collective-permute-done.35 = bf16[2,32,1536]{2,1,0:T(8,128)(2,1)S(1)} collective-permute-done((bf16[2,32,1536]{2,1,0:T(8,128)(2,1)S(1)}, bf16[2,32,1536]{2,1,0:T(8,128)(2,1)S(1)}, u32[]{:S(2)}, u32[]{:S(2)}) %collective-permute-start.35) | collective-permute-done | bytes 196640 | tf_op jit(solution)/shard_map/ppermute | solution.py:255
  (118 shorter events, 17.0 us)
Async XLA Ops:
  5.8 38.9 %all-to-all-start = ((bf16[8,32,4608]{2,1,0:T(8,128)(2,1)}), bf16[8,32,4608]{2,1,0:T(8,128)(2,1)S(1)}, u32[]{:S(2)}, u32[]{:S(2)}) async-start(bf16[8,32,4608]{2,1,0:T(8,128)(2,1)} %copies.2), calls=%async_computation | async-start | bytes 4718592 | tf_op jit(solution)/shard_map/all_to_all | solution.py:98
  9.5 9.7 %collective-permute-start.1 = (bf16[32,4608]{1,0:T(8,128)(2,1)S(1)}, bf16[32,4608]{1,0:T(8,128)(2,1)S(1)}, u32[]{:S(2)}, u32[]{:S(2)}) collective-permute-start(bf16[32,4608]{1,0:T(8,128)(2,1)S(1)} %copy-done.1), channel_id=1, source_target_pairs={{4,0},{30,2},{8,4},{2,6},{12,8},{6,10},{16,12},{10,14},{20,16},{14... | collective-permute-start | bytes 884744 | tf_op jit(solution)/shard_map/ppermute | solution.py:47
  10.9 11.2 %collective-permute-start.2 = (bf16[32,4608]{1,0:T(8,128)(2,1)S(1)}, bf16[32,4608]{1,0:T(8,128)(2,1)S(1)}, u32[]{:S(2)}, u32[]{:S(2)}) collective-permute-start(bf16[32,4608]{1,0:T(8,128)(2,1)S(1)} %collective-permute-done.refs_1_.refs_17_), channel_id=1, source_target_pairs={{4,0},{30,2},{8,4},{2,6},{12,8},{6,10},{16,12},{10,14},{20,16},{14... | collective-permute-start | bytes 884744 | tf_op jit(solution)/shard_map/ppermute | solution.py:47
  19.3 7.1 %collective-permute-start.5 = (bf16[32,4608]{1,0:T(8,128)(2,1)S(1)}, bf16[32,4608]{1,0:T(8,128)(2,1)S(1)}, u32[]{:S(2)}, u32[]{:S(2)}) collective-permute-start(bf16[32,4608]{1,0:T(8,128)(2,1)S(1)} %collective-permute-done.1.refs_2_.refs_18_), channel_id=1, source_target_pairs={{4,0},{30,2},{8,4},{2,6},{12,8},{6,10},{16,12},{10,14},{20,16},{14... | collective-permute-start | bytes 884744 | tf_op jit(solution)/shard_map/ppermute | solution.py:47
  22.1 9.2 %collective-permute-start.6 = (bf16[32,4608]{1,0:T(8,128)(2,1)S(1)}, bf16[32,4608]{1,0:T(8,128)(2,1)S(1)}, u32[]{:S(2)}, u32[]{:S(2)}) collective-permute-start(bf16[32,4608]{1,0:T(8,128)(2,1)S(1)} %collective-permute-done.2.refs_3_.refs_19_), channel_id=1, source_target_pairs={{4,0},{30,2},{8,4},{2,6},{12,8},{6,10},{16,12},{10,14},{20,16},{14... | collective-permute-start | bytes 884744 | tf_op jit(solution)/shard_map/ppermute | solution.py:47
  26.3 7.1 %collective-permute-start.9 = (bf16[32,4608]{1,0:T(8,128)(2,1)S(1)}, bf16[32,4608]{1,0:T(8,128)(2,1)}, u32[]{:S(2)}, u32[]{:S(2)}) collective-permute-start(bf16[32,4608]{1,0:T(8,128)(2,1)S(1)} %collective-permute-done.5.refs_6_.refs_22_), channel_id=1, source_target_pairs={{4,0},{30,2},{8,4},{2,6},{12,8},{6,10},{16,12},{10,14},{20,16},{14... | collective-permute-start | bytes 884744 | tf_op jit(solution)/shard_map/ppermute | solution.py:47
  26.3 13.0 %collective-permute-start.4 = (bf16[32,4608]{1,0:T(8,128)(2,1)S(1)}, bf16[32,4608]{1,0:T(8,128)(2,1)S(1)}, u32[]{:S(2)}, u32[]{:S(2)}) collective-permute-start(bf16[32,4608]{1,0:T(8,128)(2,1)S(1)} %collective-permute-done.1.refs_2_.refs_18_), channel_id=1, source_target_pairs={{0,2},{2,0},{1,3},{3,1},{4,6},{6,4},{5,7},{7,5},{8,10},{10,8},{9,1... | collective-permute-start | bytes 884744 | tf_op jit(solution)/shard_map/ppermute | solution.py:36
  31.3 8.1 %collective-permute-start.3 = (bf16[32,4608]{1,0:T(8,128)(2,1)S(1)}, bf16[32,4608]{1,0:T(8,128)(2,1)S(1)}, u32[]{:S(2)}, u32[]{:S(2)}) collective-permute-start(bf16[32,4608]{1,0:T(8,128)(2,1)S(1)} %collective-permute-done.2.refs_3_.refs_19_), channel_id=1, source_target_pairs={{0,2},{2,0},{1,3},{3,1},{4,6},{6,4},{5,7},{7,5},{8,10},{10,8},{9,1... | collective-permute-start | bytes 884744 | tf_op jit(solution)/shard_map/ppermute | solution.py:36
  31.3 8.6 %collective-permute-start.10 = (bf16[32,4608]{1,0:T(8,128)(2,1)S(1)}, bf16[32,4608]{1,0:T(8,128)(2,1)}, u32[]{:S(2)}, u32[]{:S(2)}) collective-permute-start(bf16[32,4608]{1,0:T(8,128)(2,1)S(1)} %collective-permute-done.6.refs_7_.refs_23_), channel_id=1, source_target_pairs={{4,0},{30,2},{8,4},{2,6},{12,8},{6,10},{16,12},{10,14},{20,16},{14... | collective-permute-start | bytes 884744 | tf_op jit(solution)/shard_map/ppermute | solution.py:47
  33.4 8.2 %collective-permute-start.14 = (bf16[32,4608]{1,0:T(8,128)(2,1)}, bf16[32,4608]{1,0:T(8,128)(2,1)S(1)}, u32[]{:S(2)}, u32[]{:S(2)}) collective-permute-start(bf16[32,4608]{1,0:T(8,128)(2,1)} %collective-permute-done.9.refs_10_.refs_26_), channel_id=1, source_target_pairs={{4,0},{30,2},{8,4},{2,6},{12,8},{6,10},{16,12},{10,14},{20,16},{14... | collective-permute-start | bytes 884744 | tf_op jit(solution)/shard_map/ppermute | solution.py:47
  33.4 10.5 %collective-permute-start.8 = (bf16[32,4608]{1,0:T(8,128)(2,1)S(1)}, bf16[32,4608]{1,0:T(8,128)(2,1)S(1)}, u32[]{:S(2)}, u32[]{:S(2)}) collective-permute-start(bf16[32,4608]{1,0:T(8,128)(2,1)S(1)} %collective-permute-done.5.refs_6_.refs_22_), channel_id=1, source_target_pairs={{0,2},{2,0},{1,3},{3,1},{4,6},{6,4},{5,7},{7,5},{8,10},{10,8},{9,1... | collective-permute-start | bytes 884744 | tf_op jit(solution)/shard_map/ppermute | solution.py:36
  39.4 11.4 %collective-permute-start.13 = (bf16[32,4608]{1,0:T(8,128)(2,1)}, bf16[32,4608]{1,0:T(8,128)(2,1)S(1)}, u32[]{:S(2)}, u32[]{:S(2)}) collective-permute-start(bf16[32,4608]{1,0:T(8,128)(2,1)} %collective-permute-done.9.refs_10_.refs_26_), channel_id=1, source_target_pairs={{0,2},{2,0},{1,3},{3,1},{4,6},{6,4},{5,7},{7,5},{8,10},{10,8},{9,1... | collective-permute-start | bytes 884744 | tf_op jit(solution)/shard_map/ppermute | solution.py:36
  39.9 11.0 %collective-permute-start.12 = (bf16[32,4608]{1,0:T(8,128)(2,1)}, bf16[32,4608]{1,0:T(8,128)(2,1)S(1)}, u32[]{:S(2)}, u32[]{:S(2)}) collective-permute-start(bf16[32,4608]{1,0:T(8,128)(2,1)} %collective-permute-done.10.refs_11_.refs_27_), channel_id=1, source_target_pairs={{0,2},{2,0},{1,3},{3,1},{4,6},{6,4},{5,7},{7,5},{8,10},{10,8},{9,1... | collective-permute-start | bytes 884744 | tf_op jit(solution)/shard_map/ppermute | solution.py:36
  41.6 9.2 %collective-permute-start.15 = (bf16[32,4608]{1,0:T(8,128)(2,1)S(1)}, bf16[32,4608]{1,0:T(8,128)(2,1)S(1)}, u32[]{:S(2)}, u32[]{:S(2)}) collective-permute-start(bf16[32,4608]{1,0:T(8,128)(2,1)S(1)} %collective-permute-done.14.refs_2_.refs_30_), channel_id=1, source_target_pairs={{0,2},{2,0},{1,3},{3,1},{4,6},{6,4},{5,7},{7,5},{8,10},{10,8},{9,1... | collective-permute-start | bytes 884744 | tf_op jit(solution)/shard_map/ppermute | solution.py:36
  48.1 8.9 %collective-permute-start.11 = (bf16[384,256]{1,0:T(8,128)(2,1)S(1)}, bf16[384,256]{1,0:T(8,128)(2,1)S(1)}, u32[]{:S(2)}, u32[]{:S(2)}) collective-permute-start(bf16[384,256]{1,0:T(8,128)(2,1)S(1)} %get-tuple-element.20), channel_id=1, source_target_pairs={{0,1},{1,0},{2,3},{3,2},{4,5},{5,4},{6,7},{7,6},{8,9},{9,8},{10,11... | collective-permute-start | bytes 589832 | tf_op jit(solution)/shard_map/ppermute | solution.py:40
  60.5 37.4 %all-to-all-start.1 = ((bf16[8,512,256]{2,1,0:T(8,128)(2,1)}), bf16[8,512,256]{2,1,0:T(8,128)(2,1)S(1)}, u32[]{:S(2)}, u32[]{:S(2)}) async-start(bf16[8,512,256]{2,1,0:T(8,128)(2,1)} %copies.3), calls=%async_computation.1 | async-start | bytes 4194304 | tf_op jit(solution)/shard_map/all_to_all | solution.py:98
  65.4 8.3 %collective-permute-start.18 = (bf16[512,256]{1,0:T(8,128)(2,1)S(1)}, bf16[512,256]{1,0:T(8,128)(2,1)S(1)}, u32[]{:S(2)}, u32[]{:S(2)}) collective-permute-start(bf16[512,256]{1,0:T(8,128)(2,1)S(1)} %bitcast.18), channel_id=1, source_target_pairs={{4,0},{30,2},{8,4},{2,6},{12,8},{6,10},{16,12},{10,14},{20,16},{14... | collective-permute-start | bytes 786440 | tf_op jit(solution)/shard_map/ppermute | solution.py:47
  65.8 10.8 %collective-permute-start.19 = (bf16[512,256]{1,0:T(8,128)(2,1)S(1)}, bf16[512,256]{1,0:T(8,128)(2,1)S(1)}, u32[]{:S(2)}, u32[]{:S(2)}) collective-permute-start(bf16[512,256]{1,0:T(8,128)(2,1)S(1)} %collective-permute-done.17.refs_1_), channel_id=1, source_target_pairs={{4,0},{30,2},{8,4},{2,6},{12,8},{6,10},{16,12},{10,14},{20,16},{14... | collective-permute-start | bytes 786440 | tf_op jit(solution)/shard_map/ppermute | solution.py:47
  73.8 6.7 %collective-permute-start.22 = (bf16[512,256]{1,0:T(8,128)(2,1)S(1)}, bf16[512,256]{1,0:T(8,128)(2,1)S(1)}, u32[]{:S(2)}, u32[]{:S(2)}) collective-permute-start(bf16[512,256]{1,0:T(8,128)(2,1)S(1)} %collective-permute-done.18.refs_2_), channel_id=1, source_target_pairs={{4,0},{30,2},{8,4},{2,6},{12,8},{6,10},{16,12},{10,14},{20,16},{14... | collective-permute-start | bytes 786440 | tf_op jit(solution)/shard_map/ppermute | solution.py:47
  76.6 8.6 %collective-permute-start.23 = (bf16[512,256]{1,0:T(8,128)(2,1)S(1)}, bf16[512,256]{1,0:T(8,128)(2,1)S(1)}, u32[]{:S(2)}, u32[]{:S(2)}) collective-permute-start(bf16[512,256]{1,0:T(8,128)(2,1)S(1)} %collective-permute-done.19.refs_3_), channel_id=1, source_target_pairs={{4,0},{30,2},{8,4},{2,6},{12,8},{6,10},{16,12},{10,14},{20,16},{14... | collective-permute-start | bytes 786440 | tf_op jit(solution)/shard_map/ppermute | solution.py:47
  80.5 6.7 %collective-permute-start.26 = (bf16[512,256]{1,0:T(8,128)(2,1)S(1)}, bf16[512,256]{1,0:T(8,128)(2,1)S(1)}, u32[]{:S(2)}, u32[]{:S(2)}) collective-permute-start(bf16[512,256]{1,0:T(8,128)(2,1)S(1)} %collective-permute-done.22.refs_6_), channel_id=1, source_target_pairs={{4,0},{30,2},{8,4},{2,6},{12,8},{6,10},{16,12},{10,14},{20,16},{14... | collective-permute-start | bytes 786440 | tf_op jit(solution)/shard_map/ppermute | solution.py:47
  80.5 12.3 %collective-permute-start.21 = (bf16[512,256]{1,0:T(8,128)(2,1)S(1)}, bf16[512,256]{1,0:T(8,128)(2,1)S(1)}, u32[]{:S(2)}, u32[]{:S(2)}) collective-permute-start(bf16[512,256]{1,0:T(8,128)(2,1)S(1)} %collective-permute-done.18.refs_2_), channel_id=1, source_target_pairs={{0,2},{2,0},{1,3},{3,1},{4,6},{6,4},{5,7},{7,5},{8,10},{10,8},{9,1... | collective-permute-start | bytes 786440 | tf_op jit(solution)/shard_map/ppermute | solution.py:36
  85.2 7.7 %collective-permute-start.20 = (bf16[512,256]{1,0:T(8,128)(2,1)S(1)}, bf16[512,256]{1,0:T(8,128)(2,1)S(1)}, u32[]{:S(2)}, u32[]{:S(2)}) collective-permute-start(bf16[512,256]{1,0:T(8,128)(2,1)S(1)} %collective-permute-done.19.refs_3_), channel_id=1, source_target_pairs={{0,2},{2,0},{1,3},{3,1},{4,6},{6,4},{5,7},{7,5},{8,10},{10,8},{9,1... | collective-permute-start | bytes 786440 | tf_op jit(solution)/shard_map/ppermute | solution.py:36
  85.2 8.1 %collective-permute-start.27 = (bf16[512,256]{1,0:T(8,128)(2,1)S(1)}, bf16[512,256]{1,0:T(8,128)(2,1)S(1)}, u32[]{:S(2)}, u32[]{:S(2)}) collective-permute-start(bf16[512,256]{1,0:T(8,128)(2,1)S(1)} %collective-permute-done.23.refs_7_), channel_id=1, source_target_pairs={{4,0},{30,2},{8,4},{2,6},{12,8},{6,10},{16,12},{10,14},{20,16},{14... | collective-permute-start | bytes 786440 | tf_op jit(solution)/shard_map/ppermute | solution.py:47
  87.3 7.6 %collective-permute-start.30 = (bf16[512,256]{1,0:T(8,128)(2,1)S(1)}, bf16[512,256]{1,0:T(8,128)(2,1)S(1)}, u32[]{:S(2)}, u32[]{:S(2)}) collective-permute-start(bf16[512,256]{1,0:T(8,128)(2,1)S(1)} %collective-permute-done.26.refs_10_), channel_id=1, source_target_pairs={{4,0},{30,2},{8,4},{2,6},{12,8},{6,10},{16,12},{10,14},{20,16},{14... | collective-permute-start | bytes 786440 | tf_op jit(solution)/shard_map/ppermute | solution.py:47
  87.3 9.5 %collective-permute-start.25 = (bf16[512,256]{1,0:T(8,128)(2,1)S(1)}, bf16[512,256]{1,0:T(8,128)(2,1)S(1)}, u32[]{:S(2)}, u32[]{:S(2)}) collective-permute-start(bf16[512,256]{1,0:T(8,128)(2,1)S(1)} %collective-permute-done.22.refs_6_), channel_id=1, source_target_pairs={{0,2},{2,0},{1,3},{3,1},{4,6},{6,4},{5,7},{7,5},{8,10},{10,8},{9,1... | collective-permute-start | bytes 786440 | tf_op jit(solution)/shard_map/ppermute | solution.py:36
  105.6 5.9 %collective-permute-start.32 = (bf16[8,32,1536]{2,1,0:T(8,128)(2,1)}, bf16[8,32,1536]{2,1,0:T(8,128)(2,1)S(1)}, u32[]{:S(2)}, u32[]{:S(2)}) collective-permute-start(bf16[8,32,1536]{2,1,0:T(8,128)(2,1)} %get-tuple-element.27), channel_id=1, source_target_pairs={{0,2},{2,0},{1,3},{3,1},{4,6},{6,4},{5,7},{7,5},{8,10},{10,8},{9,1... | collective-permute-start | bytes 2359304 | tf_op jit(solution)/shard_map/ppermute | solution.py:36
  106.0 29.1 %all-to-all-start.2 = ((bf16[8,32,3072]{2,1,0:T(8,128)(2,1)}), bf16[8,32,3072]{2,1,0:T(8,128)(2,1)S(1)}, u32[]{:S(2)}, u32[]{:S(2)}) async-start(bf16[8,32,3072]{2,1,0:T(8,128)(2,1)} %get-tuple-element.28), calls=%async_computation.2 | async-start | bytes 3145728 | tf_op jit(solution)/shard_map/all_to_all | solution.py:271
  111.7 10.9 %collective-permute-start.33 = (bf16[2,32,1536]{2,1,0:T(8,128)(2,1)S(1)}, bf16[2,32,1536]{2,1,0:T(8,128)(2,1)S(1)}, u32[]{:S(2)}, u32[]{:S(2)}) collective-permute-start(bf16[2,32,1536]{2,1,0:T(8,128)(2,1)S(1)} %get-tuple-element.29), channel_id=1, source_target_pairs={{20,0},{14,2},{24,4},{18,6},{28,8},{22,10},{0,12},{26,14},{4,16},{... | collective-permute-start | bytes 589832 | tf_op jit(solution)/shard_map/ppermute | solution.py:255
  114.7 15.4 %collective-permute-start.34 = (bf16[2,32,1536]{2,1,0:T(8,128)(2,1)S(1)}, bf16[2,32,1536]{2,1,0:T(8,128)(2,1)S(1)}, u32[]{:S(2)}, u32[]{:S(2)}) collective-permute-start(bf16[2,32,1536]{2,1,0:T(8,128)(2,1)S(1)} %get-tuple-element.31), channel_id=1, source_target_pairs={{24,0},{10,2},{28,4},{14,6},{0,8},{18,10},{4,12},{22,14},{8,16},{2... | collective-permute-start | bytes 589832 | tf_op jit(solution)/shard_map/ppermute | solution.py:255
  116.3 15.7 %collective-permute-start.35 = (bf16[2,32,1536]{2,1,0:T(8,128)(2,1)S(1)}, bf16[2,32,1536]{2,1,0:T(8,128)(2,1)S(1)}, u32[]{:S(2)}, u32[]{:S(2)}) collective-permute-start(bf16[2,32,1536]{2,1,0:T(8,128)(2,1)S(1)} %get-tuple-element.30), channel_id=1, source_target_pairs={{28,0},{6,2},{0,4},{10,6},{4,8},{14,10},{8,12},{18,14},{12,16},{22... | collective-permute-start | bytes 589832 | tf_op jit(solution)/shard_map/ppermute | solution.py:255
  116.4 15.9 %collective-permute-start.36 = (bf16[32,1536]{1,0:T(8,128)(2,1)S(1)}, bf16[32,1536]{1,0:T(8,128)(2,1)S(1)}, u32[]{:S(2)}, u32[]{:S(2)}) collective-permute-start(bf16[32,1536]{1,0:T(8,128)(2,1)S(1)} %slice_bitcast_fusion.1), channel_id=1, source_target_pairs={{16,0},{18,2},{20,4},{22,6},{24,8},{26,10},{28,12},{30,14},{0,16},... | collective-permute-start | bytes 294920 | tf_op jit(solution)/shard_map/ppermute | solution.py:255
  (36 other events, 256.3 us)

commit v9 on v8

--- a/solution.py
+++ b/solution.py
@@ -186,9 +186,8 @@
         term = jnp.dot(a[g], jnp.concatenate(right), preferred_element_type=f32)
         squared = term if squared is None else squared + term
     gram = a[0, :, pl.ds(0, TILE)].astype(f32)
-    poly = coef_cubic * gram + coef_quintic * squared
-    poly_t = poly.T.astype(bf16)
-    poly = poly.astype(bf16)
+    poly = (coef_cubic * gram + coef_quintic * squared).astype(bf16)
+    poly_t = poly.T
     loads[0].wait()
     for k in range(COLS_Z // WIDTH_Z):
         cut = pl.ds(k * WIDTH_Z, WIDTH_Z)

time: 137 us -> 137 us (level)
  no operation moved by 1% of the time
where the time goes in v9:
time: 137 us; the launch traced here: 136 us
  starting transfers between devices  63.7 us (46%)
  waiting for transfers between devices  52.8 us (39%)
  Pallas kernels  15.3 us (11%)
  local copies, waits for them, and re-layouts  2.53 us (2%)
    ppermute x14, waiting for transfers between devices, turn(): return lax.ppermute(a, (Z, C), pairs)  33.9 us
    ppermute x18, starting transfers between devices, swap(): return lax.ppermute(a, C, [(0, 1), (1, 0)])  32.1 us
    ppermute x4, waiting for transfers between devices, cast(): return lax.ppermute(a, (Z, C), pairs)  11.4 us
    ppermute x4, starting transfers between devices, cast(): return lax.ppermute(a, (Z, C), pairs)  8.95 us
    all_to_all x2, starting transfers between devices, gather_r(): return lax.all_to_all(copies, (X, YL), 0, 0, tiled=True)  8.74 us
    pallas_call x1, Pallas kernels, product_part(): pl.pallas_call(product_kernel, out_shape=(pltpu.HBM((NR, ROWS, COLS - COL...  7.67 us
    all_to_all x1, starting transfers between devices, on_device(): got = lax.all_to_all(parts, (X, YL), 0, 0, tiled=True)  5.4 us
    ppermute x14, starting transfers between devices, turn(): return lax.ppermute(a, (Z, C), pairs)  5.21 us
  transfers between devices with their start and end apart: 41, of which 17 were waited for; matrix products, arithmetic and copies ran while one was open for 0% of the time, Pallas kernels for 6%

profile of v9, /device:TPU:1, one launch (start us, length us, event | category | flops | bytes accessed | tf_op | source)
XLA Modules:
  0.0 136.2 jit_solution(1764708500767488551)
XLA Ops:
  0.0 3.2 %collective-permute-start = (bf16[32,4608]{1,0:T(8,128)(2,1)}, bf16[32,4608]{1,0:T(8,128)(2,1)S(1)}, u32[]{:S(2)}, u32[]{:S(2)}) collective-permute-start(bf16[32,4608]{1,0:T(8,128)(2,1)} %refs_16_.1), channel_id=1, source_target_pairs={{0,2},{2,0},{1,3},{3,1},{4,6},{6,4},{5,7},{7,5},{8,10},{10,8},{9,1... | collective-permute-start | bytes 884744 | tf_op jit(solution)/shard_map/ppermute | solution.py:36
  5.8 3.8 %all-to-all-start = ((bf16[8,32,4608]{2,1,0:T(8,128)(2,1)}), bf16[8,32,4608]{2,1,0:T(8,128)(2,1)S(1)}, u32[]{:S(2)}, u32[]{:S(2)}) async-start(bf16[8,32,4608]{2,1,0:T(8,128)(2,1)} %copies.2), calls=%async_computation | async-start | bytes 4718592 | tf_op jit(solution)/shard_map/all_to_all | solution.py:98
  10.9 1.6 %collective-permute-start.2 = (bf16[32,4608]{1,0:T(8,128)(2,1)S(1)}, bf16[32,4608]{1,0:T(8,128)(2,1)S(1)}, u32[]{:S(2)}, u32[]{:S(2)}) collective-permute-start(bf16[32,4608]{1,0:T(8,128)(2,1)S(1)} %collective-permute-done.refs_1_.refs_17_), channel_id=1, source_target_pairs={{4,0},{30,2},{8,4},{2,6},{12,8},{6,10},{16,12},{10,14},{20,16},{14... | collective-permute-start | bytes 884744 | tf_op jit(solution)/shard_map/ppermute | solution.py:47
  12.6 6.7 %collective-permute-done.1.refs_2_.refs_18_ = bf16[32,4608]{1,0:T(8,128)(2,1)S(1)} collective-permute-done((bf16[32,4608]{1,0:T(8,128)(2,1)S(1)}, bf16[32,4608]{1,0:T(8,128)(2,1)S(1)}, u32[]{:S(2)}, u32[]{:S(2)}) %collective-permute-start.1) | collective-permute-done | bytes 294944 | tf_op jit(solution)/shard_map/ppermute | solution.py:47
  19.3 2.9 %collective-permute-done.2.refs_3_.refs_19_ = bf16[32,4608]{1,0:T(8,128)(2,1)S(1)} collective-permute-done((bf16[32,4608]{1,0:T(8,128)(2,1)S(1)}, bf16[32,4608]{1,0:T(8,128)(2,1)S(1)}, u32[]{:S(2)}, u32[]{:S(2)}) %collective-permute-start.2) | collective-permute-done | bytes 294944 | tf_op jit(solution)/shard_map/ppermute | solution.py:47
  22.1 4.2 %collective-permute-done.5.refs_6_.refs_22_ = bf16[32,4608]{1,0:T(8,128)(2,1)S(1)} collective-permute-done((bf16[32,4608]{1,0:T(8,128)(2,1)S(1)}, bf16[32,4608]{1,0:T(8,128)(2,1)S(1)}, u32[]{:S(2)}, u32[]{:S(2)}) %collective-permute-start.5) | collective-permute-done | bytes 294944 | tf_op jit(solution)/shard_map/ppermute | solution.py:47
  26.3 4.9 %collective-permute-start.4 = (bf16[32,4608]{1,0:T(8,128)(2,1)S(1)}, bf16[32,4608]{1,0:T(8,128)(2,1)S(1)}, u32[]{:S(2)}, u32[]{:S(2)}) collective-permute-start(bf16[32,4608]{1,0:T(8,128)(2,1)S(1)} %collective-permute-done.1.refs_2_.refs_18_), channel_id=1, source_target_pairs={{0,2},{2,0},{1,3},{3,1},{4,6},{6,4},{5,7},{7,5},{8,10},{10,8},{9,1... | collective-permute-start | bytes 884744 | tf_op jit(solution)/shard_map/ppermute | solution.py:36
  31.4 2.0 %collective-permute-done.9.refs_10_.refs_26_ = bf16[32,4608]{1,0:T(8,128)(2,1)} collective-permute-done((bf16[32,4608]{1,0:T(8,128)(2,1)S(1)}, bf16[32,4608]{1,0:T(8,128)(2,1)}, u32[]{:S(2)}, u32[]{:S(2)}) %collective-permute-start.9) | collective-permute-done | bytes 294944 | tf_op jit(solution)/shard_map/ppermute | solution.py:47
  33.4 5.9 %collective-permute-start.8 = (bf16[32,4608]{1,0:T(8,128)(2,1)S(1)}, bf16[32,4608]{1,0:T(8,128)(2,1)S(1)}, u32[]{:S(2)}, u32[]{:S(2)}) collective-permute-start(bf16[32,4608]{1,0:T(8,128)(2,1)S(1)} %collective-permute-done.5.refs_6_.refs_22_), channel_id=1, source_target_pairs={{0,2},{2,0},{1,3},{3,1},{4,6},{6,4},{5,7},{7,5},{8,10},{10,8},{9,1... | collective-permute-start | bytes 884744 | tf_op jit(solution)/shard_map/ppermute | solution.py:36
  40.0 1.7 %collective-permute-done.14.refs_2_.refs_30_ = bf16[32,4608]{1,0:T(8,128)(2,1)S(1)} collective-permute-done((bf16[32,4608]{1,0:T(8,128)(2,1)}, bf16[32,4608]{1,0:T(8,128)(2,1)S(1)}, u32[]{:S(2)}, u32[]{:S(2)}) %collective-permute-start.14) | collective-permute-done | bytes 294944 | tf_op jit(solution)/shard_map/ppermute | solution.py:47
  41.6 2.3 %collective-permute-start.15 = (bf16[32,4608]{1,0:T(8,128)(2,1)S(1)}, bf16[32,4608]{1,0:T(8,128)(2,1)S(1)}, u32[]{:S(2)}, u32[]{:S(2)}) collective-permute-start(bf16[32,4608]{1,0:T(8,128)(2,1)S(1)} %collective-permute-done.14.refs_2_.refs_30_), channel_id=1, source_target_pairs={{0,2},{2,0},{1,3},{3,1},{4,6},{6,4},{5,7},{7,5},{8,10},{10,8},{9,1... | collective-permute-start | bytes 884744 | tf_op jit(solution)/shard_map/ppermute | solution.py:36
  44.7 3.5 %gram_part.2 = (f32[384,256]{1,0:T(8,128)S(1)}, bf16[384,256]{1,0:T(8,128)(2,1)S(1)}, bf16[8,32,1536]{2,1,0:T(8,128)(2,1)}) custom-call(bf16[32,4608]{1,0:T(8,128)(2,1)} %refs_16_.1, bf16[32,4608]{1,0:T(8,128)(2,1)} %copy-done.8, bf16[32,4608]{1,0:T(8,128)(2,1)} %copy-done.9, bf16[32,4608]{1,0:T(8,128)(2,1)} %copy-done.10, bf16[32,4608]{1,0:T(8,128)(2,1)} %copy-done.14, ...), custom_call_target="tpu_custom_call" | custom-call | flops 905969664 | bytes 6291456 | tf_op jit(solution)/shard_map/gram_part/pallas_call | solution.py:149
  48.1 2.7 %collective-permute-start.11 = (bf16[384,256]{1,0:T(8,128)(2,1)S(1)}, bf16[384,256]{1,0:T(8,128)(2,1)S(1)}, u32[]{:S(2)}, u32[]{:S(2)}) collective-permute-start(bf16[384,256]{1,0:T(8,128)(2,1)S(1)} %get-tuple-element.20), channel_id=1, source_target_pairs={{0,1},{1,0},{2,3},{3,2},{4,5},{5,4},{6,7},{7,6},{8,9},{9,8},{10,11... | collective-permute-start | bytes 589832 | tf_op jit(solution)/shard_map/ppermute | solution.py:40
  52.7 4.3 %collective-permute-done.16.got_b = bf16[128,256]{1,0:T(8,128)(2,1)S(1)} collective-permute-done((bf16[128,256]{1,0:T(8,128)(2,1)S(1)}, bf16[128,256]{1,0:T(8,128)(2,1)S(1)}, u32[]{:S(2)}, u32[]{:S(2)}) %collective-permute-start.16) | collective-permute-done | bytes 65568 | tf_op jit(solution)/shard_map/ppermute | solution.py:40
  57.1 1.9 %collective-permute-start.17 = (bf16[512,256]{1,0:T(8,128)(2,1)S(1)}, bf16[512,256]{1,0:T(8,128)(2,1)S(1)}, u32[]{:S(2)}, u32[]{:S(2)}) collective-permute-start(bf16[512,256]{1,0:T(8,128)(2,1)S(1)} %bitcast.16), channel_id=1, source_target_pairs={{0,2},{2,0},{1,3},{3,1},{4,6},{6,4},{5,7},{7,5},{8,10},{10,8},{9,1... | collective-permute-start | bytes 786440 | tf_op jit(solution)/shard_map/ppermute | solution.py:36
  60.5 5.0 %all-to-all-start.1 = ((bf16[8,512,256]{2,1,0:T(8,128)(2,1)}), bf16[8,512,256]{2,1,0:T(8,128)(2,1)S(1)}, u32[]{:S(2)}, u32[]{:S(2)}) async-start(bf16[8,512,256]{2,1,0:T(8,128)(2,1)} %copies.3), calls=%async_computation.1 | async-start | bytes 4194304 | tf_op jit(solution)/shard_map/all_to_all | solution.py:98
  65.8 1.6 %collective-permute-start.19 = (bf16[512,256]{1,0:T(8,128)(2,1)S(1)}, bf16[512,256]{1,0:T(8,128)(2,1)S(1)}, u32[]{:S(2)}, u32[]{:S(2)}) collective-permute-start(bf16[512,256]{1,0:T(8,128)(2,1)S(1)} %collective-permute-done.17.refs_1_), channel_id=1, source_target_pairs={{4,0},{30,2},{8,4},{2,6},{12,8},{6,10},{16,12},{10,14},{20,16},{14... | collective-permute-start | bytes 786440 | tf_op jit(solution)/shard_map/ppermute | solution.py:47
  67.4 6.3 %collective-permute-done.18.refs_2_ = bf16[512,256]{1,0:T(8,128)(2,1)S(1)} collective-permute-done((bf16[512,256]{1,0:T(8,128)(2,1)S(1)}, bf16[512,256]{1,0:T(8,128)(2,1)S(1)}, u32[]{:S(2)}, u32[]{:S(2)}) %collective-permute-start.18) | collective-permute-done | bytes 262176 | tf_op jit(solution)/shard_map/ppermute | solution.py:47
  73.8 2.8 %collective-permute-done.19.refs_3_ = bf16[512,256]{1,0:T(8,128)(2,1)S(1)} collective-permute-done((bf16[512,256]{1,0:T(8,128)(2,1)S(1)}, bf16[512,256]{1,0:T(8,128)(2,1)S(1)}, u32[]{:S(2)}, u32[]{:S(2)}) %collective-permute-start.19) | collective-permute-done | bytes 262176 | tf_op jit(solution)/shard_map/ppermute | solution.py:47
  76.6 3.9 %collective-permute-done.22.refs_6_ = bf16[512,256]{1,0:T(8,128)(2,1)S(1)} collective-permute-done((bf16[512,256]{1,0:T(8,128)(2,1)S(1)}, bf16[512,256]{1,0:T(8,128)(2,1)S(1)}, u32[]{:S(2)}, u32[]{:S(2)}) %collective-permute-start.22) | collective-permute-done | bytes 262176 | tf_op jit(solution)/shard_map/ppermute | solution.py:47
  80.5 4.7 %collective-permute-start.21 = (bf16[512,256]{1,0:T(8,128)(2,1)S(1)}, bf16[512,256]{1,0:T(8,128)(2,1)S(1)}, u32[]{:S(2)}, u32[]{:S(2)}) collective-permute-start(bf16[512,256]{1,0:T(8,128)(2,1)S(1)} %collective-permute-done.18.refs_2_), channel_id=1, source_target_pairs={{0,2},{2,0},{1,3},{3,1},{4,6},{6,4},{5,7},{7,5},{8,10},{10,8},{9,1... | collective-permute-start | bytes 786440 | tf_op jit(solution)/shard_map/ppermute | solution.py:36
  85.3 1.9 %collective-permute-done.26.refs_10_ = bf16[512,256]{1,0:T(8,128)(2,1)S(1)} collective-permute-done((bf16[512,256]{1,0:T(8,128)(2,1)S(1)}, bf16[512,256]{1,0:T(8,128)(2,1)S(1)}, u32[]{:S(2)}, u32[]{:S(2)}) %collective-permute-start.26) | collective-permute-done | bytes 262176 | tf_op jit(solution)/shard_map/ppermute | solution.py:47
  87.3 5.6 %collective-permute-start.25 = (bf16[512,256]{1,0:T(8,128)(2,1)S(1)}, bf16[512,256]{1,0:T(8,128)(2,1)S(1)}, u32[]{:S(2)}, u32[]{:S(2)}) collective-permute-start(bf16[512,256]{1,0:T(8,128)(2,1)S(1)} %collective-permute-done.22.refs_6_), channel_id=1, source_target_pairs={{0,2},{2,0},{1,3},{3,1},{4,6},{6,4},{5,7},{7,5},{8,10},{10,8},{9,1... | collective-permute-start | bytes 786440 | tf_op jit(solution)/shard_map/ppermute | solution.py:36
  94.9 1.9 %collective-permute-start.31 = (bf16[512,256]{1,0:T(8,128)(2,1)S(1)}, bf16[512,256]{1,0:T(8,128)(2,1)S(1)}, u32[]{:S(2)}, u32[]{:S(2)}) collective-permute-start(bf16[512,256]{1,0:T(8,128)(2,1)S(1)} %collective-permute-done.30.refs_14_), channel_id=1, source_target_pairs={{0,2},{2,0},{1,3},{3,1},{4,6},{6,4},{5,7},{7,5},{8,10},{10,8},{9,1... | collective-permute-start | bytes 786440 | tf_op jit(solution)/shard_map/ppermute | solution.py:36
  97.9 7.7 %product_part.1 = (bf16[8,32,3072]{2,1,0:T(8,128)(2,1)}, bf16[8,32,1536]{2,1,0:T(8,128)(2,1)}, bf16[8,32,1536]{2,1,0:T(8,128)(2,1)}) custom-call(bf16[512,256]{1,0:T(8,128)(2,1)} %bitcast.19, bf16[512,256]{1,0:T(8,128)(2,1)} %copy-done.17, bf16[512,256]{1,0:T(8,128)(2,1)} %copy-done.18, bf16[512,256]{1,0:T(8,128)(2,1)} %copy-done.19, ...), custom_call_target="tpu_custom_call" | custom-call | flops 2281701376 | bytes 14680064 | tf_op jit(solution)/shard_map/product_part/pallas_call | solution.py:223
  106.0 5.4 %all-to-all-start.2 = ((bf16[8,32,3072]{2,1,0:T(8,128)(2,1)}), bf16[8,32,3072]{2,1,0:T(8,128)(2,1)S(1)}, u32[]{:S(2)}, u32[]{:S(2)}) async-start(bf16[8,32,3072]{2,1,0:T(8,128)(2,1)} %get-tuple-element.28), calls=%async_computation.2 | async-start | bytes 3145728 | tf_op jit(solution)/shard_map/all_to_all | solution.py:270
  111.7 3.0 %collective-permute-start.33 = (bf16[2,32,1536]{2,1,0:T(8,128)(2,1)S(1)}, bf16[2,32,1536]{2,1,0:T(8,128)(2,1)S(1)}, u32[]{:S(2)}, u32[]{:S(2)}) collective-permute-start(bf16[2,32,1536]{2,1,0:T(8,128)(2,1)S(1)} %get-tuple-element.29), channel_id=1, source_target_pairs={{20,0},{14,2},{24,4},{18,6},{28,8},{22,10},{0,12},{26,14},{4,16},{... | collective-permute-start | bytes 589832 | tf_op jit(solution)/shard_map/ppermute | solution.py:254
  114.7 1.6 %collective-permute-start.34 = (bf16[2,32,1536]{2,1,0:T(8,128)(2,1)S(1)}, bf16[2,32,1536]{2,1,0:T(8,128)(2,1)S(1)}, u32[]{:S(2)}, u32[]{:S(2)}) collective-permute-start(bf16[2,32,1536]{2,1,0:T(8,128)(2,1)S(1)} %get-tuple-element.31), channel_id=1, source_target_pairs={{24,0},{10,2},{28,4},{14,6},{0,8},{18,10},{4,12},{22,14},{8,16},{2... | collective-permute-start | bytes 589832 | tf_op jit(solution)/shard_map/ppermute | solution.py:254
  116.3 4.3 %collective-permute-start.36 = (bf16[32,1536]{1,0:T(8,128)(2,1)S(1)}, bf16[32,1536]{1,0:T(8,128)(2,1)S(1)}, u32[]{:S(2)}, u32[]{:S(2)}) collective-permute-start(bf16[32,1536]{1,0:T(8,128)(2,1)S(1)} %slice_bitcast_fusion.1), channel_id=1, source_target_pairs={{16,0},{18,2},{20,4},{22,6},{24,8},{26,10},{28,12},{30,14},{0,16},... | collective-permute-start | bytes 294920 | tf_op jit(solution)/shard_map/ppermute | solution.py:254
  120.6 2.0 %collective-permute-done.33 = bf16[2,32,1536]{2,1,0:T(8,128)(2,1)S(1)} collective-permute-done((bf16[2,32,1536]{2,1,0:T(8,128)(2,1)S(1)}, bf16[2,32,1536]{2,1,0:T(8,128)(2,1)S(1)}, u32[]{:S(2)}, u32[]{:S(2)}) %collective-permute-start.33) | collective-permute-done | bytes 196640 | tf_op jit(solution)/shard_map/ppermute | solution.py:254
  122.6 7.5 %collective-permute-done.34 = bf16[2,32,1536]{2,1,0:T(8,128)(2,1)S(1)} collective-permute-done((bf16[2,32,1536]{2,1,0:T(8,128)(2,1)S(1)}, bf16[2,32,1536]{2,1,0:T(8,128)(2,1)S(1)}, u32[]{:S(2)}, u32[]{:S(2)}) %collective-permute-start.34) | collective-permute-done | bytes 196640 | tf_op jit(solution)/shard_map/ppermute | solution.py:254
  130.1 1.9 %collective-permute-done.35 = bf16[2,32,1536]{2,1,0:T(8,128)(2,1)S(1)} collective-permute-done((bf16[2,32,1536]{2,1,0:T(8,128)(2,1)S(1)}, bf16[2,32,1536]{2,1,0:T(8,128)(2,1)S(1)}, u32[]{:S(2)}, u32[]{:S(2)}) %collective-permute-start.35) | collective-permute-done | bytes 196640 | tf_op jit(solution)/shard_map/ppermute | solution.py:254
  (118 shorter events, 17.1 us)
Async XLA Ops:
  5.8 38.9 %all-to-all-start = ((bf16[8,32,4608]{2,1,0:T(8,128)(2,1)}), bf16[8,32,4608]{2,1,0:T(8,128)(2,1)S(1)}, u32[]{:S(2)}, u32[]{:S(2)}) async-start(bf16[8,32,4608]{2,1,0:T(8,128)(2,1)} %copies.2), calls=%async_computation | async-start | bytes 4718592 | tf_op jit(solution)/shard_map/all_to_all | solution.py:98
  9.5 9.7 %collective-permute-start.1 = (bf16[32,4608]{1,0:T(8,128)(2,1)S(1)}, bf16[32,4608]{1,0:T(8,128)(2,1)S(1)}, u32[]{:S(2)}, u32[]{:S(2)}) collective-permute-start(bf16[32,4608]{1,0:T(8,128)(2,1)S(1)} %copy-done.1), channel_id=1, source_target_pairs={{4,0},{30,2},{8,4},{2,6},{12,8},{6,10},{16,12},{10,14},{20,16},{14... | collective-permute-start | bytes 884744 | tf_op jit(solution)/shard_map/ppermute | solution.py:47
  10.9 11.2 %collective-permute-start.2 = (bf16[32,4608]{1,0:T(8,128)(2,1)S(1)}, bf16[32,4608]{1,0:T(8,128)(2,1)S(1)}, u32[]{:S(2)}, u32[]{:S(2)}) collective-permute-start(bf16[32,4608]{1,0:T(8,128)(2,1)S(1)} %collective-permute-done.refs_1_.refs_17_), channel_id=1, source_target_pairs={{4,0},{30,2},{8,4},{2,6},{12,8},{6,10},{16,12},{10,14},{20,16},{14... | collective-permute-start | bytes 884744 | tf_op jit(solution)/shard_map/ppermute | solution.py:47
  19.3 7.1 %collective-permute-start.5 = (bf16[32,4608]{1,0:T(8,128)(2,1)S(1)}, bf16[32,4608]{1,0:T(8,128)(2,1)S(1)}, u32[]{:S(2)}, u32[]{:S(2)}) collective-permute-start(bf16[32,4608]{1,0:T(8,128)(2,1)S(1)} %collective-permute-done.1.refs_2_.refs_18_), channel_id=1, source_target_pairs={{4,0},{30,2},{8,4},{2,6},{12,8},{6,10},{16,12},{10,14},{20,16},{14... | collective-permute-start | bytes 884744 | tf_op jit(solution)/shard_map/ppermute | solution.py:47
  22.1 9.2 %collective-permute-start.6 = (bf16[32,4608]{1,0:T(8,128)(2,1)S(1)}, bf16[32,4608]{1,0:T(8,128)(2,1)S(1)}, u32[]{:S(2)}, u32[]{:S(2)}) collective-permute-start(bf16[32,4608]{1,0:T(8,128)(2,1)S(1)} %collective-permute-done.2.refs_3_.refs_19_), channel_id=1, source_target_pairs={{4,0},{30,2},{8,4},{2,6},{12,8},{6,10},{16,12},{10,14},{20,16},{14... | collective-permute-start | bytes 884744 | tf_op jit(solution)/shard_map/ppermute | solution.py:47
  26.3 7.1 %collective-permute-start.9 = (bf16[32,4608]{1,0:T(8,128)(2,1)S(1)}, bf16[32,4608]{1,0:T(8,128)(2,1)}, u32[]{:S(2)}, u32[]{:S(2)}) collective-permute-start(bf16[32,4608]{1,0:T(8,128)(2,1)S(1)} %collective-permute-done.5.refs_6_.refs_22_), channel_id=1, source_target_pairs={{4,0},{30,2},{8,4},{2,6},{12,8},{6,10},{16,12},{10,14},{20,16},{14... | collective-permute-start | bytes 884744 | tf_op jit(solution)/shard_map/ppermute | solution.py:47
  26.3 13.0 %collective-permute-start.4 = (bf16[32,4608]{1,0:T(8,128)(2,1)S(1)}, bf16[32,4608]{1,0:T(8,128)(2,1)S(1)}, u32[]{:S(2)}, u32[]{:S(2)}) collective-permute-start(bf16[32,4608]{1,0:T(8,128)(2,1)S(1)} %collective-permute-done.1.refs_2_.refs_18_), channel_id=1, source_target_pairs={{0,2},{2,0},{1,3},{3,1},{4,6},{6,4},{5,7},{7,5},{8,10},{10,8},{9,1... | collective-permute-start | bytes 884744 | tf_op jit(solution)/shard_map/ppermute | solution.py:36
  31.3 8.1 %collective-permute-start.3 = (bf16[32,4608]{1,0:T(8,128)(2,1)S(1)}, bf16[32,4608]{1,0:T(8,128)(2,1)S(1)}, u32[]{:S(2)}, u32[]{:S(2)}) collective-permute-start(bf16[32,4608]{1,0:T(8,128)(2,1)S(1)} %collective-permute-done.2.refs_3_.refs_19_), channel_id=1, source_target_pairs={{0,2},{2,0},{1,3},{3,1},{4,6},{6,4},{5,7},{7,5},{8,10},{10,8},{9,1... | collective-permute-start | bytes 884744 | tf_op jit(solution)/shard_map/ppermute | solution.py:36
  31.3 8.6 %collective-permute-start.10 = (bf16[32,4608]{1,0:T(8,128)(2,1)S(1)}, bf16[32,4608]{1,0:T(8,128)(2,1)}, u32[]{:S(2)}, u32[]{:S(2)}) collective-permute-start(bf16[32,4608]{1,0:T(8,128)(2,1)S(1)} %collective-permute-done.6.refs_7_.refs_23_), channel_id=1, source_target_pairs={{4,0},{30,2},{8,4},{2,6},{12,8},{6,10},{16,12},{10,14},{20,16},{14... | collective-permute-start | bytes 884744 | tf_op jit(solution)/shard_map/ppermute | solution.py:47
  33.4 8.2 %collective-permute-start.14 = (bf16[32,4608]{1,0:T(8,128)(2,1)}, bf16[32,4608]{1,0:T(8,128)(2,1)S(1)}, u32[]{:S(2)}, u32[]{:S(2)}) collective-permute-start(bf16[32,4608]{1,0:T(8,128)(2,1)} %collective-permute-done.9.refs_10_.refs_26_), channel_id=1, source_target_pairs={{4,0},{30,2},{8,4},{2,6},{12,8},{6,10},{16,12},{10,14},{20,16},{14... | collective-permute-start | bytes 884744 | tf_op jit(solution)/shard_map/ppermute | solution.py:47
  33.4 10.5 %collective-permute-start.8 = (bf16[32,4608]{1,0:T(8,128)(2,1)S(1)}, bf16[32,4608]{1,0:T(8,128)(2,1)S(1)}, u32[]{:S(2)}, u32[]{:S(2)}) collective-permute-start(bf16[32,4608]{1,0:T(8,128)(2,1)S(1)} %collective-permute-done.5.refs_6_.refs_22_), channel_id=1, source_target_pairs={{0,2},{2,0},{1,3},{3,1},{4,6},{6,4},{5,7},{7,5},{8,10},{10,8},{9,1... | collective-permute-start | bytes 884744 | tf_op jit(solution)/shard_map/ppermute | solution.py:36
  39.4 11.4 %collective-permute-start.13 = (bf16[32,4608]{1,0:T(8,128)(2,1)}, bf16[32,4608]{1,0:T(8,128)(2,1)S(1)}, u32[]{:S(2)}, u32[]{:S(2)}) collective-permute-start(bf16[32,4608]{1,0:T(8,128)(2,1)} %collective-permute-done.9.refs_10_.refs_26_), channel_id=1, source_target_pairs={{0,2},{2,0},{1,3},{3,1},{4,6},{6,4},{5,7},{7,5},{8,10},{10,8},{9,1... | collective-permute-start | bytes 884744 | tf_op jit(solution)/shard_map/ppermute | solution.py:36
  39.9 11.0 %collective-permute-start.12 = (bf16[32,4608]{1,0:T(8,128)(2,1)}, bf16[32,4608]{1,0:T(8,128)(2,1)S(1)}, u32[]{:S(2)}, u32[]{:S(2)}) collective-permute-start(bf16[32,4608]{1,0:T(8,128)(2,1)} %collective-permute-done.10.refs_11_.refs_27_), channel_id=1, source_target_pairs={{0,2},{2,0},{1,3},{3,1},{4,6},{6,4},{5,7},{7,5},{8,10},{10,8},{9,1... | collective-permute-start | bytes 884744 | tf_op jit(solution)/shard_map/ppermute | solution.py:36
  41.6 9.2 %collective-permute-start.15 = (bf16[32,4608]{1,0:T(8,128)(2,1)S(1)}, bf16[32,4608]{1,0:T(8,128)(2,1)S(1)}, u32[]{:S(2)}, u32[]{:S(2)}) collective-permute-start(bf16[32,4608]{1,0:T(8,128)(2,1)S(1)} %collective-permute-done.14.refs_2_.refs_30_), channel_id=1, source_target_pairs={{0,2},{2,0},{1,3},{3,1},{4,6},{6,4},{5,7},{7,5},{8,10},{10,8},{9,1... | collective-permute-start | bytes 884744 | tf_op jit(solution)/shard_map/ppermute | solution.py:36
  48.1 8.9 %collective-permute-start.11 = (bf16[384,256]{1,0:T(8,128)(2,1)S(1)}, bf16[384,256]{1,0:T(8,128)(2,1)S(1)}, u32[]{:S(2)}, u32[]{:S(2)}) collective-permute-start(bf16[384,256]{1,0:T(8,128)(2,1)S(1)} %get-tuple-element.20), channel_id=1, source_target_pairs={{0,1},{1,0},{2,3},{3,2},{4,5},{5,4},{6,7},{7,6},{8,9},{9,8},{10,11... | collective-permute-start | bytes 589832 | tf_op jit(solution)/shard_map/ppermute | solution.py:40
  60.5 37.4 %all-to-all-start.1 = ((bf16[8,512,256]{2,1,0:T(8,128)(2,1)}), bf16[8,512,256]{2,1,0:T(8,128)(2,1)S(1)}, u32[]{:S(2)}, u32[]{:S(2)}) async-start(bf16[8,512,256]{2,1,0:T(8,128)(2,1)} %copies.3), calls=%async_computation.1 | async-start | bytes 4194304 | tf_op jit(solution)/shard_map/all_to_all | solution.py:98
  65.4 8.3 %collective-permute-start.18 = (bf16[512,256]{1,0:T(8,128)(2,1)S(1)}, bf16[512,256]{1,0:T(8,128)(2,1)S(1)}, u32[]{:S(2)}, u32[]{:S(2)}) collective-permute-start(bf16[512,256]{1,0:T(8,128)(2,1)S(1)} %bitcast.18), channel_id=1, source_target_pairs={{4,0},{30,2},{8,4},{2,6},{12,8},{6,10},{16,12},{10,14},{20,16},{14... | collective-permute-start | bytes 786440 | tf_op jit(solution)/shard_map/ppermute | solution.py:47
  65.8 10.8 %collective-permute-start.19 = (bf16[512,256]{1,0:T(8,128)(2,1)S(1)}, bf16[512,256]{1,0:T(8,128)(2,1)S(1)}, u32[]{:S(2)}, u32[]{:S(2)}) collective-permute-start(bf16[512,256]{1,0:T(8,128)(2,1)S(1)} %collective-permute-done.17.refs_1_), channel_id=1, source_target_pairs={{4,0},{30,2},{8,4},{2,6},{12,8},{6,10},{16,12},{10,14},{20,16},{14... | collective-permute-start | bytes 786440 | tf_op jit(solution)/shard_map/ppermute | solution.py:47
  73.8 6.7 %collective-permute-start.22 = (bf16[512,256]{1,0:T(8,128)(2,1)S(1)}, bf16[512,256]{1,0:T(8,128)(2,1)S(1)}, u32[]{:S(2)}, u32[]{:S(2)}) collective-permute-start(bf16[512,256]{1,0:T(8,128)(2,1)S(1)} %collective-permute-done.18.refs_2_), channel_id=1, source_target_pairs={{4,0},{30,2},{8,4},{2,6},{12,8},{6,10},{16,12},{10,14},{20,16},{14... | collective-permute-start | bytes 786440 | tf_op jit(solution)/shard_map/ppermute | solution.py:47
  76.6 8.6 %collective-permute-start.23 = (bf16[512,256]{1,0:T(8,128)(2,1)S(1)}, bf16[512,256]{1,0:T(8,128)(2,1)S(1)}, u32[]{:S(2)}, u32[]{:S(2)}) collective-permute-start(bf16[512,256]{1,0:T(8,128)(2,1)S(1)} %collective-permute-done.19.refs_3_), channel_id=1, source_target_pairs={{4,0},{30,2},{8,4},{2,6},{12,8},{6,10},{16,12},{10,14},{20,16},{14... | collective-permute-start | bytes 786440 | tf_op jit(solution)/shard_map/ppermute | solution.py:47
  80.5 6.7 %collective-permute-start.26 = (bf16[512,256]{1,0:T(8,128)(2,1)S(1)}, bf16[512,256]{1,0:T(8,128)(2,1)S(1)}, u32[]{:S(2)}, u32[]{:S(2)}) collective-permute-start(bf16[512,256]{1,0:T(8,128)(2,1)S(1)} %collective-permute-done.22.refs_6_), channel_id=1, source_target_pairs={{4,0},{30,2},{8,4},{2,6},{12,8},{6,10},{16,12},{10,14},{20,16},{14... | collective-permute-start | bytes 786440 | tf_op jit(solution)/shard_map/ppermute | solution.py:47
  80.5 12.3 %collective-permute-start.21 = (bf16[512,256]{1,0:T(8,128)(2,1)S(1)}, bf16[512,256]{1,0:T(8,128)(2,1)S(1)}, u32[]{:S(2)}, u32[]{:S(2)}) collective-permute-start(bf16[512,256]{1,0:T(8,128)(2,1)S(1)} %collective-permute-done.18.refs_2_), channel_id=1, source_target_pairs={{0,2},{2,0},{1,3},{3,1},{4,6},{6,4},{5,7},{7,5},{8,10},{10,8},{9,1... | collective-permute-start | bytes 786440 | tf_op jit(solution)/shard_map/ppermute | solution.py:36
  85.2 7.7 %collective-permute-start.20 = (bf16[512,256]{1,0:T(8,128)(2,1)S(1)}, bf16[512,256]{1,0:T(8,128)(2,1)S(1)}, u32[]{:S(2)}, u32[]{:S(2)}) collective-permute-start(bf16[512,256]{1,0:T(8,128)(2,1)S(1)} %collective-permute-done.19.refs_3_), channel_id=1, source_target_pairs={{0,2},{2,0},{1,3},{3,1},{4,6},{6,4},{5,7},{7,5},{8,10},{10,8},{9,1... | collective-permute-start | bytes 786440 | tf_op jit(solution)/shard_map/ppermute | solution.py:36
  85.2 8.1 %collective-permute-start.27 = (bf16[512,256]{1,0:T(8,128)(2,1)S(1)}, bf16[512,256]{1,0:T(8,128)(2,1)S(1)}, u32[]{:S(2)}, u32[]{:S(2)}) collective-permute-start(bf16[512,256]{1,0:T(8,128)(2,1)S(1)} %collective-permute-done.23.refs_7_), channel_id=1, source_target_pairs={{4,0},{30,2},{8,4},{2,6},{12,8},{6,10},{16,12},{10,14},{20,16},{14... | collective-permute-start | bytes 786440 | tf_op jit(solution)/shard_map/ppermute | solution.py:47
  87.3 7.6 %collective-permute-start.30 = (bf16[512,256]{1,0:T(8,128)(2,1)S(1)}, bf16[512,256]{1,0:T(8,128)(2,1)S(1)}, u32[]{:S(2)}, u32[]{:S(2)}) collective-permute-start(bf16[512,256]{1,0:T(8,128)(2,1)S(1)} %collective-permute-done.26.refs_10_), channel_id=1, source_target_pairs={{4,0},{30,2},{8,4},{2,6},{12,8},{6,10},{16,12},{10,14},{20,16},{14... | collective-permute-start | bytes 786440 | tf_op jit(solution)/shard_map/ppermute | solution.py:47
  87.3 9.5 %collective-permute-start.25 = (bf16[512,256]{1,0:T(8,128)(2,1)S(1)}, bf16[512,256]{1,0:T(8,128)(2,1)S(1)}, u32[]{:S(2)}, u32[]{:S(2)}) collective-permute-start(bf16[512,256]{1,0:T(8,128)(2,1)S(1)} %collective-permute-done.22.refs_6_), channel_id=1, source_target_pairs={{0,2},{2,0},{1,3},{3,1},{4,6},{6,4},{5,7},{7,5},{8,10},{10,8},{9,1... | collective-permute-start | bytes 786440 | tf_op jit(solution)/shard_map/ppermute | solution.py:36
  105.6 5.9 %collective-permute-start.32 = (bf16[8,32,1536]{2,1,0:T(8,128)(2,1)}, bf16[8,32,1536]{2,1,0:T(8,128)(2,1)S(1)}, u32[]{:S(2)}, u32[]{:S(2)}) collective-permute-start(bf16[8,32,1536]{2,1,0:T(8,128)(2,1)} %get-tuple-element.27), channel_id=1, source_target_pairs={{0,2},{2,0},{1,3},{3,1},{4,6},{6,4},{5,7},{7,5},{8,10},{10,8},{9,1... | collective-permute-start | bytes 2359304 | tf_op jit(solution)/shard_map/ppermute | solution.py:36
  106.0 29.1 %all-to-all-start.2 = ((bf16[8,32,3072]{2,1,0:T(8,128)(2,1)}), bf16[8,32,3072]{2,1,0:T(8,128)(2,1)S(1)}, u32[]{:S(2)}, u32[]{:S(2)}) async-start(bf16[8,32,3072]{2,1,0:T(8,128)(2,1)} %get-tuple-element.28), calls=%async_computation.2 | async-start | bytes 3145728 | tf_op jit(solution)/shard_map/all_to_all | solution.py:270
  111.7 11.0 %collective-permute-start.33 = (bf16[2,32,1536]{2,1,0:T(8,128)(2,1)S(1)}, bf16[2,32,1536]{2,1,0:T(8,128)(2,1)S(1)}, u32[]{:S(2)}, u32[]{:S(2)}) collective-permute-start(bf16[2,32,1536]{2,1,0:T(8,128)(2,1)S(1)} %get-tuple-element.29), channel_id=1, source_target_pairs={{20,0},{14,2},{24,4},{18,6},{28,8},{22,10},{0,12},{26,14},{4,16},{... | collective-permute-start | bytes 589832 | tf_op jit(solution)/shard_map/ppermute | solution.py:254
  114.7 15.4 %collective-permute-start.34 = (bf16[2,32,1536]{2,1,0:T(8,128)(2,1)S(1)}, bf16[2,32,1536]{2,1,0:T(8,128)(2,1)S(1)}, u32[]{:S(2)}, u32[]{:S(2)}) collective-permute-start(bf16[2,32,1536]{2,1,0:T(8,128)(2,1)S(1)} %get-tuple-element.31), channel_id=1, source_target_pairs={{24,0},{10,2},{28,4},{14,6},{0,8},{18,10},{4,12},{22,14},{8,16},{2... | collective-permute-start | bytes 589832 | tf_op jit(solution)/shard_map/ppermute | solution.py:254
  116.3 15.7 %collective-permute-start.35 = (bf16[2,32,1536]{2,1,0:T(8,128)(2,1)S(1)}, bf16[2,32,1536]{2,1,0:T(8,128)(2,1)S(1)}, u32[]{:S(2)}, u32[]{:S(2)}) collective-permute-start(bf16[2,32,1536]{2,1,0:T(8,128)(2,1)S(1)} %get-tuple-element.30), channel_id=1, source_target_pairs={{28,0},{6,2},{0,4},{10,6},{4,8},{14,10},{8,12},{18,14},{12,16},{22... | collective-permute-start | bytes 589832 | tf_op jit(solution)/shard_map/ppermute | solution.py:254
  116.3 15.9 %collective-permute-start.36 = (bf16[32,1536]{1,0:T(8,128)(2,1)S(1)}, bf16[32,1536]{1,0:T(8,128)(2,1)S(1)}, u32[]{:S(2)}, u32[]{:S(2)}) collective-permute-start(bf16[32,1536]{1,0:T(8,128)(2,1)S(1)} %slice_bitcast_fusion.1), channel_id=1, source_target_pairs={{16,0},{18,2},{20,4},{22,6},{24,8},{26,10},{28,12},{30,14},{0,16},... | collective-permute-start | bytes 294920 | tf_op jit(solution)/shard_map/ppermute | solution.py:254
  (36 other events, 256.3 us)

commit v10 on v8

--- a/solution.py
+++ b/solution.py
@@ -133,7 +133,11 @@
         copy.wait()
     left = x[...].reshape(count * ROWS, COLS)
     right = cols_ref[...].reshape(TILE, COLS)
-    total = lax.dot_general(left, right, (((1,), (1,)), ((), ())), preferred_element_type=f32)
+    over_columns = (((1,), (1,)), ((), ()))
+    if count * ROWS < TILE:
+        total = lax.dot_general(right, left, over_columns, preferred_element_type=f32).T
+    else:
+        total = lax.dot_general(left, right, over_columns, preferred_element_type=f32)
     own_ref[...] = total
     sent_ref[...] = total.astype(bf16)
     for copy in copies[count:]:

time: 137 us -> 137 us (level)
  no operation moved by 1% of the time
where the time goes in v10:
time: 137 us; the launch traced here: 136 us
  starting transfers between devices  63.7 us (46%)
  waiting for transfers between devices  52.9 us (39%)
  Pallas kernels  15.3 us (11%)
  local copies, waits for them, and re-layouts  2.53 us (2%)
    ppermute x14, waiting for transfers between devices, turn(): return lax.ppermute(a, (Z, C), pairs)  33.9 us
    ppermute x18, starting transfers between devices, swap(): return lax.ppermute(a, C, [(0, 1), (1, 0)])  32.1 us
    ppermute x4, waiting for transfers between devices, cast(): return lax.ppermute(a, (Z, C), pairs)  11.5 us
    ppermute x4, starting transfers between devices, cast(): return lax.ppermute(a, (Z, C), pairs)  8.95 us
    all_to_all x2, starting transfers between devices, gather_r(): return lax.all_to_all(copies, (X, YL), 0, 0, tiled=True)  8.77 us
    pallas_call x1, Pallas kernels, product_part(): pl.pallas_call(product_kernel, out_shape=(pltpu.HBM((NR, ROWS, COLS - COL...  7.69 us
    all_to_all x1, starting transfers between devices, on_device(): got = lax.all_to_all(parts, (X, YL), 0, 0, tiled=True)  5.4 us
    ppermute x14, starting transfers between devices, turn(): return lax.ppermute(a, (Z, C), pairs)  5.17 us
  transfers between devices with their start and end apart: 41, of which 17 were waited for; matrix products, arithmetic and copies ran while one was open for 0% of the time, Pallas kernels for 6%

profile of v10, /device:TPU:1, one launch (start us, length us, event | category | flops | bytes accessed | tf_op | source)
XLA Modules:
  0.0 136.2 jit_solution(13542548944116520882)
XLA Ops:
  0.0 3.2 %collective-permute-start = (bf16[32,4608]{1,0:T(8,128)(2,1)}, bf16[32,4608]{1,0:T(8,128)(2,1)S(1)}, u32[]{:S(2)}, u32[]{:S(2)}) collective-permute-start(bf16[32,4608]{1,0:T(8,128)(2,1)} %refs_16_.1), channel_id=1, source_target_pairs={{0,2},{2,0},{1,3},{3,1},{4,6},{6,4},{5,7},{7,5},{8,10},{10,8},{9,1... | collective-permute-start | bytes 884744 | tf_op jit(solution)/shard_map/ppermute | solution.py:36
  5.8 3.8 %all-to-all-start = ((bf16[8,32,4608]{2,1,0:T(8,128)(2,1)}), bf16[8,32,4608]{2,1,0:T(8,128)(2,1)S(1)}, u32[]{:S(2)}, u32[]{:S(2)}) async-start(bf16[8,32,4608]{2,1,0:T(8,128)(2,1)} %copies.2), calls=%async_computation | async-start | bytes 4718592 | tf_op jit(solution)/shard_map/all_to_all | solution.py:98
  10.9 1.6 %collective-permute-start.2 = (bf16[32,4608]{1,0:T(8,128)(2,1)S(1)}, bf16[32,4608]{1,0:T(8,128)(2,1)S(1)}, u32[]{:S(2)}, u32[]{:S(2)}) collective-permute-start(bf16[32,4608]{1,0:T(8,128)(2,1)S(1)} %collective-permute-done.refs_1_.refs_17_), channel_id=1, source_target_pairs={{4,0},{30,2},{8,4},{2,6},{12,8},{6,10},{16,12},{10,14},{20,16},{14... | collective-permute-start | bytes 884744 | tf_op jit(solution)/shard_map/ppermute | solution.py:47
  12.6 6.7 %collective-permute-done.1.refs_2_.refs_18_ = bf16[32,4608]{1,0:T(8,128)(2,1)S(1)} collective-permute-done((bf16[32,4608]{1,0:T(8,128)(2,1)S(1)}, bf16[32,4608]{1,0:T(8,128)(2,1)S(1)}, u32[]{:S(2)}, u32[]{:S(2)}) %collective-permute-start.1) | collective-permute-done | bytes 294944 | tf_op jit(solution)/shard_map/ppermute | solution.py:47
  19.3 2.9 %collective-permute-done.2.refs_3_.refs_19_ = bf16[32,4608]{1,0:T(8,128)(2,1)S(1)} collective-permute-done((bf16[32,4608]{1,0:T(8,128)(2,1)S(1)}, bf16[32,4608]{1,0:T(8,128)(2,1)S(1)}, u32[]{:S(2)}, u32[]{:S(2)}) %collective-permute-start.2) | collective-permute-done | bytes 294944 | tf_op jit(solution)/shard_map/ppermute | solution.py:47
  22.1 4.2 %collective-permute-done.5.refs_6_.refs_22_ = bf16[32,4608]{1,0:T(8,128)(2,1)S(1)} collective-permute-done((bf16[32,4608]{1,0:T(8,128)(2,1)S(1)}, bf16[32,4608]{1,0:T(8,128)(2,1)S(1)}, u32[]{:S(2)}, u32[]{:S(2)}) %collective-permute-start.5) | collective-permute-done | bytes 294944 | tf_op jit(solution)/shard_map/ppermute | solution.py:47
  26.3 4.9 %collective-permute-start.4 = (bf16[32,4608]{1,0:T(8,128)(2,1)S(1)}, bf16[32,4608]{1,0:T(8,128)(2,1)S(1)}, u32[]{:S(2)}, u32[]{:S(2)}) collective-permute-start(bf16[32,4608]{1,0:T(8,128)(2,1)S(1)} %collective-permute-done.1.refs_2_.refs_18_), channel_id=1, source_target_pairs={{0,2},{2,0},{1,3},{3,1},{4,6},{6,4},{5,7},{7,5},{8,10},{10,8},{9,1... | collective-permute-start | bytes 884744 | tf_op jit(solution)/shard_map/ppermute | solution.py:36
  31.4 2.0 %collective-permute-done.9.refs_10_.refs_26_ = bf16[32,4608]{1,0:T(8,128)(2,1)} collective-permute-done((bf16[32,4608]{1,0:T(8,128)(2,1)S(1)}, bf16[32,4608]{1,0:T(8,128)(2,1)}, u32[]{:S(2)}, u32[]{:S(2)}) %collective-permute-start.9) | collective-permute-done | bytes 294944 | tf_op jit(solution)/shard_map/ppermute | solution.py:47
  33.4 5.9 %collective-permute-start.8 = (bf16[32,4608]{1,0:T(8,128)(2,1)S(1)}, bf16[32,4608]{1,0:T(8,128)(2,1)S(1)}, u32[]{:S(2)}, u32[]{:S(2)}) collective-permute-start(bf16[32,4608]{1,0:T(8,128)(2,1)S(1)} %collective-permute-done.5.refs_6_.refs_22_), channel_id=1, source_target_pairs={{0,2},{2,0},{1,3},{3,1},{4,6},{6,4},{5,7},{7,5},{8,10},{10,8},{9,1... | collective-permute-start | bytes 884744 | tf_op jit(solution)/shard_map/ppermute | solution.py:36
  40.0 1.7 %collective-permute-done.14.refs_2_.refs_30_ = bf16[32,4608]{1,0:T(8,128)(2,1)S(1)} collective-permute-done((bf16[32,4608]{1,0:T(8,128)(2,1)}, bf16[32,4608]{1,0:T(8,128)(2,1)S(1)}, u32[]{:S(2)}, u32[]{:S(2)}) %collective-permute-start.14) | collective-permute-done | bytes 294944 | tf_op jit(solution)/shard_map/ppermute | solution.py:47
  41.6 2.3 %collective-permute-start.15 = (bf16[32,4608]{1,0:T(8,128)(2,1)S(1)}, bf16[32,4608]{1,0:T(8,128)(2,1)S(1)}, u32[]{:S(2)}, u32[]{:S(2)}) collective-permute-start(bf16[32,4608]{1,0:T(8,128)(2,1)S(1)} %collective-permute-done.14.refs_2_.refs_30_), channel_id=1, source_target_pairs={{0,2},{2,0},{1,3},{3,1},{4,6},{6,4},{5,7},{7,5},{8,10},{10,8},{9,1... | collective-permute-start | bytes 884744 | tf_op jit(solution)/shard_map/ppermute | solution.py:36
  44.7 3.5 %gram_part.2 = (f32[384,256]{1,0:T(8,128)S(1)}, bf16[384,256]{1,0:T(8,128)(2,1)S(1)}, bf16[8,32,1536]{2,1,0:T(8,128)(2,1)}) custom-call(bf16[32,4608]{1,0:T(8,128)(2,1)} %refs_16_.1, bf16[32,4608]{1,0:T(8,128)(2,1)} %copy-done.8, bf16[32,4608]{1,0:T(8,128)(2,1)} %copy-done.9, bf16[32,4608]{1,0:T(8,128)(2,1)} %copy-done.10, bf16[32,4608]{1,0:T(8,128)(2,1)} %copy-done.14, ...), custom_call_target="tpu_custom_call" | custom-call | flops 905969664 | bytes 6291456 | tf_op jit(solution)/shard_map/gram_part/pallas_call | solution.py:153
  48.1 2.7 %collective-permute-start.11 = (bf16[384,256]{1,0:T(8,128)(2,1)S(1)}, bf16[384,256]{1,0:T(8,128)(2,1)S(1)}, u32[]{:S(2)}, u32[]{:S(2)}) collective-permute-start(bf16[384,256]{1,0:T(8,128)(2,1)S(1)} %get-tuple-element.20), channel_id=1, source_target_pairs={{0,1},{1,0},{2,3},{3,2},{4,5},{5,4},{6,7},{7,6},{8,9},{9,8},{10,11... | collective-permute-start | bytes 589832 | tf_op jit(solution)/shard_map/ppermute | solution.py:40
  52.7 4.4 %collective-permute-done.16.got_b = bf16[128,256]{1,0:T(8,128)(2,1)S(1)} collective-permute-done((bf16[128,256]{1,0:T(8,128)(2,1)S(1)}, bf16[128,256]{1,0:T(8,128)(2,1)S(1)}, u32[]{:S(2)}, u32[]{:S(2)}) %collective-permute-start.16) | collective-permute-done | bytes 65568 | tf_op jit(solution)/shard_map/ppermute | solution.py:40
  57.1 1.8 %collective-permute-start.17 = (bf16[512,256]{1,0:T(8,128)(2,1)S(1)}, bf16[512,256]{1,0:T(8,128)(2,1)S(1)}, u32[]{:S(2)}, u32[]{:S(2)}) collective-permute-start(bf16[512,256]{1,0:T(8,128)(2,1)S(1)} %bitcast.16), channel_id=1, source_target_pairs={{0,2},{2,0},{1,3},{3,1},{4,6},{6,4},{5,7},{7,5},{8,10},{10,8},{9,1... | collective-permute-start | bytes 786440 | tf_op jit(solution)/shard_map/ppermute | solution.py:36
  60.4 5.0 %all-to-all-start.1 = ((bf16[8,512,256]{2,1,0:T(8,128)(2,1)}), bf16[8,512,256]{2,1,0:T(8,128)(2,1)S(1)}, u32[]{:S(2)}, u32[]{:S(2)}) async-start(bf16[8,512,256]{2,1,0:T(8,128)(2,1)} %copies.3), calls=%async_computation.1 | async-start | bytes 4194304 | tf_op jit(solution)/shard_map/all_to_all | solution.py:98
  65.8 1.6 %collective-permute-start.19 = (bf16[512,256]{1,0:T(8,128)(2,1)S(1)}, bf16[512,256]{1,0:T(8,128)(2,1)S(1)}, u32[]{:S(2)}, u32[]{:S(2)}) collective-permute-start(bf16[512,256]{1,0:T(8,128)(2,1)S(1)} %collective-permute-done.17.refs_1_), channel_id=1, source_target_pairs={{4,0},{30,2},{8,4},{2,6},{12,8},{6,10},{16,12},{10,14},{20,16},{14... | collective-permute-start | bytes 786440 | tf_op jit(solution)/shard_map/ppermute | solution.py:47
  67.4 6.3 %collective-permute-done.18.refs_2_ = bf16[512,256]{1,0:T(8,128)(2,1)S(1)} collective-permute-done((bf16[512,256]{1,0:T(8,128)(2,1)S(1)}, bf16[512,256]{1,0:T(8,128)(2,1)S(1)}, u32[]{:S(2)}, u32[]{:S(2)}) %collective-permute-start.18) | collective-permute-done | bytes 262176 | tf_op jit(solution)/shard_map/ppermute | solution.py:47
  73.8 2.8 %collective-permute-done.19.refs_3_ = bf16[512,256]{1,0:T(8,128)(2,1)S(1)} collective-permute-done((bf16[512,256]{1,0:T(8,128)(2,1)S(1)}, bf16[512,256]{1,0:T(8,128)(2,1)S(1)}, u32[]{:S(2)}, u32[]{:S(2)}) %collective-permute-start.19) | collective-permute-done | bytes 262176 | tf_op jit(solution)/shard_map/ppermute | solution.py:47
  76.6 3.9 %collective-permute-done.22.refs_6_ = bf16[512,256]{1,0:T(8,128)(2,1)S(1)} collective-permute-done((bf16[512,256]{1,0:T(8,128)(2,1)S(1)}, bf16[512,256]{1,0:T(8,128)(2,1)S(1)}, u32[]{:S(2)}, u32[]{:S(2)}) %collective-permute-start.22) | collective-permute-done | bytes 262176 | tf_op jit(solution)/shard_map/ppermute | solution.py:47
  80.5 4.7 %collective-permute-start.21 = (bf16[512,256]{1,0:T(8,128)(2,1)S(1)}, bf16[512,256]{1,0:T(8,128)(2,1)S(1)}, u32[]{:S(2)}, u32[]{:S(2)}) collective-permute-start(bf16[512,256]{1,0:T(8,128)(2,1)S(1)} %collective-permute-done.18.refs_2_), channel_id=1, source_target_pairs={{0,2},{2,0},{1,3},{3,1},{4,6},{6,4},{5,7},{7,5},{8,10},{10,8},{9,1... | collective-permute-start | bytes 786440 | tf_op jit(solution)/shard_map/ppermute | solution.py:36
  85.3 1.9 %collective-permute-done.26.refs_10_ = bf16[512,256]{1,0:T(8,128)(2,1)S(1)} collective-permute-done((bf16[512,256]{1,0:T(8,128)(2,1)S(1)}, bf16[512,256]{1,0:T(8,128)(2,1)S(1)}, u32[]{:S(2)}, u32[]{:S(2)}) %collective-permute-start.26) | collective-permute-done | bytes 262176 | tf_op jit(solution)/shard_map/ppermute | solution.py:47
  87.2 5.6 %collective-permute-start.25 = (bf16[512,256]{1,0:T(8,128)(2,1)S(1)}, bf16[512,256]{1,0:T(8,128)(2,1)S(1)}, u32[]{:S(2)}, u32[]{:S(2)}) collective-permute-start(bf16[512,256]{1,0:T(8,128)(2,1)S(1)} %collective-permute-done.22.refs_6_), channel_id=1, source_target_pairs={{0,2},{2,0},{1,3},{3,1},{4,6},{6,4},{5,7},{7,5},{8,10},{10,8},{9,1... | collective-permute-start | bytes 786440 | tf_op jit(solution)/shard_map/ppermute | solution.py:36
  94.8 1.9 %collective-permute-start.31 = (bf16[512,256]{1,0:T(8,128)(2,1)S(1)}, bf16[512,256]{1,0:T(8,128)(2,1)S(1)}, u32[]{:S(2)}, u32[]{:S(2)}) collective-permute-start(bf16[512,256]{1,0:T(8,128)(2,1)S(1)} %collective-permute-done.30.refs_14_), channel_id=1, source_target_pairs={{0,2},{2,0},{1,3},{3,1},{4,6},{6,4},{5,7},{7,5},{8,10},{10,8},{9,1... | collective-permute-start | bytes 786440 | tf_op jit(solution)/shard_map/ppermute | solution.py:36
  97.8 7.7 %product_part.1 = (bf16[8,32,3072]{2,1,0:T(8,128)(2,1)}, bf16[8,32,1536]{2,1,0:T(8,128)(2,1)}, bf16[8,32,1536]{2,1,0:T(8,128)(2,1)}) custom-call(bf16[512,256]{1,0:T(8,128)(2,1)} %bitcast.19, bf16[512,256]{1,0:T(8,128)(2,1)} %copy-done.17, bf16[512,256]{1,0:T(8,128)(2,1)} %copy-done.18, bf16[512,256]{1,0:T(8,128)(2,1)} %copy-done.19, ...), custom_call_target="tpu_custom_call" | custom-call | flops 2281701376 | bytes 14680064 | tf_op jit(solution)/shard_map/product_part/pallas_call | solution.py:228
  106.0 5.4 %all-to-all-start.2 = ((bf16[8,32,3072]{2,1,0:T(8,128)(2,1)}), bf16[8,32,3072]{2,1,0:T(8,128)(2,1)S(1)}, u32[]{:S(2)}, u32[]{:S(2)}) async-start(bf16[8,32,3072]{2,1,0:T(8,128)(2,1)} %get-tuple-element.28), calls=%async_computation.2 | async-start | bytes 3145728 | tf_op jit(solution)/shard_map/all_to_all | solution.py:275
  111.7 3.0 %collective-permute-start.33 = (bf16[2,32,1536]{2,1,0:T(8,128)(2,1)S(1)}, bf16[2,32,1536]{2,1,0:T(8,128)(2,1)S(1)}, u32[]{:S(2)}, u32[]{:S(2)}) collective-permute-start(bf16[2,32,1536]{2,1,0:T(8,128)(2,1)S(1)} %get-tuple-element.29), channel_id=1, source_target_pairs={{20,0},{14,2},{24,4},{18,6},{28,8},{22,10},{0,12},{26,14},{4,16},{... | collective-permute-start | bytes 589832 | tf_op jit(solution)/shard_map/ppermute | solution.py:259
  114.7 1.6 %collective-permute-start.34 = (bf16[2,32,1536]{2,1,0:T(8,128)(2,1)S(1)}, bf16[2,32,1536]{2,1,0:T(8,128)(2,1)S(1)}, u32[]{:S(2)}, u32[]{:S(2)}) collective-permute-start(bf16[2,32,1536]{2,1,0:T(8,128)(2,1)S(1)} %get-tuple-element.31), channel_id=1, source_target_pairs={{24,0},{10,2},{28,4},{14,6},{0,8},{18,10},{4,12},{22,14},{8,16},{2... | collective-permute-start | bytes 589832 | tf_op jit(solution)/shard_map/ppermute | solution.py:259
  116.3 4.3 %collective-permute-start.36 = (bf16[32,1536]{1,0:T(8,128)(2,1)S(1)}, bf16[32,1536]{1,0:T(8,128)(2,1)S(1)}, u32[]{:S(2)}, u32[]{:S(2)}) collective-permute-start(bf16[32,1536]{1,0:T(8,128)(2,1)S(1)} %slice_bitcast_fusion.1), channel_id=1, source_target_pairs={{16,0},{18,2},{20,4},{22,6},{24,8},{26,10},{28,12},{30,14},{0,16},... | collective-permute-start | bytes 294920 | tf_op jit(solution)/shard_map/ppermute | solution.py:259
  120.6 2.0 %collective-permute-done.33 = bf16[2,32,1536]{2,1,0:T(8,128)(2,1)S(1)} collective-permute-done((bf16[2,32,1536]{2,1,0:T(8,128)(2,1)S(1)}, bf16[2,32,1536]{2,1,0:T(8,128)(2,1)S(1)}, u32[]{:S(2)}, u32[]{:S(2)}) %collective-permute-start.33) | collective-permute-done | bytes 196640 | tf_op jit(solution)/shard_map/ppermute | solution.py:259
  122.6 7.5 %collective-permute-done.34 = bf16[2,32,1536]{2,1,0:T(8,128)(2,1)S(1)} collective-permute-done((bf16[2,32,1536]{2,1,0:T(8,128)(2,1)S(1)}, bf16[2,32,1536]{2,1,0:T(8,128)(2,1)S(1)}, u32[]{:S(2)}, u32[]{:S(2)}) %collective-permute-start.34) | collective-permute-done | bytes 196640 | tf_op jit(solution)/shard_map/ppermute | solution.py:259
  130.1 2.0 %collective-permute-done.35 = bf16[2,32,1536]{2,1,0:T(8,128)(2,1)S(1)} collective-permute-done((bf16[2,32,1536]{2,1,0:T(8,128)(2,1)S(1)}, bf16[2,32,1536]{2,1,0:T(8,128)(2,1)S(1)}, u32[]{:S(2)}, u32[]{:S(2)}) %collective-permute-start.35) | collective-permute-done | bytes 196640 | tf_op jit(solution)/shard_map/ppermute | solution.py:259
  (118 shorter events, 16.9 us)
Async XLA Ops:
  5.8 38.9 %all-to-all-start = ((bf16[8,32,4608]{2,1,0:T(8,128)(2,1)}), bf16[8,32,4608]{2,1,0:T(8,128)(2,1)S(1)}, u32[]{:S(2)}, u32[]{:S(2)}) async-start(bf16[8,32,4608]{2,1,0:T(8,128)(2,1)} %copies.2), calls=%async_computation | async-start | bytes 4718592 | tf_op jit(solution)/shard_map/all_to_all | solution.py:98
  9.5 9.7 %collective-permute-start.1 = (bf16[32,4608]{1,0:T(8,128)(2,1)S(1)}, bf16[32,4608]{1,0:T(8,128)(2,1)S(1)}, u32[]{:S(2)}, u32[]{:S(2)}) collective-permute-start(bf16[32,4608]{1,0:T(8,128)(2,1)S(1)} %copy-done.1), channel_id=1, source_target_pairs={{4,0},{30,2},{8,4},{2,6},{12,8},{6,10},{16,12},{10,14},{20,16},{14... | collective-permute-start | bytes 884744 | tf_op jit(solution)/shard_map/ppermute | solution.py:47
  10.9 11.2 %collective-permute-start.2 = (bf16[32,4608]{1,0:T(8,128)(2,1)S(1)}, bf16[32,4608]{1,0:T(8,128)(2,1)S(1)}, u32[]{:S(2)}, u32[]{:S(2)}) collective-permute-start(bf16[32,4608]{1,0:T(8,128)(2,1)S(1)} %collective-permute-done.refs_1_.refs_17_), channel_id=1, source_target_pairs={{4,0},{30,2},{8,4},{2,6},{12,8},{6,10},{16,12},{10,14},{20,16},{14... | collective-permute-start | bytes 884744 | tf_op jit(solution)/shard_map/ppermute | solution.py:47
  19.3 7.1 %collective-permute-start.5 = (bf16[32,4608]{1,0:T(8,128)(2,1)S(1)}, bf16[32,4608]{1,0:T(8,128)(2,1)S(1)}, u32[]{:S(2)}, u32[]{:S(2)}) collective-permute-start(bf16[32,4608]{1,0:T(8,128)(2,1)S(1)} %collective-permute-done.1.refs_2_.refs_18_), channel_id=1, source_target_pairs={{4,0},{30,2},{8,4},{2,6},{12,8},{6,10},{16,12},{10,14},{20,16},{14... | collective-permute-start | bytes 884744 | tf_op jit(solution)/shard_map/ppermute | solution.py:47
  22.1 9.2 %collective-permute-start.6 = (bf16[32,4608]{1,0:T(8,128)(2,1)S(1)}, bf16[32,4608]{1,0:T(8,128)(2,1)S(1)}, u32[]{:S(2)}, u32[]{:S(2)}) collective-permute-start(bf16[32,4608]{1,0:T(8,128)(2,1)S(1)} %collective-permute-done.2.refs_3_.refs_19_), channel_id=1, source_target_pairs={{4,0},{30,2},{8,4},{2,6},{12,8},{6,10},{16,12},{10,14},{20,16},{14... | collective-permute-start | bytes 884744 | tf_op jit(solution)/shard_map/ppermute | solution.py:47
  26.3 7.1 %collective-permute-start.9 = (bf16[32,4608]{1,0:T(8,128)(2,1)S(1)}, bf16[32,4608]{1,0:T(8,128)(2,1)}, u32[]{:S(2)}, u32[]{:S(2)}) collective-permute-start(bf16[32,4608]{1,0:T(8,128)(2,1)S(1)} %collective-permute-done.5.refs_6_.refs_22_), channel_id=1, source_target_pairs={{4,0},{30,2},{8,4},{2,6},{12,8},{6,10},{16,12},{10,14},{20,16},{14... | collective-permute-start | bytes 884744 | tf_op jit(solution)/shard_map/ppermute | solution.py:47
  26.3 13.0 %collective-permute-start.4 = (bf16[32,4608]{1,0:T(8,128)(2,1)S(1)}, bf16[32,4608]{1,0:T(8,128)(2,1)S(1)}, u32[]{:S(2)}, u32[]{:S(2)}) collective-permute-start(bf16[32,4608]{1,0:T(8,128)(2,1)S(1)} %collective-permute-done.1.refs_2_.refs_18_), channel_id=1, source_target_pairs={{0,2},{2,0},{1,3},{3,1},{4,6},{6,4},{5,7},{7,5},{8,10},{10,8},{9,1... | collective-permute-start | bytes 884744 | tf_op jit(solution)/shard_map/ppermute | solution.py:36
  31.3 8.1 %collective-permute-start.3 = (bf16[32,4608]{1,0:T(8,128)(2,1)S(1)}, bf16[32,4608]{1,0:T(8,128)(2,1)S(1)}, u32[]{:S(2)}, u32[]{:S(2)}) collective-permute-start(bf16[32,4608]{1,0:T(8,128)(2,1)S(1)} %collective-permute-done.2.refs_3_.refs_19_), channel_id=1, source_target_pairs={{0,2},{2,0},{1,3},{3,1},{4,6},{6,4},{5,7},{7,5},{8,10},{10,8},{9,1... | collective-permute-start | bytes 884744 | tf_op jit(solution)/shard_map/ppermute | solution.py:36
  31.3 8.6 %collective-permute-start.10 = (bf16[32,4608]{1,0:T(8,128)(2,1)S(1)}, bf16[32,4608]{1,0:T(8,128)(2,1)}, u32[]{:S(2)}, u32[]{:S(2)}) collective-permute-start(bf16[32,4608]{1,0:T(8,128)(2,1)S(1)} %collective-permute-done.6.refs_7_.refs_23_), channel_id=1, source_target_pairs={{4,0},{30,2},{8,4},{2,6},{12,8},{6,10},{16,12},{10,14},{20,16},{14... | collective-permute-start | bytes 884744 | tf_op jit(solution)/shard_map/ppermute | solution.py:47
  33.4 8.2 %collective-permute-start.14 = (bf16[32,4608]{1,0:T(8,128)(2,1)}, bf16[32,4608]{1,0:T(8,128)(2,1)S(1)}, u32[]{:S(2)}, u32[]{:S(2)}) collective-permute-start(bf16[32,4608]{1,0:T(8,128)(2,1)} %collective-permute-done.9.refs_10_.refs_26_), channel_id=1, source_target_pairs={{4,0},{30,2},{8,4},{2,6},{12,8},{6,10},{16,12},{10,14},{20,16},{14... | collective-permute-start | bytes 884744 | tf_op jit(solution)/shard_map/ppermute | solution.py:47
  33.4 10.5 %collective-permute-start.8 = (bf16[32,4608]{1,0:T(8,128)(2,1)S(1)}, bf16[32,4608]{1,0:T(8,128)(2,1)S(1)}, u32[]{:S(2)}, u32[]{:S(2)}) collective-permute-start(bf16[32,4608]{1,0:T(8,128)(2,1)S(1)} %collective-permute-done.5.refs_6_.refs_22_), channel_id=1, source_target_pairs={{0,2},{2,0},{1,3},{3,1},{4,6},{6,4},{5,7},{7,5},{8,10},{10,8},{9,1... | collective-permute-start | bytes 884744 | tf_op jit(solution)/shard_map/ppermute | solution.py:36
  39.4 11.4 %collective-permute-start.13 = (bf16[32,4608]{1,0:T(8,128)(2,1)}, bf16[32,4608]{1,0:T(8,128)(2,1)S(1)}, u32[]{:S(2)}, u32[]{:S(2)}) collective-permute-start(bf16[32,4608]{1,0:T(8,128)(2,1)} %collective-permute-done.9.refs_10_.refs_26_), channel_id=1, source_target_pairs={{0,2},{2,0},{1,3},{3,1},{4,6},{6,4},{5,7},{7,5},{8,10},{10,8},{9,1... | collective-permute-start | bytes 884744 | tf_op jit(solution)/shard_map/ppermute | solution.py:36
  39.9 11.0 %collective-permute-start.12 = (bf16[32,4608]{1,0:T(8,128)(2,1)}, bf16[32,4608]{1,0:T(8,128)(2,1)S(1)}, u32[]{:S(2)}, u32[]{:S(2)}) collective-permute-start(bf16[32,4608]{1,0:T(8,128)(2,1)} %collective-permute-done.10.refs_11_.refs_27_), channel_id=1, source_target_pairs={{0,2},{2,0},{1,3},{3,1},{4,6},{6,4},{5,7},{7,5},{8,10},{10,8},{9,1... | collective-permute-start | bytes 884744 | tf_op jit(solution)/shard_map/ppermute | solution.py:36
  41.6 9.2 %collective-permute-start.15 = (bf16[32,4608]{1,0:T(8,128)(2,1)S(1)}, bf16[32,4608]{1,0:T(8,128)(2,1)S(1)}, u32[]{:S(2)}, u32[]{:S(2)}) collective-permute-start(bf16[32,4608]{1,0:T(8,128)(2,1)S(1)} %collective-permute-done.14.refs_2_.refs_30_), channel_id=1, source_target_pairs={{0,2},{2,0},{1,3},{3,1},{4,6},{6,4},{5,7},{7,5},{8,10},{10,8},{9,1... | collective-permute-start | bytes 884744 | tf_op jit(solution)/shard_map/ppermute | solution.py:36
  48.1 8.9 %collective-permute-start.11 = (bf16[384,256]{1,0:T(8,128)(2,1)S(1)}, bf16[384,256]{1,0:T(8,128)(2,1)S(1)}, u32[]{:S(2)}, u32[]{:S(2)}) collective-permute-start(bf16[384,256]{1,0:T(8,128)(2,1)S(1)} %get-tuple-element.20), channel_id=1, source_target_pairs={{0,1},{1,0},{2,3},{3,2},{4,5},{5,4},{6,7},{7,6},{8,9},{9,8},{10,11... | collective-permute-start | bytes 589832 | tf_op jit(solution)/shard_map/ppermute | solution.py:40
  60.4 37.4 %all-to-all-start.1 = ((bf16[8,512,256]{2,1,0:T(8,128)(2,1)}), bf16[8,512,256]{2,1,0:T(8,128)(2,1)S(1)}, u32[]{:S(2)}, u32[]{:S(2)}) async-start(bf16[8,512,256]{2,1,0:T(8,128)(2,1)} %copies.3), calls=%async_computation.1 | async-start | bytes 4194304 | tf_op jit(solution)/shard_map/all_to_all | solution.py:98
  65.4 8.3 %collective-permute-start.18 = (bf16[512,256]{1,0:T(8,128)(2,1)S(1)}, bf16[512,256]{1,0:T(8,128)(2,1)S(1)}, u32[]{:S(2)}, u32[]{:S(2)}) collective-permute-start(bf16[512,256]{1,0:T(8,128)(2,1)S(1)} %bitcast.18), channel_id=1, source_target_pairs={{4,0},{30,2},{8,4},{2,6},{12,8},{6,10},{16,12},{10,14},{20,16},{14... | collective-permute-start | bytes 786440 | tf_op jit(solution)/shard_map/ppermute | solution.py:47
  65.8 10.8 %collective-permute-start.19 = (bf16[512,256]{1,0:T(8,128)(2,1)S(1)}, bf16[512,256]{1,0:T(8,128)(2,1)S(1)}, u32[]{:S(2)}, u32[]{:S(2)}) collective-permute-start(bf16[512,256]{1,0:T(8,128)(2,1)S(1)} %collective-permute-done.17.refs_1_), channel_id=1, source_target_pairs={{4,0},{30,2},{8,4},{2,6},{12,8},{6,10},{16,12},{10,14},{20,16},{14... | collective-permute-start | bytes 786440 | tf_op jit(solution)/shard_map/ppermute | solution.py:47
  73.8 6.7 %collective-permute-start.22 = (bf16[512,256]{1,0:T(8,128)(2,1)S(1)}, bf16[512,256]{1,0:T(8,128)(2,1)S(1)}, u32[]{:S(2)}, u32[]{:S(2)}) collective-permute-start(bf16[512,256]{1,0:T(8,128)(2,1)S(1)} %collective-permute-done.18.refs_2_), channel_id=1, source_target_pairs={{4,0},{30,2},{8,4},{2,6},{12,8},{6,10},{16,12},{10,14},{20,16},{14... | collective-permute-start | bytes 786440 | tf_op jit(solution)/shard_map/ppermute | solution.py:47
  76.6 8.6 %collective-permute-start.23 = (bf16[512,256]{1,0:T(8,128)(2,1)S(1)}, bf16[512,256]{1,0:T(8,128)(2,1)S(1)}, u32[]{:S(2)}, u32[]{:S(2)}) collective-permute-start(bf16[512,256]{1,0:T(8,128)(2,1)S(1)} %collective-permute-done.19.refs_3_), channel_id=1, source_target_pairs={{4,0},{30,2},{8,4},{2,6},{12,8},{6,10},{16,12},{10,14},{20,16},{14... | collective-permute-start | bytes 786440 | tf_op jit(solution)/shard_map/ppermute | solution.py:47
  80.5 6.7 %collective-permute-start.26 = (bf16[512,256]{1,0:T(8,128)(2,1)S(1)}, bf16[512,256]{1,0:T(8,128)(2,1)S(1)}, u32[]{:S(2)}, u32[]{:S(2)}) collective-permute-start(bf16[512,256]{1,0:T(8,128)(2,1)S(1)} %collective-permute-done.22.refs_6_), channel_id=1, source_target_pairs={{4,0},{30,2},{8,4},{2,6},{12,8},{6,10},{16,12},{10,14},{20,16},{14... | collective-permute-start | bytes 786440 | tf_op jit(solution)/shard_map/ppermute | solution.py:47
  80.5 12.3 %collective-permute-start.21 = (bf16[512,256]{1,0:T(8,128)(2,1)S(1)}, bf16[512,256]{1,0:T(8,128)(2,1)S(1)}, u32[]{:S(2)}, u32[]{:S(2)}) collective-permute-start(bf16[512,256]{1,0:T(8,128)(2,1)S(1)} %collective-permute-done.18.refs_2_), channel_id=1, source_target_pairs={{0,2},{2,0},{1,3},{3,1},{4,6},{6,4},{5,7},{7,5},{8,10},{10,8},{9,1... | collective-permute-start | bytes 786440 | tf_op jit(solution)/shard_map/ppermute | solution.py:36
  85.2 7.7 %collective-permute-start.20 = (bf16[512,256]{1,0:T(8,128)(2,1)S(1)}, bf16[512,256]{1,0:T(8,128)(2,1)S(1)}, u32[]{:S(2)}, u32[]{:S(2)}) collective-permute-start(bf16[512,256]{1,0:T(8,128)(2,1)S(1)} %collective-permute-done.19.refs_3_), channel_id=1, source_target_pairs={{0,2},{2,0},{1,3},{3,1},{4,6},{6,4},{5,7},{7,5},{8,10},{10,8},{9,1... | collective-permute-start | bytes 786440 | tf_op jit(solution)/shard_map/ppermute | solution.py:36
  85.2 8.1 %collective-permute-start.27 = (bf16[512,256]{1,0:T(8,128)(2,1)S(1)}, bf16[512,256]{1,0:T(8,128)(2,1)S(1)}, u32[]{:S(2)}, u32[]{:S(2)}) collective-permute-start(bf16[512,256]{1,0:T(8,128)(2,1)S(1)} %collective-permute-done.23.refs_7_), channel_id=1, source_target_pairs={{4,0},{30,2},{8,4},{2,6},{12,8},{6,10},{16,12},{10,14},{20,16},{14... | collective-permute-start | bytes 786440 | tf_op jit(solution)/shard_map/ppermute | solution.py:47
  87.2 7.6 %collective-permute-start.30 = (bf16[512,256]{1,0:T(8,128)(2,1)S(1)}, bf16[512,256]{1,0:T(8,128)(2,1)S(1)}, u32[]{:S(2)}, u32[]{:S(2)}) collective-permute-start(bf16[512,256]{1,0:T(8,128)(2,1)S(1)} %collective-permute-done.26.refs_10_), channel_id=1, source_target_pairs={{4,0},{30,2},{8,4},{2,6},{12,8},{6,10},{16,12},{10,14},{20,16},{14... | collective-permute-start | bytes 786440 | tf_op jit(solution)/shard_map/ppermute | solution.py:47
  87.2 9.5 %collective-permute-start.25 = (bf16[512,256]{1,0:T(8,128)(2,1)S(1)}, bf16[512,256]{1,0:T(8,128)(2,1)S(1)}, u32[]{:S(2)}, u32[]{:S(2)}) collective-permute-start(bf16[512,256]{1,0:T(8,128)(2,1)S(1)} %collective-permute-done.22.refs_6_), channel_id=1, source_target_pairs={{0,2},{2,0},{1,3},{3,1},{4,6},{6,4},{5,7},{7,5},{8,10},{10,8},{9,1... | collective-permute-start | bytes 786440 | tf_op jit(solution)/shard_map/ppermute | solution.py:36
  105.5 5.9 %collective-permute-start.32 = (bf16[8,32,1536]{2,1,0:T(8,128)(2,1)}, bf16[8,32,1536]{2,1,0:T(8,128)(2,1)S(1)}, u32[]{:S(2)}, u32[]{:S(2)}) collective-permute-start(bf16[8,32,1536]{2,1,0:T(8,128)(2,1)} %get-tuple-element.27), channel_id=1, source_target_pairs={{0,2},{2,0},{1,3},{3,1},{4,6},{6,4},{5,7},{7,5},{8,10},{10,8},{9,1... | collective-permute-start | bytes 2359304 | tf_op jit(solution)/shard_map/ppermute | solution.py:36
  106.0 29.1 %all-to-all-start.2 = ((bf16[8,32,3072]{2,1,0:T(8,128)(2,1)}), bf16[8,32,3072]{2,1,0:T(8,128)(2,1)S(1)}, u32[]{:S(2)}, u32[]{:S(2)}) async-start(bf16[8,32,3072]{2,1,0:T(8,128)(2,1)} %get-tuple-element.28), calls=%async_computation.2 | async-start | bytes 3145728 | tf_op jit(solution)/shard_map/all_to_all | solution.py:275
  111.7 10.9 %collective-permute-start.33 = (bf16[2,32,1536]{2,1,0:T(8,128)(2,1)S(1)}, bf16[2,32,1536]{2,1,0:T(8,128)(2,1)S(1)}, u32[]{:S(2)}, u32[]{:S(2)}) collective-permute-start(bf16[2,32,1536]{2,1,0:T(8,128)(2,1)S(1)} %get-tuple-element.29), channel_id=1, source_target_pairs={{20,0},{14,2},{24,4},{18,6},{28,8},{22,10},{0,12},{26,14},{4,16},{... | collective-permute-start | bytes 589832 | tf_op jit(solution)/shard_map/ppermute | solution.py:259
  114.7 15.4 %collective-permute-start.34 = (bf16[2,32,1536]{2,1,0:T(8,128)(2,1)S(1)}, bf16[2,32,1536]{2,1,0:T(8,128)(2,1)S(1)}, u32[]{:S(2)}, u32[]{:S(2)}) collective-permute-start(bf16[2,32,1536]{2,1,0:T(8,128)(2,1)S(1)} %get-tuple-element.31), channel_id=1, source_target_pairs={{24,0},{10,2},{28,4},{14,6},{0,8},{18,10},{4,12},{22,14},{8,16},{2... | collective-permute-start | bytes 589832 | tf_op jit(solution)/shard_map/ppermute | solution.py:259
  116.3 15.8 %collective-permute-start.35 = (bf16[2,32,1536]{2,1,0:T(8,128)(2,1)S(1)}, bf16[2,32,1536]{2,1,0:T(8,128)(2,1)S(1)}, u32[]{:S(2)}, u32[]{:S(2)}) collective-permute-start(bf16[2,32,1536]{2,1,0:T(8,128)(2,1)S(1)} %get-tuple-element.30), channel_id=1, source_target_pairs={{28,0},{6,2},{0,4},{10,6},{4,8},{14,10},{8,12},{18,14},{12,16},{22... | collective-permute-start | bytes 589832 | tf_op jit(solution)/shard_map/ppermute | solution.py:259
  116.3 16.0 %collective-permute-start.36 = (bf16[32,1536]{1,0:T(8,128)(2,1)S(1)}, bf16[32,1536]{1,0:T(8,128)(2,1)S(1)}, u32[]{:S(2)}, u32[]{:S(2)}) collective-permute-start(bf16[32,1536]{1,0:T(8,128)(2,1)S(1)} %slice_bitcast_fusion.1), channel_id=1, source_target_pairs={{16,0},{18,2},{20,4},{22,6},{24,8},{26,10},{28,12},{30,14},{0,16},... | collective-permute-start | bytes 294920 | tf_op jit(solution)/shard_map/ppermute | solution.py:259
  (36 other events, 256.1 us)
